TPU v7x, 768 devices: a whole 4x8x12 slice. The times are simulated.
768 devices in a mesh: pb: 12 (over z), pool: 64 (over y, x, core).
Axes of the slice: x: 4, y: 8, z: 12, core: 2. Of those that a mesh axis runs over, the one named last changes fastest.
Arguments:
- queries: bfloat16 [98304, 4096], P(('pb', 'pool')), may hold values from -1 to 1
- passages: bfloat16 [98304, 4096], P(('pb', 'pool')), may hold values from -1 to 1
- pool_passages: bfloat16 [1536, 4096], P(('pb', 'pool')), may hold values from -0.09375 to 0.09375
- positives: int32 [98304], P(('pb', 'pool')), may hold values from 0 to 127
- tile_ids: int32 [12, 64, 12, 2], P('pb', 'pool'), may hold values from 0 to 15
- tile_count: int32 [12, 64, 12], P('pb', 'pool'), may hold values from 1 to 2, as said below
Outputs:
- grad_queries: bfloat16 [98304, 4096], P(('pb', 'pool'))
- grad_passages: bfloat16 [98304, 4096], P(('pb', 'pool'))
- grad_pool: bfloat16 [1536, 4096], P(('pb', 'pool'))
Inputs may be any that keep to these rules, and one draw needn't show every extreme that they name: `tile_count`: every entry is at most 2; at some index of pool, one destination receives 2 slots from every source.
All inputs are finite; a program needn't handle non-finite values.
Results may differ from a plain program's by a relative error of at most 0.0041.
Values may be sent and summed in bfloat16 or wider, within the bound.
No kernel may reach another device: no remote copies, remote signals or barrier semaphores. Data moves between devices by JAX's collectives and lax.ppermute only.
A program may use at most 32 MiB of HBM per device.

v0:
```python
import jax
import jax.numpy as jnp
from jax import lax
from jax.sharding import PartitionSpec as P

TILE = 8


SHARPNESS = 50.0


def contract(left, right):
    return lax.dot_general(
        left, right, (((1,), (1,)), ((), ())), preferred_element_type=jnp.float32
    )


def transposed(left, right):
    return lax.dot_general(
        left, right, (((0,), (0,)), ((), ())), preferred_element_type=jnp.float32
    )


def body(queries, passages, pool_passages, positives, tile_ids, tile_count):
    rows, width = queries.shape
    picks = tile_ids[0, 0]
    peers, slots = picks.shape
    own_tiles = passages.reshape(rows // TILE, TILE, width)
    outgoing = own_tiles[picks]
    incoming = lax.all_to_all(outgoing, "pb", split_axis=0, concat_axis=0, tiled=True)
    hard_rows = incoming.reshape(peers * slots * TILE, width)
    live = jnp.arange(slots, dtype=jnp.int32)[None, :] < tile_count[0, 0][:, None]
    hard_mask = jnp.broadcast_to(live[:, :, None], (peers, slots, TILE)).reshape(
        peers * slots * TILE
    )
    pooled = lax.all_gather(pool_passages, "pool", axis=0, tiled=True)
    local_logit = SHARPNESS * contract(queries, passages)
    pool_logit = SHARPNESS * contract(queries, pooled)
    hard_logit = jnp.where(hard_mask[None, :], SHARPNESS * contract(queries, hard_rows), -jnp.inf)
    highest = jnp.maximum(
        jnp.max(local_logit, axis=1, keepdims=True), jnp.max(pool_logit, axis=1, keepdims=True)
    )
    highest = jnp.maximum(highest, jnp.max(hard_logit, axis=1, keepdims=True))
    local_exp = jnp.exp(local_logit - highest)
    pool_exp = jnp.exp(pool_logit - highest)
    hard_exp = jnp.exp(hard_logit - highest)
    total = (
        jnp.sum(local_exp, axis=1, keepdims=True)
        + jnp.sum(pool_exp, axis=1, keepdims=True)
        + jnp.sum(hard_exp, axis=1, keepdims=True)
    )
    target = (positives[:, None] == jnp.arange(rows, dtype=jnp.int32)[None, :]).astype(jnp.float32)
    local_weight = (local_exp / total - target).astype(jnp.bfloat16)
    pool_weight = (pool_exp / total).astype(jnp.bfloat16)
    hard_weight = (hard_exp / total).astype(jnp.bfloat16)
    grad_hard = (SHARPNESS * transposed(hard_weight, queries)).astype(jnp.bfloat16)
    returned = lax.all_to_all(
        grad_hard.reshape(peers, slots, TILE, width), "pb", split_axis=0, concat_axis=0, tiled=True
    )
    grad_query = jnp.dot(local_weight, passages, preferred_element_type=jnp.float32)
    grad_query = grad_query + jnp.dot(pool_weight, pooled, preferred_element_type=jnp.float32)
    grad_query = grad_query + jnp.dot(hard_weight, hard_rows, preferred_element_type=jnp.float32)
    grad_queries = (SHARPNESS * grad_query).astype(jnp.bfloat16)
    grad_local = SHARPNESS * transposed(local_weight, queries)
    summed = (
        grad_local.reshape(rows // TILE, TILE, width)
        .at[picks.reshape(-1)]
        .add(returned.reshape(peers * slots, TILE, width).astype(jnp.float32))
    )
    grad_passages = summed.reshape(rows, width).astype(jnp.bfloat16)
    owned = pool_passages.shape[0]
    pool_term = SHARPNESS * transposed(pool_weight, queries)
    pool_whole = lax.psum(pool_term, "pool")
    pool_mine = lax.dynamic_slice_in_dim(pool_whole, lax.axis_index("pool") * owned, owned, 0)
    grad_pool = pool_mine.astype(jnp.bfloat16)
    return (grad_queries, grad_passages, grad_pool)


def solution(mesh):
    return jax.shard_map(
        body,
        mesh=mesh,
        in_specs=(
            P(("pb", "pool"), None),
            P(("pb", "pool"), None),
            P(("pb", "pool"), None),
            P(("pb", "pool")),
            P("pb", "pool", None, None),
            P("pb", "pool", None),
        ),
        out_specs=(P(("pb", "pool"), None), P(("pb", "pool"), None), P(("pb", "pool"), None)),
        check_vma=False,
    )
```

profile of v0, /device:TPU:32, one launch (start us, length us, event | category | flops | bytes accessed | tf_op | source)
XLA Modules:
  0.0 432.6 jit_solution(5832368089098642266)
XLA Ops:
  7.2 0.0 copy-start
  7.2 0.8 compare_select_fusion
  8.0 0.1 copy.13
  8.0 0.1 reshape.132
  8.1 3.1 gather_fusion
  11.2 0.0 copy-start.7
  11.2 15.3 %all-to-all-start = ((bf16[12,2,8,4096]{3,2,1,0:T(8,128)(2,1)}), bf16[12,2,8,4096]{3,2,1,0:T(8,128)(2,1)S(1)}, u32[]{:S(2)}, u32[]{:S(2)}) async-start(bf16[12,2,8,4096]{3,2,1,0:T(8,128)(2,1)} %bitcast.35), calls=%async_computation | async-start | bytes 3145728 | tf_op jit(solution)/shard_map/all_to_all | solution.py:30
  26.5 0.0 all-gather.3.cloned.1.call-start
  26.6 0.7 all-gather.3.cloned.1.call-update
  27.3 0.0 copy-done.7
  27.3 0.1 iota_compare_fusion.1
  27.3 0.1 broadcast_in_dim.16
  27.4 0.1 broadcast_in_dim.17
  27.5 0.0 copy-done
  27.5 1.7 fusion.11
  29.2 87.7 %all-gather.3.cloned.1.call-done = bf16[64,2,4096]{2,1,0:T(2,128)(2,1)} async-done(((bf16[1,2,4096]{2,1,0:T(2,128)(2,1)}), bf16[64,2,4096]{2,1,0:T(2,128)(2,1)}) %all-gather.3.cloned.1.call-update) | async-done | bytes 1048592 | tf_op jit(solution)/shard_map/all_gather | solution.py:36
  116.9 2.2 reshape.148
  119.2 1.7 fusion.12
  120.8 0.0 all-to-all-done
  120.9 0.0 copy-start.1
  120.9 0.6 fusion.10
  121.6 1.7 fusion
  123.3 0.0 copy-done.1
  123.3 0.0 copy-start.5
  123.3 10.3 %all-to-all-start.1 = ((bf16[12,2,8,4096]{3,2,1,0:T(8,128)(2,1)}), bf16[12,2,8,4096]{3,2,1,0:T(8,128)(2,1)}, u32[]{:S(2)}, u32[]{:S(2)}) async-start(bf16[12,2,8,4096]{3,2,1,0:T(8,128)(2,1)} %bitcast.34), calls=%async_computation.1 | async-start | bytes 3145728 | tf_op jit(solution)/shard_map/all_to_all | solution.py:57
  133.6 0.0 copy-done.5
  133.6 0.0 copy-start.6
  133.6 0.1 copy.14
  133.7 0.1 reshape_squeeze.3
  133.8 1.8 convolution_multiply_fusion.1
  135.6 0.0 copy-done.6
  135.6 0.0 copy-start.3
  135.6 0.4 fusion.1
  136.1 0.8 copy-done.3
  136.9 0.0 copy-start.4
  136.9 0.5 fusion.9
  137.3 0.8 copy-done.4
  138.1 0.0 copy-start.2
  138.1 0.5 convolution_add_fusion.1
  138.6 0.9 copy-done.2
  139.5 1.4 fusion.3
  140.9 272.7 %all-reduce.1 = bf16[128,4096]{1,0:T(8,128)(2,1)} all-reduce(f32[128,4096]{1,0:T(8,128)} %convolution_multiply_fusion.1), channel_id=1, replica_groups=mesh['pb'=12,'pool'=64] {'pool'}, use_global_device_ids=true, to_apply=%region_7.8 | all-reduce | flops 524288 | bytes 3145728 | tf_op jit(solution)/shard_map/psum | solution.py:73
  413.7 1.5 dynamic-slice_convert_fusion
  415.1 0.0 all-to-all-done.1
  415.1 3.4 bitcast_convert_fusion
  418.5 6.1 %scatter_fusion = f32[16,8,4096]{2,1,0:T(8,128)S(1)} fusion(f32[16,8,4096]{2,1,0:T(8,128)S(1)} %fusion.1, s32[24]{0:T(128)S(1)} %fusion.8, f32[24,8,4096]{2,1,0:T(8,128)} %bitcast_convert_fusion), kind=kCustom, calls=%fused_computation.1 | custom fusion | flops 786432 | bytes 9437280 | tf_op jit(solution)/shard_map/scatter-add | solution.py:68
  424.6 1.1 convert_bitcast_fusion
  (6 shorter events, 0.1 us)
Async XLA Ops:
  7.2 20.4 %copy-start = (bf16[128,4096]{1,0:T(8,128)(2,1)S(1)}, bf16[128,4096]{1,0:T(8,128)(2,1)}, u32[]{:S(2)}) copy-start(bf16[128,4096]{1,0:T(8,128)(2,1)} %param.6) | copy-start | bytes 3145732
  11.2 16.0 %copy-start.7 = (s32[1,1,12]{2,1,0:T(1,128)S(1)}, s32[1,1,12]{2,1,0:T(1,128)}, u32[]{:S(2)}) copy-start(s32[1,1,12]{2,1,0:T(1,128)} %param.11) | copy-start | bytes 148
  11.2 109.6 %all-to-all-start = ((bf16[12,2,8,4096]{3,2,1,0:T(8,128)(2,1)}), bf16[12,2,8,4096]{3,2,1,0:T(8,128)(2,1)S(1)}, u32[]{:S(2)}, u32[]{:S(2)}) async-start(bf16[12,2,8,4096]{3,2,1,0:T(8,128)(2,1)} %bitcast.35), calls=%async_computation | async-start | bytes 3145728 | tf_op jit(solution)/shard_map/all_to_all | solution.py:30
  26.5 90.4 %all-gather.3.cloned.1.call-start = ((), (), s32[]{:S(2)}) async-start(), calls=%async_computation.2 | async-start | bytes 1064960 | tf_op jit(solution)/shard_map/all_gather | solution.py:36
  120.9 2.4 copy-start.1
  123.3 10.3 %copy-start.5 = (s32[1,1,12,2]{2,3,1,0:T(2,128)S(1)}, s32[1,1,12,2]{2,3,1,0:T(2,128)}, u32[]{:S(2)}) copy-start(s32[1,1,12,2]{2,3,1,0:T(2,128)} %param.10) | copy-start | bytes 292
  123.3 291.8 %all-to-all-start.1 = ((bf16[12,2,8,4096]{3,2,1,0:T(8,128)(2,1)}), bf16[12,2,8,4096]{3,2,1,0:T(8,128)(2,1)}, u32[]{:S(2)}, u32[]{:S(2)}) async-start(bf16[12,2,8,4096]{3,2,1,0:T(8,128)(2,1)} %bitcast.34), calls=%async_computation.1 | async-start | bytes 3145728 | tf_op jit(solution)/shard_map/all_to_all | solution.py:57
  133.6 2.0 copy-start.6
  135.6 1.2 copy-start.3
  136.9 1.2 copy-start.4
  138.1 1.4 copy-start.2
Sparse Core Ops, SparseCore 0:
  31.3 85.5 all-gather.2
where the time goes:
time: 434 us; the launch traced here: 433 us
  blocking collectives  273 us (63%)
  waiting for transfers between devices  88.4 us (20%)
  starting transfers between devices  25.6 us (6%)
  between operations  14.2 us (3%)
  other arithmetic  11.6 us (3%)
  matrix products  10.3 us (2%)
  local copies, waits for them, and re-layouts  9.82 us (2%)
    psum x1, blocking collectives, body(): pool_whole = lax.psum(pool_term, 'pool')  273 us
    all_gather x1, waiting for transfers between devices, body(): pooled = lax.all_gather(pool_passages, 'pool', axis=0, tiled=True)  87.7 us
    all_to_all x1, starting transfers between devices, body(): lax.all_to_all(outgoing, 'pb', split_axis=0, concat_axis=0, tiled=True)  15.3 us
    all_to_all x1, starting transfers between devices, body(): lax.all_to_all(grad_hard.reshape(peers, slots, TILE, width), 'pb', split_...  10.3 us
  transfers between devices with their start and end apart: 3, of which 1 were waited for; matrix products, arithmetic and copies ran while one was open for 3% of the time, Pallas kernels for 0%

commit v1 on v0

--- a/solution.py
+++ b/solution.py
@@ -21,19 +21,29 @@
     )
 
 
-def body(queries, passages, pool_passages, positives, tile_ids, tile_count):
+def exchange(block, bit, size):
+    return lax.ppermute(block, "pool", [(j, j ^ bit) for j in range(size)])
+
+
+def body(bits, wide, queries, passages, pool_passages, positives, tile_ids, tile_count):
     rows, width = queries.shape
     picks = tile_ids[0, 0]
     peers, slots = picks.shape
-    own_tiles = passages.reshape(rows // TILE, TILE, width)
-    outgoing = own_tiles[picks]
-    incoming = lax.all_to_all(outgoing, "pb", split_axis=0, concat_axis=0, tiled=True)
-    hard_rows = incoming.reshape(peers * slots * TILE, width)
+    hard = peers * slots * TILE
+    size = 1 << len(bits)
+    wanted = (
+        picks.reshape(-1)[:, None] * TILE + jnp.arange(TILE, dtype=jnp.int32)[None, :]
+    ).reshape(hard)
+    chosen = (wanted[:, None] == jnp.arange(rows, dtype=jnp.int32)[None, :]).astype(jnp.bfloat16)
+    outgoing = jnp.dot(chosen, passages, preferred_element_type=jnp.float32).astype(jnp.bfloat16)
+    hard_rows = lax.all_to_all(
+        outgoing.reshape(peers, slots * TILE, width), "pb", split_axis=0, concat_axis=0, tiled=True
+    ).reshape(hard, width)
     live = jnp.arange(slots, dtype=jnp.int32)[None, :] < tile_count[0, 0][:, None]
-    hard_mask = jnp.broadcast_to(live[:, :, None], (peers, slots, TILE)).reshape(
-        peers * slots * TILE
-    )
-    pooled = lax.all_gather(pool_passages, "pool", axis=0, tiled=True)
+    hard_mask = jnp.broadcast_to(live[:, :, None], (peers, slots, TILE)).reshape(hard)
+    pooled = pool_passages
+    for bit in bits:
+        pooled = jnp.concatenate([pooled, exchange(pooled, bit, size)], axis=0)
     local_logit = SHARPNESS * contract(queries, passages)
     pool_logit = SHARPNESS * contract(queries, pooled)
     hard_logit = jnp.where(hard_mask[None, :], SHARPNESS * contract(queries, hard_rows), -jnp.inf)
@@ -55,30 +65,31 @@
     hard_weight = (hard_exp / total).astype(jnp.bfloat16)
     grad_hard = (SHARPNESS * transposed(hard_weight, queries)).astype(jnp.bfloat16)
     returned = lax.all_to_all(
-        grad_hard.reshape(peers, slots, TILE, width), "pb", split_axis=0, concat_axis=0, tiled=True
-    )
+        grad_hard.reshape(peers, slots * TILE, width), "pb", split_axis=0, concat_axis=0, tiled=True
+    ).reshape(hard, width)
+    term = SHARPNESS * transposed(pool_weight, queries)
+    for bit in reversed(bits):
+        half = term.shape[0] // 2
+        sent = term[half:]
+        if bit not in wide:
+            sent = sent.astype(jnp.bfloat16)
+        term = term[:half] + exchange(sent, bit, size).astype(jnp.float32)
+    grad_pool = term.astype(jnp.bfloat16)
     grad_query = jnp.dot(local_weight, passages, preferred_element_type=jnp.float32)
     grad_query = grad_query + jnp.dot(pool_weight, pooled, preferred_element_type=jnp.float32)
     grad_query = grad_query + jnp.dot(hard_weight, hard_rows, preferred_element_type=jnp.float32)
     grad_queries = (SHARPNESS * grad_query).astype(jnp.bfloat16)
     grad_local = SHARPNESS * transposed(local_weight, queries)
-    summed = (
-        grad_local.reshape(rows // TILE, TILE, width)
-        .at[picks.reshape(-1)]
-        .add(returned.reshape(peers * slots, TILE, width).astype(jnp.float32))
-    )
-    grad_passages = summed.reshape(rows, width).astype(jnp.bfloat16)
-    owned = pool_passages.shape[0]
-    pool_term = SHARPNESS * transposed(pool_weight, queries)
-    pool_whole = lax.psum(pool_term, "pool")
-    pool_mine = lax.dynamic_slice_in_dim(pool_whole, lax.axis_index("pool") * owned, owned, 0)
-    grad_pool = pool_mine.astype(jnp.bfloat16)
+    summed = grad_local + transposed(chosen, returned)
+    grad_passages = summed.astype(jnp.bfloat16)
     return (grad_queries, grad_passages, grad_pool)
 
 
 def solution(mesh):
+    bits = (32, 16, 8, 4, 2, 1)
+    wide = (1, 8, 16, 32)
     return jax.shard_map(
-        body,
+        lambda *args: body(bits, wide, *args),
         mesh=mesh,
         in_specs=(
             P(("pb", "pool"), None),

time: 434 us -> 170 us (0.39)
  the two profiles are of different devices: /device:TPU:32 before, /device:TPU:6 now
where the time goes in v1:
time: 170 us; the launch traced here: 167 us
  starting transfers between devices  69.1 us (41%)
  waiting for transfers between devices  64.5 us (38%)
  matrix products  20.4 us (12%)
  local copies, waits for them, and re-layouts  10 us (6%)
  other arithmetic  2.2 us (1%)
    ppermute x12, starting transfers between devices, exchange(): return lax.ppermute(block, 'pool', [(j, j ^ bit) for j in range(size)])  48.4 us
    all_to_all x1, waiting for transfers between devices, body(): lax.all_to_all(grad_hard.reshape(peers, slots * TILE, width), 'pb', split...  32.3 us
    ppermute x12, waiting for transfers between devices, exchange(): return lax.ppermute(block, 'pool', [(j, j ^ bit) for j in range(size)])  27.9 us
    all_to_all x1, starting transfers between devices, body(): lax.all_to_all(outgoing.reshape(peers, slots * TILE, width), 'pb', split_...  15.3 us
    concatenate x3, local copies, waits for them, and re-layouts, body(): pooled = jnp.concatenate([pooled, exchange(pooled, bit, size)], axis=0)  8.71 us
    dot_general x4, matrix products, transposed(): lax.dot_general(left, right, (((0,), (0,)), ((), ())), preferred_element_...  7.65 us
    all_to_all x1, starting transfers between devices, body(): lax.all_to_all(grad_hard.reshape(peers, slots * TILE, width), 'pb', split...  5.4 us
    all_to_all x1, waiting for transfers between devices, body(): lax.all_to_all(outgoing.reshape(peers, slots * TILE, width), 'pb', split_...  4.35 us
  transfers between devices with their start and end apart: 14, of which 13 were waited for; matrix products, arithmetic and copies ran while one was open for 13% of the time, Pallas kernels for 0%

profile of v1, /device:TPU:6, one launch (start us, length us, event | category | flops | bytes accessed | tf_op | source)
XLA Modules:
  0.0 167.1 jit_solution(10793040300259518207)
XLA Ops:
  0.6 0.0 copy-start
  0.6 0.8 broadcast_multiply_fusion
  1.4 0.1 copy.12
  1.5 0.1 mul.43
  1.6 0.1 iota_add_fusion
  1.7 0.1 add.66
  1.8 3.0 %convolution_convert_fusion = bf16[192,4096]{1,0:T(8,128)(2,1)} fusion(bf16[128,4096]{1,0:T(8,128)(2,1)} %param.7, s32[192]{0:T(256)S(1)} %add.66), kind=kOutput, calls=%fused_computation.2 | convolution fusion | flops 202137600 | bytes 2622208 | tf_op jit(solution)/shard_map/dot_general | solution.py:38
  4.8 15.3 %all-to-all-start = ((bf16[12,16,4096]{2,1,0:T(8,128)(2,1)}), bf16[12,16,4096]{2,1,0:T(8,128)(2,1)S(1)}, u32[]{:S(2)}, u32[]{:S(2)}) async-start(bf16[12,16,4096]{2,1,0:T(8,128)(2,1)} %bitcast.21), calls=%async_computation | async-start | bytes 3145728 | tf_op jit(solution)/shard_map/all_to_all | solution.py:39
  20.1 0.0 copy-done.2
  20.1 7.7 %collective-permute-start = (bf16[2,4096]{1,0:T(2,128)(2,1)S(1)}, bf16[2,4096]{1,0:T(2,128)(2,1)S(1)}, u32[]{:S(2)}, u32[]{:S(2)}) collective-permute-start(bf16[2,4096]{1,0:T(2,128)(2,1)S(1)} %copy-done.2), channel_id=1, source_target_pairs={{0,32},{1,33},{2,34},{3,35},{4,36},{5,37},{6,38},{7,39},{8,40},{9,... | collective-permute-start | bytes 49160 | tf_op jit(solution)/shard_map/ppermute | solution.py:25
  27.8 1.8 %collective-permute-done = bf16[2,4096]{1,0:T(2,128)(2,1)S(1)} collective-permute-done((bf16[2,4096]{1,0:T(2,128)(2,1)S(1)}, bf16[2,4096]{1,0:T(2,128)(2,1)S(1)}, u32[]{:S(2)}, u32[]{:S(2)}) %collective-permute-start) | collective-permute-done | bytes 16416 | tf_op jit(solution)/shard_map/ppermute | solution.py:25
  29.6 4.5 %collective-permute-start.1 = (bf16[4,4096]{1,0:T(4,128)(2,1)S(1)}, bf16[4,4096]{1,0:T(4,128)(2,1)S(1)}, u32[]{:S(2)}, u32[]{:S(2)}) collective-permute-start(bf16[4,4096]{1,0:T(4,128)(2,1)S(1)} %pad_maximum_fusion.2), channel_id=1, source_target_pairs={{0,16},{1,17},{2,18},{3,19},{4,20},{5,21},{6,22},{7,23},{8,24},{9,... | collective-permute-start | bytes 98312 | tf_op jit(solution)/shard_map/ppermute | solution.py:25
  34.1 2.2 %collective-permute-done.1 = bf16[4,4096]{1,0:T(4,128)(2,1)S(1)} collective-permute-done((bf16[4,4096]{1,0:T(4,128)(2,1)S(1)}, bf16[4,4096]{1,0:T(4,128)(2,1)S(1)}, u32[]{:S(2)}, u32[]{:S(2)}) %collective-permute-start.1) | collective-permute-done | bytes 32800 | tf_op jit(solution)/shard_map/ppermute | solution.py:25
  36.4 0.1 pad_maximum_fusion.1
  36.4 3.5 %collective-permute-start.2 = (bf16[8,4096]{1,0:T(8,128)(2,1)S(1)}, bf16[8,4096]{1,0:T(8,128)(2,1)S(1)}, u32[]{:S(2)}, u32[]{:S(2)}) collective-permute-start(bf16[8,4096]{1,0:T(8,128)(2,1)S(1)} %pad_maximum_fusion.1), channel_id=1, source_target_pairs={{0,8},{1,9},{2,10},{3,11},{4,12},{5,13},{6,14},{7,15},{8,0},{9,1},... | collective-permute-start | bytes 196616 | tf_op jit(solution)/shard_map/ppermute | solution.py:25
  39.9 2.7 %collective-permute-done.2 = bf16[8,4096]{1,0:T(8,128)(2,1)S(1)} collective-permute-done((bf16[8,4096]{1,0:T(8,128)(2,1)S(1)}, bf16[8,4096]{1,0:T(8,128)(2,1)S(1)}, u32[]{:S(2)}, u32[]{:S(2)}) %collective-permute-start.2) | collective-permute-done | bytes 65568 | tf_op jit(solution)/shard_map/ppermute | solution.py:25
  42.6 0.1 pad_maximum_fusion
  42.7 3.3 %collective-permute-start.3 = (bf16[16,4096]{1,0:T(8,128)(2,1)S(1)}, bf16[16,4096]{1,0:T(8,128)(2,1)S(1)}, u32[]{:S(2)}, u32[]{:S(2)}) collective-permute-start(bf16[16,4096]{1,0:T(8,128)(2,1)S(1)} %pad_maximum_fusion), channel_id=1, source_target_pairs={{0,4},{1,5},{2,6},{3,7},{4,0},{5,1},{6,2},{7,3},{8,12},{9,13},{10,... | collective-permute-start | bytes 393224 | tf_op jit(solution)/shard_map/ppermute | solution.py:25
  46.0 5.0 %collective-permute-done.3 = bf16[16,4096]{1,0:T(8,128)(2,1)S(1)} collective-permute-done((bf16[16,4096]{1,0:T(8,128)(2,1)S(1)}, bf16[16,4096]{1,0:T(8,128)(2,1)S(1)}, u32[]{:S(2)}, u32[]{:S(2)}) %collective-permute-start.3) | collective-permute-done | bytes 131104 | tf_op jit(solution)/shard_map/ppermute | solution.py:25
  51.0 0.1 concatenate.26
  51.1 2.7 %collective-permute-start.4 = (bf16[32,4096]{1,0:T(8,128)(2,1)S(1)}, bf16[32,4096]{1,0:T(8,128)(2,1)S(1)}, u32[]{:S(2)}, u32[]{:S(2)}) collective-permute-start(bf16[32,4096]{1,0:T(8,128)(2,1)S(1)} %concatenate.26), channel_id=1, source_target_pairs={{0,2},{1,3},{2,0},{3,1},{4,6},{5,7},{6,4},{7,5},{8,10},{9,11},{10,... | collective-permute-start | bytes 786440 | tf_op jit(solution)/shard_map/ppermute | solution.py:25
  53.9 5.5 %collective-permute-done.4 = bf16[32,4096]{1,0:T(8,128)(2,1)S(1)} collective-permute-done((bf16[32,4096]{1,0:T(8,128)(2,1)S(1)}, bf16[32,4096]{1,0:T(8,128)(2,1)S(1)}, u32[]{:S(2)}, u32[]{:S(2)}) %collective-permute-start.4) | collective-permute-done | bytes 262176 | tf_op jit(solution)/shard_map/ppermute | solution.py:25
  59.4 2.7 %concatenate.27 = bf16[64,4096]{1,0:T(8,128)(2,1)} concatenate(bf16[2,4096]{1,0:T(2,128)(2,1)S(1)} %copy-done.2, bf16[2,4096]{1,0:T(2,128)(2,1)S(1)} %collective-permute-done, bf16[4,4096]{1,0:T(4,128)(2,1)S(1)} %collective-permute-done.1, bf16[8,4096]{1,0:T(8,128)(2,1)S(1)} %collective-permute-done.2, bf16[16,4096]{1,0:T(8,128)(2,1)S(1)} %collective-permute-done.3, ...), dimensions={0} | concatenate | bytes 1048576 | tf_op jit(solution)/shard_map/concatenate | solution.py:46
  62.1 1.9 %collective-permute-start.5 = (bf16[64,4096]{1,0:T(8,128)(2,1)}, bf16[64,4096]{1,0:T(8,128)(2,1)}, u32[]{:S(2)}, u32[]{:S(2)}) collective-permute-start(bf16[64,4096]{1,0:T(8,128)(2,1)} %concatenate.27), channel_id=1, source_target_pairs={{0,1},{1,0},{2,3},{3,2},{4,5},{5,4},{6,7},{7,6},{8,9},{9,8},{10,11... | collective-permute-start | bytes 1572872 | tf_op jit(solution)/shard_map/ppermute | solution.py:25
  64.0 0.0 copy-done.4
  64.1 0.1 iota_compare_fusion.4
  64.1 0.1 broadcast_in_dim.16
  64.2 0.1 broadcast_in_dim.17
  64.3 0.0 copy-done
  64.3 1.7 %fusion.13 = (f32[128]{0:T(128)S(1)}, f32[128,128]{0,1:T(8,128)S(1)}) fusion(bf16[128,4096]{1,0:T(8,128)(2,1)S(1)} %copy-done, bf16[128,4096]{1,0:T(8,128)(2,1)} %param.7), kind=kOutput, calls=%fused_computation.47 | convolution fusion | flops 134250368 | bytes 2163200 | tf_op jit(solution)/shard_map/dot_general | solution.py:13
  66.0 0.3 collective-permute-done.5
  66.3 5.9 %concatenate.28 = bf16[128,4096]{1,0:T(8,128)(2,1)} concatenate(bf16[2,4096]{1,0:T(2,128)(2,1)S(1)} %copy-done.2, bf16[2,4096]{1,0:T(2,128)(2,1)S(1)} %collective-permute-done, bf16[4,4096]{1,0:T(4,128)(2,1)S(1)} %collective-permute-done.1, bf16[8,4096]{1,0:T(8,128)(2,1)S(1)} %collective-permute-done.2, bf16[16,4096]{1,0:T(8,128)(2,1)S(1)} %collective-permute-done.3, ...), dimensions={0} | concatenate | bytes 2097152 | tf_op jit(solution)/shard_map/concatenate | solution.py:46
  72.1 1.7 %fusion.14 = (f32[128]{0:T(128)S(1)}, f32[128,128]{0,1:T(8,128)S(1)}) fusion(bf16[128,4096]{1,0:T(8,128)(2,1)} %concatenate.28, bf16[128,4096]{1,0:T(8,128)(2,1)S(1)} %copy-done), kind=kOutput, calls=%fused_computation.48 | convolution fusion | flops 134250368 | bytes 2163200 | tf_op jit(solution)/shard_map/dot_general | solution.py:13
  73.9 4.4 %all-to-all-done = bf16[12,16,4096]{2,1,0:T(8,128)(2,1)S(1)} async-done(((bf16[12,16,4096]{2,1,0:T(8,128)(2,1)}), bf16[12,16,4096]{2,1,0:T(8,128)(2,1)S(1)}, u32[]{:S(2)}, u32[]{:S(2)}) %all-to-all-start) | async-done | bytes 1572896 | tf_op jit(solution)/shard_map/all_to_all | solution.py:39
  78.2 0.6 fusion.12
  78.9 0.2 fusion.7
  79.1 0.6 convolution_multiply_fusion.1
  79.6 0.1 slice.51
  79.7 0.0 copy-start.1
  79.7 0.0 copy-start.3
  79.7 2.1 %collective-permute-start.6 = (f32[64,4096]{1,0:T(8,128)S(1)}, f32[64,4096]{1,0:T(8,128)S(1)}, u32[]{:S(2)}, u32[]{:S(2)}) collective-permute-start(f32[64,4096]{1,0:T(8,128)S(1)} %slice.51), channel_id=1, source_target_pairs={{0,1},{1,0},{2,3},{3,2},{4,5},{5,4},{6,7},{7,6},{8,9},{9,8},{10,11... | collective-permute-start | bytes 3145736 | tf_op jit(solution)/shard_map/ppermute | solution.py:25
  81.8 2.6 %collective-permute-done.6 = f32[64,4096]{1,0:T(8,128)S(1)} collective-permute-done((f32[64,4096]{1,0:T(8,128)S(1)}, f32[64,4096]{1,0:T(8,128)S(1)}, u32[]{:S(2)}, u32[]{:S(2)}) %collective-permute-start.6) | collective-permute-done | bytes 1048608 | tf_op jit(solution)/shard_map/ppermute | solution.py:25
  84.4 0.1 slice_add_fusion
  84.6 2.7 %collective-permute-start.7 = (bf16[32,4096]{1,0:T(8,128)(2,1)S(1)}, bf16[32,4096]{1,0:T(8,128)(2,1)S(1)}, u32[]{:S(2)}, u32[]{:S(2)}) collective-permute-start(bf16[32,4096]{1,0:T(8,128)(2,1)S(1)} %slice.72), channel_id=1, source_target_pairs={{0,2},{1,3},{2,0},{3,1},{4,6},{5,7},{6,4},{7,5},{8,10},{9,11},{10,... | collective-permute-start | bytes 786440 | tf_op jit(solution)/shard_map/ppermute | solution.py:25
  87.3 0.0 copy-done.1
  87.3 1.8 %fusion.11 = f32[128,4096]{1,0:T(8,128)} fusion(bf16[128,4096]{1,0:T(8,128)(2,1)S(1)} %copy-done.1, f32[128,128]{0,1:T(8,128)S(1)} %get-tuple-element.8, s32[128]{0:T(128)S(1)} %copy-done.3, f32[128]{0:T(128)S(1)} %add_add_fusion, f32[128]{0:T(128)S(1)} %maximum_maximum_fusion), kind=kOutput, calls=%fused_computation.45 | convolution fusion | flops 134316032 | bytes 3212800 | tf_op jit(solution)/shard_map/dot_general | solution.py:78
  89.2 5.7 %collective-permute-done.7 = bf16[32,4096]{1,0:T(8,128)(2,1)S(1)} collective-permute-done((bf16[32,4096]{1,0:T(8,128)(2,1)S(1)}, bf16[32,4096]{1,0:T(8,128)(2,1)S(1)}, u32[]{:S(2)}, u32[]{:S(2)}) %collective-permute-start.7) | collective-permute-done | bytes 262176 | tf_op jit(solution)/shard_map/ppermute | solution.py:25
  94.9 0.7 slice.73
  95.5 3.3 %collective-permute-start.8 = (bf16[16,4096]{1,0:T(8,128)(2,1)}, bf16[16,4096]{1,0:T(8,128)(2,1)S(1)}, u32[]{:S(2)}, u32[]{:S(2)}) collective-permute-start(bf16[16,4096]{1,0:T(8,128)(2,1)} %slice.73), channel_id=1, source_target_pairs={{0,4},{1,5},{2,6},{3,7},{4,0},{5,1},{6,2},{7,3},{8,12},{9,13},{10,... | collective-permute-start | bytes 393224 | tf_op jit(solution)/shard_map/ppermute | solution.py:25
  98.8 1.7 %fusion = bf16[192,4096]{1,0:T(8,128)(2,1)} fusion(bf16[128,4096]{1,0:T(8,128)(2,1)S(1)} %copy-done, f32[192,128]{1,0:T(8,128)S(1)} %get-tuple-element.6, f32[128]{0:T(128)S(1)} %add_add_fusion, f32[128]{0:T(128)S(1)} %maximum_maximum_fusion), kind=kOutput, calls=%fused_computation.1 | convolution fusion | flops 202973184 | bytes 2720768 | tf_op jit(solution)/shard_map/dot_general | solution.py:19
  100.6 5.4 %all-to-all-start.1 = ((bf16[12,16,4096]{2,1,0:T(8,128)(2,1)}), bf16[12,16,4096]{2,1,0:T(8,128)(2,1)}, u32[]{:S(2)}, u32[]{:S(2)}) async-start(bf16[12,16,4096]{2,1,0:T(8,128)(2,1)} %bitcast.22), calls=%async_computation.1 | async-start | bytes 3145728 | tf_op jit(solution)/shard_map/all_to_all | solution.py:67
  106.0 0.0 collective-permute-done.8
  106.0 3.5 %collective-permute-start.9 = (f32[8,4096]{1,0:T(8,128)S(1)}, f32[8,4096]{1,0:T(8,128)S(1)}, u32[]{:S(2)}, u32[]{:S(2)}) collective-permute-start(f32[8,4096]{1,0:T(8,128)S(1)} %slice.57), channel_id=1, source_target_pairs={{0,8},{1,9},{2,10},{3,11},{4,12},{5,13},{6,14},{7,15},{8,0},{9,1},... | collective-permute-start | bytes 393224 | tf_op jit(solution)/shard_map/ppermute | solution.py:25
  109.5 2.4 %convolution_add_fusion.2 = f32[128,4096]{1,0:T(8,128)S(1)} fusion(f32[128,4096]{1,0:T(8,128)} %fusion.11, bf16[128,4096]{1,0:T(8,128)(2,1)} %concatenate.28, f32[128,128]{0,1:T(8,128)S(1)} %get-tuple-element.10, f32[128]{0:T(128)S(1)} %add_add_fusion, f32[128]{0:T(128)S(1)} %maximum_maximum_fusion), kind=kOutput, calls=%fused_computation.8 | convolution fusion | flops 134791168 | bytes 5309440 | tf_op jit(solution)/shard_map/dot_general | solution.py:79
  111.9 1.0 collective-permute-done.9
  112.9 4.5 %collective-permute-start.10 = (f32[4,4096]{1,0:T(4,128)S(1)}, f32[4,4096]{1,0:T(4,128)S(1)}, u32[]{:S(2)}, u32[]{:S(2)}) collective-permute-start(f32[4,4096]{1,0:T(4,128)S(1)} %slice.59), channel_id=1, source_target_pairs={{0,16},{1,17},{2,18},{3,19},{4,20},{5,21},{6,22},{7,23},{8,24},{9,... | collective-permute-start | bytes 196616 | tf_op jit(solution)/shard_map/ppermute | solution.py:25
  117.5 1.5 fusion.2
  119.0 1.0 collective-permute-done.10
  120.0 8.7 %collective-permute-start.11 = (f32[2,4096]{1,0:T(2,128)S(1)}, f32[2,4096]{1,0:T(2,128)S(1)}, u32[]{:S(2)}, u32[]{:S(2)}) collective-permute-start(f32[2,4096]{1,0:T(2,128)S(1)} %slice.61), channel_id=1, source_target_pairs={{0,32},{1,33},{2,34},{3,35},{4,36},{5,37},{6,38},{7,39},{8,40},{9,... | collective-permute-start | bytes 98312 | tf_op jit(solution)/shard_map/ppermute | solution.py:25
  128.7 1.8 %convolution_multiply_fusion.2 = f32[128,4096]{1,0:T(8,128)} fusion(bf16[128,4096]{1,0:T(8,128)(2,1)S(1)} %copy-done, f32[128,128]{0,1:T(8,128)S(1)} %get-tuple-element.8, s32[128]{0:T(128)S(1)} %copy-done.3, f32[128]{0:T(128)S(1)} %add_add_fusion, f32[128]{0:T(128)S(1)} %maximum_maximum_fusion), kind=kOutput, calls=%fused_computation.5 | convolution fusion | flops 134840320 | bytes 3212800 | tf_op jit(solution)/shard_map/dot_general | solution.py:19
  130.5 0.1 collective-permute-done.11
  130.6 0.6 fusion.10
  131.2 32.3 %all-to-all-done.1 = bf16[12,16,4096]{2,1,0:T(8,128)(2,1)} async-done(((bf16[12,16,4096]{2,1,0:T(8,128)(2,1)}), bf16[12,16,4096]{2,1,0:T(8,128)(2,1)}, u32[]{:S(2)}, u32[]{:S(2)}) %all-to-all-start.1) | async-done | bytes 1572896 | tf_op jit(solution)/shard_map/all_to_all | solution.py:67
  163.5 3.6 %fusion.3 = bf16[128,4096]{1,0:T(8,128)(2,1)} fusion(f32[128,4096]{1,0:T(8,128)} %convolution_multiply_fusion.2, bf16[192,4096]{1,0:T(8,128)(2,1)} %bitcast.4, s32[192]{0:T(256)S(1)} %add.66), kind=kOutput, calls=%fused_computation.10 | convolution fusion | flops 202399744 | bytes 4719360 | tf_op jit(solution)/shard_map/dot_general | solution.py:19
  (15 shorter events, 0.3 us)
Async XLA Ops:
  0.6 63.7 %copy-start = (bf16[128,4096]{1,0:T(8,128)(2,1)S(1)}, bf16[128,4096]{1,0:T(8,128)(2,1)}, u32[]{:S(2)}) copy-start(bf16[128,4096]{1,0:T(8,128)(2,1)} %param.6) | copy-start | bytes 3145732
  4.7 15.3 %copy-start.2 = (bf16[2,4096]{1,0:T(2,128)(2,1)S(1)}, bf16[2,4096]{1,0:T(2,128)(2,1)}, u32[]{:S(2)}) copy-start(bf16[2,4096]{1,0:T(2,128)(2,1)} %param.8) | copy-start | bytes 49156
  4.8 59.3 %copy-start.4 = (s32[1,1,12]{2,1,0:T(1,128)S(1)}, s32[1,1,12]{2,1,0:T(1,128)}, u32[]{:S(2)}) copy-start(s32[1,1,12]{2,1,0:T(1,128)} %param.11) | copy-start | bytes 148
  4.8 73.5 %all-to-all-start = ((bf16[12,16,4096]{2,1,0:T(8,128)(2,1)}), bf16[12,16,4096]{2,1,0:T(8,128)(2,1)S(1)}, u32[]{:S(2)}, u32[]{:S(2)}) async-start(bf16[12,16,4096]{2,1,0:T(8,128)(2,1)} %bitcast.21), calls=%async_computation | async-start | bytes 3145728 | tf_op jit(solution)/shard_map/all_to_all | solution.py:39
  20.1 9.5 %collective-permute-start = (bf16[2,4096]{1,0:T(2,128)(2,1)S(1)}, bf16[2,4096]{1,0:T(2,128)(2,1)S(1)}, u32[]{:S(2)}, u32[]{:S(2)}) collective-permute-start(bf16[2,4096]{1,0:T(2,128)(2,1)S(1)} %copy-done.2), channel_id=1, source_target_pairs={{0,32},{1,33},{2,34},{3,35},{4,36},{5,37},{6,38},{7,39},{8,40},{9,... | collective-permute-start | bytes 49160 | tf_op jit(solution)/shard_map/ppermute | solution.py:25
  29.6 6.7 %collective-permute-start.1 = (bf16[4,4096]{1,0:T(4,128)(2,1)S(1)}, bf16[4,4096]{1,0:T(4,128)(2,1)S(1)}, u32[]{:S(2)}, u32[]{:S(2)}) collective-permute-start(bf16[4,4096]{1,0:T(4,128)(2,1)S(1)} %pad_maximum_fusion.2), channel_id=1, source_target_pairs={{0,16},{1,17},{2,18},{3,19},{4,20},{5,21},{6,22},{7,23},{8,24},{9,... | collective-permute-start | bytes 98312 | tf_op jit(solution)/shard_map/ppermute | solution.py:25
  36.4 6.2 %collective-permute-start.2 = (bf16[8,4096]{1,0:T(8,128)(2,1)S(1)}, bf16[8,4096]{1,0:T(8,128)(2,1)S(1)}, u32[]{:S(2)}, u32[]{:S(2)}) collective-permute-start(bf16[8,4096]{1,0:T(8,128)(2,1)S(1)} %pad_maximum_fusion.1), channel_id=1, source_target_pairs={{0,8},{1,9},{2,10},{3,11},{4,12},{5,13},{6,14},{7,15},{8,0},{9,1},... | collective-permute-start | bytes 196616 | tf_op jit(solution)/shard_map/ppermute | solution.py:25
  42.7 8.4 %collective-permute-start.3 = (bf16[16,4096]{1,0:T(8,128)(2,1)S(1)}, bf16[16,4096]{1,0:T(8,128)(2,1)S(1)}, u32[]{:S(2)}, u32[]{:S(2)}) collective-permute-start(bf16[16,4096]{1,0:T(8,128)(2,1)S(1)} %pad_maximum_fusion), channel_id=1, source_target_pairs={{0,4},{1,5},{2,6},{3,7},{4,0},{5,1},{6,2},{7,3},{8,12},{9,13},{10,... | collective-permute-start | bytes 393224 | tf_op jit(solution)/shard_map/ppermute | solution.py:25
  51.1 8.3 %collective-permute-start.4 = (bf16[32,4096]{1,0:T(8,128)(2,1)S(1)}, bf16[32,4096]{1,0:T(8,128)(2,1)S(1)}, u32[]{:S(2)}, u32[]{:S(2)}) collective-permute-start(bf16[32,4096]{1,0:T(8,128)(2,1)S(1)} %concatenate.26), channel_id=1, source_target_pairs={{0,2},{1,3},{2,0},{3,1},{4,6},{5,7},{6,4},{7,5},{8,10},{9,11},{10,... | collective-permute-start | bytes 786440 | tf_op jit(solution)/shard_map/ppermute | solution.py:25
  62.1 4.1 %collective-permute-start.5 = (bf16[64,4096]{1,0:T(8,128)(2,1)}, bf16[64,4096]{1,0:T(8,128)(2,1)}, u32[]{:S(2)}, u32[]{:S(2)}) collective-permute-start(bf16[64,4096]{1,0:T(8,128)(2,1)} %concatenate.27), channel_id=1, source_target_pairs={{0,1},{1,0},{2,3},{3,2},{4,5},{5,4},{6,7},{7,6},{8,9},{9,8},{10,11... | collective-permute-start | bytes 1572872 | tf_op jit(solution)/shard_map/ppermute | solution.py:25
  79.7 7.6 %copy-start.1 = (bf16[128,4096]{1,0:T(8,128)(2,1)S(1)}, bf16[128,4096]{1,0:T(8,128)(2,1)}, u32[]{:S(2)}) copy-start(bf16[128,4096]{1,0:T(8,128)(2,1)} %param.7) | copy-start | bytes 3145732
  79.7 7.6 %copy-start.3 = (s32[128]{0:T(128)S(1)}, s32[128]{0:T(128)}, u32[]{:S(2)}) copy-start(s32[128]{0:T(128)} %param.9) | copy-start | bytes 1540
  79.7 4.7 %collective-permute-start.6 = (f32[64,4096]{1,0:T(8,128)S(1)}, f32[64,4096]{1,0:T(8,128)S(1)}, u32[]{:S(2)}, u32[]{:S(2)}) collective-permute-start(f32[64,4096]{1,0:T(8,128)S(1)} %slice.51), channel_id=1, source_target_pairs={{0,1},{1,0},{2,3},{3,2},{4,5},{5,4},{6,7},{7,6},{8,9},{9,8},{10,11... | collective-permute-start | bytes 3145736 | tf_op jit(solution)/shard_map/ppermute | solution.py:25
  84.6 10.2 %collective-permute-start.7 = (bf16[32,4096]{1,0:T(8,128)(2,1)S(1)}, bf16[32,4096]{1,0:T(8,128)(2,1)S(1)}, u32[]{:S(2)}, u32[]{:S(2)}) collective-permute-start(bf16[32,4096]{1,0:T(8,128)(2,1)S(1)} %slice.72), channel_id=1, source_target_pairs={{0,2},{1,3},{2,0},{3,1},{4,6},{5,7},{6,4},{7,5},{8,10},{9,11},{10,... | collective-permute-start | bytes 786440 | tf_op jit(solution)/shard_map/ppermute | solution.py:25
  95.5 10.4 %collective-permute-start.8 = (bf16[16,4096]{1,0:T(8,128)(2,1)}, bf16[16,4096]{1,0:T(8,128)(2,1)S(1)}, u32[]{:S(2)}, u32[]{:S(2)}) collective-permute-start(bf16[16,4096]{1,0:T(8,128)(2,1)} %slice.73), channel_id=1, source_target_pairs={{0,4},{1,5},{2,6},{3,7},{4,0},{5,1},{6,2},{7,3},{8,12},{9,13},{10,... | collective-permute-start | bytes 393224 | tf_op jit(solution)/shard_map/ppermute | solution.py:25
  100.6 62.9 %all-to-all-start.1 = ((bf16[12,16,4096]{2,1,0:T(8,128)(2,1)}), bf16[12,16,4096]{2,1,0:T(8,128)(2,1)}, u32[]{:S(2)}, u32[]{:S(2)}) async-start(bf16[12,16,4096]{2,1,0:T(8,128)(2,1)} %bitcast.22), calls=%async_computation.1 | async-start | bytes 3145728 | tf_op jit(solution)/shard_map/all_to_all | solution.py:67
  106.0 6.9 %collective-permute-start.9 = (f32[8,4096]{1,0:T(8,128)S(1)}, f32[8,4096]{1,0:T(8,128)S(1)}, u32[]{:S(2)}, u32[]{:S(2)}) collective-permute-start(f32[8,4096]{1,0:T(8,128)S(1)} %slice.57), channel_id=1, source_target_pairs={{0,8},{1,9},{2,10},{3,11},{4,12},{5,13},{6,14},{7,15},{8,0},{9,1},... | collective-permute-start | bytes 393224 | tf_op jit(solution)/shard_map/ppermute | solution.py:25
  112.9 7.1 %collective-permute-start.10 = (f32[4,4096]{1,0:T(4,128)S(1)}, f32[4,4096]{1,0:T(4,128)S(1)}, u32[]{:S(2)}, u32[]{:S(2)}) collective-permute-start(f32[4,4096]{1,0:T(4,128)S(1)} %slice.59), channel_id=1, source_target_pairs={{0,16},{1,17},{2,18},{3,19},{4,20},{5,21},{6,22},{7,23},{8,24},{9,... | collective-permute-start | bytes 196616 | tf_op jit(solution)/shard_map/ppermute | solution.py:25
  120.0 10.5 %collective-permute-start.11 = (f32[2,4096]{1,0:T(2,128)S(1)}, f32[2,4096]{1,0:T(2,128)S(1)}, u32[]{:S(2)}, u32[]{:S(2)}) collective-permute-start(f32[2,4096]{1,0:T(2,128)S(1)} %slice.61), channel_id=1, source_target_pairs={{0,32},{1,33},{2,34},{3,35},{4,36},{5,37},{6,38},{7,39},{8,40},{9,... | collective-permute-start | bytes 98312 | tf_op jit(solution)/shard_map/ppermute | solution.py:25

commit v2 on v1

--- a/solution.py
+++ b/solution.py
@@ -21,16 +21,19 @@
     )
 
 
-def exchange(block, bit, size):
-    return lax.ppermute(block, "pool", [(j, j ^ bit) for j in range(size)])
+def shifts(block, step, count, move, sign):
+    def moved(j):
+        digit = j // step % count
+        return j + ((digit + sign * move) % count - digit) * step
+
+    return lax.ppermute(block, "pool", [(j, moved(j)) for j in range(lax.axis_size("pool"))])
 
 
-def body(bits, wide, queries, passages, pool_passages, positives, tile_ids, tile_count):
+def body(digits, queries, passages, pool_passages, positives, tile_ids, tile_count):
     rows, width = queries.shape
     picks = tile_ids[0, 0]
     peers, slots = picks.shape
     hard = peers * slots * TILE
-    size = 1 << len(bits)
     wanted = (
         picks.reshape(-1)[:, None] * TILE + jnp.arange(TILE, dtype=jnp.int32)[None, :]
     ).reshape(hard)
@@ -42,8 +45,10 @@
     live = jnp.arange(slots, dtype=jnp.int32)[None, :] < tile_count[0, 0][:, None]
     hard_mask = jnp.broadcast_to(live[:, :, None], (peers, slots, TILE)).reshape(hard)
     pooled = pool_passages
-    for bit in bits:
-        pooled = jnp.concatenate([pooled, exchange(pooled, bit, size)], axis=0)
+    for step, count, _ in digits:
+        pooled = jnp.concatenate(
+            [pooled] + [shifts(pooled, step, count, m, -1) for m in range(1, count)], axis=0
+        )
     local_logit = SHARPNESS * contract(queries, passages)
     pool_logit = SHARPNESS * contract(queries, pooled)
     hard_logit = jnp.where(hard_mask[None, :], SHARPNESS * contract(queries, hard_rows), -jnp.inf)
@@ -68,12 +73,12 @@
         grad_hard.reshape(peers, slots * TILE, width), "pb", split_axis=0, concat_axis=0, tiled=True
     ).reshape(hard, width)
     term = SHARPNESS * transposed(pool_weight, queries)
-    for bit in reversed(bits):
-        half = term.shape[0] // 2
-        sent = term[half:]
-        if bit not in wide:
-            sent = sent.astype(jnp.bfloat16)
-        term = term[:half] + exchange(sent, bit, size).astype(jnp.float32)
+    for step, count, link in reversed(digits):
+        size = term.shape[0] // count
+        pieces = [term[m * size : (m + 1) * size] for m in range(count)]
+        term = pieces[0]
+        for m in range(1, count):
+            term = term + shifts(pieces[m].astype(link), step, count, m, 1).astype(jnp.float32)
     grad_pool = term.astype(jnp.bfloat16)
     grad_query = jnp.dot(local_weight, passages, preferred_element_type=jnp.float32)
     grad_query = grad_query + jnp.dot(pool_weight, pooled, preferred_element_type=jnp.float32)
@@ -86,10 +91,9 @@
 
 
 def solution(mesh):
-    bits = (32, 16, 8, 4, 2, 1)
-    wide = (1, 8, 16, 32)
+    digits = ((8, 8, jnp.float32), (2, 4, jnp.bfloat16), (1, 2, jnp.float32))
     return jax.shard_map(
-        lambda *args: body(bits, wide, *args),
+        lambda *args: body(digits, *args),
         mesh=mesh,
         in_specs=(
             P(("pb", "pool"), None),

time: 170 us -> 165 us (0.971)
  waiting for transfers between devices: 64.5 us -> 19.5 us
  starting transfers between devices: 69.1 us -> 105 us
  local copies, waits for them, and re-layouts: 10 us -> 13.2 us
  other arithmetic: 2.2 us -> 4.01 us
    ppermute x12 -> x22, starting transfers between devices: 48.4 us -> 80.4 us  [shifts(): lax.ppermute(block, 'pool', [(j, moved(j)) for j in range(lax.axis_size('...]
    all_to_all x1, waiting for transfers between devices: 32.3 us -> 6.3 us  [body(): lax.all_to_all(grad_hard.reshape(peers, slots * TILE, width), 'pb', split...]
    ppermute x12 -> x22, waiting for transfers between devices: 27.9 us -> 13.2 us  [shifts(): lax.ppermute(block, 'pool', [(j, moved(j)) for j in range(lax.axis_size('...]
    all_to_all x1, starting transfers between devices: 5.4 us -> 9.75 us  [body(): lax.all_to_all(grad_hard.reshape(peers, slots * TILE, width), 'pb', split...]
    all_to_all x1, waiting for transfers between devices: 4.35 us -> 0.01 us  [body(): lax.all_to_all(outgoing.reshape(peers, slots * TILE, width), 'pb', split_...]
    dot_general x1, matrix products: 2.4 us -> 0.48 us  [body(): jnp.dot(pool_weight, pooled, preferred_element_type=jnp.float32)]
  transfers between devices with their start and end apart: 14 -> 24, of which waited for: 13 -> 7; matrix products, arithmetic and copies ran while one was open for 13% -> 15% of each run, Pallas kernels for 0% -> 0%
where the time goes in v2:
time: 165 us; the launch traced here: 162 us
  starting transfers between devices  105 us (64%)
  waiting for transfers between devices  19.5 us (12%)
  matrix products  19.1 us (12%)
  local copies, waits for them, and re-layouts  13.2 us (8%)
  other arithmetic  4.01 us (2%)
    ppermute x22, starting transfers between devices, shifts(): lax.ppermute(block, 'pool', [(j, moved(j)) for j in range(lax.axis_size('...  80.4 us
    all_to_all x1, starting transfers between devices, body(): lax.all_to_all(outgoing.reshape(peers, slots * TILE, width), 'pb', split_...  15.3 us
    ppermute x22, waiting for transfers between devices, shifts(): lax.ppermute(block, 'pool', [(j, moved(j)) for j in range(lax.axis_size('...  13.2 us
    all_to_all x1, starting transfers between devices, body(): lax.all_to_all(grad_hard.reshape(peers, slots * TILE, width), 'pb', split...  9.75 us
    concatenate x3, local copies, waits for them, and re-layouts, body(): jnp.concatenate([pooled] + [shifts(pooled, step, count, m, -1) for m in r...  9.57 us
    dot_general x4, matrix products, transposed(): lax.dot_general(left, right, (((0,), (0,)), ((), ())), preferred_element_...  7.68 us
    all_to_all x1, waiting for transfers between devices, body(): lax.all_to_all(grad_hard.reshape(peers, slots * TILE, width), 'pb', split...  6.3 us
    dot_general x3, matrix products, contract(): lax.dot_general(left, right, (((1,), (1,)), ((), ())), preferred_element_...  4.57 us
  transfers between devices with their start and end apart: 24, of which 7 were waited for; matrix products, arithmetic and copies ran while one was open for 15% of the time, Pallas kernels for 0%

profile of v2, /device:TPU:6, one launch (start us, length us, event | category | flops | bytes accessed | tf_op | source)
XLA Modules:
  0.0 162.4 jit_solution(8873397145777961283)
XLA Ops:
  0.6 0.0 copy-start
  0.6 0.8 broadcast_multiply_fusion
  1.4 0.1 copy.12
  1.5 0.1 mul.43
  1.6 0.1 iota_add_fusion
  1.7 0.1 add.81
  1.8 3.0 %convolution_convert_fusion = bf16[192,4096]{1,0:T(8,128)(2,1)} fusion(bf16[128,4096]{1,0:T(8,128)(2,1)} %param.7, s32[192]{0:T(256)S(1)} %add.81), kind=kOutput, calls=%fused_computation.2 | convolution fusion | flops 202137600 | bytes 2622208 | tf_op jit(solution)/shard_map/dot_general | solution.py:41
  4.8 15.3 %all-to-all-start = ((bf16[12,16,4096]{2,1,0:T(8,128)(2,1)}), bf16[12,16,4096]{2,1,0:T(8,128)(2,1)S(1)}, u32[]{:S(2)}, u32[]{:S(2)}) async-start(bf16[12,16,4096]{2,1,0:T(8,128)(2,1)} %bitcast.22), calls=%async_computation | async-start | bytes 3145728 | tf_op jit(solution)/shard_map/all_to_all | solution.py:42
  20.1 5.4 %collective-permute-start = (bf16[2,4096]{1,0:T(2,128)(2,1)S(1)}, bf16[2,4096]{1,0:T(2,128)(2,1)S(1)}, u32[]{:S(2)}, u32[]{:S(2)}) collective-permute-start(bf16[2,4096]{1,0:T(2,128)(2,1)S(1)} %copy-done.4), channel_id=1, source_target_pairs={{0,56},{1,57},{2,58},{3,59},{4,60},{5,61},{6,62},{7,63},{8,0},{9,1... | collective-permute-start | bytes 49160 | tf_op jit(solution)/shard_map/ppermute | solution.py:29
  25.5 4.0 %collective-permute-start.1 = (bf16[2,4096]{1,0:T(2,128)(2,1)S(1)}, bf16[2,4096]{1,0:T(2,128)(2,1)S(1)}, u32[]{:S(2)}, u32[]{:S(2)}) collective-permute-start(bf16[2,4096]{1,0:T(2,128)(2,1)S(1)} %copy-done.4), channel_id=1, source_target_pairs={{0,48},{1,49},{2,50},{3,51},{4,52},{5,53},{6,54},{7,55},{8,56},{9,... | collective-permute-start | bytes 49160 | tf_op jit(solution)/shard_map/ppermute | solution.py:29
  29.5 3.0 %collective-permute-start.2 = (bf16[2,4096]{1,0:T(2,128)(2,1)S(1)}, bf16[2,4096]{1,0:T(2,128)(2,1)S(1)}, u32[]{:S(2)}, u32[]{:S(2)}) collective-permute-start(bf16[2,4096]{1,0:T(2,128)(2,1)S(1)} %copy-done.4), channel_id=1, source_target_pairs={{0,40},{1,41},{2,42},{3,43},{4,44},{5,45},{6,46},{7,47},{8,48},{9,... | collective-permute-start | bytes 49160 | tf_op jit(solution)/shard_map/ppermute | solution.py:29
  32.6 5.9 %collective-permute-start.3 = (bf16[2,4096]{1,0:T(2,128)(2,1)S(1)}, bf16[2,4096]{1,0:T(2,128)(2,1)S(1)}, u32[]{:S(2)}, u32[]{:S(2)}) collective-permute-start(bf16[2,4096]{1,0:T(2,128)(2,1)S(1)} %copy-done.4), channel_id=1, source_target_pairs={{0,32},{1,33},{2,34},{3,35},{4,36},{5,37},{6,38},{7,39},{8,40},{9,... | collective-permute-start | bytes 49160 | tf_op jit(solution)/shard_map/ppermute | solution.py:29
  38.5 1.9 %collective-permute-start.4 = (bf16[2,4096]{1,0:T(2,128)(2,1)S(1)}, bf16[2,4096]{1,0:T(2,128)(2,1)S(1)}, u32[]{:S(2)}, u32[]{:S(2)}) collective-permute-start(bf16[2,4096]{1,0:T(2,128)(2,1)S(1)} %copy-done.4), channel_id=1, source_target_pairs={{0,24},{1,25},{2,26},{3,27},{4,28},{5,29},{6,30},{7,31},{8,32},{9,... | collective-permute-start | bytes 49160 | tf_op jit(solution)/shard_map/ppermute | solution.py:29
  40.5 5.4 %collective-permute-start.5 = (bf16[2,4096]{1,0:T(2,128)(2,1)S(1)}, bf16[2,4096]{1,0:T(2,128)(2,1)S(1)}, u32[]{:S(2)}, u32[]{:S(2)}) collective-permute-start(bf16[2,4096]{1,0:T(2,128)(2,1)S(1)} %copy-done.4), channel_id=1, source_target_pairs={{0,16},{1,17},{2,18},{3,19},{4,20},{5,21},{6,22},{7,23},{8,24},{9,... | collective-permute-start | bytes 49160 | tf_op jit(solution)/shard_map/ppermute | solution.py:29
  45.9 3.5 %collective-permute-start.6 = (bf16[2,4096]{1,0:T(2,128)(2,1)S(1)}, bf16[2,4096]{1,0:T(2,128)(2,1)S(1)}, u32[]{:S(2)}, u32[]{:S(2)}) collective-permute-start(bf16[2,4096]{1,0:T(2,128)(2,1)S(1)} %copy-done.4), channel_id=1, source_target_pairs={{0,8},{1,9},{2,10},{3,11},{4,12},{5,13},{6,14},{7,15},{8,16},{9,17... | collective-permute-start | bytes 49160 | tf_op jit(solution)/shard_map/ppermute | solution.py:29
  49.4 0.0 copy-start.5
  49.4 3.3 %collective-permute-done.6 = bf16[2,4096]{1,0:T(2,128)(2,1)S(1)} collective-permute-done((bf16[2,4096]{1,0:T(2,128)(2,1)S(1)}, bf16[2,4096]{1,0:T(2,128)(2,1)S(1)}, u32[]{:S(2)}, u32[]{:S(2)}) %collective-permute-start.6) | collective-permute-done | bytes 16416 | tf_op jit(solution)/shard_map/ppermute | solution.py:29
  52.7 0.2 concatenate.11
  52.9 2.7 %collective-permute-start.7 = (bf16[16,4096]{1,0:T(8,128)(2,1)S(1)}, bf16[16,4096]{1,0:T(8,128)(2,1)S(1)}, u32[]{:S(2)}, u32[]{:S(2)}) collective-permute-start(bf16[16,4096]{1,0:T(8,128)(2,1)S(1)} %concatenate.11), channel_id=1, source_target_pairs={{0,6},{1,7},{2,0},{3,1},{4,2},{5,3},{6,4},{7,5},{8,14},{9,15},{10,... | collective-permute-start | bytes 393224 | tf_op jit(solution)/shard_map/ppermute | solution.py:29
  55.6 3.0 %collective-permute-start.8 = (bf16[16,4096]{1,0:T(8,128)(2,1)S(1)}, bf16[16,4096]{1,0:T(8,128)(2,1)S(1)}, u32[]{:S(2)}, u32[]{:S(2)}) collective-permute-start(bf16[16,4096]{1,0:T(8,128)(2,1)S(1)} %concatenate.11), channel_id=1, source_target_pairs={{0,4},{1,5},{2,6},{3,7},{4,0},{5,1},{6,2},{7,3},{8,12},{9,13},{10,... | collective-permute-start | bytes 393224 | tf_op jit(solution)/shard_map/ppermute | solution.py:29
  58.7 4.0 %collective-permute-start.9 = (bf16[16,4096]{1,0:T(8,128)(2,1)S(1)}, bf16[16,4096]{1,0:T(8,128)(2,1)}, u32[]{:S(2)}, u32[]{:S(2)}) collective-permute-start(bf16[16,4096]{1,0:T(8,128)(2,1)S(1)} %concatenate.11), channel_id=1, source_target_pairs={{0,2},{1,3},{2,4},{3,5},{4,6},{5,7},{6,0},{7,1},{8,10},{9,11},{10,... | collective-permute-start | bytes 393224 | tf_op jit(solution)/shard_map/ppermute | solution.py:29
  62.7 1.3 collective-permute-done.8
  64.0 1.8 %collective-permute-done.9 = bf16[16,4096]{1,0:T(8,128)(2,1)} collective-permute-done((bf16[16,4096]{1,0:T(8,128)(2,1)S(1)}, bf16[16,4096]{1,0:T(8,128)(2,1)}, u32[]{:S(2)}, u32[]{:S(2)}) %collective-permute-start.9) | collective-permute-done | bytes 131104 | tf_op jit(solution)/shard_map/ppermute | solution.py:29
  65.8 1.1 concatenate.12
  66.9 1.9 %collective-permute-start.10 = (bf16[64,4096]{1,0:T(8,128)(2,1)S(1)}, bf16[64,4096]{1,0:T(8,128)(2,1)}, u32[]{:S(2)}, u32[]{:S(2)}) collective-permute-start(bf16[64,4096]{1,0:T(8,128)(2,1)S(1)} %concatenate.12), channel_id=1, source_target_pairs={{0,1},{1,0},{2,3},{3,2},{4,5},{5,4},{6,7},{7,6},{8,9},{9,8},{10,11... | collective-permute-start | bytes 1572872 | tf_op jit(solution)/shard_map/ppermute | solution.py:29
  68.8 0.7 iota_compare_fusion.4
  69.6 0.1 broadcast_in_dim.16
  69.7 0.7 broadcast_in_dim.17
  70.4 2.3 %fusion.22 = (f32[128]{0:T(128)}, f32[128,128]{0,1:T(8,128)S(1)}) fusion(bf16[128,4096]{1,0:T(8,128)(2,1)S(1)} %copy-done, bf16[128,4096]{1,0:T(8,128)(2,1)} %param.7), kind=kOutput, calls=%fused_computation.49 | convolution fusion | flops 134250368 | bytes 2163200 | tf_op jit(solution)/shard_map/dot_general | solution.py:13
  72.6 8.2 %concatenate.13 = bf16[128,4096]{1,0:T(8,128)(2,1)} concatenate(bf16[2,4096]{1,0:T(2,128)(2,1)S(1)} %copy-done.4, bf16[2,4096]{1,0:T(2,128)(2,1)S(1)} %collective-permute-done, bf16[2,4096]{1,0:T(2,128)(2,1)S(1)} %collective-permute-done.1, bf16[2,4096]{1,0:T(2,128)(2,1)S(1)} %collective-permute-done.2, bf16[2,4096]{1,0:T(2,128)(2,1)S(1)} %collective-permute-done.3, ...), dimensions={0} | concatenate | bytes 2097152 | tf_op jit(solution)/shard_map/concatenate | solution.py:49
  80.9 1.7 %fusion.23 = (f32[128]{0:T(128)S(1)}, f32[128,128]{0,1:T(8,128)S(1)}) fusion(bf16[128,4096]{1,0:T(8,128)(2,1)} %concatenate.13, bf16[128,4096]{1,0:T(8,128)(2,1)S(1)} %copy-done), kind=kOutput, calls=%fused_computation.50 | convolution fusion | flops 134250368 | bytes 2163200 | tf_op jit(solution)/shard_map/dot_general | solution.py:13
  82.6 0.6 fusion.21
  83.3 0.2 fusion.9
  83.5 0.6 convolution_multiply_fusion.1
  84.1 1.3 copy-done.2
  85.4 1.0 slice.60
  86.5 2.4 %collective-permute-start.11 = (f32[64,4096]{1,0:T(8,128)}, f32[64,4096]{1,0:T(8,128)}, u32[]{:S(2)}, u32[]{:S(2)}) collective-permute-start(f32[64,4096]{1,0:T(8,128)} %slice.60), channel_id=1, source_target_pairs={{0,1},{1,0},{2,3},{3,2},{4,5},{5,4},{6,7},{7,6},{8,9},{9,8},{10,11... | collective-permute-start | bytes 3145736 | tf_op jit(solution)/shard_map/ppermute | solution.py:29
  88.9 1.7 %fusion = bf16[192,4096]{1,0:T(8,128)(2,1)} fusion(bf16[128,4096]{1,0:T(8,128)(2,1)S(1)} %copy-done, f32[192,128]{1,0:T(8,128)S(1)} %get-tuple-element.18, f32[128]{0:T(128)S(1)} %add_add_fusion, f32[128]{0:T(128)S(1)} %maximum_maximum_fusion), kind=kOutput, calls=%fused_computation.1 | convolution fusion | flops 202973184 | bytes 2720768 | tf_op jit(solution)/shard_map/dot_general | solution.py:19
  90.6 9.7 %all-to-all-start.1 = ((bf16[12,16,4096]{2,1,0:T(8,128)(2,1)}), bf16[12,16,4096]{2,1,0:T(8,128)(2,1)}, u32[]{:S(2)}, u32[]{:S(2)}) async-start(bf16[12,16,4096]{2,1,0:T(8,128)(2,1)} %bitcast.21), calls=%async_computation.1 | async-start | bytes 3145728 | tf_op jit(solution)/shard_map/all_to_all | solution.py:72
  100.4 1.8 %fusion.17 = f32[128,4096]{1,0:T(8,128)S(1)} fusion(bf16[128,4096]{1,0:T(8,128)(2,1)} %param.7, f32[128,128]{0,1:T(8,128)S(1)} %get-tuple-element.20, s32[128]{0:T(128)S(1)} %copy-done.10, f32[128]{0:T(128)S(1)} %add_add_fusion, f32[128]{0:T(128)S(1)} %maximum_maximum_fusion), kind=kOutput, calls=%fused_computation.44 | convolution fusion | flops 134316032 | bytes 3212800 | tf_op jit(solution)/shard_map/dot_general | solution.py:83
  102.2 0.0 copy-start.1
  102.2 0.0 copy-done.3
  102.3 1.5 fusion.18
  103.8 3.9 %collective-permute-start.14 = (bf16[16,4096]{1,0:T(8,128)(2,1)S(1)}, bf16[16,4096]{1,0:T(8,128)(2,1)S(1)}, u32[]{:S(2)}, u32[]{:S(2)}) collective-permute-start(bf16[16,4096]{1,0:T(8,128)(2,1)S(1)} %get-tuple-element.8), channel_id=1, source_target_pairs={{0,6},{1,7},{2,0},{3,1},{4,2},{5,3},{6,4},{7,5},{8,14},{9,15},{10,... | collective-permute-start | bytes 393224 | tf_op jit(solution)/shard_map/ppermute | solution.py:29
  107.7 4.5 %collective-permute-start.13 = (bf16[16,4096]{1,0:T(8,128)(2,1)S(1)}, bf16[16,4096]{1,0:T(8,128)(2,1)S(1)}, u32[]{:S(2)}, u32[]{:S(2)}) collective-permute-start(bf16[16,4096]{1,0:T(8,128)(2,1)S(1)} %get-tuple-element.9), channel_id=1, source_target_pairs={{0,4},{1,5},{2,6},{3,7},{4,0},{5,1},{6,2},{7,3},{8,12},{9,13},{10,... | collective-permute-start | bytes 393224 | tf_op jit(solution)/shard_map/ppermute | solution.py:29
  112.2 2.2 %collective-permute-start.12 = (bf16[16,4096]{1,0:T(8,128)(2,1)S(1)}, bf16[16,4096]{1,0:T(8,128)(2,1)S(1)}, u32[]{:S(2)}, u32[]{:S(2)}) collective-permute-start(bf16[16,4096]{1,0:T(8,128)(2,1)S(1)} %get-tuple-element.7), channel_id=1, source_target_pairs={{0,2},{1,3},{2,4},{3,5},{4,6},{5,7},{6,0},{7,1},{8,10},{9,11},{10,... | collective-permute-start | bytes 393224 | tf_op jit(solution)/shard_map/ppermute | solution.py:29
  114.4 0.5 convolution_add_fusion.2
  114.9 1.3 collective-permute-done.13
  116.2 2.9 %collective-permute-done.12 = bf16[16,4096]{1,0:T(8,128)(2,1)S(1)} collective-permute-done((bf16[16,4096]{1,0:T(8,128)(2,1)S(1)}, bf16[16,4096]{1,0:T(8,128)(2,1)S(1)}, u32[]{:S(2)}, u32[]{:S(2)}) %collective-permute-start.12) | collective-permute-done | bytes 131104 | tf_op jit(solution)/shard_map/ppermute | solution.py:29
  119.1 0.1 fusion.6
  119.2 0.1 fusion.20
  119.2 2.3 %collective-permute-start.21 = (f32[2,4096]{1,0:T(2,128)S(1)}, f32[2,4096]{1,0:T(2,128)S(1)}, u32[]{:S(2)}, u32[]{:S(2)}) collective-permute-start(f32[2,4096]{1,0:T(2,128)S(1)} %get-tuple-element.11), channel_id=1, source_target_pairs={{0,56},{1,57},{2,58},{3,59},{4,60},{5,61},{6,62},{7,63},{8,0},{9,1... | collective-permute-start | bytes 98312 | tf_op jit(solution)/shard_map/ppermute | solution.py:29
  121.6 2.7 %collective-permute-start.20 = (f32[2,4096]{1,0:T(2,128)S(1)}, f32[2,4096]{1,0:T(2,128)S(1)}, u32[]{:S(2)}, u32[]{:S(2)}) collective-permute-start(f32[2,4096]{1,0:T(2,128)S(1)} %get-tuple-element.12), channel_id=1, source_target_pairs={{0,48},{1,49},{2,50},{3,51},{4,52},{5,53},{6,54},{7,55},{8,56},{9,... | collective-permute-start | bytes 98312 | tf_op jit(solution)/shard_map/ppermute | solution.py:29
  124.3 1.5 fusion.2
  125.8 5.4 %collective-permute-start.19 = (f32[2,4096]{1,0:T(2,128)S(1)}, f32[2,4096]{1,0:T(2,128)S(1)}, u32[]{:S(2)}, u32[]{:S(2)}) collective-permute-start(f32[2,4096]{1,0:T(2,128)S(1)} %get-tuple-element.13), channel_id=1, source_target_pairs={{0,40},{1,41},{2,42},{3,43},{4,44},{5,45},{6,46},{7,47},{8,48},{9,... | collective-permute-start | bytes 98312 | tf_op jit(solution)/shard_map/ppermute | solution.py:29
  131.2 3.8 %collective-permute-start.18 = (f32[2,4096]{1,0:T(2,128)S(1)}, f32[2,4096]{1,0:T(2,128)S(1)}, u32[]{:S(2)}, u32[]{:S(2)}) collective-permute-start(f32[2,4096]{1,0:T(2,128)S(1)} %get-tuple-element.14), channel_id=1, source_target_pairs={{0,32},{1,33},{2,34},{3,35},{4,36},{5,37},{6,38},{7,39},{8,40},{9,... | collective-permute-start | bytes 98312 | tf_op jit(solution)/shard_map/ppermute | solution.py:29
  135.0 4.6 %collective-permute-start.17 = (f32[2,4096]{1,0:T(2,128)S(1)}, f32[2,4096]{1,0:T(2,128)S(1)}, u32[]{:S(2)}, u32[]{:S(2)}) collective-permute-start(f32[2,4096]{1,0:T(2,128)S(1)} %get-tuple-element.15), channel_id=1, source_target_pairs={{0,24},{1,25},{2,26},{3,27},{4,28},{5,29},{6,30},{7,31},{8,32},{9,... | collective-permute-start | bytes 98312 | tf_op jit(solution)/shard_map/ppermute | solution.py:29
  139.7 5.1 %collective-permute-start.16 = (f32[2,4096]{1,0:T(2,128)S(1)}, f32[2,4096]{1,0:T(2,128)S(1)}, u32[]{:S(2)}, u32[]{:S(2)}) collective-permute-start(f32[2,4096]{1,0:T(2,128)S(1)} %get-tuple-element.16), channel_id=1, source_target_pairs={{0,16},{1,17},{2,18},{3,19},{4,20},{5,21},{6,22},{7,23},{8,24},{9,... | collective-permute-start | bytes 98312 | tf_op jit(solution)/shard_map/ppermute | solution.py:29
  144.8 2.6 %collective-permute-start.15 = (f32[2,4096]{1,0:T(2,128)S(1)}, f32[2,4096]{1,0:T(2,128)S(1)}, u32[]{:S(2)}, u32[]{:S(2)}) collective-permute-start(f32[2,4096]{1,0:T(2,128)S(1)} %get-tuple-element.10), channel_id=1, source_target_pairs={{0,8},{1,9},{2,10},{3,11},{4,12},{5,13},{6,14},{7,15},{8,16},{9,17... | collective-permute-start | bytes 98312 | tf_op jit(solution)/shard_map/ppermute | solution.py:29
  147.4 1.8 %convolution_multiply_fusion.2 = f32[128,4096]{1,0:T(8,128)} fusion(bf16[128,4096]{1,0:T(8,128)(2,1)S(1)} %copy-done, f32[128,128]{0,1:T(8,128)S(1)} %get-tuple-element.20, s32[128]{0:T(128)S(1)} %copy-done.10, f32[128]{0:T(128)S(1)} %add_add_fusion, f32[128]{0:T(128)S(1)} %maximum_maximum_fusion), kind=kOutput, calls=%fused_computation.5 | convolution fusion | flops 134840320 | bytes 3212800 | tf_op jit(solution)/shard_map/dot_general | solution.py:19
  149.2 2.6 %collective-permute-done.15 = f32[2,4096]{1,0:T(2,128)S(1)} collective-permute-done((f32[2,4096]{1,0:T(2,128)S(1)}, f32[2,4096]{1,0:T(2,128)S(1)}, u32[]{:S(2)}, u32[]{:S(2)}) %collective-permute-start.15) | collective-permute-done | bytes 32800 | tf_op jit(solution)/shard_map/ppermute | solution.py:29
  151.8 0.7 add_convert_fusion
  152.5 6.3 %all-to-all-done.1 = bf16[12,16,4096]{2,1,0:T(8,128)(2,1)} async-done(((bf16[12,16,4096]{2,1,0:T(8,128)(2,1)}), bf16[12,16,4096]{2,1,0:T(8,128)(2,1)}, u32[]{:S(2)}, u32[]{:S(2)}) %all-to-all-start.1) | async-done | bytes 1572896 | tf_op jit(solution)/shard_map/all_to_all | solution.py:72
  158.8 3.6 %fusion.3 = bf16[128,4096]{1,0:T(8,128)(2,1)} fusion(f32[128,4096]{1,0:T(8,128)} %convolution_multiply_fusion.2, bf16[192,4096]{1,0:T(8,128)(2,1)} %bitcast.4, s32[192]{0:T(256)S(1)} %copy-done.9), kind=kOutput, calls=%fused_computation.10 | convolution fusion | flops 202399744 | bytes 4719360 | tf_op jit(solution)/shard_map/dot_general | solution.py:19
  (42 shorter events, 0.2 us)
Async XLA Ops:
  0.6 69.8 %copy-start = (bf16[128,4096]{1,0:T(8,128)(2,1)S(1)}, bf16[128,4096]{1,0:T(8,128)(2,1)}, u32[]{:S(2)}) copy-start(bf16[128,4096]{1,0:T(8,128)(2,1)} %param.6) | copy-start | bytes 3145732
  1.8 3.0 %copy-start.8 = (s32[192]{0:T(256)}, s32[192]{0:T(256)S(1)}, u32[]{:S(2)}) copy-start(s32[192]{0:T(256)S(1)} %add.81) | copy-start | bytes 2308
  4.8 15.3 %copy-start.4 = (bf16[2,4096]{1,0:T(2,128)(2,1)S(1)}, bf16[2,4096]{1,0:T(2,128)(2,1)}, u32[]{:S(2)}) copy-start(bf16[2,4096]{1,0:T(2,128)(2,1)} %param.8) | copy-start | bytes 49156
  4.8 77.8 %all-to-all-start = ((bf16[12,16,4096]{2,1,0:T(8,128)(2,1)}), bf16[12,16,4096]{2,1,0:T(8,128)(2,1)S(1)}, u32[]{:S(2)}, u32[]{:S(2)}) async-start(bf16[12,16,4096]{2,1,0:T(8,128)(2,1)} %bitcast.22), calls=%async_computation | async-start | bytes 3145728 | tf_op jit(solution)/shard_map/all_to_all | solution.py:42
  20.1 20.4 %collective-permute-start = (bf16[2,4096]{1,0:T(2,128)(2,1)S(1)}, bf16[2,4096]{1,0:T(2,128)(2,1)S(1)}, u32[]{:S(2)}, u32[]{:S(2)}) collective-permute-start(bf16[2,4096]{1,0:T(2,128)(2,1)S(1)} %copy-done.4), channel_id=1, source_target_pairs={{0,56},{1,57},{2,58},{3,59},{4,60},{5,61},{6,62},{7,63},{8,0},{9,1... | collective-permute-start | bytes 49160 | tf_op jit(solution)/shard_map/ppermute | solution.py:29
  25.5 20.4 %collective-permute-start.1 = (bf16[2,4096]{1,0:T(2,128)(2,1)S(1)}, bf16[2,4096]{1,0:T(2,128)(2,1)S(1)}, u32[]{:S(2)}, u32[]{:S(2)}) collective-permute-start(bf16[2,4096]{1,0:T(2,128)(2,1)S(1)} %copy-done.4), channel_id=1, source_target_pairs={{0,48},{1,49},{2,50},{3,51},{4,52},{5,53},{6,54},{7,55},{8,56},{9,... | collective-permute-start | bytes 49160 | tf_op jit(solution)/shard_map/ppermute | solution.py:29
  29.5 19.8 %collective-permute-start.2 = (bf16[2,4096]{1,0:T(2,128)(2,1)S(1)}, bf16[2,4096]{1,0:T(2,128)(2,1)S(1)}, u32[]{:S(2)}, u32[]{:S(2)}) collective-permute-start(bf16[2,4096]{1,0:T(2,128)(2,1)S(1)} %copy-done.4), channel_id=1, source_target_pairs={{0,40},{1,41},{2,42},{3,43},{4,44},{5,45},{6,46},{7,47},{8,48},{9,... | collective-permute-start | bytes 49160 | tf_op jit(solution)/shard_map/ppermute | solution.py:29
  32.6 16.8 %collective-permute-start.3 = (bf16[2,4096]{1,0:T(2,128)(2,1)S(1)}, bf16[2,4096]{1,0:T(2,128)(2,1)S(1)}, u32[]{:S(2)}, u32[]{:S(2)}) collective-permute-start(bf16[2,4096]{1,0:T(2,128)(2,1)S(1)} %copy-done.4), channel_id=1, source_target_pairs={{0,32},{1,33},{2,34},{3,35},{4,36},{5,37},{6,38},{7,39},{8,40},{9,... | collective-permute-start | bytes 49160 | tf_op jit(solution)/shard_map/ppermute | solution.py:29
  38.5 10.8 %collective-permute-start.4 = (bf16[2,4096]{1,0:T(2,128)(2,1)S(1)}, bf16[2,4096]{1,0:T(2,128)(2,1)S(1)}, u32[]{:S(2)}, u32[]{:S(2)}) collective-permute-start(bf16[2,4096]{1,0:T(2,128)(2,1)S(1)} %copy-done.4), channel_id=1, source_target_pairs={{0,24},{1,25},{2,26},{3,27},{4,28},{5,29},{6,30},{7,31},{8,32},{9,... | collective-permute-start | bytes 49160 | tf_op jit(solution)/shard_map/ppermute | solution.py:29
  40.5 8.9 %collective-permute-start.5 = (bf16[2,4096]{1,0:T(2,128)(2,1)S(1)}, bf16[2,4096]{1,0:T(2,128)(2,1)S(1)}, u32[]{:S(2)}, u32[]{:S(2)}) collective-permute-start(bf16[2,4096]{1,0:T(2,128)(2,1)S(1)} %copy-done.4), channel_id=1, source_target_pairs={{0,16},{1,17},{2,18},{3,19},{4,20},{5,21},{6,22},{7,23},{8,24},{9,... | collective-permute-start | bytes 49160 | tf_op jit(solution)/shard_map/ppermute | solution.py:29
  45.9 6.8 %collective-permute-start.6 = (bf16[2,4096]{1,0:T(2,128)(2,1)S(1)}, bf16[2,4096]{1,0:T(2,128)(2,1)S(1)}, u32[]{:S(2)}, u32[]{:S(2)}) collective-permute-start(bf16[2,4096]{1,0:T(2,128)(2,1)S(1)} %copy-done.4), channel_id=1, source_target_pairs={{0,8},{1,9},{2,10},{3,11},{4,12},{5,13},{6,14},{7,15},{8,16},{9,17... | collective-permute-start | bytes 49160 | tf_op jit(solution)/shard_map/ppermute | solution.py:29
  49.4 20.3 %copy-start.5 = (bf16[2,4096]{1,0:T(2,128)(2,1)}, bf16[2,4096]{1,0:T(2,128)(2,1)S(1)}, u32[]{:S(2)}) copy-start(bf16[2,4096]{1,0:T(2,128)(2,1)S(1)} %collective-permute-done.4) | copy-start | bytes 49156
  49.4 20.3 %copy-start.6 = (bf16[2,4096]{1,0:T(2,128)(2,1)}, bf16[2,4096]{1,0:T(2,128)(2,1)S(1)}, u32[]{:S(2)}) copy-start(bf16[2,4096]{1,0:T(2,128)(2,1)S(1)} %collective-permute-done.5) | copy-start | bytes 49156
  52.7 17.0 %copy-start.7 = (bf16[2,4096]{1,0:T(2,128)(2,1)}, bf16[2,4096]{1,0:T(2,128)(2,1)S(1)}, u32[]{:S(2)}) copy-start(bf16[2,4096]{1,0:T(2,128)(2,1)S(1)} %collective-permute-done.6) | copy-start | bytes 49156
  52.9 9.8 %collective-permute-start.7 = (bf16[16,4096]{1,0:T(8,128)(2,1)S(1)}, bf16[16,4096]{1,0:T(8,128)(2,1)S(1)}, u32[]{:S(2)}, u32[]{:S(2)}) collective-permute-start(bf16[16,4096]{1,0:T(8,128)(2,1)S(1)} %concatenate.11), channel_id=1, source_target_pairs={{0,6},{1,7},{2,0},{3,1},{4,2},{5,3},{6,4},{7,5},{8,14},{9,15},{10,... | collective-permute-start | bytes 393224 | tf_op jit(solution)/shard_map/ppermute | solution.py:29
  55.6 8.4 %collective-permute-start.8 = (bf16[16,4096]{1,0:T(8,128)(2,1)S(1)}, bf16[16,4096]{1,0:T(8,128)(2,1)S(1)}, u32[]{:S(2)}, u32[]{:S(2)}) collective-permute-start(bf16[16,4096]{1,0:T(8,128)(2,1)S(1)} %concatenate.11), channel_id=1, source_target_pairs={{0,4},{1,5},{2,6},{3,7},{4,0},{5,1},{6,2},{7,3},{8,12},{9,13},{10,... | collective-permute-start | bytes 393224 | tf_op jit(solution)/shard_map/ppermute | solution.py:29
  58.7 7.1 %collective-permute-start.9 = (bf16[16,4096]{1,0:T(8,128)(2,1)S(1)}, bf16[16,4096]{1,0:T(8,128)(2,1)}, u32[]{:S(2)}, u32[]{:S(2)}) collective-permute-start(bf16[16,4096]{1,0:T(8,128)(2,1)S(1)} %concatenate.11), channel_id=1, source_target_pairs={{0,2},{1,3},{2,4},{3,5},{4,6},{5,7},{6,0},{7,1},{8,10},{9,11},{10,... | collective-permute-start | bytes 393224 | tf_op jit(solution)/shard_map/ppermute | solution.py:29
  66.9 5.7 %collective-permute-start.10 = (bf16[64,4096]{1,0:T(8,128)(2,1)S(1)}, bf16[64,4096]{1,0:T(8,128)(2,1)}, u32[]{:S(2)}, u32[]{:S(2)}) collective-permute-start(bf16[64,4096]{1,0:T(8,128)(2,1)S(1)} %concatenate.12), channel_id=1, source_target_pairs={{0,1},{1,0},{2,3},{3,2},{4,5},{5,4},{6,7},{7,6},{8,9},{9,8},{10,11... | collective-permute-start | bytes 1572872 | tf_op jit(solution)/shard_map/ppermute | solution.py:29
  72.6 10.0 %copy-start.12 = (pred[192]{0:T(512)(128)(4,1)S(1)}, pred[192]{0:T(512)(128)(4,1)}, u32[]{:S(2)}) copy-start(pred[192]{0:T(512)(128)(4,1)} %broadcast_in_dim.17) | copy-start | bytes 580
  80.9 2.3 %copy-start.11 = (f32[128]{0:T(128)S(1)}, f32[128]{0:T(128)}, u32[]{:S(2)}) copy-start(f32[128]{0:T(128)} %get-tuple-element.19) | copy-start | bytes 1540
  84.1 1.3 copy-start.2
  86.5 15.8 %collective-permute-start.11 = (f32[64,4096]{1,0:T(8,128)}, f32[64,4096]{1,0:T(8,128)}, u32[]{:S(2)}, u32[]{:S(2)}) collective-permute-start(f32[64,4096]{1,0:T(8,128)} %slice.60), channel_id=1, source_target_pairs={{0,1},{1,0},{2,3},{3,2},{4,5},{5,4},{6,7},{7,6},{8,9},{9,8},{10,11... | collective-permute-start | bytes 3145736 | tf_op jit(solution)/shard_map/ppermute | solution.py:29
  90.6 9.8 %copy-start.10 = (s32[128]{0:T(128)S(1)}, s32[128]{0:T(128)}, u32[]{:S(2)}) copy-start(s32[128]{0:T(128)} %param.9) | copy-start | bytes 1540
  90.6 68.2 %all-to-all-start.1 = ((bf16[12,16,4096]{2,1,0:T(8,128)(2,1)}), bf16[12,16,4096]{2,1,0:T(8,128)(2,1)}, u32[]{:S(2)}, u32[]{:S(2)}) async-start(bf16[12,16,4096]{2,1,0:T(8,128)(2,1)} %bitcast.21), calls=%async_computation.1 | async-start | bytes 3145728 | tf_op jit(solution)/shard_map/all_to_all | solution.py:72
  100.4 1.9 %copy-start.3 = (f32[128,4096]{1,0:T(8,128)S(1)}, f32[128,4096]{1,0:T(8,128)}, u32[]{:S(2)}) copy-start(f32[128,4096]{1,0:T(8,128)} %copy-done.2) | copy-start | bytes 6291460
  102.2 12.2 %copy-start.1 = (bf16[128,4096]{1,0:T(8,128)(2,1)S(1)}, bf16[128,4096]{1,0:T(8,128)(2,1)}, u32[]{:S(2)}) copy-start(bf16[128,4096]{1,0:T(8,128)(2,1)} %concatenate.13) | copy-start | bytes 3145732
  103.8 11.2 %collective-permute-start.14 = (bf16[16,4096]{1,0:T(8,128)(2,1)S(1)}, bf16[16,4096]{1,0:T(8,128)(2,1)S(1)}, u32[]{:S(2)}, u32[]{:S(2)}) collective-permute-start(bf16[16,4096]{1,0:T(8,128)(2,1)S(1)} %get-tuple-element.8), channel_id=1, source_target_pairs={{0,6},{1,7},{2,0},{3,1},{4,2},{5,3},{6,4},{7,5},{8,14},{9,15},{10,... | collective-permute-start | bytes 393224 | tf_op jit(solution)/shard_map/ppermute | solution.py:29
  107.7 8.5 %collective-permute-start.13 = (bf16[16,4096]{1,0:T(8,128)(2,1)S(1)}, bf16[16,4096]{1,0:T(8,128)(2,1)S(1)}, u32[]{:S(2)}, u32[]{:S(2)}) collective-permute-start(bf16[16,4096]{1,0:T(8,128)(2,1)S(1)} %get-tuple-element.9), channel_id=1, source_target_pairs={{0,4},{1,5},{2,6},{3,7},{4,0},{5,1},{6,2},{7,3},{8,12},{9,13},{10,... | collective-permute-start | bytes 393224 | tf_op jit(solution)/shard_map/ppermute | solution.py:29
  112.2 6.9 %collective-permute-start.12 = (bf16[16,4096]{1,0:T(8,128)(2,1)S(1)}, bf16[16,4096]{1,0:T(8,128)(2,1)S(1)}, u32[]{:S(2)}, u32[]{:S(2)}) collective-permute-start(bf16[16,4096]{1,0:T(8,128)(2,1)S(1)} %get-tuple-element.7), channel_id=1, source_target_pairs={{0,2},{1,3},{2,4},{3,5},{4,6},{5,7},{6,0},{7,1},{8,10},{9,11},{10,... | collective-permute-start | bytes 393224 | tf_op jit(solution)/shard_map/ppermute | solution.py:29
  119.2 20.4 %collective-permute-start.21 = (f32[2,4096]{1,0:T(2,128)S(1)}, f32[2,4096]{1,0:T(2,128)S(1)}, u32[]{:S(2)}, u32[]{:S(2)}) collective-permute-start(f32[2,4096]{1,0:T(2,128)S(1)} %get-tuple-element.11), channel_id=1, source_target_pairs={{0,56},{1,57},{2,58},{3,59},{4,60},{5,61},{6,62},{7,63},{8,0},{9,1... | collective-permute-start | bytes 98312 | tf_op jit(solution)/shard_map/ppermute | solution.py:29
  121.6 23.2 %collective-permute-start.20 = (f32[2,4096]{1,0:T(2,128)S(1)}, f32[2,4096]{1,0:T(2,128)S(1)}, u32[]{:S(2)}, u32[]{:S(2)}) collective-permute-start(f32[2,4096]{1,0:T(2,128)S(1)} %get-tuple-element.12), channel_id=1, source_target_pairs={{0,48},{1,49},{2,50},{3,51},{4,52},{5,53},{6,54},{7,55},{8,56},{9,... | collective-permute-start | bytes 98312 | tf_op jit(solution)/shard_map/ppermute | solution.py:29
  125.8 33.0 %copy-start.9 = (s32[192]{0:T(256)S(1)}, s32[192]{0:T(256)}, u32[]{:S(2)}) copy-start(s32[192]{0:T(256)} %copy-done.8) | copy-start | bytes 2308
  125.8 23.4 %collective-permute-start.19 = (f32[2,4096]{1,0:T(2,128)S(1)}, f32[2,4096]{1,0:T(2,128)S(1)}, u32[]{:S(2)}, u32[]{:S(2)}) collective-permute-start(f32[2,4096]{1,0:T(2,128)S(1)} %get-tuple-element.13), channel_id=1, source_target_pairs={{0,40},{1,41},{2,42},{3,43},{4,44},{5,45},{6,46},{7,47},{8,48},{9,... | collective-permute-start | bytes 98312 | tf_op jit(solution)/shard_map/ppermute | solution.py:29
  131.2 18.0 %collective-permute-start.18 = (f32[2,4096]{1,0:T(2,128)S(1)}, f32[2,4096]{1,0:T(2,128)S(1)}, u32[]{:S(2)}, u32[]{:S(2)}) collective-permute-start(f32[2,4096]{1,0:T(2,128)S(1)} %get-tuple-element.14), channel_id=1, source_target_pairs={{0,32},{1,33},{2,34},{3,35},{4,36},{5,37},{6,38},{7,39},{8,40},{9,... | collective-permute-start | bytes 98312 | tf_op jit(solution)/shard_map/ppermute | solution.py:29
  135.0 14.2 %collective-permute-start.17 = (f32[2,4096]{1,0:T(2,128)S(1)}, f32[2,4096]{1,0:T(2,128)S(1)}, u32[]{:S(2)}, u32[]{:S(2)}) collective-permute-start(f32[2,4096]{1,0:T(2,128)S(1)} %get-tuple-element.15), channel_id=1, source_target_pairs={{0,24},{1,25},{2,26},{3,27},{4,28},{5,29},{6,30},{7,31},{8,32},{9,... | collective-permute-start | bytes 98312 | tf_op jit(solution)/shard_map/ppermute | solution.py:29
  139.7 9.5 %collective-permute-start.16 = (f32[2,4096]{1,0:T(2,128)S(1)}, f32[2,4096]{1,0:T(2,128)S(1)}, u32[]{:S(2)}, u32[]{:S(2)}) collective-permute-start(f32[2,4096]{1,0:T(2,128)S(1)} %get-tuple-element.16), channel_id=1, source_target_pairs={{0,16},{1,17},{2,18},{3,19},{4,20},{5,21},{6,22},{7,23},{8,24},{9,... | collective-permute-start | bytes 98312 | tf_op jit(solution)/shard_map/ppermute | solution.py:29
  144.8 7.0 %collective-permute-start.15 = (f32[2,4096]{1,0:T(2,128)S(1)}, f32[2,4096]{1,0:T(2,128)S(1)}, u32[]{:S(2)}, u32[]{:S(2)}) collective-permute-start(f32[2,4096]{1,0:T(2,128)S(1)} %get-tuple-element.10), channel_id=1, source_target_pairs={{0,8},{1,9},{2,10},{3,11},{4,12},{5,13},{6,14},{7,15},{8,16},{9,17... | collective-permute-start | bytes 98312 | tf_op jit(solution)/shard_map/ppermute | solution.py:29

commit v3 on v2

v3 whole, which is shorter than its diff:
```python
import functools

import jax
import jax.numpy as jnp
from jax import lax
from jax.experimental import pallas as pl
from jax.experimental.pallas import tpu as pltpu
from jax.sharding import PartitionSpec as P

TILE = 8


SHARPNESS = 50.0

VMEM = pl.BlockSpec(memory_space=pltpu.VMEM)
SMEM = pl.BlockSpec(memory_space=pltpu.SMEM)
ANY = pl.BlockSpec(memory_space=pl.ANY)


def contract(left, right):
    return lax.dot_general(
        left, right, (((1,), (1,)), ((), ())), preferred_element_type=jnp.float32
    )


def transposed(left, right):
    return lax.dot_general(
        left, right, (((0,), (0,)), ((), ())), preferred_element_type=jnp.float32
    )


def shifts(block, step, count, move, sign):
    def moved(j):
        digit = j // step % count
        return j + ((digit + sign * move) % count - digit) * step

    return lax.ppermute(block, "pool", [(j, moved(j)) for j in range(lax.axis_size("pool"))])


def gather_kernel(picks_ref, tiles_ref, out_ref, sems):
    slots, peers = picks_ref.shape
    copies = []
    for peer in range(peers):
        for slot in range(slots):
            j = peer * slots + slot
            copy = pltpu.make_async_copy(
                tiles_ref.at[picks_ref[slot, peer]], out_ref.at[j], sems.at[j]
            )
            copy.start()
            copies.append(copy)
    for copy in copies:
        copy.wait()


def gather_tiles(picks, tiles):
    slots, peers = picks.shape
    return pl.pallas_call(
        gather_kernel,
        out_shape=jax.ShapeDtypeStruct((peers * slots,) + tiles.shape[1:], tiles.dtype),
        in_specs=[SMEM, ANY],
        out_specs=ANY,
        scratch_shapes=[pltpu.SemaphoreType.DMA((peers * slots,))],
        cost_estimate=pl.CostEstimate(flops=0, bytes_accessed=3 << 20, transcendentals=0),
        name="gather_tiles",
    )(picks, tiles)


def scores_kernel(keys_ref, queries_ref, out_ref):
    out_ref[...] = SHARPNESS * contract(keys_ref[...], queries_ref[...])


def scores(keys, queries):
    return pl.pallas_call(
        scores_kernel,
        out_shape=jax.ShapeDtypeStruct((keys.shape[0], queries.shape[0]), jnp.float32),
        in_specs=[VMEM, VMEM],
        out_specs=VMEM,
        cost_estimate=pl.CostEstimate(flops=1 << 20, bytes_accessed=1 << 20, transcendentals=0),
        name="scores",
    )(keys, queries)


def weights_kernel(
    chunk, queries_ref, hard_ref, local_ref, near_ref, far_ref, mask_ref, positives_ref,
    grad_ref, local_out, near_out, far_out, hard_out, buffer, sems,
):
    local, near, far = local_ref[...], near_ref[...], far_ref[...]
    hard = SHARPNESS * contract(hard_ref[...], queries_ref[...])
    hard = jnp.where(mask_ref[...] > 0.0, hard, -jnp.inf)
    top = lambda x: jnp.max(x, axis=0, keepdims=True)
    highest = jnp.maximum(jnp.maximum(top(local), top(near)), jnp.maximum(top(far), top(hard)))
    local, near, far = jnp.exp(local - highest), jnp.exp(near - highest), jnp.exp(far - highest)
    hard = jnp.exp(hard - highest)
    add = lambda x: jnp.sum(x, axis=0, keepdims=True)
    total = add(local) + add(near) + add(far) + add(hard)
    weight = (hard / total).astype(jnp.bfloat16)
    copies = []
    for i in range(queries_ref.shape[1] // chunk):
        columns = pl.ds(i * chunk, chunk)
        part = jnp.dot(weight, queries_ref[:, columns], preferred_element_type=jnp.float32)
        buffer[:, columns] = (SHARPNESS * part).astype(jnp.bfloat16)
        copy = pltpu.make_async_copy(buffer.at[:, columns], grad_ref.at[:, columns], sems.at[i])
        copy.start()
        copies.append(copy)
    hard_out[...] = weight
    rows = lax.broadcasted_iota(jnp.int32, local.shape, 0)
    target = (rows == positives_ref[...]).astype(jnp.float32)
    local_out[...] = (local / total - target).astype(jnp.bfloat16)
    near_out[...] = (near / total).astype(jnp.bfloat16)
    far_out[...] = (far / total).astype(jnp.bfloat16)
    for copy in copies:
        copy.wait()


def weights(queries, hard_rows, local, near, far, mask, positives, chunk=1024):
    hard, width = hard_rows.shape
    like = lambda x: jax.ShapeDtypeStruct(x.shape, jnp.bfloat16)
    return pl.pallas_call(
        functools.partial(weights_kernel, chunk),
        out_shape=(
            jax.ShapeDtypeStruct((hard, width), jnp.bfloat16),
            like(local), like(near), like(far), like(mask),
        ),
        in_specs=[VMEM] * 7,
        out_specs=(ANY, VMEM, VMEM, VMEM, VMEM),
        scratch_shapes=[
            pltpu.VMEM((hard, width), jnp.bfloat16),
            pltpu.SemaphoreType.DMA((width // chunk,)),
        ],
        cost_estimate=pl.CostEstimate(flops=1 << 20, bytes_accessed=1 << 20, transcendentals=0),
        name="weights",
    )(queries, hard_rows, local, near, far, mask, positives)


def pool_kernel(near_ref, far_ref, queries_ref, near_out, far_out):
    near_out[...] = SHARPNESS * jnp.dot(
        near_ref[...], queries_ref[...], preferred_element_type=jnp.float32
    )
    far = SHARPNESS * jnp.dot(far_ref[...], queries_ref[...], preferred_element_type=jnp.float32)
    far_out[...] = far.astype(far_out.dtype)


def pool_terms(near, far, queries, link):
    shape = (near.shape[0], queries.shape[1])
    return pl.pallas_call(
        pool_kernel,
        out_shape=(jax.ShapeDtypeStruct(shape, jnp.float32), jax.ShapeDtypeStruct(shape, link)),
        in_specs=[VMEM] * 3,
        out_specs=(VMEM, VMEM),
        cost_estimate=pl.CostEstimate(flops=1 << 20, bytes_accessed=1 << 20, transcendentals=0),
        name="pool_terms",
    )(near, far, queries)


def queries_kernel(chunk, *refs):
    pairs, (out_ref, buffer, sems) = refs[:-3], refs[-3:]
    count = len(pairs) // 2
    copies = []
    for i in range(out_ref.shape[1] // chunk):
        columns = pl.ds(i * chunk, chunk)
        part = transposed(pairs[0][...], pairs[count][:, columns])
        for k in range(1, count):
            part = part + transposed(pairs[k][...], pairs[count + k][:, columns])
        buffer[:, columns] = (SHARPNESS * part).astype(jnp.bfloat16)
        copy = pltpu.make_async_copy(buffer.at[:, columns], out_ref.at[:, columns], sems.at[i])
        copy.start()
        copies.append(copy)
    for copy in copies:
        copy.wait()


def query_gradient(weight, keys, chunk=1024):
    rows, width = weight[0].shape[1], keys[0].shape[1]
    return pl.pallas_call(
        functools.partial(queries_kernel, chunk),
        out_shape=jax.ShapeDtypeStruct((rows, width), jnp.bfloat16),
        in_specs=[VMEM] * (len(weight) + len(keys)),
        out_specs=ANY,
        scratch_shapes=[
            pltpu.VMEM((rows, width), jnp.bfloat16),
            pltpu.SemaphoreType.DMA((width // chunk,)),
        ],
        cost_estimate=pl.CostEstimate(flops=1 << 20, bytes_accessed=1 << 20, transcendentals=0),
        name="query_gradient",
    )(*weight, *keys)


def passages_kernel(
    chunk, weight_ref, queries_ref, wanted_ref, returned_ref, out_ref, buffer, sems
):
    weight = weight_ref[...]
    rows, hard = weight.shape[0], wanted_ref.shape[1]
    chosen = (
        lax.broadcasted_iota(jnp.int32, (rows, hard), 0) == wanted_ref[...]
    ).astype(jnp.bfloat16)
    copies = []
    for i in range(out_ref.shape[1] // chunk):
        columns = pl.ds(i * chunk, chunk)
        part = SHARPNESS * jnp.dot(
            weight, queries_ref[:, columns], preferred_element_type=jnp.float32
        )
        part = part + jnp.dot(
            chosen, returned_ref[:, columns], preferred_element_type=jnp.float32
        )
        buffer[:, columns] = part.astype(jnp.bfloat16)
        copy = pltpu.make_async_copy(buffer.at[:, columns], out_ref.at[:, columns], sems.at[i])
        copy.start()
        copies.append(copy)
    for copy in copies:
        copy.wait()


def passage_gradient(weight, queries, wanted, returned, chunk=1024):
    rows, width = weight.shape[0], queries.shape[1]
    return pl.pallas_call(
        functools.partial(passages_kernel, chunk),
        out_shape=jax.ShapeDtypeStruct((rows, width), jnp.bfloat16),
        in_specs=[VMEM] * 4,
        out_specs=ANY,
        scratch_shapes=[
            pltpu.VMEM((rows, width), jnp.bfloat16),
            pltpu.SemaphoreType.DMA((width // chunk,)),
        ],
        cost_estimate=pl.CostEstimate(flops=1 << 20, bytes_accessed=1 << 20, transcendentals=0),
        name="passage_gradient",
    )(weight, queries, wanted, returned)


def body(digits, queries, passages, pool_passages, positives, tile_ids, tile_count):
    rows, width = queries.shape
    picks = tile_ids[0, 0]
    peers, slots = picks.shape
    hard = peers * slots * TILE
    outgoing = gather_tiles(picks.T, passages.reshape(rows // TILE, TILE, width))
    hard_rows = lax.all_to_all(
        outgoing.reshape(peers, slots * TILE, width), "pb", split_axis=0, concat_axis=0, tiled=True
    ).reshape(hard, width)
    pooled = pool_passages
    for step, count, _ in digits[:-1]:
        pooled = jnp.concatenate(
            [pooled] + [shifts(pooled, step, count, m, -1) for m in range(1, count)], axis=0
        )
    near = pooled
    last_step, last_count, last_link = digits[-1]
    far = shifts(pooled, last_step, last_count, 1, -1)
    live = jnp.arange(slots, dtype=jnp.int32)[None, :] < tile_count[0, 0][:, None]
    mask = jnp.broadcast_to(live[:, :, None, None], (peers, slots, TILE, rows))
    mask = mask.reshape(hard, rows).astype(jnp.float32)
    grad_hard, local_weight, near_weight, far_weight, hard_weight = weights(
        queries, hard_rows, scores(passages, queries), scores(near, queries), scores(far, queries),
        mask, positives[None, :],
    )
    returned = lax.all_to_all(
        grad_hard.reshape(peers, slots * TILE, width), "pb", split_axis=0, concat_axis=0, tiled=True
    ).reshape(hard, width)
    term, sent = pool_terms(near_weight, far_weight, queries, last_link)
    term = term + shifts(sent, last_step, last_count, 1, 1).astype(jnp.float32)
    for step, count, link in reversed(digits[:-1]):
        size = term.shape[0] // count
        pieces = [term[m * size : (m + 1) * size] for m in range(count)]
        term = pieces[0]
        for m in range(1, count):
            term = term + shifts(pieces[m].astype(link), step, count, m, 1).astype(jnp.float32)
    grad_pool = term.astype(jnp.bfloat16)
    grad_queries = query_gradient(
        (local_weight, near_weight, far_weight, hard_weight), (passages, near, far, hard_rows)
    )
    wanted = (
        picks.reshape(-1)[:, None] * TILE + jnp.arange(TILE, dtype=jnp.int32)[None, :]
    ).reshape(1, hard)
    grad_passages = passage_gradient(local_weight, queries, wanted, returned)
    return (grad_queries, grad_passages, grad_pool)


def solution(mesh):
    digits = ((8, 8, jnp.float32), (2, 4, jnp.bfloat16), (1, 2, jnp.float32))
    return jax.shard_map(
        lambda *args: body(digits, *args),
        mesh=mesh,
        in_specs=(
            P(("pb", "pool"), None),
            P(("pb", "pool"), None),
            P(("pb", "pool"), None),
            P(("pb", "pool")),
            P("pb", "pool", None, None),
            P("pb", "pool", None),
        ),
        out_specs=(P(("pb", "pool"), None), P(("pb", "pool"), None), P(("pb", "pool"), None)),
        check_vma=False,
    )
```

time: 165 us -> 209 us (1.27)
  Pallas kernels: 0 us -> 72.6 us
  matrix products: 19.1 us -> 0 us
  local copies, waits for them, and re-layouts: 13.2 us -> 4.77 us
  waiting for transfers between devices: 19.5 us -> 26 us
  starting transfers between devices: 105 us -> 102 us
    pallas_call x0 -> x8, Pallas kernels: none -> 72.6 us  [the longest x1 49.7 us: gather_tiles(): pl.pallas_call(gather_kernel, out_shape=jax.ShapeDtypeStruct((peers * slo...]
    dot_general x11 -> x0, matrix products: 19.1 us -> none  [the longest x4 7.68 us: transposed(): lax.dot_general(left, right, (((0,), (0,)), ((), ())), preferred_element_...]
    concatenate x3 -> x2, local copies, waits for them, and re-layouts: 9.57 us -> 0.42 us  [body(): jnp.concatenate([pooled] + [shifts(pooled, step, count, m, -1) for m in r...]
    all_to_all x1, waiting for transfers between devices: 6.3 us -> 11.1 us  [body(): lax.all_to_all(grad_hard.reshape(peers, slots * TILE, width), 'pb', split...]
    ppermute x22, starting transfers between devices: 80.4 us -> 76.7 us  [shifts(): lax.ppermute(block, 'pool', [(j, moved(j)) for j in range(lax.axis_size('...]
  transfers between devices with their start and end apart: 24 -> 24, of which waited for: 7 -> 6; matrix products, arithmetic and copies ran while one was open for 15% -> 2% of each run, Pallas kernels for 0% -> 6%
where the time goes in v3:
time: 209 us; the launch traced here: 208 us
  starting transfers between devices  102 us (49%)
  Pallas kernels  72.6 us (35%)
  waiting for transfers between devices  26 us (12%)
  local copies, waits for them, and re-layouts  4.77 us (2%)
  other arithmetic  2.23 us (1%)
    ppermute x22, starting transfers between devices, shifts(): lax.ppermute(block, 'pool', [(j, moved(j)) for j in range(lax.axis_size('...  76.7 us
    pallas_call x1, Pallas kernels, gather_tiles(): pl.pallas_call(gather_kernel, out_shape=jax.ShapeDtypeStruct((peers * slo...  49.7 us
    all_to_all x1, starting transfers between devices, body(): lax.all_to_all(outgoing.reshape(peers, slots * TILE, width), 'pb', split_...  15.2 us
    ppermute x22, waiting for transfers between devices, shifts(): lax.ppermute(block, 'pool', [(j, moved(j)) for j in range(lax.axis_size('...  14.9 us
    all_to_all x1, waiting for transfers between devices, body(): lax.all_to_all(grad_hard.reshape(peers, slots * TILE, width), 'pb', split...  11.1 us
    all_to_all x1, starting transfers between devices, body(): lax.all_to_all(grad_hard.reshape(peers, slots * TILE, width), 'pb', split...  9.74 us
    pallas_call x3, Pallas kernels, scores(): pl.pallas_call(scores_kernel, out_shape=jax.ShapeDtypeStruct((keys.shape[...  7.58 us
    pallas_call x1, Pallas kernels, weights(): pl.pallas_call(functools.partial(weights_kernel, chunk), out_shape=(jax.S...  5.17 us
  transfers between devices with their start and end apart: 24, of which 6 were waited for; matrix products, arithmetic and copies ran while one was open for 2% of the time, Pallas kernels for 6%

profile of v3, /device:TPU:6, one launch (start us, length us, event | category | flops | bytes accessed | tf_op | source)
XLA Modules:
  0.0 208.3 jit_solution(4024002099017804018)
XLA Ops:
  0.6 49.7 %gather_tiles.1 = bf16[24,8,4096]{2,1,0:T(8,128)(2,1)} custom-call(s32[2,12]{1,0:T(2,128)} %bitcast.16, bf16[16,8,4096]{2,1,0:T(8,128)(2,1)} %bitcast.12), custom_call_target="tpu_custom_call" | custom-call | bytes 3145728 | tf_op jit(solution)/shard_map/gather_tiles/pallas_call | solution.py:57
  50.3 0.0 copy-start.5
  50.3 0.0 copy-start.7
  50.3 15.2 %all-to-all-start = ((bf16[12,16,4096]{2,1,0:T(8,128)(2,1)}), bf16[12,16,4096]{2,1,0:T(8,128)(2,1)S(1)}, u32[]{:S(2)}, u32[]{:S(2)}) async-start(bf16[12,16,4096]{2,1,0:T(8,128)(2,1)} %bitcast.14), calls=%async_computation | async-start | bytes 3145728 | tf_op jit(solution)/shard_map/all_to_all | solution.py:235
  65.5 3.5 %collective-permute-start.6 = (bf16[2,4096]{1,0:T(2,128)(2,1)S(1)}, bf16[2,4096]{1,0:T(2,128)(2,1)S(1)}, u32[]{:S(2)}, u32[]{:S(2)}) collective-permute-start(bf16[2,4096]{1,0:T(2,128)(2,1)S(1)} %copy-done.5), channel_id=1, source_target_pairs={{0,8},{1,9},{2,10},{3,11},{4,12},{5,13},{6,14},{7,15},{8,16},{9,17... | collective-permute-start | bytes 49160 | tf_op jit(solution)/shard_map/ppermute | solution.py:37
  69.0 4.5 %collective-permute-start.5 = (bf16[2,4096]{1,0:T(2,128)(2,1)S(1)}, bf16[2,4096]{1,0:T(2,128)(2,1)S(1)}, u32[]{:S(2)}, u32[]{:S(2)}) collective-permute-start(bf16[2,4096]{1,0:T(2,128)(2,1)S(1)} %copy-done.5), channel_id=1, source_target_pairs={{0,16},{1,17},{2,18},{3,19},{4,20},{5,21},{6,22},{7,23},{8,24},{9,... | collective-permute-start | bytes 49160 | tf_op jit(solution)/shard_map/ppermute | solution.py:37
  73.5 4.9 %collective-permute-start.4 = (bf16[2,4096]{1,0:T(2,128)(2,1)S(1)}, bf16[2,4096]{1,0:T(2,128)(2,1)S(1)}, u32[]{:S(2)}, u32[]{:S(2)}) collective-permute-start(bf16[2,4096]{1,0:T(2,128)(2,1)S(1)} %copy-done.5), channel_id=1, source_target_pairs={{0,24},{1,25},{2,26},{3,27},{4,28},{5,29},{6,30},{7,31},{8,32},{9,... | collective-permute-start | bytes 49160 | tf_op jit(solution)/shard_map/ppermute | solution.py:37
  78.4 3.8 %collective-permute-start.3 = (bf16[2,4096]{1,0:T(2,128)(2,1)S(1)}, bf16[2,4096]{1,0:T(2,128)(2,1)S(1)}, u32[]{:S(2)}, u32[]{:S(2)}) collective-permute-start(bf16[2,4096]{1,0:T(2,128)(2,1)S(1)} %copy-done.5), channel_id=1, source_target_pairs={{0,32},{1,33},{2,34},{3,35},{4,36},{5,37},{6,38},{7,39},{8,40},{9,... | collective-permute-start | bytes 49160 | tf_op jit(solution)/shard_map/ppermute | solution.py:37
  82.2 5.2 %collective-permute-start.2 = (bf16[2,4096]{1,0:T(2,128)(2,1)S(1)}, bf16[2,4096]{1,0:T(2,128)(2,1)S(1)}, u32[]{:S(2)}, u32[]{:S(2)}) collective-permute-start(bf16[2,4096]{1,0:T(2,128)(2,1)S(1)} %copy-done.5), channel_id=1, source_target_pairs={{0,40},{1,41},{2,42},{3,43},{4,44},{5,45},{6,46},{7,47},{8,48},{9,... | collective-permute-start | bytes 49160 | tf_op jit(solution)/shard_map/ppermute | solution.py:37
  87.4 5.3 %collective-permute-start.1 = (bf16[2,4096]{1,0:T(2,128)(2,1)S(1)}, bf16[2,4096]{1,0:T(2,128)(2,1)S(1)}, u32[]{:S(2)}, u32[]{:S(2)}) collective-permute-start(bf16[2,4096]{1,0:T(2,128)(2,1)S(1)} %copy-done.5), channel_id=1, source_target_pairs={{0,48},{1,49},{2,50},{3,51},{4,52},{5,53},{6,54},{7,55},{8,56},{9,... | collective-permute-start | bytes 49160 | tf_op jit(solution)/shard_map/ppermute | solution.py:37
  92.7 0.0 collective-permute-done.5
  92.7 3.3 %collective-permute-start = (bf16[2,4096]{1,0:T(2,128)(2,1)S(1)}, bf16[2,4096]{1,0:T(2,128)(2,1)S(1)}, u32[]{:S(2)}, u32[]{:S(2)}) collective-permute-start(bf16[2,4096]{1,0:T(2,128)(2,1)S(1)} %copy-done.5), channel_id=1, source_target_pairs={{0,56},{1,57},{2,58},{3,59},{4,60},{5,61},{6,62},{7,63},{8,0},{9,1... | collective-permute-start | bytes 49160 | tf_op jit(solution)/shard_map/ppermute | solution.py:37
  96.0 0.0 collective-permute-done.3
  96.0 0.0 collective-permute-done.2
  96.0 2.3 %collective-permute-done = bf16[2,4096]{1,0:T(2,128)(2,1)S(1)} collective-permute-done((bf16[2,4096]{1,0:T(2,128)(2,1)S(1)}, bf16[2,4096]{1,0:T(2,128)(2,1)S(1)}, u32[]{:S(2)}, u32[]{:S(2)}) %collective-permute-start) | collective-permute-done | bytes 16416 | tf_op jit(solution)/shard_map/ppermute | solution.py:37
  98.3 0.2 concatenate.7
  98.5 2.4 %collective-permute-start.9 = (bf16[16,4096]{1,0:T(8,128)(2,1)S(1)}, bf16[16,4096]{1,0:T(8,128)(2,1)S(1)}, u32[]{:S(2)}, u32[]{:S(2)}) collective-permute-start(bf16[16,4096]{1,0:T(8,128)(2,1)S(1)} %concatenate.7), channel_id=1, source_target_pairs={{0,2},{1,3},{2,4},{3,5},{4,6},{5,7},{6,0},{7,1},{8,10},{9,11},{10,... | collective-permute-start | bytes 393224 | tf_op jit(solution)/shard_map/ppermute | solution.py:37
  100.9 4.3 %collective-permute-start.8 = (bf16[16,4096]{1,0:T(8,128)(2,1)S(1)}, bf16[16,4096]{1,0:T(8,128)(2,1)S(1)}, u32[]{:S(2)}, u32[]{:S(2)}) collective-permute-start(bf16[16,4096]{1,0:T(8,128)(2,1)S(1)} %concatenate.7), channel_id=1, source_target_pairs={{0,4},{1,5},{2,6},{3,7},{4,0},{5,1},{6,2},{7,3},{8,12},{9,13},{10,... | collective-permute-start | bytes 393224 | tf_op jit(solution)/shard_map/ppermute | solution.py:37
  105.3 1.9 collective-permute-start.7
  107.2 0.0 collective-permute-done.9
  107.2 3.1 %collective-permute-done.8 = bf16[16,4096]{1,0:T(8,128)(2,1)S(1)} collective-permute-done((bf16[16,4096]{1,0:T(8,128)(2,1)S(1)}, bf16[16,4096]{1,0:T(8,128)(2,1)S(1)}, u32[]{:S(2)}, u32[]{:S(2)}) %collective-permute-start.8) | collective-permute-done | bytes 131104 | tf_op jit(solution)/shard_map/ppermute | solution.py:37
  110.2 3.1 %collective-permute-done.7 = bf16[16,4096]{1,0:T(8,128)(2,1)S(1)} collective-permute-done((bf16[16,4096]{1,0:T(8,128)(2,1)S(1)}, bf16[16,4096]{1,0:T(8,128)(2,1)S(1)}, u32[]{:S(2)}, u32[]{:S(2)}) %collective-permute-start.7) | collective-permute-done | bytes 131104 | tf_op jit(solution)/shard_map/ppermute | solution.py:37
  113.3 0.2 concatenate.8.keys_ref.refs_5_
  113.6 1.9 collective-permute-start.10
  115.5 0.1 fusion.7
  115.6 0.1 broadcast_in_dim.6
  115.6 0.1 convert_element_type.21
  115.8 2.6 %scores.3.local_ref = f32[128,128]{1,0:T(8,128)} custom-call(bf16[128,4096]{1,0:T(8,128)(2,1)} %refs_4_.1, bf16[128,4096]{1,0:T(8,128)(2,1)} %queries_ref.11), custom_call_target="tpu_custom_call" | custom-call | flops 1048576 | bytes 1048576 | tf_op jit(solution)/shard_map/scores/pallas_call | solution.py:73
  118.4 2.5 %scores.4.near_ref = f32[64,128]{1,0:T(8,128)} custom-call(bf16[64,4096]{1,0:T(8,128)(2,1)} %copy-done.2, bf16[128,4096]{1,0:T(8,128)(2,1)} %queries_ref.11), custom_call_target="tpu_custom_call" | custom-call | flops 1048576 | bytes 1048576 | tf_op jit(solution)/shard_map/scores/pallas_call | solution.py:73
  120.8 0.0 collective-permute-done.10.keys_ref.refs_6_
  120.9 0.8 copy-done.3
  121.7 2.5 %scores.5.far_ref = f32[64,128]{1,0:T(8,128)} custom-call(bf16[64,4096]{1,0:T(8,128)(2,1)} %copy-done.3, bf16[128,4096]{1,0:T(8,128)(2,1)} %queries_ref.11), custom_call_target="tpu_custom_call" | custom-call | flops 1048576 | bytes 1048576 | tf_op jit(solution)/shard_map/scores/pallas_call | solution.py:73
  124.2 0.8 broadcast_in_dim.14.mask_ref
  125.0 0.4 copy-done
  125.4 5.2 %weights.1 = (bf16[192,4096]{1,0:T(8,128)(2,1)}, bf16[128,128]{1,0:T(8,128)(2,1)}, bf16[64,128]{1,0:T(8,128)(2,1)}, bf16[64,128]{1,0:T(8,128)(2,1)}, bf16[192,128]{1,0:T(8,128)(2,1)}) custom-call(bf16[128,4096]{1,0:T(8,128)(2,1)} %queries_ref.11, bf16[192,4096]{1,0:T(8,128)(2,1)} %bitcast.10, f32[128,128]{1,0:T(8,128)} %scores.3.local_ref, ...), custom_call_target="tpu_custom_call" | custom-call | flops 1048576 | bytes 1048576 | tf_op jit(solution)/shard_map/weights/pallas_call | solution.py:118
  130.5 2.9 %pool_terms.1 = (f32[64,4096]{1,0:T(8,128)}, f32[64,4096]{1,0:T(8,128)}) custom-call(bf16[64,128]{1,0:T(8,128)(2,1)} %get-tuple-element.11.refs_1_.near_ref, bf16[64,128]{1,0:T(8,128)(2,1)} %get-tuple-element.12.refs_2_.far_ref, bf16[128,4096]{1,0:T(8,128)(2,1)} %queries_ref.11), custom_call_target="tpu_custom_call" | custom-call | flops 1048576 | bytes 1048576 | tf_op jit(solution)/shard_map/pool_terms/pallas_call | solution.py:145
  133.4 2.4 %collective-permute-start.11 = (f32[64,4096]{1,0:T(8,128)}, f32[64,4096]{1,0:T(8,128)}, u32[]{:S(2)}, u32[]{:S(2)}) collective-permute-start(f32[64,4096]{1,0:T(8,128)} %get-tuple-element.16), channel_id=1, source_target_pairs={{0,1},{1,0},{2,3},{3,2},{4,5},{5,4},{6,7},{7,6},{8,9},{9,8},{10,11... | collective-permute-start | bytes 3145736 | tf_op jit(solution)/shard_map/ppermute | solution.py:37
  135.8 0.0 copy-start.4
  135.8 9.7 %all-to-all-start.1 = ((bf16[12,16,4096]{2,1,0:T(8,128)(2,1)}), bf16[12,16,4096]{2,1,0:T(8,128)(2,1)S(1)}, u32[]{:S(2)}, u32[]{:S(2)}) async-start(bf16[12,16,4096]{2,1,0:T(8,128)(2,1)} %bitcast.15), calls=%async_computation.1 | async-start | bytes 3145728 | tf_op jit(solution)/shard_map/all_to_all | solution.py:253
  145.6 1.3 fusion.8
  147.0 0.0 copy-start.6
  147.0 2.5 %collective-permute-start.12 = (bf16[16,4096]{1,0:T(8,128)(2,1)S(1)}, bf16[16,4096]{1,0:T(8,128)(2,1)S(1)}, u32[]{:S(2)}, u32[]{:S(2)}) collective-permute-start(bf16[16,4096]{1,0:T(8,128)(2,1)S(1)} %get-tuple-element.19), channel_id=1, source_target_pairs={{0,2},{1,3},{2,4},{3,5},{4,6},{5,7},{6,0},{7,1},{8,10},{9,11},{10,... | collective-permute-start | bytes 393224 | tf_op jit(solution)/shard_map/ppermute | solution.py:37
  149.5 3.3 %collective-permute-start.14 = (bf16[16,4096]{1,0:T(8,128)(2,1)S(1)}, bf16[16,4096]{1,0:T(8,128)(2,1)S(1)}, u32[]{:S(2)}, u32[]{:S(2)}) collective-permute-start(bf16[16,4096]{1,0:T(8,128)(2,1)S(1)} %get-tuple-element.20), channel_id=1, source_target_pairs={{0,6},{1,7},{2,0},{3,1},{4,2},{5,3},{6,4},{7,5},{8,14},{9,15},{10,... | collective-permute-start | bytes 393224 | tf_op jit(solution)/shard_map/ppermute | solution.py:37
  152.9 2.0 collective-permute-start.13
  154.8 2.8 %collective-permute-done.14 = bf16[16,4096]{1,0:T(8,128)(2,1)S(1)} collective-permute-done((bf16[16,4096]{1,0:T(8,128)(2,1)S(1)}, bf16[16,4096]{1,0:T(8,128)(2,1)S(1)}, u32[]{:S(2)}, u32[]{:S(2)}) %collective-permute-start.14) | collective-permute-done | bytes 131104 | tf_op jit(solution)/shard_map/ppermute | solution.py:37
  157.6 3.6 %collective-permute-done.13 = bf16[16,4096]{1,0:T(8,128)(2,1)S(1)} collective-permute-done((bf16[16,4096]{1,0:T(8,128)(2,1)S(1)}, bf16[16,4096]{1,0:T(8,128)(2,1)S(1)}, u32[]{:S(2)}, u32[]{:S(2)}) %collective-permute-start.13) | collective-permute-done | bytes 131104 | tf_op jit(solution)/shard_map/ppermute | solution.py:37
  161.2 0.1 fusion.1
  161.3 0.1 fusion.10
  161.4 1.9 collective-permute-start.15
  163.3 5.1 %collective-permute-start.21 = (f32[2,4096]{1,0:T(2,128)S(1)}, f32[2,4096]{1,0:T(2,128)S(1)}, u32[]{:S(2)}, u32[]{:S(2)}) collective-permute-start(f32[2,4096]{1,0:T(2,128)S(1)} %get-tuple-element.23), channel_id=1, source_target_pairs={{0,56},{1,57},{2,58},{3,59},{4,60},{5,61},{6,62},{7,63},{8,0},{9,1... | collective-permute-start | bytes 98312 | tf_op jit(solution)/shard_map/ppermute | solution.py:37
  168.5 0.1 copy.10
  168.6 0.1 mul.12
  168.7 2.7 %collective-permute-start.20 = (f32[2,4096]{1,0:T(2,128)S(1)}, f32[2,4096]{1,0:T(2,128)S(1)}, u32[]{:S(2)}, u32[]{:S(2)}) collective-permute-start(f32[2,4096]{1,0:T(2,128)S(1)} %get-tuple-element.24), channel_id=1, source_target_pairs={{0,48},{1,49},{2,50},{3,51},{4,52},{5,53},{6,54},{7,55},{8,56},{9,... | collective-permute-start | bytes 98312 | tf_op jit(solution)/shard_map/ppermute | solution.py:37
  171.4 2.8 %collective-permute-start.19 = (f32[2,4096]{1,0:T(2,128)S(1)}, f32[2,4096]{1,0:T(2,128)S(1)}, u32[]{:S(2)}, u32[]{:S(2)}) collective-permute-start(f32[2,4096]{1,0:T(2,128)S(1)} %get-tuple-element.25), channel_id=1, source_target_pairs={{0,40},{1,41},{2,42},{3,43},{4,44},{5,45},{6,46},{7,47},{8,48},{9,... | collective-permute-start | bytes 98312 | tf_op jit(solution)/shard_map/ppermute | solution.py:37
  174.2 7.5 %collective-permute-start.18 = (f32[2,4096]{1,0:T(2,128)S(1)}, f32[2,4096]{1,0:T(2,128)S(1)}, u32[]{:S(2)}, u32[]{:S(2)}) collective-permute-start(f32[2,4096]{1,0:T(2,128)S(1)} %get-tuple-element.26), channel_id=1, source_target_pairs={{0,32},{1,33},{2,34},{3,35},{4,36},{5,37},{6,38},{7,39},{8,40},{9,... | collective-permute-start | bytes 98312 | tf_op jit(solution)/shard_map/ppermute | solution.py:37
  181.7 1.9 collective-permute-start.17
  183.6 3.6 %collective-permute-start.16 = (f32[2,4096]{1,0:T(2,128)S(1)}, f32[2,4096]{1,0:T(2,128)S(1)}, u32[]{:S(2)}, u32[]{:S(2)}) collective-permute-start(f32[2,4096]{1,0:T(2,128)S(1)} %get-tuple-element.28), channel_id=1, source_target_pairs={{0,16},{1,17},{2,18},{3,19},{4,20},{5,21},{6,22},{7,23},{8,24},{9,... | collective-permute-start | bytes 98312 | tf_op jit(solution)/shard_map/ppermute | solution.py:37
  187.2 0.1 iota_add_fusion
  187.3 0.6 add.59.wanted_ref
  187.9 4.1 %query_gradient.1 = bf16[128,4096]{1,0:T(8,128)(2,1)} custom-call(bf16[128,128]{1,0:T(8,128)(2,1)} %get-tuple-element.10.refs_0_.weight_ref, bf16[64,128]{1,0:T(8,128)(2,1)} %get-tuple-element.11.refs_1_.near_ref, bf16[64,128]{1,0:T(8,128)(2,1)} %get-tuple-element.12.refs_2_.far_ref, bf16[192,128]{1,0:T(8,128)(2,1)} %get-tuple-element.13.refs_3_, ...), custom_call_target="tpu_custom_call" | custom-call | flops 1048576 | bytes 1048576 | tf_op jit(solution)/shard_map/query_gradient/pallas_call | solution.py:174
  192.1 0.7 add_convert_fusion
  192.8 11.1 %all-to-all-done.1 = bf16[12,16,4096]{2,1,0:T(8,128)(2,1)S(1)} async-done(((bf16[12,16,4096]{2,1,0:T(8,128)(2,1)}), bf16[12,16,4096]{2,1,0:T(8,128)(2,1)S(1)}, u32[]{:S(2)}, u32[]{:S(2)}) %all-to-all-start.1) | async-done | bytes 1572896 | tf_op jit(solution)/shard_map/all_to_all | solution.py:253
  203.9 1.2 copy-done.1
  205.1 3.2 %passage_gradient.1 = bf16[128,4096]{1,0:T(8,128)(2,1)} custom-call(bf16[128,128]{1,0:T(8,128)(2,1)} %get-tuple-element.10.refs_0_.weight_ref, bf16[128,4096]{1,0:T(8,128)(2,1)} %queries_ref.11, s32[1,192]{1,0:T(1,128)} %add.59.wanted_ref, bf16[192,4096]{1,0:T(8,128)(2,1)} %bitcast.13), custom_call_target="tpu_custom_call" | custom-call | flops 1048576 | bytes 1048576 | tf_op jit(solution)/shard_map/passage_gradient/pallas_call | solution.py:215
  (24 shorter events, 0.1 us)
Async XLA Ops:
  50.3 15.2 %copy-start.5 = (bf16[2,4096]{1,0:T(2,128)(2,1)S(1)}, bf16[2,4096]{1,0:T(2,128)(2,1)}, u32[]{:S(2)}) copy-start(bf16[2,4096]{1,0:T(2,128)(2,1)} %param.8) | copy-start | bytes 49156
  50.3 65.2 %copy-start.7 = (s32[1,1,12]{2,1,0:T(1,128)S(1)}, s32[1,1,12]{2,1,0:T(1,128)}, u32[]{:S(2)}) copy-start(s32[1,1,12]{2,1,0:T(1,128)} %param.11) | copy-start | bytes 148
  50.3 73.8 %all-to-all-start = ((bf16[12,16,4096]{2,1,0:T(8,128)(2,1)}), bf16[12,16,4096]{2,1,0:T(8,128)(2,1)S(1)}, u32[]{:S(2)}, u32[]{:S(2)}) async-start(bf16[12,16,4096]{2,1,0:T(8,128)(2,1)} %bitcast.14), calls=%async_computation | async-start | bytes 3145728 | tf_op jit(solution)/shard_map/all_to_all | solution.py:235
  65.5 21.9 %collective-permute-start.6 = (bf16[2,4096]{1,0:T(2,128)(2,1)S(1)}, bf16[2,4096]{1,0:T(2,128)(2,1)S(1)}, u32[]{:S(2)}, u32[]{:S(2)}) collective-permute-start(bf16[2,4096]{1,0:T(2,128)(2,1)S(1)} %copy-done.5), channel_id=1, source_target_pairs={{0,8},{1,9},{2,10},{3,11},{4,12},{5,13},{6,14},{7,15},{8,16},{9,17... | collective-permute-start | bytes 49160 | tf_op jit(solution)/shard_map/ppermute | solution.py:37
  69.0 23.7 %collective-permute-start.5 = (bf16[2,4096]{1,0:T(2,128)(2,1)S(1)}, bf16[2,4096]{1,0:T(2,128)(2,1)S(1)}, u32[]{:S(2)}, u32[]{:S(2)}) collective-permute-start(bf16[2,4096]{1,0:T(2,128)(2,1)S(1)} %copy-done.5), channel_id=1, source_target_pairs={{0,16},{1,17},{2,18},{3,19},{4,20},{5,21},{6,22},{7,23},{8,24},{9,... | collective-permute-start | bytes 49160 | tf_op jit(solution)/shard_map/ppermute | solution.py:37
  73.5 22.5 %collective-permute-start.4 = (bf16[2,4096]{1,0:T(2,128)(2,1)S(1)}, bf16[2,4096]{1,0:T(2,128)(2,1)S(1)}, u32[]{:S(2)}, u32[]{:S(2)}) collective-permute-start(bf16[2,4096]{1,0:T(2,128)(2,1)S(1)} %copy-done.5), channel_id=1, source_target_pairs={{0,24},{1,25},{2,26},{3,27},{4,28},{5,29},{6,30},{7,31},{8,32},{9,... | collective-permute-start | bytes 49160 | tf_op jit(solution)/shard_map/ppermute | solution.py:37
  78.4 17.5 %collective-permute-start.3 = (bf16[2,4096]{1,0:T(2,128)(2,1)S(1)}, bf16[2,4096]{1,0:T(2,128)(2,1)S(1)}, u32[]{:S(2)}, u32[]{:S(2)}) collective-permute-start(bf16[2,4096]{1,0:T(2,128)(2,1)S(1)} %copy-done.5), channel_id=1, source_target_pairs={{0,32},{1,33},{2,34},{3,35},{4,36},{5,37},{6,38},{7,39},{8,40},{9,... | collective-permute-start | bytes 49160 | tf_op jit(solution)/shard_map/ppermute | solution.py:37
  82.2 13.7 %collective-permute-start.2 = (bf16[2,4096]{1,0:T(2,128)(2,1)S(1)}, bf16[2,4096]{1,0:T(2,128)(2,1)S(1)}, u32[]{:S(2)}, u32[]{:S(2)}) collective-permute-start(bf16[2,4096]{1,0:T(2,128)(2,1)S(1)} %copy-done.5), channel_id=1, source_target_pairs={{0,40},{1,41},{2,42},{3,43},{4,44},{5,45},{6,46},{7,47},{8,48},{9,... | collective-permute-start | bytes 49160 | tf_op jit(solution)/shard_map/ppermute | solution.py:37
  87.4 8.6 %collective-permute-start.1 = (bf16[2,4096]{1,0:T(2,128)(2,1)S(1)}, bf16[2,4096]{1,0:T(2,128)(2,1)S(1)}, u32[]{:S(2)}, u32[]{:S(2)}) collective-permute-start(bf16[2,4096]{1,0:T(2,128)(2,1)S(1)} %copy-done.5), channel_id=1, source_target_pairs={{0,48},{1,49},{2,50},{3,51},{4,52},{5,53},{6,54},{7,55},{8,56},{9,... | collective-permute-start | bytes 49160 | tf_op jit(solution)/shard_map/ppermute | solution.py:37
  92.7 5.6 %collective-permute-start = (bf16[2,4096]{1,0:T(2,128)(2,1)S(1)}, bf16[2,4096]{1,0:T(2,128)(2,1)S(1)}, u32[]{:S(2)}, u32[]{:S(2)}) collective-permute-start(bf16[2,4096]{1,0:T(2,128)(2,1)S(1)} %copy-done.5), channel_id=1, source_target_pairs={{0,56},{1,57},{2,58},{3,59},{4,60},{5,61},{6,62},{7,63},{8,0},{9,1... | collective-permute-start | bytes 49160 | tf_op jit(solution)/shard_map/ppermute | solution.py:37
  98.5 8.7 %collective-permute-start.9 = (bf16[16,4096]{1,0:T(8,128)(2,1)S(1)}, bf16[16,4096]{1,0:T(8,128)(2,1)S(1)}, u32[]{:S(2)}, u32[]{:S(2)}) collective-permute-start(bf16[16,4096]{1,0:T(8,128)(2,1)S(1)} %concatenate.7), channel_id=1, source_target_pairs={{0,2},{1,3},{2,4},{3,5},{4,6},{5,7},{6,0},{7,1},{8,10},{9,11},{10,... | collective-permute-start | bytes 393224 | tf_op jit(solution)/shard_map/ppermute | solution.py:37
  100.9 9.3 %collective-permute-start.8 = (bf16[16,4096]{1,0:T(8,128)(2,1)S(1)}, bf16[16,4096]{1,0:T(8,128)(2,1)S(1)}, u32[]{:S(2)}, u32[]{:S(2)}) collective-permute-start(bf16[16,4096]{1,0:T(8,128)(2,1)S(1)} %concatenate.7), channel_id=1, source_target_pairs={{0,4},{1,5},{2,6},{3,7},{4,0},{5,1},{6,2},{7,3},{8,12},{9,13},{10,... | collective-permute-start | bytes 393224 | tf_op jit(solution)/shard_map/ppermute | solution.py:37
  105.3 8.1 %collective-permute-start.7 = (bf16[16,4096]{1,0:T(8,128)(2,1)S(1)}, bf16[16,4096]{1,0:T(8,128)(2,1)S(1)}, u32[]{:S(2)}, u32[]{:S(2)}) collective-permute-start(bf16[16,4096]{1,0:T(8,128)(2,1)S(1)} %concatenate.7), channel_id=1, source_target_pairs={{0,6},{1,7},{2,0},{3,1},{4,2},{5,3},{6,4},{7,5},{8,14},{9,15},{10,... | collective-permute-start | bytes 393224 | tf_op jit(solution)/shard_map/ppermute | solution.py:37
  113.6 4.8 %copy-start.2 = (bf16[64,4096]{1,0:T(8,128)(2,1)}, bf16[64,4096]{1,0:T(8,128)(2,1)S(1)}, u32[]{:S(2)}) copy-start(bf16[64,4096]{1,0:T(8,128)(2,1)S(1)} %concatenate.8.keys_ref.refs_5_) | copy-start | bytes 1572868
  113.6 7.3 %collective-permute-start.10 = (bf16[64,4096]{1,0:T(8,128)(2,1)S(1)}, bf16[64,4096]{1,0:T(8,128)(2,1)S(1)}, u32[]{:S(2)}, u32[]{:S(2)}) collective-permute-start(bf16[64,4096]{1,0:T(8,128)(2,1)S(1)} %concatenate.8.keys_ref.refs_5_), channel_id=1, source_target_pairs={{0,1},{1,0},{2,3},{3,2},{4,5},{5,4},{6,7},{7,6},{8,9},{9,8},{10,11... | collective-permute-start | bytes 1572872 | tf_op jit(solution)/shard_map/ppermute | solution.py:37
  120.9 0.8 copy-start.3
  124.1 1.2 copy-start
  133.4 12.2 %collective-permute-start.11 = (f32[64,4096]{1,0:T(8,128)}, f32[64,4096]{1,0:T(8,128)}, u32[]{:S(2)}, u32[]{:S(2)}) collective-permute-start(f32[64,4096]{1,0:T(8,128)} %get-tuple-element.16), channel_id=1, source_target_pairs={{0,1},{1,0},{2,3},{3,2},{4,5},{5,4},{6,7},{7,6},{8,9},{9,8},{10,11... | collective-permute-start | bytes 3145736 | tf_op jit(solution)/shard_map/ppermute | solution.py:37
  135.8 9.8 %copy-start.4 = (f32[64,4096]{1,0:T(8,128)S(1)}, f32[64,4096]{1,0:T(8,128)}, u32[]{:S(2)}) copy-start(f32[64,4096]{1,0:T(8,128)} %get-tuple-element.15) | copy-start | bytes 3145732
  135.8 68.1 %all-to-all-start.1 = ((bf16[12,16,4096]{2,1,0:T(8,128)(2,1)}), bf16[12,16,4096]{2,1,0:T(8,128)(2,1)S(1)}, u32[]{:S(2)}, u32[]{:S(2)}) async-start(bf16[12,16,4096]{2,1,0:T(8,128)(2,1)} %bitcast.15), calls=%async_computation.1 | async-start | bytes 3145728 | tf_op jit(solution)/shard_map/all_to_all | solution.py:253
  147.0 21.5 %copy-start.6 = (s32[1,1,12,2]{2,3,1,0:T(2,128)S(1)}, s32[1,1,12,2]{2,3,1,0:T(2,128)}, u32[]{:S(2)}) copy-start(s32[1,1,12,2]{2,3,1,0:T(2,128)} %param.10) | copy-start | bytes 292
  147.0 7.8 %collective-permute-start.12 = (bf16[16,4096]{1,0:T(8,128)(2,1)S(1)}, bf16[16,4096]{1,0:T(8,128)(2,1)S(1)}, u32[]{:S(2)}, u32[]{:S(2)}) collective-permute-start(bf16[16,4096]{1,0:T(8,128)(2,1)S(1)} %get-tuple-element.19), channel_id=1, source_target_pairs={{0,2},{1,3},{2,4},{3,5},{4,6},{5,7},{6,0},{7,1},{8,10},{9,11},{10,... | collective-permute-start | bytes 393224 | tf_op jit(solution)/shard_map/ppermute | solution.py:37
  149.5 8.1 %collective-permute-start.14 = (bf16[16,4096]{1,0:T(8,128)(2,1)S(1)}, bf16[16,4096]{1,0:T(8,128)(2,1)S(1)}, u32[]{:S(2)}, u32[]{:S(2)}) collective-permute-start(bf16[16,4096]{1,0:T(8,128)(2,1)S(1)} %get-tuple-element.20), channel_id=1, source_target_pairs={{0,6},{1,7},{2,0},{3,1},{4,2},{5,3},{6,4},{7,5},{8,14},{9,15},{10,... | collective-permute-start | bytes 393224 | tf_op jit(solution)/shard_map/ppermute | solution.py:37
  152.9 8.4 %collective-permute-start.13 = (bf16[16,4096]{1,0:T(8,128)(2,1)S(1)}, bf16[16,4096]{1,0:T(8,128)(2,1)S(1)}, u32[]{:S(2)}, u32[]{:S(2)}) collective-permute-start(bf16[16,4096]{1,0:T(8,128)(2,1)S(1)} %get-tuple-element.21), channel_id=1, source_target_pairs={{0,4},{1,5},{2,6},{3,7},{4,0},{5,1},{6,2},{7,3},{8,12},{9,13},{10,... | collective-permute-start | bytes 393224 | tf_op jit(solution)/shard_map/ppermute | solution.py:37
  161.4 20.3 %collective-permute-start.15 = (f32[2,4096]{1,0:T(2,128)S(1)}, f32[2,4096]{1,0:T(2,128)S(1)}, u32[]{:S(2)}, u32[]{:S(2)}) collective-permute-start(f32[2,4096]{1,0:T(2,128)S(1)} %get-tuple-element.22), channel_id=1, source_target_pairs={{0,8},{1,9},{2,10},{3,11},{4,12},{5,13},{6,14},{7,15},{8,16},{9,17... | collective-permute-start | bytes 98312 | tf_op jit(solution)/shard_map/ppermute | solution.py:37
  163.3 20.3 %collective-permute-start.21 = (f32[2,4096]{1,0:T(2,128)S(1)}, f32[2,4096]{1,0:T(2,128)S(1)}, u32[]{:S(2)}, u32[]{:S(2)}) collective-permute-start(f32[2,4096]{1,0:T(2,128)S(1)} %get-tuple-element.23), channel_id=1, source_target_pairs={{0,56},{1,57},{2,58},{3,59},{4,60},{5,61},{6,62},{7,63},{8,0},{9,1... | collective-permute-start | bytes 98312 | tf_op jit(solution)/shard_map/ppermute | solution.py:37
  168.7 23.4 %collective-permute-start.20 = (f32[2,4096]{1,0:T(2,128)S(1)}, f32[2,4096]{1,0:T(2,128)S(1)}, u32[]{:S(2)}, u32[]{:S(2)}) collective-permute-start(f32[2,4096]{1,0:T(2,128)S(1)} %get-tuple-element.24), channel_id=1, source_target_pairs={{0,48},{1,49},{2,50},{3,51},{4,52},{5,53},{6,54},{7,55},{8,56},{9,... | collective-permute-start | bytes 98312 | tf_op jit(solution)/shard_map/ppermute | solution.py:37
  171.4 20.7 %collective-permute-start.19 = (f32[2,4096]{1,0:T(2,128)S(1)}, f32[2,4096]{1,0:T(2,128)S(1)}, u32[]{:S(2)}, u32[]{:S(2)}) collective-permute-start(f32[2,4096]{1,0:T(2,128)S(1)} %get-tuple-element.25), channel_id=1, source_target_pairs={{0,40},{1,41},{2,42},{3,43},{4,44},{5,45},{6,46},{7,47},{8,48},{9,... | collective-permute-start | bytes 98312 | tf_op jit(solution)/shard_map/ppermute | solution.py:37
  174.2 17.9 %collective-permute-start.18 = (f32[2,4096]{1,0:T(2,128)S(1)}, f32[2,4096]{1,0:T(2,128)S(1)}, u32[]{:S(2)}, u32[]{:S(2)}) collective-permute-start(f32[2,4096]{1,0:T(2,128)S(1)} %get-tuple-element.26), channel_id=1, source_target_pairs={{0,32},{1,33},{2,34},{3,35},{4,36},{5,37},{6,38},{7,39},{8,40},{9,... | collective-permute-start | bytes 98312 | tf_op jit(solution)/shard_map/ppermute | solution.py:37
  181.7 10.4 %collective-permute-start.17 = (f32[2,4096]{1,0:T(2,128)S(1)}, f32[2,4096]{1,0:T(2,128)S(1)}, u32[]{:S(2)}, u32[]{:S(2)}) collective-permute-start(f32[2,4096]{1,0:T(2,128)S(1)} %get-tuple-element.27), channel_id=1, source_target_pairs={{0,24},{1,25},{2,26},{3,27},{4,28},{5,29},{6,30},{7,31},{8,32},{9,... | collective-permute-start | bytes 98312 | tf_op jit(solution)/shard_map/ppermute | solution.py:37
  183.6 8.5 %collective-permute-start.16 = (f32[2,4096]{1,0:T(2,128)S(1)}, f32[2,4096]{1,0:T(2,128)S(1)}, u32[]{:S(2)}, u32[]{:S(2)}) collective-permute-start(f32[2,4096]{1,0:T(2,128)S(1)} %get-tuple-element.28), channel_id=1, source_target_pairs={{0,16},{1,17},{2,18},{3,19},{4,20},{5,21},{6,22},{7,23},{8,24},{9,... | collective-permute-start | bytes 98312 | tf_op jit(solution)/shard_map/ppermute | solution.py:37
  203.9 1.2 copy-start.1

commit v4 on v3

v4 whole, which is shorter than its diff:
```python
import functools

import jax
import jax.numpy as jnp
from jax import lax
from jax.experimental import pallas as pl
from jax.experimental.pallas import tpu as pltpu
from jax.sharding import PartitionSpec as P

TILE = 8


SHARPNESS = 50.0

VMEM = pl.BlockSpec(memory_space=pltpu.VMEM)
SMEM = pl.BlockSpec(memory_space=pltpu.SMEM)
HBM = pl.BlockSpec(memory_space=pltpu.HBM)
PARAMS = pltpu.CompilerParams(vmem_limit_bytes=8 << 20)
CHEAP = pl.CostEstimate(flops=1 << 20, bytes_accessed=1 << 20, transcendentals=0)


def contract(left, right):
    return lax.dot_general(
        left, right, (((1,), (1,)), ((), ())), preferred_element_type=jnp.float32
    )


def transposed(left, right):
    return lax.dot_general(
        left, right, (((0,), (0,)), ((), ())), preferred_element_type=jnp.float32
    )


def shifts(block, moves, sign):
    def moved(j):
        for step, count, move in moves:
            digit = j // step % count
            j += ((digit + sign * move) % count - digit) * step
        return j

    return lax.ppermute(block, "pool", [(j, moved(j)) for j in range(lax.axis_size("pool"))])


def gather_kernel(picks_ref, tiles_ref, out_ref, buffer, load_sems, store_sems):
    slots, peers = picks_ref.shape
    loads, stores = [], []
    for j in range(peers * slots):
        tile = tiles_ref.at[picks_ref[j % slots, j // slots]]
        loads.append(pltpu.make_async_copy(tile, buffer.at[j], load_sems.at[j]))
        loads[-1].start()
    for j, load in enumerate(loads):
        load.wait()
        stores.append(pltpu.make_async_copy(buffer.at[j], out_ref.at[j], store_sems.at[j]))
        stores[-1].start()
    for store in stores:
        store.wait()


def gather_tiles(picks, tiles):
    slots, peers = picks.shape
    shape = (peers * slots,) + tiles.shape[1:]
    return pl.pallas_call(
        gather_kernel,
        out_shape=pltpu.HBM(shape, tiles.dtype),
        in_specs=[SMEM, HBM],
        out_specs=HBM,
        scratch_shapes=[
            pltpu.VMEM(shape, tiles.dtype),
            pltpu.SemaphoreType.DMA((peers * slots,)),
            pltpu.SemaphoreType.DMA((peers * slots,)),
        ],
        compiler_params=PARAMS,
        cost_estimate=pl.CostEstimate(flops=0, bytes_accessed=3 << 20, transcendentals=0),
        name="gather_tiles",
    )(picks, pltpu.with_memory_space_constraint(tiles, pltpu.HBM))


def scores_kernel(keys_ref, queries_ref, out_ref):
    out_ref[...] = SHARPNESS * contract(keys_ref[...], queries_ref[...])


def scores(keys, queries):
    return pl.pallas_call(
        scores_kernel,
        out_shape=jax.ShapeDtypeStruct((keys.shape[0], queries.shape[0]), jnp.float32),
        in_specs=[VMEM, VMEM],
        out_specs=VMEM,
        compiler_params=PARAMS,
        cost_estimate=CHEAP,
        name="scores",
    )(keys, queries)


def weights_kernel(
    chunk, queries_ref, hard_ref, local_ref, near_ref, far_ref, counts_ref, positives_ref,
    grad_ref, local_out, near_out, far_out, hard_out, buffer, sems,
):
    local, near, far = local_ref[...], near_ref[...], far_ref[...]
    hard = SHARPNESS * contract(hard_ref[...], queries_ref[...])
    peers = counts_ref.shape[1]
    size = hard.shape[0] // peers
    slot = lax.broadcasted_iota(jnp.int32, (size, hard.shape[1]), 0) // TILE
    hard = jnp.concatenate(
        [
            jnp.where(slot < counts_ref[0, i], hard[i * size : (i + 1) * size], -jnp.inf)
            for i in range(peers)
        ],
        axis=0,
    )
    top = lambda x: jnp.max(x, axis=0, keepdims=True)
    highest = jnp.maximum(jnp.maximum(top(local), top(near)), jnp.maximum(top(far), top(hard)))
    local, near, far = jnp.exp(local - highest), jnp.exp(near - highest), jnp.exp(far - highest)
    hard = jnp.exp(hard - highest)
    add = lambda x: jnp.sum(x, axis=0, keepdims=True)
    total = add(local) + add(near) + add(far) + add(hard)
    weight = (hard / total).astype(jnp.bfloat16)
    copies = []
    for i in range(queries_ref.shape[1] // chunk):
        columns = pl.ds(i * chunk, chunk)
        part = jnp.dot(weight, queries_ref[:, columns], preferred_element_type=jnp.float32)
        buffer[:, columns] = (SHARPNESS * part).astype(jnp.bfloat16)
        copy = pltpu.make_async_copy(buffer.at[:, columns], grad_ref.at[:, columns], sems.at[i])
        copy.start()
        copies.append(copy)
    hard_out[...] = weight
    rows = lax.broadcasted_iota(jnp.int32, local.shape, 0)
    target = (rows == positives_ref[...]).astype(jnp.float32)
    local_out[...] = (local / total - target).astype(jnp.bfloat16)
    near_out[...] = (near / total).astype(jnp.bfloat16)
    far_out[...] = (far / total).astype(jnp.bfloat16)
    for copy in copies:
        copy.wait()


def weights(queries, hard_rows, local, near, far, counts, positives, chunk=1024):
    hard, width = hard_rows.shape
    like = lambda x: jax.ShapeDtypeStruct(x.shape, jnp.bfloat16)
    return pl.pallas_call(
        functools.partial(weights_kernel, chunk),
        out_shape=(
            pltpu.HBM((hard, width), jnp.bfloat16),
            like(local), like(near), like(far),
            jax.ShapeDtypeStruct((hard, queries.shape[0]), jnp.bfloat16),
        ),
        in_specs=[VMEM] * 5 + [SMEM, VMEM],
        out_specs=(HBM, VMEM, VMEM, VMEM, VMEM),
        scratch_shapes=[
            pltpu.VMEM((hard, width), jnp.bfloat16),
            pltpu.SemaphoreType.DMA((width // chunk,)),
        ],
        compiler_params=PARAMS,
        cost_estimate=CHEAP,
        name="weights",
    )(queries, hard_rows, local, near, far, counts, positives)


def pool_kernel(near_ref, far_ref, queries_ref, kept_out, *sent_out):
    size = kept_out.shape[0]
    pieces = near_ref.shape[0] // size
    near = jnp.dot(near_ref[...], queries_ref[...], preferred_element_type=jnp.float32)
    kept_out[...] = SHARPNESS * near[:size]
    for m in range(1, pieces):
        piece = SHARPNESS * near[m * size : (m + 1) * size]
        sent_out[m - 1][...] = piece.astype(sent_out[m - 1].dtype)
    far = jnp.dot(far_ref[...], queries_ref[...], preferred_element_type=jnp.float32)
    for m in range(pieces):
        piece = SHARPNESS * far[m * size : (m + 1) * size]
        sent_out[pieces - 1 + m][...] = piece.astype(sent_out[pieces - 1 + m].dtype)


def pool_terms(near, far, queries, size, link):
    shape = (size, queries.shape[1])
    count = 2 * near.shape[0] // size
    return pl.pallas_call(
        pool_kernel,
        out_shape=(jax.ShapeDtypeStruct(shape, jnp.float32),)
        + (jax.ShapeDtypeStruct(shape, link),) * (count - 1),
        in_specs=[VMEM] * 3,
        out_specs=(VMEM,) * count,
        compiler_params=PARAMS,
        cost_estimate=CHEAP,
        name="pool_terms",
    )(near, far, queries)


def queries_kernel(chunk, *refs):
    pairs, (out_ref, buffer, sems) = refs[:-3], refs[-3:]
    count = len(pairs) // 2
    copies = []
    for i in range(out_ref.shape[1] // chunk):
        columns = pl.ds(i * chunk, chunk)
        part = transposed(pairs[0][...], pairs[count][:, columns])
        for k in range(1, count):
            part = part + transposed(pairs[k][...], pairs[count + k][:, columns])
        buffer[:, columns] = (SHARPNESS * part).astype(jnp.bfloat16)
        copy = pltpu.make_async_copy(buffer.at[:, columns], out_ref.at[:, columns], sems.at[i])
        copy.start()
        copies.append(copy)
    for copy in copies:
        copy.wait()


def query_gradient(weight, keys, chunk=1024):
    rows, width = weight[0].shape[1], keys[0].shape[1]
    return pl.pallas_call(
        functools.partial(queries_kernel, chunk),
        out_shape=jax.ShapeDtypeStruct((rows, width), jnp.bfloat16),
        in_specs=[VMEM] * (len(weight) + len(keys)),
        out_specs=HBM,
        scratch_shapes=[
            pltpu.VMEM((rows, width), jnp.bfloat16),
            pltpu.SemaphoreType.DMA((width // chunk,)),
        ],
        compiler_params=PARAMS,
        cost_estimate=CHEAP,
        name="query_gradient",
    )(*weight, *keys)


def passages_kernel(
    chunk, weight_ref, queries_ref, wanted_ref, returned_ref, out_ref,
    incoming, buffer, load_sems, store_sems,
):
    spans = [pl.ds(i * chunk, chunk) for i in range(out_ref.shape[1] // chunk)]
    loads = [
        pltpu.make_async_copy(returned_ref.at[:, span], incoming.at[:, span], load_sems.at[i])
        for i, span in enumerate(spans)
    ]
    for load in loads:
        load.start()
    weight = weight_ref[...]
    rows, hard = weight.shape[0], wanted_ref.shape[1]
    chosen = (
        lax.broadcasted_iota(jnp.int32, (rows, hard), 0) == wanted_ref[...]
    ).astype(jnp.bfloat16)
    stores = []
    for i, span in enumerate(spans):
        part = SHARPNESS * jnp.dot(
            weight, queries_ref[:, span], preferred_element_type=jnp.float32
        )
        loads[i].wait()
        part = part + jnp.dot(chosen, incoming[:, span], preferred_element_type=jnp.float32)
        buffer[:, span] = part.astype(jnp.bfloat16)
        store = pltpu.make_async_copy(buffer.at[:, span], out_ref.at[:, span], store_sems.at[i])
        store.start()
        stores.append(store)
    for store in stores:
        store.wait()


def passage_gradient(weight, queries, wanted, returned, chunk=1024):
    rows, width = weight.shape[0], queries.shape[1]
    return pl.pallas_call(
        functools.partial(passages_kernel, chunk),
        out_shape=jax.ShapeDtypeStruct((rows, width), jnp.bfloat16),
        in_specs=[VMEM] * 3 + [HBM],
        out_specs=HBM,
        scratch_shapes=[
            pltpu.VMEM(returned.shape, jnp.bfloat16),
            pltpu.VMEM((rows, width), jnp.bfloat16),
            pltpu.SemaphoreType.DMA((width // chunk,)),
            pltpu.SemaphoreType.DMA((width // chunk,)),
        ],
        compiler_params=PARAMS,
        cost_estimate=CHEAP,
        name="passage_gradient",
    )(weight, queries, wanted, pltpu.with_memory_space_constraint(returned, pltpu.HBM))


def body(digits, queries, passages, pool_passages, positives, tile_ids, tile_count):
    rows, width = queries.shape
    picks = tile_ids[0, 0]
    peers, slots = picks.shape
    hard = peers * slots * TILE
    outgoing = gather_tiles(picks.T, passages.reshape(rows // TILE, TILE, width))
    hard_rows = lax.all_to_all(
        outgoing.reshape(peers, slots * TILE, width), "pb", split_axis=0, concat_axis=0, tiled=True
    ).reshape(hard, width)
    pooled = pool_passages
    for step, count in digits[:-1]:
        pooled = jnp.concatenate(
            [pooled] + [shifts(pooled, ((step, count, m),), -1) for m in range(1, count)], axis=0
        )
    near = pooled
    far = shifts(near, (digits[-1] + (1,),), -1)
    grad_hard, local_weight, near_weight, far_weight, hard_weight = weights(
        queries, hard_rows, scores(passages, queries), scores(near, queries), scores(far, queries),
        tile_count[0], positives[None, :],
    )
    returned = lax.all_to_all(
        grad_hard.reshape(peers, slots * TILE, width), "pb", split_axis=0, concat_axis=0, tiled=True
    ).reshape(hard, width)
    (y_step, y_count), (x_step, x_count), (core_step, core_count) = digits
    size = y_count * pool_passages.shape[0]
    term, *sent = pool_terms(near_weight, far_weight, queries, size, jnp.bfloat16)
    moves = [(x, core) for core in range(core_count) for x in range(x_count)][1:]
    for piece, (x, core) in zip(sent, moves):
        pair = ((x_step, x_count, x), (core_step, core_count, core))
        term = term + shifts(piece, pair, 1).astype(jnp.float32)
    size = size // y_count
    pieces = [term[m * size : (m + 1) * size] for m in range(y_count)]
    term = pieces[0]
    for m in range(1, y_count):
        term = term + shifts(pieces[m], ((y_step, y_count, m),), 1)
    grad_pool = term.astype(jnp.bfloat16)
    grad_queries = query_gradient(
        (local_weight, near_weight, far_weight, hard_weight), (passages, near, far, hard_rows)
    )
    wanted = (
        picks.reshape(-1)[:, None] * TILE + jnp.arange(TILE, dtype=jnp.int32)[None, :]
    ).reshape(1, hard)
    grad_passages = passage_gradient(local_weight, queries, wanted, returned)
    return (grad_queries, grad_passages, grad_pool)


def solution(mesh):
    digits = ((8, 8), (2, 4), (1, 2))
    return jax.shard_map(
        lambda *args: body(digits, *args),
        mesh=mesh,
        in_specs=(
            P(("pb", "pool"), None),
            P(("pb", "pool"), None),
            P(("pb", "pool"), None),
            P(("pb", "pool")),
            P("pb", "pool", None, None),
            P("pb", "pool", None),
        ),
        out_specs=(P(("pb", "pool"), None), P(("pb", "pool"), None), P(("pb", "pool"), None)),
        check_vma=False,
    )
```

time: 209 us -> 158 us (0.76)
  the two profiles are of different devices: /device:TPU:6 before, /device:TPU:64 now
where the time goes in v4:
time: 158 us; the launch traced here: 157 us
  starting transfers between devices  113 us (72%)
  waiting for transfers between devices  16.1 us (10%)
  Pallas kernels  13.5 us (9%)
  local copies, waits for them, and re-layouts  10.4 us (7%)
  other arithmetic  2.86 us (2%)
    ppermute x25, starting transfers between devices, shifts(): lax.ppermute(block, 'pool', [(j, moved(j)) for j in range(lax.axis_size('...  90.3 us
    all_to_all x1, starting transfers between devices, body(): lax.all_to_all(outgoing.reshape(peers, slots * TILE, width), 'pb', split_...  15 us
    ppermute x25, waiting for transfers between devices, shifts(): lax.ppermute(block, 'pool', [(j, moved(j)) for j in range(lax.axis_size('...  14.1 us
    all_to_all x1, starting transfers between devices, body(): lax.all_to_all(grad_hard.reshape(peers, slots * TILE, width), 'pb', split...  7.55 us
    unnamed x34, local copies, waits for them, and re-layouts  5.01 us
    pallas_call x1, Pallas kernels, gather_tiles(): pl.pallas_call(gather_kernel, out_shape=pltpu.HBM(shape, tiles.dtype), in...  3.45 us
    pallas_call x1, Pallas kernels, weights(): pl.pallas_call(functools.partial(weights_kernel, chunk), out_shape=(pltpu...  3.35 us
  transfers between devices with their start and end apart: 27, of which 6 were waited for; matrix products, arithmetic and copies ran while one was open for 5% of the time, Pallas kernels for 2%

profile of v4, /device:TPU:64, one launch (start us, length us, event | category | flops | bytes accessed | tf_op | source)
XLA Modules:
  0.0 156.9 jit_solution(6917171008696701734)
XLA Ops:
  0.6 0.0 copy-start.5
  0.6 0.7 copy-done.5
  1.3 3.5 %gather_tiles.1 = bf16[24,8,4096]{2,1,0:T(8,128)(2,1)} custom-call(s32[2,12]{1,0:T(2,128)S(1)} %bitcast.13, bf16[16,8,4096]{2,1,0:T(8,128)(2,1)} %bitcast.12), custom_call_target="tpu_custom_call" | custom-call | bytes 3145728 | tf_op jit(solution)/shard_map/gather_tiles/pallas_call | solution.py:62
  4.8 0.0 copy-start.9
  4.8 0.0 copy-start
  4.8 15.0 %all-to-all-start = ((bf16[12,16,4096]{2,1,0:T(8,128)(2,1)}), bf16[12,16,4096]{2,1,0:T(8,128)(2,1)S(1)}, u32[]{:S(2)}, u32[]{:S(2)}) async-start(bf16[12,16,4096]{2,1,0:T(8,128)(2,1)} %bitcast.16), calls=%async_computation | async-start | bytes 3145728 | tf_op jit(solution)/shard_map/all_to_all | solution.py:276
  19.8 5.3 %collective-permute-start = (bf16[2,4096]{1,0:T(2,128)(2,1)S(1)}, bf16[2,4096]{1,0:T(2,128)(2,1)S(1)}, u32[]{:S(2)}, u32[]{:S(2)}) collective-permute-start(bf16[2,4096]{1,0:T(2,128)(2,1)S(1)} %copy-done.9), channel_id=1, source_target_pairs={{0,56},{1,57},{2,58},{3,59},{4,60},{5,61},{6,62},{7,63},{8,0},{9,1... | collective-permute-start | bytes 49160 | tf_op jit(solution)/shard_map/ppermute | solution.py:41
  25.1 4.0 %collective-permute-start.1 = (bf16[2,4096]{1,0:T(2,128)(2,1)S(1)}, bf16[2,4096]{1,0:T(2,128)(2,1)S(1)}, u32[]{:S(2)}, u32[]{:S(2)}) collective-permute-start(bf16[2,4096]{1,0:T(2,128)(2,1)S(1)} %copy-done.9), channel_id=1, source_target_pairs={{0,48},{1,49},{2,50},{3,51},{4,52},{5,53},{6,54},{7,55},{8,56},{9,... | collective-permute-start | bytes 49160 | tf_op jit(solution)/shard_map/ppermute | solution.py:41
  29.1 3.2 %collective-permute-start.2 = (bf16[2,4096]{1,0:T(2,128)(2,1)S(1)}, bf16[2,4096]{1,0:T(2,128)(2,1)S(1)}, u32[]{:S(2)}, u32[]{:S(2)}) collective-permute-start(bf16[2,4096]{1,0:T(2,128)(2,1)S(1)} %copy-done.9), channel_id=1, source_target_pairs={{0,40},{1,41},{2,42},{3,43},{4,44},{5,45},{6,46},{7,47},{8,48},{9,... | collective-permute-start | bytes 49160 | tf_op jit(solution)/shard_map/ppermute | solution.py:41
  32.4 5.9 %collective-permute-start.3 = (bf16[2,4096]{1,0:T(2,128)(2,1)S(1)}, bf16[2,4096]{1,0:T(2,128)(2,1)S(1)}, u32[]{:S(2)}, u32[]{:S(2)}) collective-permute-start(bf16[2,4096]{1,0:T(2,128)(2,1)S(1)} %copy-done.9), channel_id=1, source_target_pairs={{0,32},{1,33},{2,34},{3,35},{4,36},{5,37},{6,38},{7,39},{8,40},{9,... | collective-permute-start | bytes 49160 | tf_op jit(solution)/shard_map/ppermute | solution.py:41
  38.2 1.9 %collective-permute-start.4 = (bf16[2,4096]{1,0:T(2,128)(2,1)S(1)}, bf16[2,4096]{1,0:T(2,128)(2,1)S(1)}, u32[]{:S(2)}, u32[]{:S(2)}) collective-permute-start(bf16[2,4096]{1,0:T(2,128)(2,1)S(1)} %copy-done.9), channel_id=1, source_target_pairs={{0,24},{1,25},{2,26},{3,27},{4,28},{5,29},{6,30},{7,31},{8,32},{9,... | collective-permute-start | bytes 49160 | tf_op jit(solution)/shard_map/ppermute | solution.py:41
  40.2 0.0 copy-start.10
  40.2 5.3 %collective-permute-start.5 = (bf16[2,4096]{1,0:T(2,128)(2,1)S(1)}, bf16[2,4096]{1,0:T(2,128)(2,1)S(1)}, u32[]{:S(2)}, u32[]{:S(2)}) collective-permute-start(bf16[2,4096]{1,0:T(2,128)(2,1)S(1)} %copy-done.9), channel_id=1, source_target_pairs={{0,16},{1,17},{2,18},{3,19},{4,20},{5,21},{6,22},{7,23},{8,24},{9,... | collective-permute-start | bytes 49160 | tf_op jit(solution)/shard_map/ppermute | solution.py:41
  45.5 0.0 copy-start.11
  45.5 3.5 %collective-permute-start.6 = (bf16[2,4096]{1,0:T(2,128)(2,1)S(1)}, bf16[2,4096]{1,0:T(2,128)(2,1)S(1)}, u32[]{:S(2)}, u32[]{:S(2)}) collective-permute-start(bf16[2,4096]{1,0:T(2,128)(2,1)S(1)} %copy-done.9), channel_id=1, source_target_pairs={{0,8},{1,9},{2,10},{3,11},{4,12},{5,13},{6,14},{7,15},{8,16},{9,17... | collective-permute-start | bytes 49160 | tf_op jit(solution)/shard_map/ppermute | solution.py:41
  49.0 0.0 copy-start.12
  49.1 3.2 %collective-permute-done.6 = bf16[2,4096]{1,0:T(2,128)(2,1)S(1)} collective-permute-done((bf16[2,4096]{1,0:T(2,128)(2,1)S(1)}, bf16[2,4096]{1,0:T(2,128)(2,1)S(1)}, u32[]{:S(2)}, u32[]{:S(2)}) %collective-permute-start.6) | collective-permute-done | bytes 16416 | tf_op jit(solution)/shard_map/ppermute | solution.py:41
  52.3 0.2 concatenate.7
  52.5 4.7 %collective-permute-start.7 = (bf16[16,4096]{1,0:T(8,128)(2,1)S(1)}, bf16[16,4096]{1,0:T(8,128)(2,1)S(1)}, u32[]{:S(2)}, u32[]{:S(2)}) collective-permute-start(bf16[16,4096]{1,0:T(8,128)(2,1)S(1)} %concatenate.7), channel_id=1, source_target_pairs={{0,6},{1,7},{2,0},{3,1},{4,2},{5,3},{6,4},{7,5},{8,14},{9,15},{10,... | collective-permute-start | bytes 393224 | tf_op jit(solution)/shard_map/ppermute | solution.py:41
  57.2 2.9 %collective-permute-start.8 = (bf16[16,4096]{1,0:T(8,128)(2,1)S(1)}, bf16[16,4096]{1,0:T(8,128)(2,1)S(1)}, u32[]{:S(2)}, u32[]{:S(2)}) collective-permute-start(bf16[16,4096]{1,0:T(8,128)(2,1)S(1)} %concatenate.7), channel_id=1, source_target_pairs={{0,4},{1,5},{2,6},{3,7},{4,0},{5,1},{6,2},{7,3},{8,12},{9,13},{10,... | collective-permute-start | bytes 393224 | tf_op jit(solution)/shard_map/ppermute | solution.py:41
  60.2 2.6 %collective-permute-start.9 = (bf16[16,4096]{1,0:T(8,128)(2,1)S(1)}, bf16[16,4096]{1,0:T(8,128)(2,1)S(1)}, u32[]{:S(2)}, u32[]{:S(2)}) collective-permute-start(bf16[16,4096]{1,0:T(8,128)(2,1)S(1)} %concatenate.7), channel_id=1, source_target_pairs={{0,2},{1,3},{2,4},{3,5},{4,6},{5,7},{6,0},{7,1},{8,10},{9,11},{10,... | collective-permute-start | bytes 393224 | tf_op jit(solution)/shard_map/ppermute | solution.py:41
  62.8 2.8 %collective-permute-done.8 = bf16[16,4096]{1,0:T(8,128)(2,1)S(1)} collective-permute-done((bf16[16,4096]{1,0:T(8,128)(2,1)S(1)}, bf16[16,4096]{1,0:T(8,128)(2,1)S(1)}, u32[]{:S(2)}, u32[]{:S(2)}) %collective-permute-start.8) | collective-permute-done | bytes 131104 | tf_op jit(solution)/shard_map/ppermute | solution.py:41
  65.7 2.6 %collective-permute-done.9 = bf16[16,4096]{1,0:T(8,128)(2,1)S(1)} collective-permute-done((bf16[16,4096]{1,0:T(8,128)(2,1)S(1)}, bf16[16,4096]{1,0:T(8,128)(2,1)S(1)}, u32[]{:S(2)}, u32[]{:S(2)}) %collective-permute-start.9) | collective-permute-done | bytes 131104 | tf_op jit(solution)/shard_map/ppermute | solution.py:41
  68.2 1.7 %concatenate.8.keys_ref.refs_5_ = bf16[64,4096]{1,0:T(8,128)(2,1)S(1)} concatenate(bf16[2,4096]{1,0:T(2,128)(2,1)S(1)} %copy-done.9, bf16[2,4096]{1,0:T(2,128)(2,1)} %copy-done.10, bf16[2,4096]{1,0:T(2,128)(2,1)} %copy-done.11, bf16[2,4096]{1,0:T(2,128)(2,1)} %copy-done.12, bf16[2,4096]{1,0:T(2,128)(2,1)} %copy-done.13, bf16[2,4096]{1,0:T(2,128)(2,1)} %copy-done.14, ...), dimensions={0} | concatenate | bytes 1048576 | tf_op jit(solution)/shard_map/concatenate | solution.py:281
  70.0 1.9 %collective-permute-start.10 = (bf16[64,4096]{1,0:T(8,128)(2,1)S(1)}, bf16[64,4096]{1,0:T(8,128)(2,1)S(1)}, u32[]{:S(2)}, u32[]{:S(2)}) collective-permute-start(bf16[64,4096]{1,0:T(8,128)(2,1)S(1)} %concatenate.8.keys_ref.refs_5_), channel_id=1, source_target_pairs={{0,1},{1,0},{2,3},{3,2},{4,5},{5,4},{6,7},{7,6},{8,9},{9,8},{10,11... | collective-permute-start | bytes 1572872 | tf_op jit(solution)/shard_map/ppermute | solution.py:41
  71.9 0.0 copy-start.1
  71.9 1.2 copy-done.1
  73.1 0.4 scores.3.local_ref
  73.6 0.5 scores.4.near_ref
  74.1 0.5 scores.5.far_ref
  74.6 0.8 copy-done.3
  75.4 2.1 %all-to-all-done = bf16[12,16,4096]{2,1,0:T(8,128)(2,1)S(1)} async-done(((bf16[12,16,4096]{2,1,0:T(8,128)(2,1)}), bf16[12,16,4096]{2,1,0:T(8,128)(2,1)S(1)}, u32[]{:S(2)}, u32[]{:S(2)}) %all-to-all-start) | async-done | bytes 1572896 | tf_op jit(solution)/shard_map/all_to_all | solution.py:276
  77.5 3.3 %weights.1 = (bf16[192,4096]{1,0:T(8,128)(2,1)}, bf16[128,128]{1,0:T(8,128)(2,1)S(1)}, bf16[64,128]{1,0:T(8,128)(2,1)S(1)}, bf16[64,128]{1,0:T(8,128)(2,1)S(1)}, bf16[192,128]{1,0:T(8,128)(2,1)S(1)}) custom-call(bf16[128,4096]{1,0:T(8,128)(2,1)S(1)} %copy-done, bf16[192,4096]{1,0:T(8,128)(2,1)S(1)} %bitcast.10, f32[128,128]{1,0:T(8,128)S(1)} %scores.3.local_ref, ...), custom_call_target="tpu_custom_call" | custom-call | flops 1048576 | bytes 1048576 | tf_op jit(solution)/shard_map/weights/pallas_call | solution.py:138
  80.8 7.5 %all-to-all-start.1 = ((bf16[12,16,4096]{2,1,0:T(8,128)(2,1)}), bf16[12,16,4096]{2,1,0:T(8,128)(2,1)}, u32[]{:S(2)}, u32[]{:S(2)}) async-start(bf16[12,16,4096]{2,1,0:T(8,128)(2,1)} %bitcast.17), calls=%async_computation.1 | async-start | bytes 3145728 | tf_op jit(solution)/shard_map/all_to_all | solution.py:290
  88.4 0.4 pool_terms.1
  88.8 1.9 %collective-permute-start.17 = (bf16[16,4096]{1,0:T(8,128)(2,1)S(1)}, bf16[16,4096]{1,0:T(8,128)(2,1)S(1)}, u32[]{:S(2)}, u32[]{:S(2)}) collective-permute-start(bf16[16,4096]{1,0:T(8,128)(2,1)S(1)} %get-tuple-element.28), channel_id=1, source_target_pairs={{0,7},{1,6},{2,1},{3,0},{4,3},{5,2},{6,5},{7,4},{8,15},{9,14},{10,... | collective-permute-start | bytes 393224 | tf_op jit(solution)/shard_map/ppermute | solution.py:41
  90.7 3.2 %collective-permute-start.16 = (bf16[16,4096]{1,0:T(8,128)(2,1)S(1)}, bf16[16,4096]{1,0:T(8,128)(2,1)S(1)}, u32[]{:S(2)}, u32[]{:S(2)}) collective-permute-start(bf16[16,4096]{1,0:T(8,128)(2,1)S(1)} %get-tuple-element.27), channel_id=1, source_target_pairs={{0,5},{1,4},{2,7},{3,6},{4,1},{5,0},{6,3},{7,2},{8,13},{9,12},{10,... | collective-permute-start | bytes 393224 | tf_op jit(solution)/shard_map/ppermute | solution.py:41
  93.9 2.6 %collective-permute-start.15 = (bf16[16,4096]{1,0:T(8,128)(2,1)S(1)}, bf16[16,4096]{1,0:T(8,128)(2,1)S(1)}, u32[]{:S(2)}, u32[]{:S(2)}) collective-permute-start(bf16[16,4096]{1,0:T(8,128)(2,1)S(1)} %get-tuple-element.26), channel_id=1, source_target_pairs={{0,3},{1,2},{2,5},{3,4},{4,7},{5,6},{6,1},{7,0},{8,11},{9,10},{10,... | collective-permute-start | bytes 393224 | tf_op jit(solution)/shard_map/ppermute | solution.py:41
  96.6 2.5 %collective-permute-start.14 = (bf16[16,4096]{1,0:T(8,128)(2,1)S(1)}, bf16[16,4096]{1,0:T(8,128)(2,1)S(1)}, u32[]{:S(2)}, u32[]{:S(2)}) collective-permute-start(bf16[16,4096]{1,0:T(8,128)(2,1)S(1)} %get-tuple-element.25), channel_id=1, source_target_pairs={{0,1},{1,0},{2,3},{3,2},{4,5},{5,4},{6,7},{7,6},{8,9},{9,8},{10,11... | collective-permute-start | bytes 393224 | tf_op jit(solution)/shard_map/ppermute | solution.py:41
  99.1 4.0 %collective-permute-start.13 = (bf16[16,4096]{1,0:T(8,128)(2,1)S(1)}, bf16[16,4096]{1,0:T(8,128)(2,1)S(1)}, u32[]{:S(2)}, u32[]{:S(2)}) collective-permute-start(bf16[16,4096]{1,0:T(8,128)(2,1)S(1)} %get-tuple-element.24), channel_id=1, source_target_pairs={{0,6},{1,7},{2,0},{3,1},{4,2},{5,3},{6,4},{7,5},{8,14},{9,15},{10,... | collective-permute-start | bytes 393224 | tf_op jit(solution)/shard_map/ppermute | solution.py:41
  103.0 3.3 %collective-permute-start.12 = (bf16[16,4096]{1,0:T(8,128)(2,1)S(1)}, bf16[16,4096]{1,0:T(8,128)(2,1)S(1)}, u32[]{:S(2)}, u32[]{:S(2)}) collective-permute-start(bf16[16,4096]{1,0:T(8,128)(2,1)S(1)} %get-tuple-element.23), channel_id=1, source_target_pairs={{0,4},{1,5},{2,6},{3,7},{4,0},{5,1},{6,2},{7,3},{8,12},{9,13},{10,... | collective-permute-start | bytes 393224 | tf_op jit(solution)/shard_map/ppermute | solution.py:41
  106.3 3.3 %collective-permute-start.11 = (bf16[16,4096]{1,0:T(8,128)(2,1)S(1)}, bf16[16,4096]{1,0:T(8,128)(2,1)S(1)}, u32[]{:S(2)}, u32[]{:S(2)}) collective-permute-start(bf16[16,4096]{1,0:T(8,128)(2,1)S(1)} %get-tuple-element.22), channel_id=1, source_target_pairs={{0,2},{1,3},{2,4},{3,5},{4,6},{5,7},{6,0},{7,1},{8,10},{9,11},{10,... | collective-permute-start | bytes 393224 | tf_op jit(solution)/shard_map/ppermute | solution.py:41
  109.7 3.0 %collective-permute-done.12 = bf16[16,4096]{1,0:T(8,128)(2,1)S(1)} collective-permute-done((bf16[16,4096]{1,0:T(8,128)(2,1)S(1)}, bf16[16,4096]{1,0:T(8,128)(2,1)S(1)}, u32[]{:S(2)}, u32[]{:S(2)}) %collective-permute-start.12) | collective-permute-done | bytes 131104 | tf_op jit(solution)/shard_map/ppermute | solution.py:41
  112.7 2.3 %collective-permute-done.11 = bf16[16,4096]{1,0:T(8,128)(2,1)S(1)} collective-permute-done((bf16[16,4096]{1,0:T(8,128)(2,1)S(1)}, bf16[16,4096]{1,0:T(8,128)(2,1)S(1)}, u32[]{:S(2)}, u32[]{:S(2)}) %collective-permute-start.11) | collective-permute-done | bytes 131104 | tf_op jit(solution)/shard_map/ppermute | solution.py:41
  115.1 0.1 convert_add_fusion
  115.2 0.7 fusion.5
  115.9 4.5 %collective-permute-start.24 = (f32[2,4096]{1,0:T(2,128)}, f32[2,4096]{1,0:T(2,128)}, u32[]{:S(2)}, u32[]{:S(2)}) collective-permute-start(f32[2,4096]{1,0:T(2,128)} %get-tuple-element.30), channel_id=1, source_target_pairs={{0,56},{1,57},{2,58},{3,59},{4,60},{5,61},{6,62},{7,63},{8,0},{9,1... | collective-permute-start | bytes 98312 | tf_op jit(solution)/shard_map/ppermute | solution.py:41
  120.5 4.0 %collective-permute-start.23 = (f32[2,4096]{1,0:T(2,128)S(1)}, f32[2,4096]{1,0:T(2,128)}, u32[]{:S(2)}, u32[]{:S(2)}) collective-permute-start(f32[2,4096]{1,0:T(2,128)S(1)} %get-tuple-element.31), channel_id=1, source_target_pairs={{0,48},{1,49},{2,50},{3,51},{4,52},{5,53},{6,54},{7,55},{8,56},{9,... | collective-permute-start | bytes 98312 | tf_op jit(solution)/shard_map/ppermute | solution.py:41
  124.4 0.5 broadcast_multiply_fusion
  125.0 1.3 copy.10
  126.3 1.3 mul.12
  127.6 3.0 %collective-permute-start.22 = (f32[2,4096]{1,0:T(2,128)}, f32[2,4096]{1,0:T(2,128)}, u32[]{:S(2)}, u32[]{:S(2)}) collective-permute-start(f32[2,4096]{1,0:T(2,128)} %get-tuple-element.32), channel_id=1, source_target_pairs={{0,40},{1,41},{2,42},{3,43},{4,44},{5,45},{6,46},{7,47},{8,48},{9,... | collective-permute-start | bytes 98312 | tf_op jit(solution)/shard_map/ppermute | solution.py:41
  130.6 6.0 %collective-permute-start.21 = (f32[2,4096]{1,0:T(2,128)}, f32[2,4096]{1,0:T(2,128)}, u32[]{:S(2)}, u32[]{:S(2)}) collective-permute-start(f32[2,4096]{1,0:T(2,128)} %get-tuple-element.33), channel_id=1, source_target_pairs={{0,32},{1,33},{2,34},{3,35},{4,36},{5,37},{6,38},{7,39},{8,40},{9,... | collective-permute-start | bytes 98312 | tf_op jit(solution)/shard_map/ppermute | solution.py:41
  136.6 1.9 %collective-permute-start.20 = (f32[2,4096]{1,0:T(2,128)}, f32[2,4096]{1,0:T(2,128)}, u32[]{:S(2)}, u32[]{:S(2)}) collective-permute-start(f32[2,4096]{1,0:T(2,128)} %get-tuple-element.34), channel_id=1, source_target_pairs={{0,24},{1,25},{2,26},{3,27},{4,28},{5,29},{6,30},{7,31},{8,32},{9,... | collective-permute-start | bytes 98312 | tf_op jit(solution)/shard_map/ppermute | solution.py:41
  138.5 5.3 %collective-permute-start.19 = (f32[2,4096]{1,0:T(2,128)}, f32[2,4096]{1,0:T(2,128)}, u32[]{:S(2)}, u32[]{:S(2)}) collective-permute-start(f32[2,4096]{1,0:T(2,128)} %get-tuple-element.35), channel_id=1, source_target_pairs={{0,16},{1,17},{2,18},{3,19},{4,20},{5,21},{6,22},{7,23},{8,24},{9,... | collective-permute-start | bytes 98312 | tf_op jit(solution)/shard_map/ppermute | solution.py:41
  143.8 3.6 %collective-permute-start.18 = (f32[2,4096]{1,0:T(2,128)}, f32[2,4096]{1,0:T(2,128)}, u32[]{:S(2)}, u32[]{:S(2)}) collective-permute-start(f32[2,4096]{1,0:T(2,128)} %get-tuple-element.29), channel_id=1, source_target_pairs={{0,8},{1,9},{2,10},{3,11},{4,12},{5,13},{6,14},{7,15},{8,16},{9,17... | collective-permute-start | bytes 98312 | tf_op jit(solution)/shard_map/ppermute | solution.py:41
  147.4 0.7 iota_add_fusion
  148.1 0.1 add.68.wanted_ref
  148.2 0.0 copy-start.2
  148.2 1.2 copy-done.2
  149.4 1.0 copy-done.4
  150.4 2.0 %query_gradient.1 = bf16[128,4096]{1,0:T(8,128)(2,1)} custom-call(bf16[128,128]{1,0:T(8,128)(2,1)S(1)} %get-tuple-element.16.refs_0_.weight_ref, bf16[64,128]{1,0:T(8,128)(2,1)S(1)} %get-tuple-element.17.refs_1_.near_ref, bf16[64,128]{1,0:T(8,128)(2,1)S(1)} %get-tuple-element.18.refs_2_.far_ref, bf16[192,128]{1,0:T(8,128)(2,1)S(1)} %get-tuple-element.19.refs_3_, ...), custom_call_target="tpu_custom_call" | custom-call | flops 1048576 | bytes 1048576 | tf_op jit(solution)/shard_map/query_gradient/pallas_call | solution.py:205
  152.5 1.5 add_convert_fusion
  154.0 2.9 %passage_gradient.1 = bf16[128,4096]{1,0:T(8,128)(2,1)} custom-call(bf16[128,128]{1,0:T(8,128)(2,1)S(1)} %get-tuple-element.16.refs_0_.weight_ref, bf16[128,4096]{1,0:T(8,128)(2,1)S(1)} %copy-done, s32[1,192]{1,0:T(1,128)S(1)} %add.68.wanted_ref, bf16[192,4096]{1,0:T(8,128)(2,1)} %bitcast.8.returned_ref), custom_call_target="tpu_custom_call" | custom-call | flops 1048576 | bytes 1048576 | tf_op jit(solution)/shard_map/passage_gradient/pallas_call | solution.py:253
  (42 shorter events, 0.1 us)
Async XLA Ops:
  0.6 0.7 copy-start.5
  4.8 15.0 %copy-start.9 = (bf16[2,4096]{1,0:T(2,128)(2,1)S(1)}, bf16[2,4096]{1,0:T(2,128)(2,1)}, u32[]{:S(2)}) copy-start(bf16[2,4096]{1,0:T(2,128)(2,1)} %param.8) | copy-start | bytes 49156
  4.8 67.1 %copy-start = (bf16[128,4096]{1,0:T(8,128)(2,1)S(1)}, bf16[128,4096]{1,0:T(8,128)(2,1)}, u32[]{:S(2)}) copy-start(bf16[128,4096]{1,0:T(8,128)(2,1)} %queries_ref.11) | copy-start | bytes 3145732
  4.8 72.7 %all-to-all-start = ((bf16[12,16,4096]{2,1,0:T(8,128)(2,1)}), bf16[12,16,4096]{2,1,0:T(8,128)(2,1)S(1)}, u32[]{:S(2)}, u32[]{:S(2)}) async-start(bf16[12,16,4096]{2,1,0:T(8,128)(2,1)} %bitcast.16), calls=%async_computation | async-start | bytes 3145728 | tf_op jit(solution)/shard_map/all_to_all | solution.py:276
  19.8 20.4 %collective-permute-start = (bf16[2,4096]{1,0:T(2,128)(2,1)S(1)}, bf16[2,4096]{1,0:T(2,128)(2,1)S(1)}, u32[]{:S(2)}, u32[]{:S(2)}) collective-permute-start(bf16[2,4096]{1,0:T(2,128)(2,1)S(1)} %copy-done.9), channel_id=1, source_target_pairs={{0,56},{1,57},{2,58},{3,59},{4,60},{5,61},{6,62},{7,63},{8,0},{9,1... | collective-permute-start | bytes 49160 | tf_op jit(solution)/shard_map/ppermute | solution.py:41
  25.1 20.3 %collective-permute-start.1 = (bf16[2,4096]{1,0:T(2,128)(2,1)S(1)}, bf16[2,4096]{1,0:T(2,128)(2,1)S(1)}, u32[]{:S(2)}, u32[]{:S(2)}) collective-permute-start(bf16[2,4096]{1,0:T(2,128)(2,1)S(1)} %copy-done.9), channel_id=1, source_target_pairs={{0,48},{1,49},{2,50},{3,51},{4,52},{5,53},{6,54},{7,55},{8,56},{9,... | collective-permute-start | bytes 49160 | tf_op jit(solution)/shard_map/ppermute | solution.py:41
  29.1 19.9 %collective-permute-start.2 = (bf16[2,4096]{1,0:T(2,128)(2,1)S(1)}, bf16[2,4096]{1,0:T(2,128)(2,1)S(1)}, u32[]{:S(2)}, u32[]{:S(2)}) collective-permute-start(bf16[2,4096]{1,0:T(2,128)(2,1)S(1)} %copy-done.9), channel_id=1, source_target_pairs={{0,40},{1,41},{2,42},{3,43},{4,44},{5,45},{6,46},{7,47},{8,48},{9,... | collective-permute-start | bytes 49160 | tf_op jit(solution)/shard_map/ppermute | solution.py:41
  32.4 16.7 %collective-permute-start.3 = (bf16[2,4096]{1,0:T(2,128)(2,1)S(1)}, bf16[2,4096]{1,0:T(2,128)(2,1)S(1)}, u32[]{:S(2)}, u32[]{:S(2)}) collective-permute-start(bf16[2,4096]{1,0:T(2,128)(2,1)S(1)} %copy-done.9), channel_id=1, source_target_pairs={{0,32},{1,33},{2,34},{3,35},{4,36},{5,37},{6,38},{7,39},{8,40},{9,... | collective-permute-start | bytes 49160 | tf_op jit(solution)/shard_map/ppermute | solution.py:41
  38.2 10.8 %collective-permute-start.4 = (bf16[2,4096]{1,0:T(2,128)(2,1)S(1)}, bf16[2,4096]{1,0:T(2,128)(2,1)S(1)}, u32[]{:S(2)}, u32[]{:S(2)}) collective-permute-start(bf16[2,4096]{1,0:T(2,128)(2,1)S(1)} %copy-done.9), channel_id=1, source_target_pairs={{0,24},{1,25},{2,26},{3,27},{4,28},{5,29},{6,30},{7,31},{8,32},{9,... | collective-permute-start | bytes 49160 | tf_op jit(solution)/shard_map/ppermute | solution.py:41
  40.2 25.4 %copy-start.10 = (bf16[2,4096]{1,0:T(2,128)(2,1)}, bf16[2,4096]{1,0:T(2,128)(2,1)S(1)}, u32[]{:S(2)}) copy-start(bf16[2,4096]{1,0:T(2,128)(2,1)S(1)} %collective-permute-done) | copy-start | bytes 49156
  40.2 8.9 %collective-permute-start.5 = (bf16[2,4096]{1,0:T(2,128)(2,1)S(1)}, bf16[2,4096]{1,0:T(2,128)(2,1)S(1)}, u32[]{:S(2)}, u32[]{:S(2)}) collective-permute-start(bf16[2,4096]{1,0:T(2,128)(2,1)S(1)} %copy-done.9), channel_id=1, source_target_pairs={{0,16},{1,17},{2,18},{3,19},{4,20},{5,21},{6,22},{7,23},{8,24},{9,... | collective-permute-start | bytes 49160 | tf_op jit(solution)/shard_map/ppermute | solution.py:41
  45.5 20.1 %copy-start.11 = (bf16[2,4096]{1,0:T(2,128)(2,1)}, bf16[2,4096]{1,0:T(2,128)(2,1)S(1)}, u32[]{:S(2)}) copy-start(bf16[2,4096]{1,0:T(2,128)(2,1)S(1)} %collective-permute-done.1) | copy-start | bytes 49156
  45.5 6.8 %collective-permute-start.6 = (bf16[2,4096]{1,0:T(2,128)(2,1)S(1)}, bf16[2,4096]{1,0:T(2,128)(2,1)S(1)}, u32[]{:S(2)}, u32[]{:S(2)}) collective-permute-start(bf16[2,4096]{1,0:T(2,128)(2,1)S(1)} %copy-done.9), channel_id=1, source_target_pairs={{0,8},{1,9},{2,10},{3,11},{4,12},{5,13},{6,14},{7,15},{8,16},{9,17... | collective-permute-start | bytes 49160 | tf_op jit(solution)/shard_map/ppermute | solution.py:41
  49.0 16.6 %copy-start.12 = (bf16[2,4096]{1,0:T(2,128)(2,1)}, bf16[2,4096]{1,0:T(2,128)(2,1)S(1)}, u32[]{:S(2)}) copy-start(bf16[2,4096]{1,0:T(2,128)(2,1)S(1)} %collective-permute-done.2) | copy-start | bytes 49156
  49.0 16.6 %copy-start.13 = (bf16[2,4096]{1,0:T(2,128)(2,1)}, bf16[2,4096]{1,0:T(2,128)(2,1)S(1)}, u32[]{:S(2)}) copy-start(bf16[2,4096]{1,0:T(2,128)(2,1)S(1)} %collective-permute-done.3) | copy-start | bytes 49156
  49.1 16.6 %copy-start.14 = (bf16[2,4096]{1,0:T(2,128)(2,1)}, bf16[2,4096]{1,0:T(2,128)(2,1)S(1)}, u32[]{:S(2)}) copy-start(bf16[2,4096]{1,0:T(2,128)(2,1)S(1)} %collective-permute-done.4) | copy-start | bytes 49156
  49.1 16.6 %copy-start.15 = (bf16[2,4096]{1,0:T(2,128)(2,1)}, bf16[2,4096]{1,0:T(2,128)(2,1)S(1)}, u32[]{:S(2)}) copy-start(bf16[2,4096]{1,0:T(2,128)(2,1)S(1)} %collective-permute-done.5) | copy-start | bytes 49156
  52.3 13.3 %copy-start.16 = (bf16[2,4096]{1,0:T(2,128)(2,1)}, bf16[2,4096]{1,0:T(2,128)(2,1)S(1)}, u32[]{:S(2)}) copy-start(bf16[2,4096]{1,0:T(2,128)(2,1)S(1)} %collective-permute-done.6) | copy-start | bytes 49156
  52.5 10.2 %collective-permute-start.7 = (bf16[16,4096]{1,0:T(8,128)(2,1)S(1)}, bf16[16,4096]{1,0:T(8,128)(2,1)S(1)}, u32[]{:S(2)}, u32[]{:S(2)}) collective-permute-start(bf16[16,4096]{1,0:T(8,128)(2,1)S(1)} %concatenate.7), channel_id=1, source_target_pairs={{0,6},{1,7},{2,0},{3,1},{4,2},{5,3},{6,4},{7,5},{8,14},{9,15},{10,... | collective-permute-start | bytes 393224 | tf_op jit(solution)/shard_map/ppermute | solution.py:41
  57.2 8.4 %collective-permute-start.8 = (bf16[16,4096]{1,0:T(8,128)(2,1)S(1)}, bf16[16,4096]{1,0:T(8,128)(2,1)S(1)}, u32[]{:S(2)}, u32[]{:S(2)}) collective-permute-start(bf16[16,4096]{1,0:T(8,128)(2,1)S(1)} %concatenate.7), channel_id=1, source_target_pairs={{0,4},{1,5},{2,6},{3,7},{4,0},{5,1},{6,2},{7,3},{8,12},{9,13},{10,... | collective-permute-start | bytes 393224 | tf_op jit(solution)/shard_map/ppermute | solution.py:41
  60.2 8.1 %collective-permute-start.9 = (bf16[16,4096]{1,0:T(8,128)(2,1)S(1)}, bf16[16,4096]{1,0:T(8,128)(2,1)S(1)}, u32[]{:S(2)}, u32[]{:S(2)}) collective-permute-start(bf16[16,4096]{1,0:T(8,128)(2,1)S(1)} %concatenate.7), channel_id=1, source_target_pairs={{0,2},{1,3},{2,4},{3,5},{4,6},{5,7},{6,0},{7,1},{8,10},{9,11},{10,... | collective-permute-start | bytes 393224 | tf_op jit(solution)/shard_map/ppermute | solution.py:41
  70.0 4.1 %collective-permute-start.10 = (bf16[64,4096]{1,0:T(8,128)(2,1)S(1)}, bf16[64,4096]{1,0:T(8,128)(2,1)S(1)}, u32[]{:S(2)}, u32[]{:S(2)}) collective-permute-start(bf16[64,4096]{1,0:T(8,128)(2,1)S(1)} %concatenate.8.keys_ref.refs_5_), channel_id=1, source_target_pairs={{0,1},{1,0},{2,3},{3,2},{4,5},{5,4},{6,7},{7,6},{8,9},{9,8},{10,11... | collective-permute-start | bytes 1572872 | tf_op jit(solution)/shard_map/ppermute | solution.py:41
  71.9 1.2 copy-start.1
  73.6 3.9 %copy-start.7 = (s32[1,1,12]{2,1,0:T(1,128)S(1)}, s32[1,1,12]{2,1,0:T(1,128)}, u32[]{:S(2)}) copy-start(s32[1,1,12]{2,1,0:T(1,128)} %param.11) | copy-start | bytes 148
  73.6 3.9 %copy-start.8 = (s32[128]{0:T(128)S(1)}, s32[128]{0:T(128)}, u32[]{:S(2)}) copy-start(s32[128]{0:T(128)} %param.9) | copy-start | bytes 1540
  74.6 0.8 copy-start.3
  80.8 73.2 %all-to-all-start.1 = ((bf16[12,16,4096]{2,1,0:T(8,128)(2,1)}), bf16[12,16,4096]{2,1,0:T(8,128)(2,1)}, u32[]{:S(2)}, u32[]{:S(2)}) async-start(bf16[12,16,4096]{2,1,0:T(8,128)(2,1)} %bitcast.17), calls=%async_computation.1 | async-start | bytes 3145728 | tf_op jit(solution)/shard_map/all_to_all | solution.py:290
  88.4 36.1 %copy-start.6 = (s32[1,1,12,2]{2,3,1,0:T(2,128)S(1)}, s32[1,1,12,2]{2,3,1,0:T(2,128)}, u32[]{:S(2)}) copy-start(s32[1,1,12,2]{2,3,1,0:T(2,128)} %param.10) | copy-start | bytes 292
  88.8 14.2 %collective-permute-start.17 = (bf16[16,4096]{1,0:T(8,128)(2,1)S(1)}, bf16[16,4096]{1,0:T(8,128)(2,1)S(1)}, u32[]{:S(2)}, u32[]{:S(2)}) collective-permute-start(bf16[16,4096]{1,0:T(8,128)(2,1)S(1)} %get-tuple-element.28), channel_id=1, source_target_pairs={{0,7},{1,6},{2,1},{3,0},{4,3},{5,2},{6,5},{7,4},{8,15},{9,14},{10,... | collective-permute-start | bytes 393224 | tf_op jit(solution)/shard_map/ppermute | solution.py:41
  90.7 15.6 %collective-permute-start.16 = (bf16[16,4096]{1,0:T(8,128)(2,1)S(1)}, bf16[16,4096]{1,0:T(8,128)(2,1)S(1)}, u32[]{:S(2)}, u32[]{:S(2)}) collective-permute-start(bf16[16,4096]{1,0:T(8,128)(2,1)S(1)} %get-tuple-element.27), channel_id=1, source_target_pairs={{0,5},{1,4},{2,7},{3,6},{4,1},{5,0},{6,3},{7,2},{8,13},{9,12},{10,... | collective-permute-start | bytes 393224 | tf_op jit(solution)/shard_map/ppermute | solution.py:41
  93.9 15.7 %collective-permute-start.15 = (bf16[16,4096]{1,0:T(8,128)(2,1)S(1)}, bf16[16,4096]{1,0:T(8,128)(2,1)S(1)}, u32[]{:S(2)}, u32[]{:S(2)}) collective-permute-start(bf16[16,4096]{1,0:T(8,128)(2,1)S(1)} %get-tuple-element.26), channel_id=1, source_target_pairs={{0,3},{1,2},{2,5},{3,4},{4,7},{5,6},{6,1},{7,0},{8,11},{9,10},{10,... | collective-permute-start | bytes 393224 | tf_op jit(solution)/shard_map/ppermute | solution.py:41
  96.6 13.1 %collective-permute-start.14 = (bf16[16,4096]{1,0:T(8,128)(2,1)S(1)}, bf16[16,4096]{1,0:T(8,128)(2,1)S(1)}, u32[]{:S(2)}, u32[]{:S(2)}) collective-permute-start(bf16[16,4096]{1,0:T(8,128)(2,1)S(1)} %get-tuple-element.25), channel_id=1, source_target_pairs={{0,1},{1,0},{2,3},{3,2},{4,5},{5,4},{6,7},{7,6},{8,9},{9,8},{10,11... | collective-permute-start | bytes 393224 | tf_op jit(solution)/shard_map/ppermute | solution.py:41
  99.1 10.6 %collective-permute-start.13 = (bf16[16,4096]{1,0:T(8,128)(2,1)S(1)}, bf16[16,4096]{1,0:T(8,128)(2,1)S(1)}, u32[]{:S(2)}, u32[]{:S(2)}) collective-permute-start(bf16[16,4096]{1,0:T(8,128)(2,1)S(1)} %get-tuple-element.24), channel_id=1, source_target_pairs={{0,6},{1,7},{2,0},{3,1},{4,2},{5,3},{6,4},{7,5},{8,14},{9,15},{10,... | collective-permute-start | bytes 393224 | tf_op jit(solution)/shard_map/ppermute | solution.py:41
  103.0 9.7 %collective-permute-start.12 = (bf16[16,4096]{1,0:T(8,128)(2,1)S(1)}, bf16[16,4096]{1,0:T(8,128)(2,1)S(1)}, u32[]{:S(2)}, u32[]{:S(2)}) collective-permute-start(bf16[16,4096]{1,0:T(8,128)(2,1)S(1)} %get-tuple-element.23), channel_id=1, source_target_pairs={{0,4},{1,5},{2,6},{3,7},{4,0},{5,1},{6,2},{7,3},{8,12},{9,13},{10,... | collective-permute-start | bytes 393224 | tf_op jit(solution)/shard_map/ppermute | solution.py:41
  106.3 8.7 %collective-permute-start.11 = (bf16[16,4096]{1,0:T(8,128)(2,1)S(1)}, bf16[16,4096]{1,0:T(8,128)(2,1)S(1)}, u32[]{:S(2)}, u32[]{:S(2)}) collective-permute-start(bf16[16,4096]{1,0:T(8,128)(2,1)S(1)} %get-tuple-element.22), channel_id=1, source_target_pairs={{0,2},{1,3},{2,4},{3,5},{4,6},{5,7},{6,0},{7,1},{8,10},{9,11},{10,... | collective-permute-start | bytes 393224 | tf_op jit(solution)/shard_map/ppermute | solution.py:41
  115.9 22.5 %collective-permute-start.24 = (f32[2,4096]{1,0:T(2,128)}, f32[2,4096]{1,0:T(2,128)}, u32[]{:S(2)}, u32[]{:S(2)}) collective-permute-start(f32[2,4096]{1,0:T(2,128)} %get-tuple-element.30), channel_id=1, source_target_pairs={{0,56},{1,57},{2,58},{3,59},{4,60},{5,61},{6,62},{7,63},{8,0},{9,1... | collective-permute-start | bytes 98312 | tf_op jit(solution)/shard_map/ppermute | solution.py:41
  120.5 23.3 %collective-permute-start.23 = (f32[2,4096]{1,0:T(2,128)S(1)}, f32[2,4096]{1,0:T(2,128)}, u32[]{:S(2)}, u32[]{:S(2)}) collective-permute-start(f32[2,4096]{1,0:T(2,128)S(1)} %get-tuple-element.31), channel_id=1, source_target_pairs={{0,48},{1,49},{2,50},{3,51},{4,52},{5,53},{6,54},{7,55},{8,56},{9,... | collective-permute-start | bytes 98312 | tf_op jit(solution)/shard_map/ppermute | solution.py:41
  127.6 24.9 %collective-permute-start.22 = (f32[2,4096]{1,0:T(2,128)}, f32[2,4096]{1,0:T(2,128)}, u32[]{:S(2)}, u32[]{:S(2)}) collective-permute-start(f32[2,4096]{1,0:T(2,128)} %get-tuple-element.32), channel_id=1, source_target_pairs={{0,40},{1,41},{2,42},{3,43},{4,44},{5,45},{6,46},{7,47},{8,48},{9,... | collective-permute-start | bytes 98312 | tf_op jit(solution)/shard_map/ppermute | solution.py:41
  130.6 21.9 %collective-permute-start.21 = (f32[2,4096]{1,0:T(2,128)}, f32[2,4096]{1,0:T(2,128)}, u32[]{:S(2)}, u32[]{:S(2)}) collective-permute-start(f32[2,4096]{1,0:T(2,128)} %get-tuple-element.33), channel_id=1, source_target_pairs={{0,32},{1,33},{2,34},{3,35},{4,36},{5,37},{6,38},{7,39},{8,40},{9,... | collective-permute-start | bytes 98312 | tf_op jit(solution)/shard_map/ppermute | solution.py:41
  136.6 15.9 %collective-permute-start.20 = (f32[2,4096]{1,0:T(2,128)}, f32[2,4096]{1,0:T(2,128)}, u32[]{:S(2)}, u32[]{:S(2)}) collective-permute-start(f32[2,4096]{1,0:T(2,128)} %get-tuple-element.34), channel_id=1, source_target_pairs={{0,24},{1,25},{2,26},{3,27},{4,28},{5,29},{6,30},{7,31},{8,32},{9,... | collective-permute-start | bytes 98312 | tf_op jit(solution)/shard_map/ppermute | solution.py:41
  138.5 14.0 %collective-permute-start.19 = (f32[2,4096]{1,0:T(2,128)}, f32[2,4096]{1,0:T(2,128)}, u32[]{:S(2)}, u32[]{:S(2)}) collective-permute-start(f32[2,4096]{1,0:T(2,128)} %get-tuple-element.35), channel_id=1, source_target_pairs={{0,16},{1,17},{2,18},{3,19},{4,20},{5,21},{6,22},{7,23},{8,24},{9,... | collective-permute-start | bytes 98312 | tf_op jit(solution)/shard_map/ppermute | solution.py:41
  143.8 8.7 %collective-permute-start.18 = (f32[2,4096]{1,0:T(2,128)}, f32[2,4096]{1,0:T(2,128)}, u32[]{:S(2)}, u32[]{:S(2)}) collective-permute-start(f32[2,4096]{1,0:T(2,128)} %get-tuple-element.29), channel_id=1, source_target_pairs={{0,8},{1,9},{2,10},{3,11},{4,12},{5,13},{6,14},{7,15},{8,16},{9,17... | collective-permute-start | bytes 98312 | tf_op jit(solution)/shard_map/ppermute | solution.py:41
  148.2 1.2 copy-start.2
  149.4 1.0 copy-start.4

commit v5 on v4

--- a/solution.py
+++ b/solution.py
@@ -41,32 +41,36 @@
     return lax.ppermute(block, "pool", [(j, moved(j)) for j in range(lax.axis_size("pool"))])
 
 
-def gather_kernel(picks_ref, tiles_ref, out_ref, buffer, load_sems, store_sems):
+def gather_kernel(parts, picks_ref, tiles_ref, out_ref, buffer, load_sems, store_sems):
     slots, peers = picks_ref.shape
-    loads, stores = [], []
+    size = tiles_ref.shape[0] // parts
+    loads = []
+    for i in range(parts):
+        span = pl.ds(i * size, size)
+        loads.append(pltpu.make_async_copy(tiles_ref.at[span], buffer.at[span], load_sems.at[i]))
+        loads[-1].start()
+    for load in loads:
+        load.wait()
+    stores = []
     for j in range(peers * slots):
-        tile = tiles_ref.at[picks_ref[j % slots, j // slots]]
-        loads.append(pltpu.make_async_copy(tile, buffer.at[j], load_sems.at[j]))
-        loads[-1].start()
-    for j, load in enumerate(loads):
-        load.wait()
-        stores.append(pltpu.make_async_copy(buffer.at[j], out_ref.at[j], store_sems.at[j]))
+        tile = buffer.at[picks_ref[j % slots, j // slots]]
+        stores.append(pltpu.make_async_copy(tile, out_ref.at[j], store_sems.at[j]))
         stores[-1].start()
     for store in stores:
         store.wait()
 
 
-def gather_tiles(picks, tiles):
+def gather_tiles(picks, tiles, parts=4):
     slots, peers = picks.shape
     shape = (peers * slots,) + tiles.shape[1:]
     return pl.pallas_call(
-        gather_kernel,
+        functools.partial(gather_kernel, parts),
         out_shape=pltpu.HBM(shape, tiles.dtype),
         in_specs=[SMEM, HBM],
         out_specs=HBM,
         scratch_shapes=[
-            pltpu.VMEM(shape, tiles.dtype),
-            pltpu.SemaphoreType.DMA((peers * slots,)),
+            pltpu.VMEM(tiles.shape, tiles.dtype),
+            pltpu.SemaphoreType.DMA((parts,)),
             pltpu.SemaphoreType.DMA((peers * slots,)),
         ],
         compiler_params=PARAMS,
@@ -132,7 +136,7 @@
         copy.wait()
 
 
-def weights(queries, hard_rows, local, near, far, counts, positives, chunk=1024):
+def weights(queries, hard_rows, local, near, far, counts, positives, chunk=512):
     hard, width = hard_rows.shape
     like = lambda x: jax.ShapeDtypeStruct(x.shape, jnp.bfloat16)
     return pl.pallas_call(
@@ -183,42 +187,84 @@
     )(near, far, queries)
 
 
-def queries_kernel(chunk, *refs):
-    pairs, (out_ref, buffer, sems) = refs[:-3], refs[-3:]
-    count = len(pairs) // 2
-    copies = []
-    for i in range(out_ref.shape[1] // chunk):
-        columns = pl.ds(i * chunk, chunk)
-        part = transposed(pairs[0][...], pairs[count][:, columns])
-        for k in range(1, count):
-            part = part + transposed(pairs[k][...], pairs[count + k][:, columns])
-        buffer[:, columns] = (SHARPNESS * part).astype(jnp.bfloat16)
-        copy = pltpu.make_async_copy(buffer.at[:, columns], out_ref.at[:, columns], sems.at[i])
-        copy.start()
-        copies.append(copy)
-    for copy in copies:
-        copy.wait()
-
-
-def query_gradient(weight, keys, chunk=1024):
-    rows, width = weight[0].shape[1], keys[0].shape[1]
-    return pl.pallas_call(
-        functools.partial(queries_kernel, chunk),
-        out_shape=jax.ShapeDtypeStruct((rows, width), jnp.bfloat16),
-        in_specs=[VMEM] * (len(weight) + len(keys)),
-        out_specs=HBM,
+def queries_kernel(chunk, weight_refs, picks_ref, hard_ref, key_refs, outs, scratch):
+    out_ref, chosen_ref = outs
+    held, buffer, load_sems, store_sems = scratch
+    spans = [pl.ds(i * chunk, chunk) for i in range(out_ref.shape[1] // chunk)]
+    loads, views, start = [], [], 0
+    for k, key in enumerate(key_refs):
+        view = held.at[pl.ds(start, key.shape[0])]
+        start += key.shape[0]
+        views.append(view)
+        loads.append(
+            [
+                pltpu.make_async_copy(key.at[:, span], view.at[:, span], load_sems.at[k, i])
+                for i, span in enumerate(spans)
+            ]
+        )
+    for i in range(len(spans)):
+        for load in loads:
+            load[i].start()
+    slots, peers = picks_ref.shape
+    lane = lax.broadcasted_iota(jnp.int32, (1, chosen_ref.shape[1]), 1)
+    wanted = lane % TILE
+    for j in range(peers * slots):
+        pick = picks_ref[j % slots, j // slots]
+        wanted = wanted + jnp.where(lane // TILE == j, pick * TILE, 0)
+    rows = lax.broadcasted_iota(jnp.int32, chosen_ref.shape, 0)
+    chosen_ref[...] = (rows == wanted).astype(jnp.float32).astype(jnp.bfloat16)
+    hard_weight, weight = weight_refs[0][...], [ref[...] for ref in weight_refs[1:]]
+    stores = []
+    for i, span in enumerate(spans):
+        part = transposed(hard_weight, hard_ref[:, span])
+        for k, view in enumerate(views):
+            loads[k][i].wait()
+            part = part + transposed(weight[k], view[:, span])
+        buffer[:, span] = (SHARPNESS * part).astype(jnp.bfloat16)
+        store = pltpu.make_async_copy(buffer.at[:, span], out_ref.at[:, span], store_sems.at[i])
+        store.start()
+        stores.append(store)
+    for store in stores:
+        store.wait()
+
+
+def query_gradient(hard_weight, weight, picks, hard_rows, keys, chunk=1024):
+    (hard, rows), width = hard_weight.shape, hard_rows.shape[1]
+    held = sum(key.shape[0] for key in keys)
+    count = len(keys)
+
+    def kernel(*refs):
+        inputs, outs, scratch = refs[: 3 + 2 * count], refs[3 + 2 * count : 5 + 2 * count], refs[5 + 2 * count :]
+        queries_kernel(
+            chunk, inputs[: 1 + count], inputs[1 + count], inputs[2 + count],
+            inputs[3 + count :], outs, scratch,
+        )
+
+    return pl.pallas_call(
+        kernel,
+        out_shape=(
+            pltpu.HBM((rows, width), jnp.bfloat16),
+            jax.ShapeDtypeStruct((rows, hard), jnp.bfloat16),
+        ),
+        in_specs=[VMEM] * (1 + count) + [SMEM, VMEM] + [HBM] * count,
+        out_specs=(HBM, VMEM),
         scratch_shapes=[
+            pltpu.VMEM((held, width), jnp.bfloat16),
             pltpu.VMEM((rows, width), jnp.bfloat16),
+            pltpu.SemaphoreType.DMA((count, width // chunk)),
             pltpu.SemaphoreType.DMA((width // chunk,)),
         ],
         compiler_params=PARAMS,
         cost_estimate=CHEAP,
         name="query_gradient",
-    )(*weight, *keys)
+    )(
+        hard_weight, *weight, picks, hard_rows,
+        *[pltpu.with_memory_space_constraint(key, pltpu.HBM) for key in keys],
+    )
 
 
 def passages_kernel(
-    chunk, weight_ref, queries_ref, wanted_ref, returned_ref, out_ref,
+    chunk, weight_ref, queries_ref, chosen_ref, returned_ref, out_ref,
     incoming, buffer, load_sems, store_sems,
 ):
     spans = [pl.ds(i * chunk, chunk) for i in range(out_ref.shape[1] // chunk)]
@@ -229,10 +275,7 @@
     for load in loads:
         load.start()
     weight = weight_ref[...]
-    rows, hard = weight.shape[0], wanted_ref.shape[1]
-    chosen = (
-        lax.broadcasted_iota(jnp.int32, (rows, hard), 0) == wanted_ref[...]
-    ).astype(jnp.bfloat16)
+    chosen = chosen_ref[...]
     stores = []
     for i, span in enumerate(spans):
         part = SHARPNESS * jnp.dot(
@@ -248,7 +291,7 @@
         store.wait()
 
 
-def passage_gradient(weight, queries, wanted, returned, chunk=1024):
+def passage_gradient(weight, queries, chosen, returned, chunk=1024):
     rows, width = weight.shape[0], queries.shape[1]
     return pl.pallas_call(
         functools.partial(passages_kernel, chunk),
@@ -264,7 +307,7 @@
         compiler_params=PARAMS,
         cost_estimate=CHEAP,
         name="passage_gradient",
-    )(weight, queries, wanted, pltpu.with_memory_space_constraint(returned, pltpu.HBM))
+    )(weight, queries, chosen, pltpu.with_memory_space_constraint(returned, pltpu.HBM))
 
 
 def body(digits, queries, passages, pool_passages, positives, tile_ids, tile_count):
@@ -290,31 +333,30 @@
     returned = lax.all_to_all(
         grad_hard.reshape(peers, slots * TILE, width), "pb", split_axis=0, concat_axis=0, tiled=True
     ).reshape(hard, width)
-    (y_step, y_count), (x_step, x_count), (core_step, core_count) = digits
-    size = y_count * pool_passages.shape[0]
+    *y_digits, (x_step, x_count), (core_step, core_count) = digits
+    size = pooled.shape[0] // x_count
     term, *sent = pool_terms(near_weight, far_weight, queries, size, jnp.bfloat16)
     moves = [(x, core) for core in range(core_count) for x in range(x_count)][1:]
     for piece, (x, core) in zip(sent, moves):
         pair = ((x_step, x_count, x), (core_step, core_count, core))
         term = term + shifts(piece, pair, 1).astype(jnp.float32)
-    size = size // y_count
-    pieces = [term[m * size : (m + 1) * size] for m in range(y_count)]
-    term = pieces[0]
-    for m in range(1, y_count):
-        term = term + shifts(pieces[m], ((y_step, y_count, m),), 1)
+    for step, count in reversed(y_digits):
+        size = size // count
+        pieces = [term[m * size : (m + 1) * size] for m in range(count)]
+        term = pieces[0]
+        for m in range(1, count):
+            term = term + shifts(pieces[m], ((step, count, m),), 1)
     grad_pool = term.astype(jnp.bfloat16)
-    grad_queries = query_gradient(
-        (local_weight, near_weight, far_weight, hard_weight), (passages, near, far, hard_rows)
-    )
-    wanted = (
-        picks.reshape(-1)[:, None] * TILE + jnp.arange(TILE, dtype=jnp.int32)[None, :]
-    ).reshape(1, hard)
-    grad_passages = passage_gradient(local_weight, queries, wanted, returned)
+    grad_queries, chosen = query_gradient(
+        hard_weight, (local_weight, near_weight, far_weight), picks.T, hard_rows,
+        (passages, near, far),
+    )
+    grad_passages = passage_gradient(local_weight, queries, chosen, returned)
     return (grad_queries, grad_passages, grad_pool)
 
 
 def solution(mesh):
-    digits = ((8, 8), (2, 4), (1, 2))
+    digits = ((8, 4), (32, 2), (2, 4), (1, 2))
     return jax.shard_map(
         lambda *args: body(digits, *args),
         mesh=mesh,

time: 158 us -> 149 us (0.943)
  the two profiles are of different devices: /device:TPU:64 before, /device:TPU:6 now
where the time goes in v5:
time: 149 us; the launch traced here: 147 us
  starting transfers between devices  88.9 us (60%)
  waiting for transfers between devices  35 us (23%)
  Pallas kernels  15.5 us (10%)
  local copies, waits for them, and re-layouts  5.47 us (4%)
    ppermute x19, starting transfers between devices, shifts(): lax.ppermute(block, 'pool', [(j, moved(j)) for j in range(lax.axis_size('...  69.2 us
    ppermute x19, waiting for transfers between devices, shifts(): lax.ppermute(block, 'pool', [(j, moved(j)) for j in range(lax.axis_size('...  23.2 us
    all_to_all x1, starting transfers between devices, body(): lax.all_to_all(outgoing.reshape(peers, slots * TILE, width), 'pb', split_...  15.3 us
    all_to_all x1, waiting for transfers between devices, body(): lax.all_to_all(outgoing.reshape(peers, slots * TILE, width), 'pb', split_...  11.8 us
    all_to_all x1, starting transfers between devices, body(): lax.all_to_all(grad_hard.reshape(peers, slots * TILE, width), 'pb', split...  4.43 us
    pallas_call x1, Pallas kernels, query_gradient(): pl.pallas_call(kernel, out_shape=(pltpu.HBM((rows, width), jnp.bfloat16),...  4.34 us
    unnamed x20, local copies, waits for them, and re-layouts  3.37 us
    pallas_call x1, Pallas kernels, weights(): pl.pallas_call(functools.partial(weights_kernel, chunk), out_shape=(pltpu...  3.29 us
  transfers between devices with their start and end apart: 21, of which 8 were waited for; matrix products, arithmetic and copies ran while one was open for 2% of the time, Pallas kernels for 4%

profile of v5, /device:TPU:6, one launch (start us, length us, event | category | flops | bytes accessed | tf_op | source)
XLA Modules:
  0.0 146.8 jit_solution(62052046519727274)
XLA Ops:
  0.6 0.0 copy-start.4
  0.6 0.7 copy-done.4
  1.3 3.2 %gather_tiles.1 = bf16[24,8,4096]{2,1,0:T(8,128)(2,1)} custom-call(s32[2,12]{1,0:T(2,128)S(1)} %bitcast.13, bf16[16,8,4096]{2,1,0:T(8,128)(2,1)} %bitcast.12), custom_call_target="tpu_custom_call" | custom-call | bytes 3145728 | tf_op jit(solution)/shard_map/gather_tiles/pallas_call | solution.py:66
  4.5 0.0 copy-start.8
  4.5 0.0 copy-start
  4.5 15.3 %all-to-all-start = ((bf16[12,16,4096]{2,1,0:T(8,128)(2,1)}), bf16[12,16,4096]{2,1,0:T(8,128)(2,1)S(1)}, u32[]{:S(2)}, u32[]{:S(2)}) async-start(bf16[12,16,4096]{2,1,0:T(8,128)(2,1)} %bitcast.17), calls=%async_computation | async-start | bytes 3145728 | tf_op jit(solution)/shard_map/all_to_all | solution.py:319
  19.8 3.5 %collective-permute-start.2 = (bf16[2,4096]{1,0:T(2,128)(2,1)S(1)}, bf16[2,4096]{1,0:T(2,128)(2,1)S(1)}, u32[]{:S(2)}, u32[]{:S(2)}) collective-permute-start(bf16[2,4096]{1,0:T(2,128)(2,1)S(1)} %copy-done.8), channel_id=1, source_target_pairs={{0,8},{1,9},{2,10},{3,11},{4,12},{5,13},{6,14},{7,15},{8,16},{9,17... | collective-permute-start | bytes 49160 | tf_op jit(solution)/shard_map/ppermute | solution.py:41
  23.3 4.5 %collective-permute-start.1 = (bf16[2,4096]{1,0:T(2,128)(2,1)S(1)}, bf16[2,4096]{1,0:T(2,128)(2,1)S(1)}, u32[]{:S(2)}, u32[]{:S(2)}) collective-permute-start(bf16[2,4096]{1,0:T(2,128)(2,1)S(1)} %copy-done.8), channel_id=1, source_target_pairs={{0,16},{1,17},{2,18},{3,19},{4,20},{5,21},{6,22},{7,23},{8,24},{9,... | collective-permute-start | bytes 49160 | tf_op jit(solution)/shard_map/ppermute | solution.py:41
  27.8 3.3 %collective-permute-start = (bf16[2,4096]{1,0:T(2,128)(2,1)S(1)}, bf16[2,4096]{1,0:T(2,128)(2,1)S(1)}, u32[]{:S(2)}, u32[]{:S(2)}) collective-permute-start(bf16[2,4096]{1,0:T(2,128)(2,1)S(1)} %copy-done.8), channel_id=1, source_target_pairs={{0,24},{1,25},{2,26},{3,27},{4,28},{5,29},{6,30},{7,31},{8,0},{9,1... | collective-permute-start | bytes 49160 | tf_op jit(solution)/shard_map/ppermute | solution.py:41
  31.1 0.0 collective-permute-done.2
  31.1 0.0 collective-permute-done.1
  31.1 2.3 %collective-permute-done = bf16[2,4096]{1,0:T(2,128)(2,1)S(1)} collective-permute-done((bf16[2,4096]{1,0:T(2,128)(2,1)S(1)}, bf16[2,4096]{1,0:T(2,128)(2,1)S(1)}, u32[]{:S(2)}, u32[]{:S(2)}) %collective-permute-start) | collective-permute-done | bytes 16416 | tf_op jit(solution)/shard_map/ppermute | solution.py:41
  33.4 0.1 pad_maximum_fusion
  33.5 5.9 %collective-permute-start.3 = (bf16[8,4096]{1,0:T(8,128)(2,1)S(1)}, bf16[8,4096]{1,0:T(8,128)(2,1)S(1)}, u32[]{:S(2)}, u32[]{:S(2)}) collective-permute-start(bf16[8,4096]{1,0:T(8,128)(2,1)S(1)} %pad_maximum_fusion), channel_id=1, source_target_pairs={{0,32},{1,33},{2,34},{3,35},{4,36},{5,37},{6,38},{7,39},{8,40},{9,... | collective-permute-start | bytes 196616 | tf_op jit(solution)/shard_map/ppermute | solution.py:41
  39.5 4.3 %collective-permute-done.3 = bf16[8,4096]{1,0:T(8,128)(2,1)S(1)} collective-permute-done((bf16[8,4096]{1,0:T(8,128)(2,1)S(1)}, bf16[8,4096]{1,0:T(8,128)(2,1)S(1)}, u32[]{:S(2)}, u32[]{:S(2)}) %collective-permute-start.3) | collective-permute-done | bytes 65568 | tf_op jit(solution)/shard_map/ppermute | solution.py:41
  43.8 0.1 concatenate.12
  43.9 2.4 %collective-permute-start.6 = (bf16[16,4096]{1,0:T(8,128)(2,1)S(1)}, bf16[16,4096]{1,0:T(8,128)(2,1)S(1)}, u32[]{:S(2)}, u32[]{:S(2)}) collective-permute-start(bf16[16,4096]{1,0:T(8,128)(2,1)S(1)} %concatenate.12), channel_id=1, source_target_pairs={{0,2},{1,3},{2,4},{3,5},{4,6},{5,7},{6,0},{7,1},{8,10},{9,11},{10,... | collective-permute-start | bytes 393224 | tf_op jit(solution)/shard_map/ppermute | solution.py:41
  46.3 4.3 %collective-permute-start.5 = (bf16[16,4096]{1,0:T(8,128)(2,1)S(1)}, bf16[16,4096]{1,0:T(8,128)(2,1)S(1)}, u32[]{:S(2)}, u32[]{:S(2)}) collective-permute-start(bf16[16,4096]{1,0:T(8,128)(2,1)S(1)} %concatenate.12), channel_id=1, source_target_pairs={{0,4},{1,5},{2,6},{3,7},{4,0},{5,1},{6,2},{7,3},{8,12},{9,13},{10,... | collective-permute-start | bytes 393224 | tf_op jit(solution)/shard_map/ppermute | solution.py:41
  50.6 1.9 %collective-permute-start.4 = (bf16[16,4096]{1,0:T(8,128)(2,1)S(1)}, bf16[16,4096]{1,0:T(8,128)(2,1)}, u32[]{:S(2)}, u32[]{:S(2)}) collective-permute-start(bf16[16,4096]{1,0:T(8,128)(2,1)S(1)} %concatenate.12), channel_id=1, source_target_pairs={{0,6},{1,7},{2,0},{3,1},{4,2},{5,3},{6,4},{7,5},{8,14},{9,15},{10,... | collective-permute-start | bytes 393224 | tf_op jit(solution)/shard_map/ppermute | solution.py:41
  52.6 0.0 collective-permute-done.6
  52.6 3.1 %collective-permute-done.5 = bf16[16,4096]{1,0:T(8,128)(2,1)S(1)} collective-permute-done((bf16[16,4096]{1,0:T(8,128)(2,1)S(1)}, bf16[16,4096]{1,0:T(8,128)(2,1)S(1)}, u32[]{:S(2)}, u32[]{:S(2)}) %collective-permute-start.5) | collective-permute-done | bytes 131104 | tf_op jit(solution)/shard_map/ppermute | solution.py:41
  55.7 0.7 copy-done.9
  56.3 2.5 %collective-permute-done.4 = bf16[16,4096]{1,0:T(8,128)(2,1)} collective-permute-done((bf16[16,4096]{1,0:T(8,128)(2,1)S(1)}, bf16[16,4096]{1,0:T(8,128)(2,1)}, u32[]{:S(2)}, u32[]{:S(2)}) %collective-permute-start.4) | collective-permute-done | bytes 131104 | tf_op jit(solution)/shard_map/ppermute | solution.py:41
  58.8 1.9 %concatenate.13.keys_ref.refs_7_ = bf16[64,4096]{1,0:T(8,128)(2,1)S(1)} concatenate(bf16[2,4096]{1,0:T(2,128)(2,1)S(1)} %copy-done.8, bf16[2,4096]{1,0:T(2,128)(2,1)S(1)} %collective-permute-done, bf16[2,4096]{1,0:T(2,128)(2,1)S(1)} %collective-permute-done.1, bf16[2,4096]{1,0:T(2,128)(2,1)S(1)} %collective-permute-done.2, bf16[8,4096]{1,0:T(8,128)(2,1)S(1)} %collective-permute-done.3, ...), dimensions={0} | concatenate | bytes 1048576 | tf_op jit(solution)/shard_map/concatenate | solution.py:324
  60.8 0.0 copy-start.2
  60.8 1.9 %collective-permute-start.7 = (bf16[64,4096]{1,0:T(8,128)(2,1)S(1)}, bf16[64,4096]{1,0:T(8,128)(2,1)S(1)}, u32[]{:S(2)}, u32[]{:S(2)}) collective-permute-start(bf16[64,4096]{1,0:T(8,128)(2,1)S(1)} %concatenate.13.keys_ref.refs_7_), channel_id=1, source_target_pairs={{0,1},{1,0},{2,3},{3,2},{4,5},{5,4},{6,7},{7,6},{8,9},{9,8},{10,11... | collective-permute-start | bytes 1572872 | tf_op jit(solution)/shard_map/ppermute | solution.py:41
  62.7 0.0 copy-start.1
  62.7 1.2 copy-done.1
  63.9 0.4 scores.3.local_ref
  64.4 0.0 copy-start.6
  64.4 0.0 copy-start.7
  64.4 0.5 scores.4.near_ref
  64.9 0.0 collective-permute-done.7.keys_ref.refs_8_
  64.9 0.5 scores.5.far_ref
  65.4 0.8 copy-done.3
  66.2 11.8 %all-to-all-done = bf16[12,16,4096]{2,1,0:T(8,128)(2,1)S(1)} async-done(((bf16[12,16,4096]{2,1,0:T(8,128)(2,1)}), bf16[12,16,4096]{2,1,0:T(8,128)(2,1)S(1)}, u32[]{:S(2)}, u32[]{:S(2)}) %all-to-all-start) | async-done | bytes 1572896 | tf_op jit(solution)/shard_map/all_to_all | solution.py:319
  78.0 3.3 %weights.1 = (bf16[192,4096]{1,0:T(8,128)(2,1)}, bf16[128,128]{1,0:T(8,128)(2,1)S(1)}, bf16[64,128]{1,0:T(8,128)(2,1)S(1)}, bf16[64,128]{1,0:T(8,128)(2,1)S(1)}, bf16[192,128]{1,0:T(8,128)(2,1)S(1)}) custom-call(bf16[128,4096]{1,0:T(8,128)(2,1)S(1)} %copy-done, bf16[192,4096]{1,0:T(8,128)(2,1)S(1)} %bitcast.10, f32[128,128]{1,0:T(8,128)S(1)} %scores.3.local_ref, ...), custom_call_target="tpu_custom_call" | custom-call | flops 1048576 | bytes 1048576 | tf_op jit(solution)/shard_map/weights/pallas_call | solution.py:142
  81.3 4.4 %all-to-all-start.1 = ((bf16[12,16,4096]{2,1,0:T(8,128)(2,1)}), bf16[12,16,4096]{2,1,0:T(8,128)(2,1)}, u32[]{:S(2)}, u32[]{:S(2)}) async-start(bf16[12,16,4096]{2,1,0:T(8,128)(2,1)} %bitcast.18), calls=%async_computation.1 | async-start | bytes 3145728 | tf_op jit(solution)/shard_map/all_to_all | solution.py:333
  85.7 0.0 copy-start.5
  85.7 0.4 pool_terms.1
  86.2 2.4 %collective-permute-start.8 = (bf16[16,4096]{1,0:T(8,128)(2,1)S(1)}, bf16[16,4096]{1,0:T(8,128)(2,1)S(1)}, u32[]{:S(2)}, u32[]{:S(2)}) collective-permute-start(bf16[16,4096]{1,0:T(8,128)(2,1)S(1)} %get-tuple-element.26), channel_id=1, source_target_pairs={{0,2},{1,3},{2,4},{3,5},{4,6},{5,7},{6,0},{7,1},{8,10},{9,11},{10,... | collective-permute-start | bytes 393224 | tf_op jit(solution)/shard_map/ppermute | solution.py:41
  88.6 4.3 %collective-permute-start.9 = (bf16[16,4096]{1,0:T(8,128)(2,1)S(1)}, bf16[16,4096]{1,0:T(8,128)(2,1)S(1)}, u32[]{:S(2)}, u32[]{:S(2)}) collective-permute-start(bf16[16,4096]{1,0:T(8,128)(2,1)S(1)} %get-tuple-element.27), channel_id=1, source_target_pairs={{0,4},{1,5},{2,6},{3,7},{4,0},{5,1},{6,2},{7,3},{8,12},{9,13},{10,... | collective-permute-start | bytes 393224 | tf_op jit(solution)/shard_map/ppermute | solution.py:41
  92.9 1.9 %collective-permute-start.10 = (bf16[16,4096]{1,0:T(8,128)(2,1)S(1)}, bf16[16,4096]{1,0:T(8,128)(2,1)S(1)}, u32[]{:S(2)}, u32[]{:S(2)}) collective-permute-start(bf16[16,4096]{1,0:T(8,128)(2,1)S(1)} %get-tuple-element.28), channel_id=1, source_target_pairs={{0,6},{1,7},{2,0},{3,1},{4,2},{5,3},{6,4},{7,5},{8,14},{9,15},{10,... | collective-permute-start | bytes 393224 | tf_op jit(solution)/shard_map/ppermute | solution.py:41
  94.8 1.9 %collective-permute-start.11 = (bf16[16,4096]{1,0:T(8,128)(2,1)S(1)}, bf16[16,4096]{1,0:T(8,128)(2,1)S(1)}, u32[]{:S(2)}, u32[]{:S(2)}) collective-permute-start(bf16[16,4096]{1,0:T(8,128)(2,1)S(1)} %get-tuple-element.29), channel_id=1, source_target_pairs={{0,1},{1,0},{2,3},{3,2},{4,5},{5,4},{6,7},{7,6},{8,9},{9,8},{10,11... | collective-permute-start | bytes 393224 | tf_op jit(solution)/shard_map/ppermute | solution.py:41
  96.8 5.2 %collective-permute-start.12 = (bf16[16,4096]{1,0:T(8,128)(2,1)S(1)}, bf16[16,4096]{1,0:T(8,128)(2,1)S(1)}, u32[]{:S(2)}, u32[]{:S(2)}) collective-permute-start(bf16[16,4096]{1,0:T(8,128)(2,1)S(1)} %get-tuple-element.30), channel_id=1, source_target_pairs={{0,3},{1,2},{2,5},{3,4},{4,7},{5,6},{6,1},{7,0},{8,11},{9,10},{10,... | collective-permute-start | bytes 393224 | tf_op jit(solution)/shard_map/ppermute | solution.py:41
  102.0 0.0 collective-permute-done.8
  102.0 1.9 %collective-permute-start.13 = (bf16[16,4096]{1,0:T(8,128)(2,1)S(1)}, bf16[16,4096]{1,0:T(8,128)(2,1)S(1)}, u32[]{:S(2)}, u32[]{:S(2)}) collective-permute-start(bf16[16,4096]{1,0:T(8,128)(2,1)S(1)} %get-tuple-element.31), channel_id=1, source_target_pairs={{0,5},{1,4},{2,7},{3,6},{4,1},{5,0},{6,3},{7,2},{8,13},{9,12},{10,... | collective-permute-start | bytes 393224 | tf_op jit(solution)/shard_map/ppermute | solution.py:41
  104.0 0.0 collective-permute-done.9
  104.0 3.0 %collective-permute-start.14 = (bf16[16,4096]{1,0:T(8,128)(2,1)S(1)}, bf16[16,4096]{1,0:T(8,128)(2,1)S(1)}, u32[]{:S(2)}, u32[]{:S(2)}) collective-permute-start(bf16[16,4096]{1,0:T(8,128)(2,1)S(1)} %get-tuple-element.32), channel_id=1, source_target_pairs={{0,7},{1,6},{2,1},{3,0},{4,3},{5,2},{6,5},{7,4},{8,15},{9,14},{10,... | collective-permute-start | bytes 393224 | tf_op jit(solution)/shard_map/ppermute | solution.py:41
  107.0 0.0 collective-permute-done.10
  107.0 0.0 collective-permute-done.11
  107.1 0.0 collective-permute-done.12
  107.1 4.1 %collective-permute-done.13 = bf16[16,4096]{1,0:T(8,128)(2,1)S(1)} collective-permute-done((bf16[16,4096]{1,0:T(8,128)(2,1)S(1)}, bf16[16,4096]{1,0:T(8,128)(2,1)S(1)}, u32[]{:S(2)}, u32[]{:S(2)}) %collective-permute-start.13) | collective-permute-done | bytes 131104 | tf_op jit(solution)/shard_map/ppermute | solution.py:41
  111.1 2.9 %collective-permute-done.14 = bf16[16,4096]{1,0:T(8,128)(2,1)S(1)} collective-permute-done((bf16[16,4096]{1,0:T(8,128)(2,1)S(1)}, bf16[16,4096]{1,0:T(8,128)(2,1)S(1)}, u32[]{:S(2)}, u32[]{:S(2)}) %collective-permute-start.14) | collective-permute-done | bytes 131104 | tf_op jit(solution)/shard_map/ppermute | solution.py:41
  114.0 0.1 convert_add_fusion
  114.2 7.7 %collective-permute-start.15 = (f32[8,4096]{1,0:T(8,128)S(1)}, f32[8,4096]{1,0:T(8,128)S(1)}, u32[]{:S(2)}, u32[]{:S(2)}) collective-permute-start(f32[8,4096]{1,0:T(8,128)S(1)} %slice.25), channel_id=1, source_target_pairs={{0,32},{1,33},{2,34},{3,35},{4,36},{5,37},{6,38},{7,39},{8,40},{9,... | collective-permute-start | bytes 393224 | tf_op jit(solution)/shard_map/ppermute | solution.py:41
  121.9 4.0 %collective-permute-done.15 = f32[8,4096]{1,0:T(8,128)S(1)} collective-permute-done((f32[8,4096]{1,0:T(8,128)S(1)}, f32[8,4096]{1,0:T(8,128)S(1)}, u32[]{:S(2)}, u32[]{:S(2)}) %collective-permute-start.15) | collective-permute-done | bytes 131104 | tf_op jit(solution)/shard_map/ppermute | solution.py:41
  125.9 5.9 %collective-permute-start.16 = (f32[2,4096]{1,0:T(2,128)S(1)}, f32[2,4096]{1,0:T(2,128)S(1)}, u32[]{:S(2)}, u32[]{:S(2)}) collective-permute-start(f32[2,4096]{1,0:T(2,128)S(1)} %get-tuple-element.33), channel_id=1, source_target_pairs={{0,8},{1,9},{2,10},{3,11},{4,12},{5,13},{6,14},{7,15},{8,16},{9,17... | collective-permute-start | bytes 98312 | tf_op jit(solution)/shard_map/ppermute | solution.py:41
  131.8 3.8 %collective-permute-start.18 = (f32[2,4096]{1,0:T(2,128)S(1)}, f32[2,4096]{1,0:T(2,128)S(1)}, u32[]{:S(2)}, u32[]{:S(2)}) collective-permute-start(f32[2,4096]{1,0:T(2,128)S(1)} %get-tuple-element.34), channel_id=1, source_target_pairs={{0,24},{1,25},{2,26},{3,27},{4,28},{5,29},{6,30},{7,31},{8,0},{9,1... | collective-permute-start | bytes 98312 | tf_op jit(solution)/shard_map/ppermute | solution.py:41
  135.6 3.3 %collective-permute-start.17 = (f32[2,4096]{1,0:T(2,128)S(1)}, f32[2,4096]{1,0:T(2,128)S(1)}, u32[]{:S(2)}, u32[]{:S(2)}) collective-permute-start(f32[2,4096]{1,0:T(2,128)S(1)} %get-tuple-element.35), channel_id=1, source_target_pairs={{0,16},{1,17},{2,18},{3,19},{4,20},{5,21},{6,22},{7,23},{8,24},{9,... | collective-permute-start | bytes 98312 | tf_op jit(solution)/shard_map/ppermute | solution.py:41
  138.9 4.3 %query_gradient.1 = (bf16[128,4096]{1,0:T(8,128)(2,1)}, bf16[128,192]{1,0:T(8,128)(2,1)S(1)}) custom-call(bf16[192,128]{1,0:T(8,128)(2,1)S(1)} %get-tuple-element.18.refs_0_, bf16[128,128]{1,0:T(8,128)(2,1)S(1)} %get-tuple-element.19.refs_1_.weight_ref, bf16[64,128]{1,0:T(8,128)(2,1)S(1)} %get-tuple-element.20.refs_2_.near_ref, ...), custom_call_target="tpu_custom_call" | custom-call | flops 1048576 | bytes 1048576 | tf_op jit(solution)/shard_map/query_gradient/pallas_call | solution.py:243
  143.3 0.0 collective-permute-done.16
  143.3 0.6 fusion.2
  143.9 2.9 %passage_gradient.1 = bf16[128,4096]{1,0:T(8,128)(2,1)} custom-call(bf16[128,128]{1,0:T(8,128)(2,1)S(1)} %get-tuple-element.19.refs_1_.weight_ref, bf16[128,4096]{1,0:T(8,128)(2,1)S(1)} %copy-done, bf16[128,192]{1,0:T(8,128)(2,1)S(1)} %get-tuple-element.23.chosen_ref, bf16[192,4096]{1,0:T(8,128)(2,1)} %bitcast.8.returned_ref), custom_call_target="tpu_custom_call" | custom-call | flops 1048576 | bytes 1048576 | tf_op jit(solution)/shard_map/passage_gradient/pallas_call | solution.py:296
  (14 shorter events, 0.1 us)
Async XLA Ops:
  0.6 0.7 copy-start.4
  4.5 15.3 %copy-start.8 = (bf16[2,4096]{1,0:T(2,128)(2,1)S(1)}, bf16[2,4096]{1,0:T(2,128)(2,1)}, u32[]{:S(2)}) copy-start(bf16[2,4096]{1,0:T(2,128)(2,1)} %param.8) | copy-start | bytes 49156
  4.5 58.2 %copy-start = (bf16[128,4096]{1,0:T(8,128)(2,1)S(1)}, bf16[128,4096]{1,0:T(8,128)(2,1)}, u32[]{:S(2)}) copy-start(bf16[128,4096]{1,0:T(8,128)(2,1)} %queries_ref.11) | copy-start | bytes 3145732
  4.5 73.5 %all-to-all-start = ((bf16[12,16,4096]{2,1,0:T(8,128)(2,1)}), bf16[12,16,4096]{2,1,0:T(8,128)(2,1)S(1)}, u32[]{:S(2)}, u32[]{:S(2)}) async-start(bf16[12,16,4096]{2,1,0:T(8,128)(2,1)} %bitcast.17), calls=%async_computation | async-start | bytes 3145728 | tf_op jit(solution)/shard_map/all_to_all | solution.py:319
  19.8 11.3 %collective-permute-start.2 = (bf16[2,4096]{1,0:T(2,128)(2,1)S(1)}, bf16[2,4096]{1,0:T(2,128)(2,1)S(1)}, u32[]{:S(2)}, u32[]{:S(2)}) collective-permute-start(bf16[2,4096]{1,0:T(2,128)(2,1)S(1)} %copy-done.8), channel_id=1, source_target_pairs={{0,8},{1,9},{2,10},{3,11},{4,12},{5,13},{6,14},{7,15},{8,16},{9,17... | collective-permute-start | bytes 49160 | tf_op jit(solution)/shard_map/ppermute | solution.py:41
  23.3 7.8 %collective-permute-start.1 = (bf16[2,4096]{1,0:T(2,128)(2,1)S(1)}, bf16[2,4096]{1,0:T(2,128)(2,1)S(1)}, u32[]{:S(2)}, u32[]{:S(2)}) collective-permute-start(bf16[2,4096]{1,0:T(2,128)(2,1)S(1)} %copy-done.8), channel_id=1, source_target_pairs={{0,16},{1,17},{2,18},{3,19},{4,20},{5,21},{6,22},{7,23},{8,24},{9,... | collective-permute-start | bytes 49160 | tf_op jit(solution)/shard_map/ppermute | solution.py:41
  27.8 5.6 %collective-permute-start = (bf16[2,4096]{1,0:T(2,128)(2,1)S(1)}, bf16[2,4096]{1,0:T(2,128)(2,1)S(1)}, u32[]{:S(2)}, u32[]{:S(2)}) collective-permute-start(bf16[2,4096]{1,0:T(2,128)(2,1)S(1)} %copy-done.8), channel_id=1, source_target_pairs={{0,24},{1,25},{2,26},{3,27},{4,28},{5,29},{6,30},{7,31},{8,0},{9,1... | collective-permute-start | bytes 49160 | tf_op jit(solution)/shard_map/ppermute | solution.py:41
  33.5 10.3 %collective-permute-start.3 = (bf16[8,4096]{1,0:T(8,128)(2,1)S(1)}, bf16[8,4096]{1,0:T(8,128)(2,1)S(1)}, u32[]{:S(2)}, u32[]{:S(2)}) collective-permute-start(bf16[8,4096]{1,0:T(8,128)(2,1)S(1)} %pad_maximum_fusion), channel_id=1, source_target_pairs={{0,32},{1,33},{2,34},{3,35},{4,36},{5,37},{6,38},{7,39},{8,40},{9,... | collective-permute-start | bytes 196616 | tf_op jit(solution)/shard_map/ppermute | solution.py:41
  43.9 8.7 %collective-permute-start.6 = (bf16[16,4096]{1,0:T(8,128)(2,1)S(1)}, bf16[16,4096]{1,0:T(8,128)(2,1)S(1)}, u32[]{:S(2)}, u32[]{:S(2)}) collective-permute-start(bf16[16,4096]{1,0:T(8,128)(2,1)S(1)} %concatenate.12), channel_id=1, source_target_pairs={{0,2},{1,3},{2,4},{3,5},{4,6},{5,7},{6,0},{7,1},{8,10},{9,11},{10,... | collective-permute-start | bytes 393224 | tf_op jit(solution)/shard_map/ppermute | solution.py:41
  46.3 9.4 %collective-permute-start.5 = (bf16[16,4096]{1,0:T(8,128)(2,1)S(1)}, bf16[16,4096]{1,0:T(8,128)(2,1)S(1)}, u32[]{:S(2)}, u32[]{:S(2)}) collective-permute-start(bf16[16,4096]{1,0:T(8,128)(2,1)S(1)} %concatenate.12), channel_id=1, source_target_pairs={{0,4},{1,5},{2,6},{3,7},{4,0},{5,1},{6,2},{7,3},{8,12},{9,13},{10,... | collective-permute-start | bytes 393224 | tf_op jit(solution)/shard_map/ppermute | solution.py:41
  50.6 8.2 %collective-permute-start.4 = (bf16[16,4096]{1,0:T(8,128)(2,1)S(1)}, bf16[16,4096]{1,0:T(8,128)(2,1)}, u32[]{:S(2)}, u32[]{:S(2)}) collective-permute-start(bf16[16,4096]{1,0:T(8,128)(2,1)S(1)} %concatenate.12), channel_id=1, source_target_pairs={{0,6},{1,7},{2,0},{3,1},{4,2},{5,3},{6,4},{7,5},{8,14},{9,15},{10,... | collective-permute-start | bytes 393224 | tf_op jit(solution)/shard_map/ppermute | solution.py:41
  55.7 0.7 copy-start.9
  60.8 4.1 %copy-start.2 = (bf16[64,4096]{1,0:T(8,128)(2,1)}, bf16[64,4096]{1,0:T(8,128)(2,1)S(1)}, u32[]{:S(2)}) copy-start(bf16[64,4096]{1,0:T(8,128)(2,1)S(1)} %concatenate.13.keys_ref.refs_7_) | copy-start | bytes 1572868
  60.8 4.1 %collective-permute-start.7 = (bf16[64,4096]{1,0:T(8,128)(2,1)S(1)}, bf16[64,4096]{1,0:T(8,128)(2,1)S(1)}, u32[]{:S(2)}, u32[]{:S(2)}) collective-permute-start(bf16[64,4096]{1,0:T(8,128)(2,1)S(1)} %concatenate.13.keys_ref.refs_7_), channel_id=1, source_target_pairs={{0,1},{1,0},{2,3},{3,2},{4,5},{5,4},{6,7},{7,6},{8,9},{9,8},{10,11... | collective-permute-start | bytes 1572872 | tf_op jit(solution)/shard_map/ppermute | solution.py:41
  62.7 1.2 copy-start.1
  64.4 13.6 %copy-start.6 = (s32[1,1,12]{2,1,0:T(1,128)S(1)}, s32[1,1,12]{2,1,0:T(1,128)}, u32[]{:S(2)}) copy-start(s32[1,1,12]{2,1,0:T(1,128)} %param.11) | copy-start | bytes 148
  64.4 13.6 %copy-start.7 = (s32[128]{0:T(128)S(1)}, s32[128]{0:T(128)}, u32[]{:S(2)}) copy-start(s32[128]{0:T(128)} %param.9) | copy-start | bytes 1540
  65.4 0.8 copy-start.3
  81.3 62.6 %all-to-all-start.1 = ((bf16[12,16,4096]{2,1,0:T(8,128)(2,1)}), bf16[12,16,4096]{2,1,0:T(8,128)(2,1)}, u32[]{:S(2)}, u32[]{:S(2)}) async-start(bf16[12,16,4096]{2,1,0:T(8,128)(2,1)} %bitcast.18), calls=%async_computation.1 | async-start | bytes 3145728 | tf_op jit(solution)/shard_map/all_to_all | solution.py:333
  85.7 53.2 %copy-start.5 = (s32[1,1,12,2]{2,3,1,0:T(2,128)S(1)}, s32[1,1,12,2]{2,3,1,0:T(2,128)}, u32[]{:S(2)}) copy-start(s32[1,1,12,2]{2,3,1,0:T(2,128)} %param.10) | copy-start | bytes 292
  86.2 15.8 %collective-permute-start.8 = (bf16[16,4096]{1,0:T(8,128)(2,1)S(1)}, bf16[16,4096]{1,0:T(8,128)(2,1)S(1)}, u32[]{:S(2)}, u32[]{:S(2)}) collective-permute-start(bf16[16,4096]{1,0:T(8,128)(2,1)S(1)} %get-tuple-element.26), channel_id=1, source_target_pairs={{0,2},{1,3},{2,4},{3,5},{4,6},{5,7},{6,0},{7,1},{8,10},{9,11},{10,... | collective-permute-start | bytes 393224 | tf_op jit(solution)/shard_map/ppermute | solution.py:41
  88.6 15.4 %collective-permute-start.9 = (bf16[16,4096]{1,0:T(8,128)(2,1)S(1)}, bf16[16,4096]{1,0:T(8,128)(2,1)S(1)}, u32[]{:S(2)}, u32[]{:S(2)}) collective-permute-start(bf16[16,4096]{1,0:T(8,128)(2,1)S(1)} %get-tuple-element.27), channel_id=1, source_target_pairs={{0,4},{1,5},{2,6},{3,7},{4,0},{5,1},{6,2},{7,3},{8,12},{9,13},{10,... | collective-permute-start | bytes 393224 | tf_op jit(solution)/shard_map/ppermute | solution.py:41
  92.9 14.1 %collective-permute-start.10 = (bf16[16,4096]{1,0:T(8,128)(2,1)S(1)}, bf16[16,4096]{1,0:T(8,128)(2,1)S(1)}, u32[]{:S(2)}, u32[]{:S(2)}) collective-permute-start(bf16[16,4096]{1,0:T(8,128)(2,1)S(1)} %get-tuple-element.28), channel_id=1, source_target_pairs={{0,6},{1,7},{2,0},{3,1},{4,2},{5,3},{6,4},{7,5},{8,14},{9,15},{10,... | collective-permute-start | bytes 393224 | tf_op jit(solution)/shard_map/ppermute | solution.py:41
  94.8 12.2 %collective-permute-start.11 = (bf16[16,4096]{1,0:T(8,128)(2,1)S(1)}, bf16[16,4096]{1,0:T(8,128)(2,1)S(1)}, u32[]{:S(2)}, u32[]{:S(2)}) collective-permute-start(bf16[16,4096]{1,0:T(8,128)(2,1)S(1)} %get-tuple-element.29), channel_id=1, source_target_pairs={{0,1},{1,0},{2,3},{3,2},{4,5},{5,4},{6,7},{7,6},{8,9},{9,8},{10,11... | collective-permute-start | bytes 393224 | tf_op jit(solution)/shard_map/ppermute | solution.py:41
  96.8 10.3 %collective-permute-start.12 = (bf16[16,4096]{1,0:T(8,128)(2,1)S(1)}, bf16[16,4096]{1,0:T(8,128)(2,1)S(1)}, u32[]{:S(2)}, u32[]{:S(2)}) collective-permute-start(bf16[16,4096]{1,0:T(8,128)(2,1)S(1)} %get-tuple-element.30), channel_id=1, source_target_pairs={{0,3},{1,2},{2,5},{3,4},{4,7},{5,6},{6,1},{7,0},{8,11},{9,10},{10,... | collective-permute-start | bytes 393224 | tf_op jit(solution)/shard_map/ppermute | solution.py:41
  102.0 9.1 %collective-permute-start.13 = (bf16[16,4096]{1,0:T(8,128)(2,1)S(1)}, bf16[16,4096]{1,0:T(8,128)(2,1)S(1)}, u32[]{:S(2)}, u32[]{:S(2)}) collective-permute-start(bf16[16,4096]{1,0:T(8,128)(2,1)S(1)} %get-tuple-element.31), channel_id=1, source_target_pairs={{0,5},{1,4},{2,7},{3,6},{4,1},{5,0},{6,3},{7,2},{8,13},{9,12},{10,... | collective-permute-start | bytes 393224 | tf_op jit(solution)/shard_map/ppermute | solution.py:41
  104.0 10.0 %collective-permute-start.14 = (bf16[16,4096]{1,0:T(8,128)(2,1)S(1)}, bf16[16,4096]{1,0:T(8,128)(2,1)S(1)}, u32[]{:S(2)}, u32[]{:S(2)}) collective-permute-start(bf16[16,4096]{1,0:T(8,128)(2,1)S(1)} %get-tuple-element.32), channel_id=1, source_target_pairs={{0,7},{1,6},{2,1},{3,0},{4,3},{5,2},{6,5},{7,4},{8,15},{9,14},{10,... | collective-permute-start | bytes 393224 | tf_op jit(solution)/shard_map/ppermute | solution.py:41
  114.2 11.7 %collective-permute-start.15 = (f32[8,4096]{1,0:T(8,128)S(1)}, f32[8,4096]{1,0:T(8,128)S(1)}, u32[]{:S(2)}, u32[]{:S(2)}) collective-permute-start(f32[8,4096]{1,0:T(8,128)S(1)} %slice.25), channel_id=1, source_target_pairs={{0,32},{1,33},{2,34},{3,35},{4,36},{5,37},{6,38},{7,39},{8,40},{9,... | collective-permute-start | bytes 393224 | tf_op jit(solution)/shard_map/ppermute | solution.py:41
  125.9 17.3 %collective-permute-start.16 = (f32[2,4096]{1,0:T(2,128)S(1)}, f32[2,4096]{1,0:T(2,128)S(1)}, u32[]{:S(2)}, u32[]{:S(2)}) collective-permute-start(f32[2,4096]{1,0:T(2,128)S(1)} %get-tuple-element.33), channel_id=1, source_target_pairs={{0,8},{1,9},{2,10},{3,11},{4,12},{5,13},{6,14},{7,15},{8,16},{9,17... | collective-permute-start | bytes 98312 | tf_op jit(solution)/shard_map/ppermute | solution.py:41
  131.8 11.4 %collective-permute-start.18 = (f32[2,4096]{1,0:T(2,128)S(1)}, f32[2,4096]{1,0:T(2,128)S(1)}, u32[]{:S(2)}, u32[]{:S(2)}) collective-permute-start(f32[2,4096]{1,0:T(2,128)S(1)} %get-tuple-element.34), channel_id=1, source_target_pairs={{0,24},{1,25},{2,26},{3,27},{4,28},{5,29},{6,30},{7,31},{8,0},{9,1... | collective-permute-start | bytes 98312 | tf_op jit(solution)/shard_map/ppermute | solution.py:41
  135.6 7.7 %collective-permute-start.17 = (f32[2,4096]{1,0:T(2,128)S(1)}, f32[2,4096]{1,0:T(2,128)S(1)}, u32[]{:S(2)}, u32[]{:S(2)}) collective-permute-start(f32[2,4096]{1,0:T(2,128)S(1)} %get-tuple-element.35), channel_id=1, source_target_pairs={{0,16},{1,17},{2,18},{3,19},{4,20},{5,21},{6,22},{7,23},{8,24},{9,... | collective-permute-start | bytes 98312 | tf_op jit(solution)/shard_map/ppermute | solution.py:41

commit v6 on v5

--- a/solution.py
+++ b/solution.py
@@ -9,6 +9,7 @@
 
 TILE = 8
 
+ORDERS = ((0, 3, 6, 9, 1, 4, 7, 10, 2, 5, 8, 11), (6, 9, 0, 3, 7, 10, 1, 8, 4, 11, 2, 5))
 
 SHARPNESS = 50.0
 
@@ -28,6 +29,19 @@
 def transposed(left, right):
     return lax.dot_general(
         left, right, (((0,), (0,)), ((), ())), preferred_element_type=jnp.float32
+    )
+
+
+def member(k):
+    first, second = ORDERS[0][k], ORDERS[1][k]
+    return first + lax.axis_index("pool") % 2 * (second - first)
+
+
+def trade(blocks):
+    size = lax.axis_size("pool")
+    groups = [[z * size + p for z in ORDERS[p % 2]] for p in range(size)]
+    return lax.all_to_all(
+        blocks, ("pb", "pool"), split_axis=0, concat_axis=0, tiled=True, axis_index_groups=groups
     )
 
 
@@ -53,7 +67,7 @@
         load.wait()
     stores = []
     for j in range(peers * slots):
-        tile = buffer.at[picks_ref[j % slots, j // slots]]
+        tile = buffer.at[picks_ref[j % slots, member(j // slots)]]
         stores.append(pltpu.make_async_copy(tile, out_ref.at[j], store_sems.at[j]))
         stores[-1].start()
     for store in stores:
@@ -93,6 +107,34 @@
         cost_estimate=CHEAP,
         name="scores",
     )(keys, queries)
+
+
+def local_kernel(keys_ref, queries_ref, picks_ref, out_ref, chosen_ref):
+    out_ref[...] = SHARPNESS * contract(keys_ref[...], queries_ref[...])
+    slots, peers = picks_ref.shape
+    lane = lax.broadcasted_iota(jnp.int32, (1, chosen_ref.shape[1]), 1)
+    wanted = lane % TILE
+    for j in range(peers * slots):
+        pick = picks_ref[j % slots, member(j // slots)]
+        wanted = wanted + jnp.where(lane // TILE == j, pick * TILE, 0)
+    rows = lax.broadcasted_iota(jnp.int32, chosen_ref.shape, 0)
+    chosen_ref[...] = (rows == wanted).astype(jnp.float32).astype(jnp.bfloat16)
+
+
+def local_scores(keys, queries, picks):
+    rows, hard = keys.shape[0], picks.size * TILE
+    return pl.pallas_call(
+        local_kernel,
+        out_shape=(
+            jax.ShapeDtypeStruct((rows, queries.shape[0]), jnp.float32),
+            jax.ShapeDtypeStruct((rows, hard), jnp.bfloat16),
+        ),
+        in_specs=[VMEM, VMEM, SMEM],
+        out_specs=(VMEM, VMEM),
+        compiler_params=PARAMS,
+        cost_estimate=CHEAP,
+        name="local_scores",
+    )(keys, queries, picks)
 
 
 def weights_kernel(
@@ -106,7 +148,7 @@
     slot = lax.broadcasted_iota(jnp.int32, (size, hard.shape[1]), 0) // TILE
     hard = jnp.concatenate(
         [
-            jnp.where(slot < counts_ref[0, i], hard[i * size : (i + 1) * size], -jnp.inf)
+            jnp.where(slot < counts_ref[0, member(i)], hard[i * size : (i + 1) * size], -jnp.inf)
             for i in range(peers)
         ],
         axis=0,
@@ -187,15 +229,15 @@
     )(near, far, queries)
 
 
-def queries_kernel(chunk, weight_refs, picks_ref, hard_ref, key_refs, outs, scratch):
-    out_ref, chosen_ref = outs
-    held, buffer, load_sems, store_sems = scratch
+def queries_kernel(
+    chunk, hard_weight_ref, local_ref, near_ref, far_ref, hard_ref, passages_ref, pool_near_ref,
+    pool_far_ref, out_ref, held, buffer, load_sems, store_sems,
+):
     spans = [pl.ds(i * chunk, chunk) for i in range(out_ref.shape[1] // chunk)]
-    loads, views, start = [], [], 0
-    for k, key in enumerate(key_refs):
+    loads, start = [], 0
+    for k, key in enumerate((passages_ref, pool_near_ref, pool_far_ref)):
         view = held.at[pl.ds(start, key.shape[0])]
         start += key.shape[0]
-        views.append(view)
         loads.append(
             [
                 pltpu.make_async_copy(key.at[:, span], view.at[:, span], load_sems.at[k, i])
@@ -205,21 +247,15 @@
     for i in range(len(spans)):
         for load in loads:
             load[i].start()
-    slots, peers = picks_ref.shape
-    lane = lax.broadcasted_iota(jnp.int32, (1, chosen_ref.shape[1]), 1)
-    wanted = lane % TILE
-    for j in range(peers * slots):
-        pick = picks_ref[j % slots, j // slots]
-        wanted = wanted + jnp.where(lane // TILE == j, pick * TILE, 0)
-    rows = lax.broadcasted_iota(jnp.int32, chosen_ref.shape, 0)
-    chosen_ref[...] = (rows == wanted).astype(jnp.float32).astype(jnp.bfloat16)
-    hard_weight, weight = weight_refs[0][...], [ref[...] for ref in weight_refs[1:]]
+    turned = lambda x: x.astype(jnp.float32).T.astype(jnp.bfloat16)
+    hard_weight = turned(hard_weight_ref[...])
+    weight = turned(jnp.concatenate([local_ref[...], near_ref[...], far_ref[...]], axis=0))
     stores = []
     for i, span in enumerate(spans):
-        part = transposed(hard_weight, hard_ref[:, span])
-        for k, view in enumerate(views):
-            loads[k][i].wait()
-            part = part + transposed(weight[k], view[:, span])
+        part = jnp.dot(hard_weight, hard_ref[:, span], preferred_element_type=jnp.float32)
+        for load in loads:
+            load[i].wait()
+        part = part + jnp.dot(weight, held[:, span], preferred_element_type=jnp.float32)
         buffer[:, span] = (SHARPNESS * part).astype(jnp.bfloat16)
         store = pltpu.make_async_copy(buffer.at[:, span], out_ref.at[:, span], store_sems.at[i])
         store.start()
@@ -228,37 +264,24 @@
         store.wait()
 
 
-def query_gradient(hard_weight, weight, picks, hard_rows, keys, chunk=1024):
-    (hard, rows), width = hard_weight.shape, hard_rows.shape[1]
-    held = sum(key.shape[0] for key in keys)
-    count = len(keys)
-
-    def kernel(*refs):
-        inputs, outs, scratch = refs[: 3 + 2 * count], refs[3 + 2 * count : 5 + 2 * count], refs[5 + 2 * count :]
-        queries_kernel(
-            chunk, inputs[: 1 + count], inputs[1 + count], inputs[2 + count],
-            inputs[3 + count :], outs, scratch,
-        )
-
-    return pl.pallas_call(
-        kernel,
-        out_shape=(
-            pltpu.HBM((rows, width), jnp.bfloat16),
-            jax.ShapeDtypeStruct((rows, hard), jnp.bfloat16),
-        ),
-        in_specs=[VMEM] * (1 + count) + [SMEM, VMEM] + [HBM] * count,
-        out_specs=(HBM, VMEM),
+def query_gradient(hard_weight, weight, hard_rows, keys, chunk=1024):
+    rows, width = hard_weight.shape[1], hard_rows.shape[1]
+    return pl.pallas_call(
+        functools.partial(queries_kernel, chunk),
+        out_shape=pltpu.HBM((rows, width), jnp.bfloat16),
+        in_specs=[VMEM] * 5 + [HBM] * 3,
+        out_specs=HBM,
         scratch_shapes=[
-            pltpu.VMEM((held, width), jnp.bfloat16),
+            pltpu.VMEM((sum(key.shape[0] for key in keys), width), jnp.bfloat16),
             pltpu.VMEM((rows, width), jnp.bfloat16),
-            pltpu.SemaphoreType.DMA((count, width // chunk)),
+            pltpu.SemaphoreType.DMA((len(keys), width // chunk)),
             pltpu.SemaphoreType.DMA((width // chunk,)),
         ],
         compiler_params=PARAMS,
         cost_estimate=CHEAP,
         name="query_gradient",
     )(
-        hard_weight, *weight, picks, hard_rows,
+        hard_weight, *weight, hard_rows,
         *[pltpu.with_memory_space_constraint(key, pltpu.HBM) for key in keys],
     )
 
@@ -316,9 +339,7 @@
     peers, slots = picks.shape
     hard = peers * slots * TILE
     outgoing = gather_tiles(picks.T, passages.reshape(rows // TILE, TILE, width))
-    hard_rows = lax.all_to_all(
-        outgoing.reshape(peers, slots * TILE, width), "pb", split_axis=0, concat_axis=0, tiled=True
-    ).reshape(hard, width)
+    hard_rows = trade(outgoing.reshape(peers, slots * TILE, width)).reshape(hard, width)
     pooled = pool_passages
     for step, count in digits[:-1]:
         pooled = jnp.concatenate(
@@ -326,13 +347,12 @@
         )
     near = pooled
     far = shifts(near, (digits[-1] + (1,),), -1)
+    local, chosen = local_scores(passages, queries, picks.T)
     grad_hard, local_weight, near_weight, far_weight, hard_weight = weights(
-        queries, hard_rows, scores(passages, queries), scores(near, queries), scores(far, queries),
+        queries, hard_rows, local, scores(near, queries), scores(far, queries),
         tile_count[0], positives[None, :],
     )
-    returned = lax.all_to_all(
-        grad_hard.reshape(peers, slots * TILE, width), "pb", split_axis=0, concat_axis=0, tiled=True
-    ).reshape(hard, width)
+    returned = trade(grad_hard.reshape(peers, slots * TILE, width)).reshape(hard, width)
     *y_digits, (x_step, x_count), (core_step, core_count) = digits
     size = pooled.shape[0] // x_count
     term, *sent = pool_terms(near_weight, far_weight, queries, size, jnp.bfloat16)
@@ -347,9 +367,8 @@
         for m in range(1, count):
             term = term + shifts(pieces[m], ((step, count, m),), 1)
     grad_pool = term.astype(jnp.bfloat16)
-    grad_queries, chosen = query_gradient(
-        hard_weight, (local_weight, near_weight, far_weight), picks.T, hard_rows,
-        (passages, near, far),
+    grad_queries = query_gradient(
+        hard_weight, (local_weight, near_weight, far_weight), hard_rows, (passages, near, far)
     )
     grad_passages = passage_gradient(local_weight, queries, chosen, returned)
     return (grad_queries, grad_passages, grad_pool)

time: 149 us -> 149 us (level)
  starting transfers between devices: 88.9 us -> 93.4 us
  waiting for transfers between devices: 35 us -> 30.6 us
    all_to_all x2, waiting for transfers between devices: 11.8 us -> 7.1 us  [trade(): lax.all_to_all(blocks, ('pb', 'pool'), split_axis=0, concat_axis=0, tiled...]
    ppermute x19, starting transfers between devices: 69.2 us -> 72 us  [shifts(): lax.ppermute(block, 'pool', [(j, moved(j)) for j in range(lax.axis_size('...]
    all_to_all x2, starting transfers between devices: 19.7 us -> 21.4 us  [trade(): lax.all_to_all(blocks, ('pb', 'pool'), split_axis=0, concat_axis=0, tiled...]
    pallas_call x1 -> x2, Pallas kernels: 4.34 us -> 4.23 us  [the longest x1 3.25 us: query_gradient(): pl.pallas_call(functools.partial(queries_kernel, chunk), out_shape=pltpu....]
    unnamed x20 -> x22, local copies, waits for them, and re-layouts: 3.37 us -> 3.39 us
  transfers between devices with their start and end apart: 21 -> 21, of which waited for: 8 -> 10; matrix products, arithmetic and copies ran while one was open for 2% -> 3% of each run, Pallas kernels for 4% -> 4%
where the time goes in v6:
time: 149 us; the launch traced here: 147 us
  starting transfers between devices  93.4 us (63%)
  waiting for transfers between devices  30.6 us (21%)
  Pallas kernels  15 us (10%)
  local copies, waits for them, and re-layouts  6.38 us (4%)
    ppermute x19, starting transfers between devices, shifts(): lax.ppermute(block, 'pool', [(j, moved(j)) for j in range(lax.axis_size('...  72 us
    ppermute x19, waiting for transfers between devices, shifts(): lax.ppermute(block, 'pool', [(j, moved(j)) for j in range(lax.axis_size('...  23.5 us
    all_to_all x2, starting transfers between devices, trade(): lax.all_to_all(blocks, ('pb', 'pool'), split_axis=0, concat_axis=0, tiled...  21.4 us
    all_to_all x2, waiting for transfers between devices, trade(): lax.all_to_all(blocks, ('pb', 'pool'), split_axis=0, concat_axis=0, tiled...  7.1 us
    unnamed x22, local copies, waits for them, and re-layouts  3.39 us
    pallas_call x1, Pallas kernels, weights(): pl.pallas_call(functools.partial(weights_kernel, chunk), out_shape=(pltpu...  3.31 us
    pallas_call x1, Pallas kernels, query_gradient(): pl.pallas_call(functools.partial(queries_kernel, chunk), out_shape=pltpu....  3.25 us
    pallas_call x1, Pallas kernels, gather_tiles(): pl.pallas_call(functools.partial(gather_kernel, parts), out_shape=pltpu.H...  3.17 us
  transfers between devices with their start and end apart: 21, of which 10 were waited for; matrix products, arithmetic and copies ran while one was open for 3% of the time, Pallas kernels for 4%

profile of v6, /device:TPU:6, one launch (start us, length us, event | category | flops | bytes accessed | tf_op | source)
XLA Modules:
  0.0 147.3 jit_solution(18284522874839170651)
XLA Ops:
  0.6 0.0 copy-start.4
  0.6 0.7 copy-done.4
  1.3 3.2 %gather_tiles.1 = bf16[24,8,4096]{2,1,0:T(8,128)(2,1)} custom-call(s32[2,12]{1,0:T(2,128)S(1)} %bitcast.13, bf16[16,8,4096]{2,1,0:T(8,128)(2,1)} %bitcast.12), custom_call_target="tpu_custom_call" | custom-call | bytes 3145728 | tf_op jit(solution)/shard_map/gather_tiles/pallas_call | solution.py:80
  4.5 0.0 copy-start.8
  4.5 0.0 copy-start
  4.5 0.0 copy-start.5
  4.5 15.3 %all-to-all-start = ((bf16[12,16,4096]{2,1,0:T(8,128)(2,1)}), bf16[12,16,4096]{2,1,0:T(8,128)(2,1)S(1)}, u32[]{:S(2)}, u32[]{:S(2)}) async-start(bf16[12,16,4096]{2,1,0:T(8,128)(2,1)} %bitcast.17), calls=%async_computation | async-start | bytes 3145728 | tf_op jit(solution)/shard_map/all_to_all | solution.py:43
  19.8 3.5 %collective-permute-start.2 = (bf16[2,4096]{1,0:T(2,128)(2,1)S(1)}, bf16[2,4096]{1,0:T(2,128)(2,1)S(1)}, u32[]{:S(2)}, u32[]{:S(2)}) collective-permute-start(bf16[2,4096]{1,0:T(2,128)(2,1)S(1)} %copy-done.8), channel_id=1, source_target_pairs={{0,8},{1,9},{2,10},{3,11},{4,12},{5,13},{6,14},{7,15},{8,16},{9,17... | collective-permute-start | bytes 49160 | tf_op jit(solution)/shard_map/ppermute | solution.py:55
  23.3 4.5 %collective-permute-start.1 = (bf16[2,4096]{1,0:T(2,128)(2,1)S(1)}, bf16[2,4096]{1,0:T(2,128)(2,1)S(1)}, u32[]{:S(2)}, u32[]{:S(2)}) collective-permute-start(bf16[2,4096]{1,0:T(2,128)(2,1)S(1)} %copy-done.8), channel_id=1, source_target_pairs={{0,16},{1,17},{2,18},{3,19},{4,20},{5,21},{6,22},{7,23},{8,24},{9,... | collective-permute-start | bytes 49160 | tf_op jit(solution)/shard_map/ppermute | solution.py:55
  27.8 3.3 %collective-permute-start = (bf16[2,4096]{1,0:T(2,128)(2,1)S(1)}, bf16[2,4096]{1,0:T(2,128)(2,1)S(1)}, u32[]{:S(2)}, u32[]{:S(2)}) collective-permute-start(bf16[2,4096]{1,0:T(2,128)(2,1)S(1)} %copy-done.8), channel_id=1, source_target_pairs={{0,24},{1,25},{2,26},{3,27},{4,28},{5,29},{6,30},{7,31},{8,0},{9,1... | collective-permute-start | bytes 49160 | tf_op jit(solution)/shard_map/ppermute | solution.py:55
  31.1 0.0 collective-permute-done.2
  31.1 0.0 collective-permute-done.1
  31.1 2.3 %collective-permute-done = bf16[2,4096]{1,0:T(2,128)(2,1)S(1)} collective-permute-done((bf16[2,4096]{1,0:T(2,128)(2,1)S(1)}, bf16[2,4096]{1,0:T(2,128)(2,1)S(1)}, u32[]{:S(2)}, u32[]{:S(2)}) %collective-permute-start) | collective-permute-done | bytes 16416 | tf_op jit(solution)/shard_map/ppermute | solution.py:55
  33.5 0.1 pad_maximum_fusion
  33.6 5.9 %collective-permute-start.3 = (bf16[8,4096]{1,0:T(8,128)(2,1)S(1)}, bf16[8,4096]{1,0:T(8,128)(2,1)S(1)}, u32[]{:S(2)}, u32[]{:S(2)}) collective-permute-start(bf16[8,4096]{1,0:T(8,128)(2,1)S(1)} %pad_maximum_fusion), channel_id=1, source_target_pairs={{0,32},{1,33},{2,34},{3,35},{4,36},{5,37},{6,38},{7,39},{8,40},{9,... | collective-permute-start | bytes 196616 | tf_op jit(solution)/shard_map/ppermute | solution.py:55
  39.5 4.2 %collective-permute-done.3 = bf16[8,4096]{1,0:T(8,128)(2,1)S(1)} collective-permute-done((bf16[8,4096]{1,0:T(8,128)(2,1)S(1)}, bf16[8,4096]{1,0:T(8,128)(2,1)S(1)}, u32[]{:S(2)}, u32[]{:S(2)}) %collective-permute-start.3) | collective-permute-done | bytes 65568 | tf_op jit(solution)/shard_map/ppermute | solution.py:55
  43.7 0.1 concatenate.12
  43.8 2.4 %collective-permute-start.6 = (bf16[16,4096]{1,0:T(8,128)(2,1)S(1)}, bf16[16,4096]{1,0:T(8,128)(2,1)S(1)}, u32[]{:S(2)}, u32[]{:S(2)}) collective-permute-start(bf16[16,4096]{1,0:T(8,128)(2,1)S(1)} %concatenate.12), channel_id=1, source_target_pairs={{0,2},{1,3},{2,4},{3,5},{4,6},{5,7},{6,0},{7,1},{8,10},{9,11},{10,... | collective-permute-start | bytes 393224 | tf_op jit(solution)/shard_map/ppermute | solution.py:55
  46.2 4.3 %collective-permute-start.5 = (bf16[16,4096]{1,0:T(8,128)(2,1)S(1)}, bf16[16,4096]{1,0:T(8,128)(2,1)S(1)}, u32[]{:S(2)}, u32[]{:S(2)}) collective-permute-start(bf16[16,4096]{1,0:T(8,128)(2,1)S(1)} %concatenate.12), channel_id=1, source_target_pairs={{0,4},{1,5},{2,6},{3,7},{4,0},{5,1},{6,2},{7,3},{8,12},{9,13},{10,... | collective-permute-start | bytes 393224 | tf_op jit(solution)/shard_map/ppermute | solution.py:55
  50.6 1.9 %collective-permute-start.4 = (bf16[16,4096]{1,0:T(8,128)(2,1)S(1)}, bf16[16,4096]{1,0:T(8,128)(2,1)}, u32[]{:S(2)}, u32[]{:S(2)}) collective-permute-start(bf16[16,4096]{1,0:T(8,128)(2,1)S(1)} %concatenate.12), channel_id=1, source_target_pairs={{0,6},{1,7},{2,0},{3,1},{4,2},{5,3},{6,4},{7,5},{8,14},{9,15},{10,... | collective-permute-start | bytes 393224 | tf_op jit(solution)/shard_map/ppermute | solution.py:55
  52.5 0.0 collective-permute-done.6
  52.5 0.0 copy-start.9
  52.5 2.1 %collective-permute-done.5 = bf16[16,4096]{1,0:T(8,128)(2,1)S(1)} collective-permute-done((bf16[16,4096]{1,0:T(8,128)(2,1)S(1)}, bf16[16,4096]{1,0:T(8,128)(2,1)S(1)}, u32[]{:S(2)}, u32[]{:S(2)}) %collective-permute-start.5) | collective-permute-done | bytes 131104 | tf_op jit(solution)/shard_map/ppermute | solution.py:55
  54.6 0.7 copy-done.10
  55.2 3.7 %collective-permute-done.4 = bf16[16,4096]{1,0:T(8,128)(2,1)} collective-permute-done((bf16[16,4096]{1,0:T(8,128)(2,1)S(1)}, bf16[16,4096]{1,0:T(8,128)(2,1)}, u32[]{:S(2)}, u32[]{:S(2)}) %collective-permute-start.4) | collective-permute-done | bytes 131104 | tf_op jit(solution)/shard_map/ppermute | solution.py:55
  59.0 2.8 %concatenate.13.keys_ref.pool_near_ref = bf16[64,4096]{1,0:T(8,128)(2,1)S(1)} concatenate(bf16[2,4096]{1,0:T(2,128)(2,1)S(1)} %copy-done.8, bf16[2,4096]{1,0:T(2,128)(2,1)S(1)} %collective-permute-done, bf16[2,4096]{1,0:T(2,128)(2,1)S(1)} %collective-permute-done.1, bf16[2,4096]{1,0:T(2,128)(2,1)S(1)} %collective-permute-done.2, bf16[8,4096]{1,0:T(8,128)(2,1)S(1)} %collective-permute-done.3, ...), dimensions={0} | concatenate | bytes 1048576 | tf_op jit(solution)/shard_map/concatenate | solution.py:345
  61.8 0.0 copy-start.2
  61.8 3.1 %collective-permute-start.7 = (bf16[64,4096]{1,0:T(8,128)(2,1)S(1)}, bf16[64,4096]{1,0:T(8,128)(2,1)S(1)}, u32[]{:S(2)}, u32[]{:S(2)}) collective-permute-start(bf16[64,4096]{1,0:T(8,128)(2,1)S(1)} %concatenate.13.keys_ref.pool_near_ref), channel_id=1, source_target_pairs={{0,1},{1,0},{2,3},{3,2},{4,5},{5,4},{6,7},{7,6},{8,9},{9,8},{10,11... | collective-permute-start | bytes 1572872 | tf_op jit(solution)/shard_map/ppermute | solution.py:55
  64.9 0.0 copy-start.1
  65.0 1.2 copy-done.1
  66.2 1.0 local_scores.1
  67.2 0.0 copy-start.6
  67.2 0.0 copy-start.7
  67.2 0.5 scores.2.near_ref
  67.7 0.5 scores.3.far_ref
  68.2 0.8 copy-done.3
  69.0 7.1 %all-to-all-done = bf16[12,16,4096]{2,1,0:T(8,128)(2,1)S(1)} async-done(((bf16[12,16,4096]{2,1,0:T(8,128)(2,1)}), bf16[12,16,4096]{2,1,0:T(8,128)(2,1)S(1)}, u32[]{:S(2)}, u32[]{:S(2)}) %all-to-all-start) | async-done | bytes 1572896 | tf_op jit(solution)/shard_map/all_to_all | solution.py:43
  76.1 3.3 %weights.1 = (bf16[192,4096]{1,0:T(8,128)(2,1)}, bf16[128,128]{1,0:T(8,128)(2,1)S(1)}, bf16[64,128]{1,0:T(8,128)(2,1)S(1)}, bf16[64,128]{1,0:T(8,128)(2,1)S(1)}, bf16[192,128]{1,0:T(8,128)(2,1)S(1)}) custom-call(bf16[128,4096]{1,0:T(8,128)(2,1)S(1)} %copy-done, bf16[192,4096]{1,0:T(8,128)(2,1)S(1)} %bitcast.10, f32[128,128]{1,0:T(8,128)S(1)} %get-tuple-element.18.local_ref, ...), custom_call_target="tpu_custom_call" | custom-call | flops 1048576 | bytes 1048576 | tf_op jit(solution)/shard_map/weights/pallas_call | solution.py:184
  79.4 6.1 %all-to-all-start.1 = ((bf16[12,16,4096]{2,1,0:T(8,128)(2,1)}), bf16[12,16,4096]{2,1,0:T(8,128)(2,1)}, u32[]{:S(2)}, u32[]{:S(2)}) async-start(bf16[12,16,4096]{2,1,0:T(8,128)(2,1)} %bitcast.18), calls=%async_computation.1 | async-start | bytes 3145728 | tf_op jit(solution)/shard_map/all_to_all | solution.py:43
  85.5 0.4 pool_terms.1
  85.9 2.4 %collective-permute-start.8 = (bf16[16,4096]{1,0:T(8,128)(2,1)S(1)}, bf16[16,4096]{1,0:T(8,128)(2,1)S(1)}, u32[]{:S(2)}, u32[]{:S(2)}) collective-permute-start(bf16[16,4096]{1,0:T(8,128)(2,1)S(1)} %get-tuple-element.26), channel_id=1, source_target_pairs={{0,2},{1,3},{2,4},{3,5},{4,6},{5,7},{6,0},{7,1},{8,10},{9,11},{10,... | collective-permute-start | bytes 393224 | tf_op jit(solution)/shard_map/ppermute | solution.py:55
  88.3 4.3 %collective-permute-start.9 = (bf16[16,4096]{1,0:T(8,128)(2,1)S(1)}, bf16[16,4096]{1,0:T(8,128)(2,1)S(1)}, u32[]{:S(2)}, u32[]{:S(2)}) collective-permute-start(bf16[16,4096]{1,0:T(8,128)(2,1)S(1)} %get-tuple-element.27), channel_id=1, source_target_pairs={{0,4},{1,5},{2,6},{3,7},{4,0},{5,1},{6,2},{7,3},{8,12},{9,13},{10,... | collective-permute-start | bytes 393224 | tf_op jit(solution)/shard_map/ppermute | solution.py:55
  92.7 1.9 %collective-permute-start.10 = (bf16[16,4096]{1,0:T(8,128)(2,1)S(1)}, bf16[16,4096]{1,0:T(8,128)(2,1)S(1)}, u32[]{:S(2)}, u32[]{:S(2)}) collective-permute-start(bf16[16,4096]{1,0:T(8,128)(2,1)S(1)} %get-tuple-element.28), channel_id=1, source_target_pairs={{0,6},{1,7},{2,0},{3,1},{4,2},{5,3},{6,4},{7,5},{8,14},{9,15},{10,... | collective-permute-start | bytes 393224 | tf_op jit(solution)/shard_map/ppermute | solution.py:55
  94.6 4.4 %collective-permute-start.11 = (bf16[16,4096]{1,0:T(8,128)(2,1)S(1)}, bf16[16,4096]{1,0:T(8,128)(2,1)S(1)}, u32[]{:S(2)}, u32[]{:S(2)}) collective-permute-start(bf16[16,4096]{1,0:T(8,128)(2,1)S(1)} %get-tuple-element.29), channel_id=1, source_target_pairs={{0,1},{1,0},{2,3},{3,2},{4,5},{5,4},{6,7},{7,6},{8,9},{9,8},{10,11... | collective-permute-start | bytes 393224 | tf_op jit(solution)/shard_map/ppermute | solution.py:55
  98.9 4.5 %collective-permute-start.12 = (bf16[16,4096]{1,0:T(8,128)(2,1)S(1)}, bf16[16,4096]{1,0:T(8,128)(2,1)S(1)}, u32[]{:S(2)}, u32[]{:S(2)}) collective-permute-start(bf16[16,4096]{1,0:T(8,128)(2,1)S(1)} %get-tuple-element.30), channel_id=1, source_target_pairs={{0,3},{1,2},{2,5},{3,4},{4,7},{5,6},{6,1},{7,0},{8,11},{9,10},{10,... | collective-permute-start | bytes 393224 | tf_op jit(solution)/shard_map/ppermute | solution.py:55
  103.4 0.0 collective-permute-done.8
  103.4 1.9 %collective-permute-start.13 = (bf16[16,4096]{1,0:T(8,128)(2,1)S(1)}, bf16[16,4096]{1,0:T(8,128)(2,1)S(1)}, u32[]{:S(2)}, u32[]{:S(2)}) collective-permute-start(bf16[16,4096]{1,0:T(8,128)(2,1)S(1)} %get-tuple-element.31), channel_id=1, source_target_pairs={{0,5},{1,4},{2,7},{3,6},{4,1},{5,0},{6,3},{7,2},{8,13},{9,12},{10,... | collective-permute-start | bytes 393224 | tf_op jit(solution)/shard_map/ppermute | solution.py:55
  105.4 0.0 collective-permute-done.9
  105.4 3.0 %collective-permute-start.14 = (bf16[16,4096]{1,0:T(8,128)(2,1)S(1)}, bf16[16,4096]{1,0:T(8,128)(2,1)S(1)}, u32[]{:S(2)}, u32[]{:S(2)}) collective-permute-start(bf16[16,4096]{1,0:T(8,128)(2,1)S(1)} %get-tuple-element.32), channel_id=1, source_target_pairs={{0,7},{1,6},{2,1},{3,0},{4,3},{5,2},{6,5},{7,4},{8,15},{9,14},{10,... | collective-permute-start | bytes 393224 | tf_op jit(solution)/shard_map/ppermute | solution.py:55
  108.5 1.5 %collective-permute-done.12 = bf16[16,4096]{1,0:T(8,128)(2,1)S(1)} collective-permute-done((bf16[16,4096]{1,0:T(8,128)(2,1)S(1)}, bf16[16,4096]{1,0:T(8,128)(2,1)S(1)}, u32[]{:S(2)}, u32[]{:S(2)}) %collective-permute-start.12) | collective-permute-done | bytes 131104 | tf_op jit(solution)/shard_map/ppermute | solution.py:55
  109.9 2.1 %collective-permute-done.13 = bf16[16,4096]{1,0:T(8,128)(2,1)S(1)} collective-permute-done((bf16[16,4096]{1,0:T(8,128)(2,1)S(1)}, bf16[16,4096]{1,0:T(8,128)(2,1)S(1)}, u32[]{:S(2)}, u32[]{:S(2)}) %collective-permute-start.13) | collective-permute-done | bytes 131104 | tf_op jit(solution)/shard_map/ppermute | solution.py:55
  112.0 3.3 %collective-permute-done.14 = bf16[16,4096]{1,0:T(8,128)(2,1)S(1)} collective-permute-done((bf16[16,4096]{1,0:T(8,128)(2,1)S(1)}, bf16[16,4096]{1,0:T(8,128)(2,1)S(1)}, u32[]{:S(2)}, u32[]{:S(2)}) %collective-permute-start.14) | collective-permute-done | bytes 131104 | tf_op jit(solution)/shard_map/ppermute | solution.py:55
  115.4 0.1 convert_add_fusion
  115.5 7.7 %collective-permute-start.15 = (f32[8,4096]{1,0:T(8,128)S(1)}, f32[8,4096]{1,0:T(8,128)S(1)}, u32[]{:S(2)}, u32[]{:S(2)}) collective-permute-start(f32[8,4096]{1,0:T(8,128)S(1)} %slice.25), channel_id=1, source_target_pairs={{0,32},{1,33},{2,34},{3,35},{4,36},{5,37},{6,38},{7,39},{8,40},{9,... | collective-permute-start | bytes 393224 | tf_op jit(solution)/shard_map/ppermute | solution.py:55
  123.2 4.1 %collective-permute-done.15 = f32[8,4096]{1,0:T(8,128)S(1)} collective-permute-done((f32[8,4096]{1,0:T(8,128)S(1)}, f32[8,4096]{1,0:T(8,128)S(1)}, u32[]{:S(2)}, u32[]{:S(2)}) %collective-permute-start.15) | collective-permute-done | bytes 131104 | tf_op jit(solution)/shard_map/ppermute | solution.py:55
  127.4 5.9 %collective-permute-start.16 = (f32[2,4096]{1,0:T(2,128)S(1)}, f32[2,4096]{1,0:T(2,128)S(1)}, u32[]{:S(2)}, u32[]{:S(2)}) collective-permute-start(f32[2,4096]{1,0:T(2,128)S(1)} %get-tuple-element.33), channel_id=1, source_target_pairs={{0,8},{1,9},{2,10},{3,11},{4,12},{5,13},{6,14},{7,15},{8,16},{9,17... | collective-permute-start | bytes 98312 | tf_op jit(solution)/shard_map/ppermute | solution.py:55
  133.2 3.8 %collective-permute-start.18 = (f32[2,4096]{1,0:T(2,128)S(1)}, f32[2,4096]{1,0:T(2,128)S(1)}, u32[]{:S(2)}, u32[]{:S(2)}) collective-permute-start(f32[2,4096]{1,0:T(2,128)S(1)} %get-tuple-element.34), channel_id=1, source_target_pairs={{0,24},{1,25},{2,26},{3,27},{4,28},{5,29},{6,30},{7,31},{8,0},{9,1... | collective-permute-start | bytes 98312 | tf_op jit(solution)/shard_map/ppermute | solution.py:55
  137.0 3.3 %collective-permute-start.17 = (f32[2,4096]{1,0:T(2,128)S(1)}, f32[2,4096]{1,0:T(2,128)S(1)}, u32[]{:S(2)}, u32[]{:S(2)}) collective-permute-start(f32[2,4096]{1,0:T(2,128)S(1)} %get-tuple-element.35), channel_id=1, source_target_pairs={{0,16},{1,17},{2,18},{3,19},{4,20},{5,21},{6,22},{7,23},{8,24},{9,... | collective-permute-start | bytes 98312 | tf_op jit(solution)/shard_map/ppermute | solution.py:55
  140.3 3.2 %query_gradient.1 = bf16[128,4096]{1,0:T(8,128)(2,1)} custom-call(bf16[192,128]{1,0:T(8,128)(2,1)S(1)} %get-tuple-element.19.hard_weight_ref, bf16[128,128]{1,0:T(8,128)(2,1)S(1)} %get-tuple-element.20.local_ref.weight_ref, bf16[64,128]{1,0:T(8,128)(2,1)S(1)} %get-tuple-element.21.near_ref, bf16[64,128]{1,0:T(8,128)(2,1)S(1)} %get-tuple-element.22.far_ref, ...), custom_call_target="tpu_custom_call" | custom-call | flops 1048576 | bytes 1048576 | tf_op jit(solution)/shard_map/query_gradient/pallas_call | solution.py:269
  143.6 0.0 collective-permute-done.18
  143.6 0.2 collective-permute-done.17
  143.7 0.6 fusion.2
  144.4 0.0 all-to-all-done.1
  144.4 2.9 %passage_gradient.1 = bf16[128,4096]{1,0:T(8,128)(2,1)} custom-call(bf16[128,128]{1,0:T(8,128)(2,1)S(1)} %get-tuple-element.20.local_ref.weight_ref, bf16[128,4096]{1,0:T(8,128)(2,1)S(1)} %copy-done, bf16[128,192]{1,0:T(8,128)(2,1)S(1)} %get-tuple-element.23.chosen_ref, bf16[192,4096]{1,0:T(8,128)(2,1)} %bitcast.9.returned_ref), custom_call_target="tpu_custom_call" | custom-call | flops 1048576 | bytes 1048576 | tf_op jit(solution)/shard_map/passage_gradient/pallas_call | solution.py:319
  (16 shorter events, 0.1 us)
Async XLA Ops:
  0.6 0.7 copy-start.4
  4.5 15.3 %copy-start.8 = (bf16[2,4096]{1,0:T(2,128)(2,1)S(1)}, bf16[2,4096]{1,0:T(2,128)(2,1)}, u32[]{:S(2)}) copy-start(bf16[2,4096]{1,0:T(2,128)(2,1)} %param.8) | copy-start | bytes 49156
  4.5 60.4 %copy-start = (bf16[128,4096]{1,0:T(8,128)(2,1)S(1)}, bf16[128,4096]{1,0:T(8,128)(2,1)}, u32[]{:S(2)}) copy-start(bf16[128,4096]{1,0:T(8,128)(2,1)} %queries_ref.11) | copy-start | bytes 3145732
  4.5 60.4 %copy-start.5 = (s32[1,1,12,2]{2,3,1,0:T(2,128)S(1)}, s32[1,1,12,2]{2,3,1,0:T(2,128)}, u32[]{:S(2)}) copy-start(s32[1,1,12,2]{2,3,1,0:T(2,128)} %param.10) | copy-start | bytes 292
  4.5 71.5 %all-to-all-start = ((bf16[12,16,4096]{2,1,0:T(8,128)(2,1)}), bf16[12,16,4096]{2,1,0:T(8,128)(2,1)S(1)}, u32[]{:S(2)}, u32[]{:S(2)}) async-start(bf16[12,16,4096]{2,1,0:T(8,128)(2,1)} %bitcast.17), calls=%async_computation | async-start | bytes 3145728 | tf_op jit(solution)/shard_map/all_to_all | solution.py:43
  19.8 11.3 %collective-permute-start.2 = (bf16[2,4096]{1,0:T(2,128)(2,1)S(1)}, bf16[2,4096]{1,0:T(2,128)(2,1)S(1)}, u32[]{:S(2)}, u32[]{:S(2)}) collective-permute-start(bf16[2,4096]{1,0:T(2,128)(2,1)S(1)} %copy-done.8), channel_id=1, source_target_pairs={{0,8},{1,9},{2,10},{3,11},{4,12},{5,13},{6,14},{7,15},{8,16},{9,17... | collective-permute-start | bytes 49160 | tf_op jit(solution)/shard_map/ppermute | solution.py:55
  23.3 7.8 %collective-permute-start.1 = (bf16[2,4096]{1,0:T(2,128)(2,1)S(1)}, bf16[2,4096]{1,0:T(2,128)(2,1)S(1)}, u32[]{:S(2)}, u32[]{:S(2)}) collective-permute-start(bf16[2,4096]{1,0:T(2,128)(2,1)S(1)} %copy-done.8), channel_id=1, source_target_pairs={{0,16},{1,17},{2,18},{3,19},{4,20},{5,21},{6,22},{7,23},{8,24},{9,... | collective-permute-start | bytes 49160 | tf_op jit(solution)/shard_map/ppermute | solution.py:55
  27.8 5.6 %collective-permute-start = (bf16[2,4096]{1,0:T(2,128)(2,1)S(1)}, bf16[2,4096]{1,0:T(2,128)(2,1)S(1)}, u32[]{:S(2)}, u32[]{:S(2)}) collective-permute-start(bf16[2,4096]{1,0:T(2,128)(2,1)S(1)} %copy-done.8), channel_id=1, source_target_pairs={{0,24},{1,25},{2,26},{3,27},{4,28},{5,29},{6,30},{7,31},{8,0},{9,1... | collective-permute-start | bytes 49160 | tf_op jit(solution)/shard_map/ppermute | solution.py:55
  33.6 10.2 %collective-permute-start.3 = (bf16[8,4096]{1,0:T(8,128)(2,1)S(1)}, bf16[8,4096]{1,0:T(8,128)(2,1)S(1)}, u32[]{:S(2)}, u32[]{:S(2)}) collective-permute-start(bf16[8,4096]{1,0:T(8,128)(2,1)S(1)} %pad_maximum_fusion), channel_id=1, source_target_pairs={{0,32},{1,33},{2,34},{3,35},{4,36},{5,37},{6,38},{7,39},{8,40},{9,... | collective-permute-start | bytes 196616 | tf_op jit(solution)/shard_map/ppermute | solution.py:55
  43.8 8.7 %collective-permute-start.6 = (bf16[16,4096]{1,0:T(8,128)(2,1)S(1)}, bf16[16,4096]{1,0:T(8,128)(2,1)S(1)}, u32[]{:S(2)}, u32[]{:S(2)}) collective-permute-start(bf16[16,4096]{1,0:T(8,128)(2,1)S(1)} %concatenate.12), channel_id=1, source_target_pairs={{0,2},{1,3},{2,4},{3,5},{4,6},{5,7},{6,0},{7,1},{8,10},{9,11},{10,... | collective-permute-start | bytes 393224 | tf_op jit(solution)/shard_map/ppermute | solution.py:55
  46.2 8.4 %collective-permute-start.5 = (bf16[16,4096]{1,0:T(8,128)(2,1)S(1)}, bf16[16,4096]{1,0:T(8,128)(2,1)S(1)}, u32[]{:S(2)}, u32[]{:S(2)}) collective-permute-start(bf16[16,4096]{1,0:T(8,128)(2,1)S(1)} %concatenate.12), channel_id=1, source_target_pairs={{0,4},{1,5},{2,6},{3,7},{4,0},{5,1},{6,2},{7,3},{8,12},{9,13},{10,... | collective-permute-start | bytes 393224 | tf_op jit(solution)/shard_map/ppermute | solution.py:55
  50.6 8.4 %collective-permute-start.4 = (bf16[16,4096]{1,0:T(8,128)(2,1)S(1)}, bf16[16,4096]{1,0:T(8,128)(2,1)}, u32[]{:S(2)}, u32[]{:S(2)}) collective-permute-start(bf16[16,4096]{1,0:T(8,128)(2,1)S(1)} %concatenate.12), channel_id=1, source_target_pairs={{0,6},{1,7},{2,0},{3,1},{4,2},{5,3},{6,4},{7,5},{8,14},{9,15},{10,... | collective-permute-start | bytes 393224 | tf_op jit(solution)/shard_map/ppermute | solution.py:55
  52.5 2.1 %copy-start.9 = (bf16[16,4096]{1,0:T(8,128)(2,1)}, bf16[16,4096]{1,0:T(8,128)(2,1)S(1)}, u32[]{:S(2)}) copy-start(bf16[16,4096]{1,0:T(8,128)(2,1)S(1)} %collective-permute-done.6) | copy-start | bytes 393220
  54.6 0.7 copy-start.10
  61.8 5.8 %copy-start.2 = (bf16[64,4096]{1,0:T(8,128)(2,1)}, bf16[64,4096]{1,0:T(8,128)(2,1)S(1)}, u32[]{:S(2)}) copy-start(bf16[64,4096]{1,0:T(8,128)(2,1)S(1)} %concatenate.13.keys_ref.pool_near_ref) | copy-start | bytes 1572868
  61.8 5.8 %collective-permute-start.7 = (bf16[64,4096]{1,0:T(8,128)(2,1)S(1)}, bf16[64,4096]{1,0:T(8,128)(2,1)S(1)}, u32[]{:S(2)}, u32[]{:S(2)}) collective-permute-start(bf16[64,4096]{1,0:T(8,128)(2,1)S(1)} %concatenate.13.keys_ref.pool_near_ref), channel_id=1, source_target_pairs={{0,1},{1,0},{2,3},{3,2},{4,5},{5,4},{6,7},{7,6},{8,9},{9,8},{10,11... | collective-permute-start | bytes 1572872 | tf_op jit(solution)/shard_map/ppermute | solution.py:55
  64.9 1.2 copy-start.1
  67.2 8.9 %copy-start.6 = (s32[1,1,12]{2,1,0:T(1,128)S(1)}, s32[1,1,12]{2,1,0:T(1,128)}, u32[]{:S(2)}) copy-start(s32[1,1,12]{2,1,0:T(1,128)} %param.11) | copy-start | bytes 148
  67.2 8.9 %copy-start.7 = (s32[128]{0:T(128)S(1)}, s32[128]{0:T(128)}, u32[]{:S(2)}) copy-start(s32[128]{0:T(128)} %param.9) | copy-start | bytes 1540
  68.2 0.8 copy-start.3
  79.4 65.0 %all-to-all-start.1 = ((bf16[12,16,4096]{2,1,0:T(8,128)(2,1)}), bf16[12,16,4096]{2,1,0:T(8,128)(2,1)}, u32[]{:S(2)}, u32[]{:S(2)}) async-start(bf16[12,16,4096]{2,1,0:T(8,128)(2,1)} %bitcast.18), calls=%async_computation.1 | async-start | bytes 3145728 | tf_op jit(solution)/shard_map/all_to_all | solution.py:43
  85.9 17.5 %collective-permute-start.8 = (bf16[16,4096]{1,0:T(8,128)(2,1)S(1)}, bf16[16,4096]{1,0:T(8,128)(2,1)S(1)}, u32[]{:S(2)}, u32[]{:S(2)}) collective-permute-start(bf16[16,4096]{1,0:T(8,128)(2,1)S(1)} %get-tuple-element.26), channel_id=1, source_target_pairs={{0,2},{1,3},{2,4},{3,5},{4,6},{5,7},{6,0},{7,1},{8,10},{9,11},{10,... | collective-permute-start | bytes 393224 | tf_op jit(solution)/shard_map/ppermute | solution.py:55
  88.3 17.1 %collective-permute-start.9 = (bf16[16,4096]{1,0:T(8,128)(2,1)S(1)}, bf16[16,4096]{1,0:T(8,128)(2,1)S(1)}, u32[]{:S(2)}, u32[]{:S(2)}) collective-permute-start(bf16[16,4096]{1,0:T(8,128)(2,1)S(1)} %get-tuple-element.27), channel_id=1, source_target_pairs={{0,4},{1,5},{2,6},{3,7},{4,0},{5,1},{6,2},{7,3},{8,12},{9,13},{10,... | collective-permute-start | bytes 393224 | tf_op jit(solution)/shard_map/ppermute | solution.py:55
  92.7 15.8 %collective-permute-start.10 = (bf16[16,4096]{1,0:T(8,128)(2,1)S(1)}, bf16[16,4096]{1,0:T(8,128)(2,1)S(1)}, u32[]{:S(2)}, u32[]{:S(2)}) collective-permute-start(bf16[16,4096]{1,0:T(8,128)(2,1)S(1)} %get-tuple-element.28), channel_id=1, source_target_pairs={{0,6},{1,7},{2,0},{3,1},{4,2},{5,3},{6,4},{7,5},{8,14},{9,15},{10,... | collective-permute-start | bytes 393224 | tf_op jit(solution)/shard_map/ppermute | solution.py:55
  94.6 13.9 %collective-permute-start.11 = (bf16[16,4096]{1,0:T(8,128)(2,1)S(1)}, bf16[16,4096]{1,0:T(8,128)(2,1)S(1)}, u32[]{:S(2)}, u32[]{:S(2)}) collective-permute-start(bf16[16,4096]{1,0:T(8,128)(2,1)S(1)} %get-tuple-element.29), channel_id=1, source_target_pairs={{0,1},{1,0},{2,3},{3,2},{4,5},{5,4},{6,7},{7,6},{8,9},{9,8},{10,11... | collective-permute-start | bytes 393224 | tf_op jit(solution)/shard_map/ppermute | solution.py:55
  98.9 11.0 %collective-permute-start.12 = (bf16[16,4096]{1,0:T(8,128)(2,1)S(1)}, bf16[16,4096]{1,0:T(8,128)(2,1)S(1)}, u32[]{:S(2)}, u32[]{:S(2)}) collective-permute-start(bf16[16,4096]{1,0:T(8,128)(2,1)S(1)} %get-tuple-element.30), channel_id=1, source_target_pairs={{0,3},{1,2},{2,5},{3,4},{4,7},{5,6},{6,1},{7,0},{8,11},{9,10},{10,... | collective-permute-start | bytes 393224 | tf_op jit(solution)/shard_map/ppermute | solution.py:55
  103.4 8.6 %collective-permute-start.13 = (bf16[16,4096]{1,0:T(8,128)(2,1)S(1)}, bf16[16,4096]{1,0:T(8,128)(2,1)S(1)}, u32[]{:S(2)}, u32[]{:S(2)}) collective-permute-start(bf16[16,4096]{1,0:T(8,128)(2,1)S(1)} %get-tuple-element.31), channel_id=1, source_target_pairs={{0,5},{1,4},{2,7},{3,6},{4,1},{5,0},{6,3},{7,2},{8,13},{9,12},{10,... | collective-permute-start | bytes 393224 | tf_op jit(solution)/shard_map/ppermute | solution.py:55
  105.4 9.9 %collective-permute-start.14 = (bf16[16,4096]{1,0:T(8,128)(2,1)S(1)}, bf16[16,4096]{1,0:T(8,128)(2,1)S(1)}, u32[]{:S(2)}, u32[]{:S(2)}) collective-permute-start(bf16[16,4096]{1,0:T(8,128)(2,1)S(1)} %get-tuple-element.32), channel_id=1, source_target_pairs={{0,7},{1,6},{2,1},{3,0},{4,3},{5,2},{6,5},{7,4},{8,15},{9,14},{10,... | collective-permute-start | bytes 393224 | tf_op jit(solution)/shard_map/ppermute | solution.py:55
  115.5 11.8 %collective-permute-start.15 = (f32[8,4096]{1,0:T(8,128)S(1)}, f32[8,4096]{1,0:T(8,128)S(1)}, u32[]{:S(2)}, u32[]{:S(2)}) collective-permute-start(f32[8,4096]{1,0:T(8,128)S(1)} %slice.25), channel_id=1, source_target_pairs={{0,32},{1,33},{2,34},{3,35},{4,36},{5,37},{6,38},{7,39},{8,40},{9,... | collective-permute-start | bytes 393224 | tf_op jit(solution)/shard_map/ppermute | solution.py:55
  127.4 16.2 %collective-permute-start.16 = (f32[2,4096]{1,0:T(2,128)S(1)}, f32[2,4096]{1,0:T(2,128)S(1)}, u32[]{:S(2)}, u32[]{:S(2)}) collective-permute-start(f32[2,4096]{1,0:T(2,128)S(1)} %get-tuple-element.33), channel_id=1, source_target_pairs={{0,8},{1,9},{2,10},{3,11},{4,12},{5,13},{6,14},{7,15},{8,16},{9,17... | collective-permute-start | bytes 98312 | tf_op jit(solution)/shard_map/ppermute | solution.py:55
  133.2 10.3 %collective-permute-start.18 = (f32[2,4096]{1,0:T(2,128)S(1)}, f32[2,4096]{1,0:T(2,128)S(1)}, u32[]{:S(2)}, u32[]{:S(2)}) collective-permute-start(f32[2,4096]{1,0:T(2,128)S(1)} %get-tuple-element.34), channel_id=1, source_target_pairs={{0,24},{1,25},{2,26},{3,27},{4,28},{5,29},{6,30},{7,31},{8,0},{9,1... | collective-permute-start | bytes 98312 | tf_op jit(solution)/shard_map/ppermute | solution.py:55
  137.0 6.7 %collective-permute-start.17 = (f32[2,4096]{1,0:T(2,128)S(1)}, f32[2,4096]{1,0:T(2,128)S(1)}, u32[]{:S(2)}, u32[]{:S(2)}) collective-permute-start(f32[2,4096]{1,0:T(2,128)S(1)} %get-tuple-element.35), channel_id=1, source_target_pairs={{0,16},{1,17},{2,18},{3,19},{4,20},{5,21},{6,22},{7,23},{8,24},{9,... | collective-permute-start | bytes 98312 | tf_op jit(solution)/shard_map/ppermute | solution.py:55

commit v7 on v6

--- a/solution.py
+++ b/solution.py
@@ -55,19 +55,24 @@
     return lax.ppermute(block, "pool", [(j, moved(j)) for j in range(lax.axis_size("pool"))])
 
 
-def gather_kernel(parts, picks_ref, tiles_ref, out_ref, buffer, load_sems, store_sems):
-    slots, peers = picks_ref.shape
+def gather_kernel(
+    parts, picks_ref, tiles_ref, out_ref, picks, buffer, picks_sem, load_sems, store_sems
+):
+    read = pltpu.make_async_copy(picks_ref, picks, picks_sem)
+    read.start()
     size = tiles_ref.shape[0] // parts
     loads = []
     for i in range(parts):
         span = pl.ds(i * size, size)
         loads.append(pltpu.make_async_copy(tiles_ref.at[span], buffer.at[span], load_sems.at[i]))
         loads[-1].start()
+    read.wait()
     for load in loads:
         load.wait()
+    slots, peers = picks_ref.shape
     stores = []
     for j in range(peers * slots):
-        tile = buffer.at[picks_ref[j % slots, member(j // slots)]]
+        tile = buffer.at[picks[j % slots, member(j // slots)]]
         stores.append(pltpu.make_async_copy(tile, out_ref.at[j], store_sems.at[j]))
         stores[-1].start()
     for store in stores:
@@ -80,17 +85,22 @@
     return pl.pallas_call(
         functools.partial(gather_kernel, parts),
         out_shape=pltpu.HBM(shape, tiles.dtype),
-        in_specs=[SMEM, HBM],
+        in_specs=[HBM, HBM],
         out_specs=HBM,
         scratch_shapes=[
+            pltpu.SMEM(picks.shape, picks.dtype),
             pltpu.VMEM(tiles.shape, tiles.dtype),
+            pltpu.SemaphoreType.DMA,
             pltpu.SemaphoreType.DMA((parts,)),
             pltpu.SemaphoreType.DMA((peers * slots,)),
         ],
         compiler_params=PARAMS,
         cost_estimate=pl.CostEstimate(flops=0, bytes_accessed=3 << 20, transcendentals=0),
         name="gather_tiles",
-    )(picks, pltpu.with_memory_space_constraint(tiles, pltpu.HBM))
+    )(
+        pltpu.with_memory_space_constraint(picks, pltpu.HBM),
+        pltpu.with_memory_space_constraint(tiles, pltpu.HBM),
+    )
 
 
 def scores_kernel(keys_ref, queries_ref, out_ref):
@@ -200,33 +210,45 @@
     )(queries, hard_rows, local, near, far, counts, positives)
 
 
-def pool_kernel(near_ref, far_ref, queries_ref, kept_out, *sent_out):
-    size = kept_out.shape[0]
-    pieces = near_ref.shape[0] // size
-    near = jnp.dot(near_ref[...], queries_ref[...], preferred_element_type=jnp.float32)
-    kept_out[...] = SHARPNESS * near[:size]
-    for m in range(1, pieces):
-        piece = SHARPNESS * near[m * size : (m + 1) * size]
-        sent_out[m - 1][...] = piece.astype(sent_out[m - 1].dtype)
-    far = jnp.dot(far_ref[...], queries_ref[...], preferred_element_type=jnp.float32)
-    for m in range(pieces):
-        piece = SHARPNESS * far[m * size : (m + 1) * size]
-        sent_out[pieces - 1 + m][...] = piece.astype(sent_out[pieces - 1 + m].dtype)
-
-
-def pool_terms(near, far, queries, size, link):
-    shape = (size, queries.shape[1])
-    count = 2 * near.shape[0] // size
+def pool_kernel(near_ref, far_ref, queries_ref, kept_out, sent_out):
+    queries = queries_ref[...]
+    far = jnp.dot(far_ref[...], queries, preferred_element_type=jnp.float32)
+    sent_out[...] = (SHARPNESS * far).astype(sent_out.dtype)
+    kept_out[...] = SHARPNESS * jnp.dot(near_ref[...], queries, preferred_element_type=jnp.float32)
+
+
+def pool_terms(near, far, queries, link):
+    shape = (near.shape[0], queries.shape[1])
     return pl.pallas_call(
         pool_kernel,
+        out_shape=(jax.ShapeDtypeStruct(shape, jnp.float32), jax.ShapeDtypeStruct(shape, link)),
+        in_specs=[VMEM] * 3,
+        out_specs=(VMEM,) * 2,
+        compiler_params=PARAMS,
+        cost_estimate=CHEAP,
+        name="pool_terms",
+    )(near, far, queries)
+
+
+def join_kernel(kept_ref, sent_ref, own_out, *piece_outs):
+    size = own_out.shape[0]
+    for m, out in enumerate((own_out,) + piece_outs):
+        rows = pl.ds(m * size, size)
+        out[...] = (kept_ref[rows] + sent_ref[rows].astype(jnp.float32)).astype(out.dtype)
+
+
+def join(kept, sent, count, link):
+    shape = (kept.shape[0] // count, kept.shape[1])
+    return pl.pallas_call(
+        join_kernel,
         out_shape=(jax.ShapeDtypeStruct(shape, jnp.float32),)
         + (jax.ShapeDtypeStruct(shape, link),) * (count - 1),
-        in_specs=[VMEM] * 3,
+        in_specs=[VMEM] * 2,
         out_specs=(VMEM,) * count,
         compiler_params=PARAMS,
         cost_estimate=CHEAP,
-        name="pool_terms",
-    )(near, far, queries)
+        name="join",
+    )(kept, sent)
 
 
 def queries_kernel(
@@ -264,7 +286,7 @@
         store.wait()
 
 
-def query_gradient(hard_weight, weight, hard_rows, keys, chunk=1024):
+def query_gradient(hard_weight, weight, hard_rows, keys, chunk=2048):
     rows, width = hard_weight.shape[1], hard_rows.shape[1]
     return pl.pallas_call(
         functools.partial(queries_kernel, chunk),
@@ -314,7 +336,7 @@
         store.wait()
 
 
-def passage_gradient(weight, queries, chosen, returned, chunk=1024):
+def passage_gradient(weight, queries, chosen, returned, chunk=2048):
     rows, width = weight.shape[0], queries.shape[1]
     return pl.pallas_call(
         functools.partial(passages_kernel, chunk),
@@ -354,18 +376,20 @@
     )
     returned = trade(grad_hard.reshape(peers, slots * TILE, width)).reshape(hard, width)
     *y_digits, (x_step, x_count), (core_step, core_count) = digits
-    size = pooled.shape[0] // x_count
-    term, *sent = pool_terms(near_weight, far_weight, queries, size, jnp.bfloat16)
-    moves = [(x, core) for core in range(core_count) for x in range(x_count)][1:]
-    for piece, (x, core) in zip(sent, moves):
-        pair = ((x_step, x_count, x), (core_step, core_count, core))
-        term = term + shifts(piece, pair, 1).astype(jnp.float32)
-    for step, count in reversed(y_digits):
-        size = size // count
-        pieces = [term[m * size : (m + 1) * size] for m in range(count)]
-        term = pieces[0]
-        for m in range(1, count):
-            term = term + shifts(pieces[m], ((step, count, m),), 1)
+    kept, sent = pool_terms(near_weight, far_weight, queries, jnp.float32)
+    sent = shifts(sent, ((core_step, core_count, 1),), 1)
+    term, *pieces = join(kept, sent, x_count, jnp.bfloat16)
+    size = term.shape[0]
+    for m, piece in enumerate(pieces, 1):
+        term = term + shifts(piece, ((x_step, x_count, m),), 1).astype(jnp.float32)
+    (low_step, low_count), (high_step, high_count) = y_digits
+    moves = [(low, high) for high in range(high_count) for low in range(low_count)]
+    size = size // len(moves)
+    pieces = [term[m * size : (m + 1) * size] for m in range(len(moves))]
+    term = pieces[0]
+    for piece, (low, high) in zip(pieces[1:], moves[1:]):
+        pair = ((low_step, low_count, low), (high_step, high_count, high))
+        term = term + shifts(piece, pair, 1)
     grad_pool = term.astype(jnp.bfloat16)
     grad_queries = query_gradient(
         hard_weight, (local_weight, near_weight, far_weight), hard_rows, (passages, near, far)

time: 149 us -> 143 us (0.960)
  starting transfers between devices: 93.4 us -> 90.9 us
    ppermute x19, starting transfers between devices: 72 us -> 69.5 us  [shifts(): lax.ppermute(block, 'pool', [(j, moved(j)) for j in range(lax.axis_size('...]
    unnamed x22 -> x20, local copies, waits for them, and re-layouts: 3.39 us -> 2.71 us
  transfers between devices with their start and end apart: 21 -> 21, of which waited for: 10 -> 9; matrix products, arithmetic and copies ran while one was open for 3% -> 3% of each run, Pallas kernels for 4% -> 4%
where the time goes in v7:
time: 143 us; the launch traced here: 142 us
  starting transfers between devices  90.9 us (64%)
  waiting for transfers between devices  29.4 us (21%)
  Pallas kernels  14.1 us (10%)
  local copies, waits for them, and re-layouts  5.74 us (4%)
    ppermute x19, starting transfers between devices, shifts(): lax.ppermute(block, 'pool', [(j, moved(j)) for j in range(lax.axis_size('...  69.5 us
    ppermute x19, waiting for transfers between devices, shifts(): lax.ppermute(block, 'pool', [(j, moved(j)) for j in range(lax.axis_size('...  22.3 us
    all_to_all x2, starting transfers between devices, trade(): lax.all_to_all(blocks, ('pb', 'pool'), split_axis=0, concat_axis=0, tiled...  21.4 us
    all_to_all x2, waiting for transfers between devices, trade(): lax.all_to_all(blocks, ('pb', 'pool'), split_axis=0, concat_axis=0, tiled...  7.1 us
    pallas_call x1, Pallas kernels, weights(): pl.pallas_call(functools.partial(weights_kernel, chunk), out_shape=(pltpu...  3.31 us
    pallas_call x1, Pallas kernels, query_gradient(): pl.pallas_call(functools.partial(queries_kernel, chunk), out_shape=pltpu....  3 us
    concatenate x2, local copies, waits for them, and re-layouts, body(): jnp.concatenate([pooled] + [shifts(pooled, ((step, count, m),), -1) for m...  2.95 us
  transfers between devices with their start and end apart: 21, of which 9 were waited for; matrix products, arithmetic and copies ran while one was open for 3% of the time, Pallas kernels for 4%

profile of v7, /device:TPU:6, one launch (start us, length us, event | category | flops | bytes accessed | tf_op | source)
XLA Modules:
  0.0 142.0 jit_solution(9603632009705400095)
XLA Ops:
  0.6 2.6 %gather_tiles.1 = bf16[24,8,4096]{2,1,0:T(8,128)(2,1)} custom-call(s32[2,12]{1,0:T(2,128)} %bitcast.13, bf16[16,8,4096]{2,1,0:T(8,128)(2,1)} %bitcast.12), custom_call_target="tpu_custom_call" | custom-call | bytes 3145728 | tf_op jit(solution)/shard_map/gather_tiles/pallas_call | solution.py:85
  3.3 0.0 copy-start.7
  3.3 0.0 copy-start
  3.3 0.0 copy-start.4
  3.3 15.3 %all-to-all-start = ((bf16[12,16,4096]{2,1,0:T(8,128)(2,1)}), bf16[12,16,4096]{2,1,0:T(8,128)(2,1)S(1)}, u32[]{:S(2)}, u32[]{:S(2)}) async-start(bf16[12,16,4096]{2,1,0:T(8,128)(2,1)} %bitcast.17), calls=%async_computation | async-start | bytes 3145728 | tf_op jit(solution)/shard_map/all_to_all | solution.py:43
  18.6 3.5 %collective-permute-start.2 = (bf16[2,4096]{1,0:T(2,128)(2,1)S(1)}, bf16[2,4096]{1,0:T(2,128)(2,1)S(1)}, u32[]{:S(2)}, u32[]{:S(2)}) collective-permute-start(bf16[2,4096]{1,0:T(2,128)(2,1)S(1)} %copy-done.7), channel_id=1, source_target_pairs={{0,8},{1,9},{2,10},{3,11},{4,12},{5,13},{6,14},{7,15},{8,16},{9,17... | collective-permute-start | bytes 49160 | tf_op jit(solution)/shard_map/ppermute | solution.py:55
  22.1 4.5 %collective-permute-start.1 = (bf16[2,4096]{1,0:T(2,128)(2,1)S(1)}, bf16[2,4096]{1,0:T(2,128)(2,1)S(1)}, u32[]{:S(2)}, u32[]{:S(2)}) collective-permute-start(bf16[2,4096]{1,0:T(2,128)(2,1)S(1)} %copy-done.7), channel_id=1, source_target_pairs={{0,16},{1,17},{2,18},{3,19},{4,20},{5,21},{6,22},{7,23},{8,24},{9,... | collective-permute-start | bytes 49160 | tf_op jit(solution)/shard_map/ppermute | solution.py:55
  26.6 3.3 %collective-permute-start = (bf16[2,4096]{1,0:T(2,128)(2,1)S(1)}, bf16[2,4096]{1,0:T(2,128)(2,1)S(1)}, u32[]{:S(2)}, u32[]{:S(2)}) collective-permute-start(bf16[2,4096]{1,0:T(2,128)(2,1)S(1)} %copy-done.7), channel_id=1, source_target_pairs={{0,24},{1,25},{2,26},{3,27},{4,28},{5,29},{6,30},{7,31},{8,0},{9,1... | collective-permute-start | bytes 49160 | tf_op jit(solution)/shard_map/ppermute | solution.py:55
  29.9 0.0 collective-permute-done.2
  29.9 2.3 %collective-permute-done = bf16[2,4096]{1,0:T(2,128)(2,1)S(1)} collective-permute-done((bf16[2,4096]{1,0:T(2,128)(2,1)S(1)}, bf16[2,4096]{1,0:T(2,128)(2,1)S(1)}, u32[]{:S(2)}, u32[]{:S(2)}) %collective-permute-start) | collective-permute-done | bytes 16416 | tf_op jit(solution)/shard_map/ppermute | solution.py:55
  32.3 0.1 pad_maximum_fusion
  32.3 5.9 %collective-permute-start.3 = (bf16[8,4096]{1,0:T(8,128)(2,1)S(1)}, bf16[8,4096]{1,0:T(8,128)(2,1)S(1)}, u32[]{:S(2)}, u32[]{:S(2)}) collective-permute-start(bf16[8,4096]{1,0:T(8,128)(2,1)S(1)} %pad_maximum_fusion), channel_id=1, source_target_pairs={{0,32},{1,33},{2,34},{3,35},{4,36},{5,37},{6,38},{7,39},{8,40},{9,... | collective-permute-start | bytes 196616 | tf_op jit(solution)/shard_map/ppermute | solution.py:55
  38.3 4.2 %collective-permute-done.3 = bf16[8,4096]{1,0:T(8,128)(2,1)S(1)} collective-permute-done((bf16[8,4096]{1,0:T(8,128)(2,1)S(1)}, bf16[8,4096]{1,0:T(8,128)(2,1)S(1)}, u32[]{:S(2)}, u32[]{:S(2)}) %collective-permute-start.3) | collective-permute-done | bytes 65568 | tf_op jit(solution)/shard_map/ppermute | solution.py:55
  42.5 0.1 concatenate.12
  42.6 2.4 %collective-permute-start.6 = (bf16[16,4096]{1,0:T(8,128)(2,1)S(1)}, bf16[16,4096]{1,0:T(8,128)(2,1)S(1)}, u32[]{:S(2)}, u32[]{:S(2)}) collective-permute-start(bf16[16,4096]{1,0:T(8,128)(2,1)S(1)} %concatenate.12), channel_id=1, source_target_pairs={{0,2},{1,3},{2,4},{3,5},{4,6},{5,7},{6,0},{7,1},{8,10},{9,11},{10,... | collective-permute-start | bytes 393224 | tf_op jit(solution)/shard_map/ppermute | solution.py:55
  45.0 4.3 %collective-permute-start.5 = (bf16[16,4096]{1,0:T(8,128)(2,1)S(1)}, bf16[16,4096]{1,0:T(8,128)(2,1)S(1)}, u32[]{:S(2)}, u32[]{:S(2)}) collective-permute-start(bf16[16,4096]{1,0:T(8,128)(2,1)S(1)} %concatenate.12), channel_id=1, source_target_pairs={{0,4},{1,5},{2,6},{3,7},{4,0},{5,1},{6,2},{7,3},{8,12},{9,13},{10,... | collective-permute-start | bytes 393224 | tf_op jit(solution)/shard_map/ppermute | solution.py:55
  49.3 1.9 %collective-permute-start.4 = (bf16[16,4096]{1,0:T(8,128)(2,1)S(1)}, bf16[16,4096]{1,0:T(8,128)(2,1)}, u32[]{:S(2)}, u32[]{:S(2)}) collective-permute-start(bf16[16,4096]{1,0:T(8,128)(2,1)S(1)} %concatenate.12), channel_id=1, source_target_pairs={{0,6},{1,7},{2,0},{3,1},{4,2},{5,3},{6,4},{7,5},{8,14},{9,15},{10,... | collective-permute-start | bytes 393224 | tf_op jit(solution)/shard_map/ppermute | solution.py:55
  51.3 0.0 collective-permute-done.6
  51.3 0.0 copy-start.8
  51.3 2.1 %collective-permute-done.5 = bf16[16,4096]{1,0:T(8,128)(2,1)S(1)} collective-permute-done((bf16[16,4096]{1,0:T(8,128)(2,1)S(1)}, bf16[16,4096]{1,0:T(8,128)(2,1)S(1)}, u32[]{:S(2)}, u32[]{:S(2)}) %collective-permute-start.5) | collective-permute-done | bytes 131104 | tf_op jit(solution)/shard_map/ppermute | solution.py:55
  53.4 0.7 copy-done.9
  54.0 3.7 %collective-permute-done.4 = bf16[16,4096]{1,0:T(8,128)(2,1)} collective-permute-done((bf16[16,4096]{1,0:T(8,128)(2,1)S(1)}, bf16[16,4096]{1,0:T(8,128)(2,1)}, u32[]{:S(2)}, u32[]{:S(2)}) %collective-permute-start.4) | collective-permute-done | bytes 131104 | tf_op jit(solution)/shard_map/ppermute | solution.py:55
  57.8 2.8 %concatenate.13.keys_ref.pool_near_ref = bf16[64,4096]{1,0:T(8,128)(2,1)S(1)} concatenate(bf16[2,4096]{1,0:T(2,128)(2,1)S(1)} %copy-done.7, bf16[2,4096]{1,0:T(2,128)(2,1)S(1)} %collective-permute-done, bf16[2,4096]{1,0:T(2,128)(2,1)S(1)} %collective-permute-done.1, bf16[2,4096]{1,0:T(2,128)(2,1)S(1)} %collective-permute-done.2, bf16[8,4096]{1,0:T(8,128)(2,1)S(1)} %collective-permute-done.3, ...), dimensions={0} | concatenate | bytes 1048576 | tf_op jit(solution)/shard_map/concatenate | solution.py:367
  60.6 0.0 copy-start.2
  60.6 3.1 %collective-permute-start.7 = (bf16[64,4096]{1,0:T(8,128)(2,1)S(1)}, bf16[64,4096]{1,0:T(8,128)(2,1)S(1)}, u32[]{:S(2)}, u32[]{:S(2)}) collective-permute-start(bf16[64,4096]{1,0:T(8,128)(2,1)S(1)} %concatenate.13.keys_ref.pool_near_ref), channel_id=1, source_target_pairs={{0,1},{1,0},{2,3},{3,2},{4,5},{5,4},{6,7},{7,6},{8,9},{9,8},{10,11... | collective-permute-start | bytes 1572872 | tf_op jit(solution)/shard_map/ppermute | solution.py:55
  63.7 0.0 copy-start.1
  63.7 1.2 copy-done.1
  65.0 1.0 local_scores.1
  65.9 0.0 copy-start.5
  66.0 0.0 copy-start.6
  66.0 0.5 scores.2.near_ref
  66.5 0.0 collective-permute-done.7.keys_ref.pool_far_ref
  66.5 0.5 scores.3.far_ref
  67.0 0.8 copy-done.3
  67.8 7.1 %all-to-all-done = bf16[12,16,4096]{2,1,0:T(8,128)(2,1)S(1)} async-done(((bf16[12,16,4096]{2,1,0:T(8,128)(2,1)}), bf16[12,16,4096]{2,1,0:T(8,128)(2,1)S(1)}, u32[]{:S(2)}, u32[]{:S(2)}) %all-to-all-start) | async-done | bytes 1572896 | tf_op jit(solution)/shard_map/all_to_all | solution.py:43
  74.9 3.3 %weights.1 = (bf16[192,4096]{1,0:T(8,128)(2,1)}, bf16[128,128]{1,0:T(8,128)(2,1)S(1)}, bf16[64,128]{1,0:T(8,128)(2,1)S(1)}, bf16[64,128]{1,0:T(8,128)(2,1)S(1)}, bf16[192,128]{1,0:T(8,128)(2,1)S(1)}) custom-call(bf16[128,4096]{1,0:T(8,128)(2,1)S(1)} %copy-done, bf16[192,4096]{1,0:T(8,128)(2,1)S(1)} %bitcast.10, f32[128,128]{1,0:T(8,128)S(1)} %get-tuple-element.16.local_ref, ...), custom_call_target="tpu_custom_call" | custom-call | flops 1048576 | bytes 1048576 | tf_op jit(solution)/shard_map/weights/pallas_call | solution.py:194
  78.2 6.1 %all-to-all-start.1 = ((bf16[12,16,4096]{2,1,0:T(8,128)(2,1)}), bf16[12,16,4096]{2,1,0:T(8,128)(2,1)}, u32[]{:S(2)}, u32[]{:S(2)}) async-start(bf16[12,16,4096]{2,1,0:T(8,128)(2,1)} %bitcast.18), calls=%async_computation.1 | async-start | bytes 3145728 | tf_op jit(solution)/shard_map/all_to_all | solution.py:43
  84.3 0.4 pool_terms.1
  84.7 4.9 %collective-permute-start.8 = (f32[64,4096]{1,0:T(8,128)S(1)}, f32[64,4096]{1,0:T(8,128)S(1)}, u32[]{:S(2)}, u32[]{:S(2)}) collective-permute-start(f32[64,4096]{1,0:T(8,128)S(1)} %get-tuple-element.24), channel_id=1, source_target_pairs={{0,1},{1,0},{2,3},{3,2},{4,5},{5,4},{6,7},{7,6},{8,9},{9,8},{10,11... | collective-permute-start | bytes 3145736 | tf_op jit(solution)/shard_map/ppermute | solution.py:55
  89.6 2.3 %collective-permute-done.8.sent_ref = f32[64,4096]{1,0:T(8,128)S(1)} collective-permute-done((f32[64,4096]{1,0:T(8,128)S(1)}, f32[64,4096]{1,0:T(8,128)S(1)}, u32[]{:S(2)}, u32[]{:S(2)}) %collective-permute-start.8) | collective-permute-done | bytes 1048608 | tf_op jit(solution)/shard_map/ppermute | solution.py:55
  91.9 0.1 join.1
  92.0 2.4 %collective-permute-start.9 = (bf16[16,4096]{1,0:T(8,128)(2,1)S(1)}, bf16[16,4096]{1,0:T(8,128)(2,1)S(1)}, u32[]{:S(2)}, u32[]{:S(2)}) collective-permute-start(bf16[16,4096]{1,0:T(8,128)(2,1)S(1)} %get-tuple-element.26), channel_id=1, source_target_pairs={{0,2},{1,3},{2,4},{3,5},{4,6},{5,7},{6,0},{7,1},{8,10},{9,11},{10,... | collective-permute-start | bytes 393224 | tf_op jit(solution)/shard_map/ppermute | solution.py:55
  94.4 4.3 %collective-permute-start.10 = (bf16[16,4096]{1,0:T(8,128)(2,1)S(1)}, bf16[16,4096]{1,0:T(8,128)(2,1)S(1)}, u32[]{:S(2)}, u32[]{:S(2)}) collective-permute-start(bf16[16,4096]{1,0:T(8,128)(2,1)S(1)} %get-tuple-element.27), channel_id=1, source_target_pairs={{0,4},{1,5},{2,6},{3,7},{4,0},{5,1},{6,2},{7,3},{8,12},{9,13},{10,... | collective-permute-start | bytes 393224 | tf_op jit(solution)/shard_map/ppermute | solution.py:55
  98.7 1.9 %collective-permute-start.11 = (bf16[16,4096]{1,0:T(8,128)(2,1)S(1)}, bf16[16,4096]{1,0:T(8,128)(2,1)S(1)}, u32[]{:S(2)}, u32[]{:S(2)}) collective-permute-start(bf16[16,4096]{1,0:T(8,128)(2,1)S(1)} %get-tuple-element.28), channel_id=1, source_target_pairs={{0,6},{1,7},{2,0},{3,1},{4,2},{5,3},{6,4},{7,5},{8,14},{9,15},{10,... | collective-permute-start | bytes 393224 | tf_op jit(solution)/shard_map/ppermute | solution.py:55
  100.7 0.0 collective-permute-done.9
  100.7 2.6 %collective-permute-done.10 = bf16[16,4096]{1,0:T(8,128)(2,1)S(1)} collective-permute-done((bf16[16,4096]{1,0:T(8,128)(2,1)S(1)}, bf16[16,4096]{1,0:T(8,128)(2,1)S(1)}, u32[]{:S(2)}, u32[]{:S(2)}) %collective-permute-start.10) | collective-permute-done | bytes 131104 | tf_op jit(solution)/shard_map/ppermute | solution.py:55
  103.3 3.8 %collective-permute-done.11 = bf16[16,4096]{1,0:T(8,128)(2,1)S(1)} collective-permute-done((bf16[16,4096]{1,0:T(8,128)(2,1)S(1)}, bf16[16,4096]{1,0:T(8,128)(2,1)S(1)}, u32[]{:S(2)}, u32[]{:S(2)}) %collective-permute-start.11) | collective-permute-done | bytes 131104 | tf_op jit(solution)/shard_map/ppermute | solution.py:55
  107.1 0.1 convert_add_fusion
  107.1 0.1 fusion.5
  107.2 3.5 %collective-permute-start.12 = (f32[2,4096]{1,0:T(2,128)S(1)}, f32[2,4096]{1,0:T(2,128)S(1)}, u32[]{:S(2)}, u32[]{:S(2)}) collective-permute-start(f32[2,4096]{1,0:T(2,128)S(1)} %get-tuple-element.29), channel_id=1, source_target_pairs={{0,8},{1,9},{2,10},{3,11},{4,12},{5,13},{6,14},{7,15},{8,16},{9,17... | collective-permute-start | bytes 98312 | tf_op jit(solution)/shard_map/ppermute | solution.py:55
  110.7 6.7 %collective-permute-start.18 = (f32[2,4096]{1,0:T(2,128)S(1)}, f32[2,4096]{1,0:T(2,128)S(1)}, u32[]{:S(2)}, u32[]{:S(2)}) collective-permute-start(f32[2,4096]{1,0:T(2,128)S(1)} %get-tuple-element.30), channel_id=1, source_target_pairs={{0,56},{1,57},{2,58},{3,59},{4,60},{5,61},{6,62},{7,63},{8,32},{9,... | collective-permute-start | bytes 98312 | tf_op jit(solution)/shard_map/ppermute | solution.py:55
  117.4 2.2 %collective-permute-start.17 = (f32[2,4096]{1,0:T(2,128)S(1)}, f32[2,4096]{1,0:T(2,128)S(1)}, u32[]{:S(2)}, u32[]{:S(2)}) collective-permute-start(f32[2,4096]{1,0:T(2,128)S(1)} %get-tuple-element.31), channel_id=1, source_target_pairs={{0,48},{1,49},{2,50},{3,51},{4,52},{5,53},{6,54},{7,55},{8,56},{9,... | collective-permute-start | bytes 98312 | tf_op jit(solution)/shard_map/ppermute | solution.py:55
  119.7 5.2 %collective-permute-start.16 = (f32[2,4096]{1,0:T(2,128)S(1)}, f32[2,4096]{1,0:T(2,128)S(1)}, u32[]{:S(2)}, u32[]{:S(2)}) collective-permute-start(f32[2,4096]{1,0:T(2,128)S(1)} %get-tuple-element.32), channel_id=1, source_target_pairs={{0,40},{1,41},{2,42},{3,43},{4,44},{5,45},{6,46},{7,47},{8,48},{9,... | collective-permute-start | bytes 98312 | tf_op jit(solution)/shard_map/ppermute | solution.py:55
  124.8 4.7 %collective-permute-start.15 = (f32[2,4096]{1,0:T(2,128)S(1)}, f32[2,4096]{1,0:T(2,128)S(1)}, u32[]{:S(2)}, u32[]{:S(2)}) collective-permute-start(f32[2,4096]{1,0:T(2,128)S(1)} %get-tuple-element.33), channel_id=1, source_target_pairs={{0,32},{1,33},{2,34},{3,35},{4,36},{5,37},{6,38},{7,39},{8,40},{9,... | collective-permute-start | bytes 98312 | tf_op jit(solution)/shard_map/ppermute | solution.py:55
  129.6 0.0 collective-permute-done.12
  129.6 2.4 %collective-permute-start.14 = (f32[2,4096]{1,0:T(2,128)S(1)}, f32[2,4096]{1,0:T(2,128)S(1)}, u32[]{:S(2)}, u32[]{:S(2)}) collective-permute-start(f32[2,4096]{1,0:T(2,128)S(1)} %get-tuple-element.34), channel_id=1, source_target_pairs={{0,24},{1,25},{2,26},{3,27},{4,28},{5,29},{6,30},{7,31},{8,0},{9,1... | collective-permute-start | bytes 98312 | tf_op jit(solution)/shard_map/ppermute | solution.py:55
  131.9 0.0 collective-permute-done.18
  131.9 2.4 %collective-permute-start.13 = (f32[2,4096]{1,0:T(2,128)S(1)}, f32[2,4096]{1,0:T(2,128)S(1)}, u32[]{:S(2)}, u32[]{:S(2)}) collective-permute-start(f32[2,4096]{1,0:T(2,128)S(1)} %get-tuple-element.35), channel_id=1, source_target_pairs={{0,16},{1,17},{2,18},{3,19},{4,20},{5,21},{6,22},{7,23},{8,24},{9,... | collective-permute-start | bytes 98312 | tf_op jit(solution)/shard_map/ppermute | solution.py:55
  134.3 3.0 %query_gradient.1 = bf16[128,4096]{1,0:T(8,128)(2,1)} custom-call(bf16[192,128]{1,0:T(8,128)(2,1)S(1)} %get-tuple-element.17.hard_weight_ref, bf16[128,128]{1,0:T(8,128)(2,1)S(1)} %get-tuple-element.18.local_ref.weight_ref, bf16[64,128]{1,0:T(8,128)(2,1)S(1)} %get-tuple-element.19.near_ref, bf16[64,128]{1,0:T(8,128)(2,1)S(1)} %get-tuple-element.20.far_ref, ...), custom_call_target="tpu_custom_call" | custom-call | flops 1048576 | bytes 1048576 | tf_op jit(solution)/shard_map/query_gradient/pallas_call | solution.py:291
  137.4 0.0 collective-permute-done.15
  137.4 1.3 collective-permute-done.13
  138.6 0.7 add_convert_fusion
  139.3 0.0 all-to-all-done.1
  139.3 2.7 %passage_gradient.1 = bf16[128,4096]{1,0:T(8,128)(2,1)} custom-call(bf16[128,128]{1,0:T(8,128)(2,1)S(1)} %get-tuple-element.18.local_ref.weight_ref, bf16[128,4096]{1,0:T(8,128)(2,1)S(1)} %copy-done, bf16[128,192]{1,0:T(8,128)(2,1)S(1)} %get-tuple-element.21.chosen_ref, bf16[192,4096]{1,0:T(8,128)(2,1)} %bitcast.9.returned_ref), custom_call_target="tpu_custom_call" | custom-call | flops 1048576 | bytes 1048576 | tf_op jit(solution)/shard_map/passage_gradient/pallas_call | solution.py:341
  (13 shorter events, 0.0 us)
Async XLA Ops:
  3.3 15.3 %copy-start.7 = (bf16[2,4096]{1,0:T(2,128)(2,1)S(1)}, bf16[2,4096]{1,0:T(2,128)(2,1)}, u32[]{:S(2)}) copy-start(bf16[2,4096]{1,0:T(2,128)(2,1)} %param.8) | copy-start | bytes 49156
  3.3 60.4 %copy-start = (bf16[128,4096]{1,0:T(8,128)(2,1)S(1)}, bf16[128,4096]{1,0:T(8,128)(2,1)}, u32[]{:S(2)}) copy-start(bf16[128,4096]{1,0:T(8,128)(2,1)} %queries_ref.11) | copy-start | bytes 3145732
  3.3 60.4 %copy-start.4 = (s32[1,1,12,2]{2,3,1,0:T(2,128)S(1)}, s32[1,1,12,2]{2,3,1,0:T(2,128)}, u32[]{:S(2)}) copy-start(s32[1,1,12,2]{2,3,1,0:T(2,128)} %param.10) | copy-start | bytes 292
  3.3 71.5 %all-to-all-start = ((bf16[12,16,4096]{2,1,0:T(8,128)(2,1)}), bf16[12,16,4096]{2,1,0:T(8,128)(2,1)S(1)}, u32[]{:S(2)}, u32[]{:S(2)}) async-start(bf16[12,16,4096]{2,1,0:T(8,128)(2,1)} %bitcast.17), calls=%async_computation | async-start | bytes 3145728 | tf_op jit(solution)/shard_map/all_to_all | solution.py:43
  18.6 11.3 %collective-permute-start.2 = (bf16[2,4096]{1,0:T(2,128)(2,1)S(1)}, bf16[2,4096]{1,0:T(2,128)(2,1)S(1)}, u32[]{:S(2)}, u32[]{:S(2)}) collective-permute-start(bf16[2,4096]{1,0:T(2,128)(2,1)S(1)} %copy-done.7), channel_id=1, source_target_pairs={{0,8},{1,9},{2,10},{3,11},{4,12},{5,13},{6,14},{7,15},{8,16},{9,17... | collective-permute-start | bytes 49160 | tf_op jit(solution)/shard_map/ppermute | solution.py:55
  22.1 7.8 %collective-permute-start.1 = (bf16[2,4096]{1,0:T(2,128)(2,1)S(1)}, bf16[2,4096]{1,0:T(2,128)(2,1)S(1)}, u32[]{:S(2)}, u32[]{:S(2)}) collective-permute-start(bf16[2,4096]{1,0:T(2,128)(2,1)S(1)} %copy-done.7), channel_id=1, source_target_pairs={{0,16},{1,17},{2,18},{3,19},{4,20},{5,21},{6,22},{7,23},{8,24},{9,... | collective-permute-start | bytes 49160 | tf_op jit(solution)/shard_map/ppermute | solution.py:55
  26.6 5.6 %collective-permute-start = (bf16[2,4096]{1,0:T(2,128)(2,1)S(1)}, bf16[2,4096]{1,0:T(2,128)(2,1)S(1)}, u32[]{:S(2)}, u32[]{:S(2)}) collective-permute-start(bf16[2,4096]{1,0:T(2,128)(2,1)S(1)} %copy-done.7), channel_id=1, source_target_pairs={{0,24},{1,25},{2,26},{3,27},{4,28},{5,29},{6,30},{7,31},{8,0},{9,1... | collective-permute-start | bytes 49160 | tf_op jit(solution)/shard_map/ppermute | solution.py:55
  32.3 10.2 %collective-permute-start.3 = (bf16[8,4096]{1,0:T(8,128)(2,1)S(1)}, bf16[8,4096]{1,0:T(8,128)(2,1)S(1)}, u32[]{:S(2)}, u32[]{:S(2)}) collective-permute-start(bf16[8,4096]{1,0:T(8,128)(2,1)S(1)} %pad_maximum_fusion), channel_id=1, source_target_pairs={{0,32},{1,33},{2,34},{3,35},{4,36},{5,37},{6,38},{7,39},{8,40},{9,... | collective-permute-start | bytes 196616 | tf_op jit(solution)/shard_map/ppermute | solution.py:55
  42.6 8.7 %collective-permute-start.6 = (bf16[16,4096]{1,0:T(8,128)(2,1)S(1)}, bf16[16,4096]{1,0:T(8,128)(2,1)S(1)}, u32[]{:S(2)}, u32[]{:S(2)}) collective-permute-start(bf16[16,4096]{1,0:T(8,128)(2,1)S(1)} %concatenate.12), channel_id=1, source_target_pairs={{0,2},{1,3},{2,4},{3,5},{4,6},{5,7},{6,0},{7,1},{8,10},{9,11},{10,... | collective-permute-start | bytes 393224 | tf_op jit(solution)/shard_map/ppermute | solution.py:55
  45.0 8.4 %collective-permute-start.5 = (bf16[16,4096]{1,0:T(8,128)(2,1)S(1)}, bf16[16,4096]{1,0:T(8,128)(2,1)S(1)}, u32[]{:S(2)}, u32[]{:S(2)}) collective-permute-start(bf16[16,4096]{1,0:T(8,128)(2,1)S(1)} %concatenate.12), channel_id=1, source_target_pairs={{0,4},{1,5},{2,6},{3,7},{4,0},{5,1},{6,2},{7,3},{8,12},{9,13},{10,... | collective-permute-start | bytes 393224 | tf_op jit(solution)/shard_map/ppermute | solution.py:55
  49.3 8.4 %collective-permute-start.4 = (bf16[16,4096]{1,0:T(8,128)(2,1)S(1)}, bf16[16,4096]{1,0:T(8,128)(2,1)}, u32[]{:S(2)}, u32[]{:S(2)}) collective-permute-start(bf16[16,4096]{1,0:T(8,128)(2,1)S(1)} %concatenate.12), channel_id=1, source_target_pairs={{0,6},{1,7},{2,0},{3,1},{4,2},{5,3},{6,4},{7,5},{8,14},{9,15},{10,... | collective-permute-start | bytes 393224 | tf_op jit(solution)/shard_map/ppermute | solution.py:55
  51.3 2.1 %copy-start.8 = (bf16[16,4096]{1,0:T(8,128)(2,1)}, bf16[16,4096]{1,0:T(8,128)(2,1)S(1)}, u32[]{:S(2)}) copy-start(bf16[16,4096]{1,0:T(8,128)(2,1)S(1)} %collective-permute-done.6) | copy-start | bytes 393220
  53.4 0.7 copy-start.9
  60.6 5.8 %copy-start.2 = (bf16[64,4096]{1,0:T(8,128)(2,1)}, bf16[64,4096]{1,0:T(8,128)(2,1)S(1)}, u32[]{:S(2)}) copy-start(bf16[64,4096]{1,0:T(8,128)(2,1)S(1)} %concatenate.13.keys_ref.pool_near_ref) | copy-start | bytes 1572868
  60.6 5.8 %collective-permute-start.7 = (bf16[64,4096]{1,0:T(8,128)(2,1)S(1)}, bf16[64,4096]{1,0:T(8,128)(2,1)S(1)}, u32[]{:S(2)}, u32[]{:S(2)}) collective-permute-start(bf16[64,4096]{1,0:T(8,128)(2,1)S(1)} %concatenate.13.keys_ref.pool_near_ref), channel_id=1, source_target_pairs={{0,1},{1,0},{2,3},{3,2},{4,5},{5,4},{6,7},{7,6},{8,9},{9,8},{10,11... | collective-permute-start | bytes 1572872 | tf_op jit(solution)/shard_map/ppermute | solution.py:55
  63.7 1.2 copy-start.1
  65.9 8.9 %copy-start.5 = (s32[1,1,12]{2,1,0:T(1,128)S(1)}, s32[1,1,12]{2,1,0:T(1,128)}, u32[]{:S(2)}) copy-start(s32[1,1,12]{2,1,0:T(1,128)} %param.11) | copy-start | bytes 148
  66.0 8.9 %copy-start.6 = (s32[128]{0:T(128)S(1)}, s32[128]{0:T(128)}, u32[]{:S(2)}) copy-start(s32[128]{0:T(128)} %param.9) | copy-start | bytes 1540
  67.0 0.8 copy-start.3
  78.2 61.1 %all-to-all-start.1 = ((bf16[12,16,4096]{2,1,0:T(8,128)(2,1)}), bf16[12,16,4096]{2,1,0:T(8,128)(2,1)}, u32[]{:S(2)}, u32[]{:S(2)}) async-start(bf16[12,16,4096]{2,1,0:T(8,128)(2,1)} %bitcast.18), calls=%async_computation.1 | async-start | bytes 3145728 | tf_op jit(solution)/shard_map/all_to_all | solution.py:43
  84.7 7.2 %collective-permute-start.8 = (f32[64,4096]{1,0:T(8,128)S(1)}, f32[64,4096]{1,0:T(8,128)S(1)}, u32[]{:S(2)}, u32[]{:S(2)}) collective-permute-start(f32[64,4096]{1,0:T(8,128)S(1)} %get-tuple-element.24), channel_id=1, source_target_pairs={{0,1},{1,0},{2,3},{3,2},{4,5},{5,4},{6,7},{7,6},{8,9},{9,8},{10,11... | collective-permute-start | bytes 3145736 | tf_op jit(solution)/shard_map/ppermute | solution.py:55
  92.0 8.7 %collective-permute-start.9 = (bf16[16,4096]{1,0:T(8,128)(2,1)S(1)}, bf16[16,4096]{1,0:T(8,128)(2,1)S(1)}, u32[]{:S(2)}, u32[]{:S(2)}) collective-permute-start(bf16[16,4096]{1,0:T(8,128)(2,1)S(1)} %get-tuple-element.26), channel_id=1, source_target_pairs={{0,2},{1,3},{2,4},{3,5},{4,6},{5,7},{6,0},{7,1},{8,10},{9,11},{10,... | collective-permute-start | bytes 393224 | tf_op jit(solution)/shard_map/ppermute | solution.py:55
  94.4 8.9 %collective-permute-start.10 = (bf16[16,4096]{1,0:T(8,128)(2,1)S(1)}, bf16[16,4096]{1,0:T(8,128)(2,1)S(1)}, u32[]{:S(2)}, u32[]{:S(2)}) collective-permute-start(bf16[16,4096]{1,0:T(8,128)(2,1)S(1)} %get-tuple-element.27), channel_id=1, source_target_pairs={{0,4},{1,5},{2,6},{3,7},{4,0},{5,1},{6,2},{7,3},{8,12},{9,13},{10,... | collective-permute-start | bytes 393224 | tf_op jit(solution)/shard_map/ppermute | solution.py:55
  98.7 8.3 %collective-permute-start.11 = (bf16[16,4096]{1,0:T(8,128)(2,1)S(1)}, bf16[16,4096]{1,0:T(8,128)(2,1)S(1)}, u32[]{:S(2)}, u32[]{:S(2)}) collective-permute-start(bf16[16,4096]{1,0:T(8,128)(2,1)S(1)} %get-tuple-element.28), channel_id=1, source_target_pairs={{0,6},{1,7},{2,0},{3,1},{4,2},{5,3},{6,4},{7,5},{8,14},{9,15},{10,... | collective-permute-start | bytes 393224 | tf_op jit(solution)/shard_map/ppermute | solution.py:55
  107.2 22.4 %collective-permute-start.12 = (f32[2,4096]{1,0:T(2,128)S(1)}, f32[2,4096]{1,0:T(2,128)S(1)}, u32[]{:S(2)}, u32[]{:S(2)}) collective-permute-start(f32[2,4096]{1,0:T(2,128)S(1)} %get-tuple-element.29), channel_id=1, source_target_pairs={{0,8},{1,9},{2,10},{3,11},{4,12},{5,13},{6,14},{7,15},{8,16},{9,17... | collective-permute-start | bytes 98312 | tf_op jit(solution)/shard_map/ppermute | solution.py:55
  110.7 21.2 %collective-permute-start.18 = (f32[2,4096]{1,0:T(2,128)S(1)}, f32[2,4096]{1,0:T(2,128)S(1)}, u32[]{:S(2)}, u32[]{:S(2)}) collective-permute-start(f32[2,4096]{1,0:T(2,128)S(1)} %get-tuple-element.30), channel_id=1, source_target_pairs={{0,56},{1,57},{2,58},{3,59},{4,60},{5,61},{6,62},{7,63},{8,32},{9,... | collective-permute-start | bytes 98312 | tf_op jit(solution)/shard_map/ppermute | solution.py:55
  117.4 19.9 %collective-permute-start.17 = (f32[2,4096]{1,0:T(2,128)S(1)}, f32[2,4096]{1,0:T(2,128)S(1)}, u32[]{:S(2)}, u32[]{:S(2)}) collective-permute-start(f32[2,4096]{1,0:T(2,128)S(1)} %get-tuple-element.31), channel_id=1, source_target_pairs={{0,48},{1,49},{2,50},{3,51},{4,52},{5,53},{6,54},{7,55},{8,56},{9,... | collective-permute-start | bytes 98312 | tf_op jit(solution)/shard_map/ppermute | solution.py:55
  119.7 17.7 %collective-permute-start.16 = (f32[2,4096]{1,0:T(2,128)S(1)}, f32[2,4096]{1,0:T(2,128)S(1)}, u32[]{:S(2)}, u32[]{:S(2)}) collective-permute-start(f32[2,4096]{1,0:T(2,128)S(1)} %get-tuple-element.32), channel_id=1, source_target_pairs={{0,40},{1,41},{2,42},{3,43},{4,44},{5,45},{6,46},{7,47},{8,48},{9,... | collective-permute-start | bytes 98312 | tf_op jit(solution)/shard_map/ppermute | solution.py:55
  124.8 12.5 %collective-permute-start.15 = (f32[2,4096]{1,0:T(2,128)S(1)}, f32[2,4096]{1,0:T(2,128)S(1)}, u32[]{:S(2)}, u32[]{:S(2)}) collective-permute-start(f32[2,4096]{1,0:T(2,128)S(1)} %get-tuple-element.33), channel_id=1, source_target_pairs={{0,32},{1,33},{2,34},{3,35},{4,36},{5,37},{6,38},{7,39},{8,40},{9,... | collective-permute-start | bytes 98312 | tf_op jit(solution)/shard_map/ppermute | solution.py:55
  129.6 7.8 %collective-permute-start.14 = (f32[2,4096]{1,0:T(2,128)S(1)}, f32[2,4096]{1,0:T(2,128)S(1)}, u32[]{:S(2)}, u32[]{:S(2)}) collective-permute-start(f32[2,4096]{1,0:T(2,128)S(1)} %get-tuple-element.34), channel_id=1, source_target_pairs={{0,24},{1,25},{2,26},{3,27},{4,28},{5,29},{6,30},{7,31},{8,0},{9,1... | collective-permute-start | bytes 98312 | tf_op jit(solution)/shard_map/ppermute | solution.py:55
  131.9 6.7 %collective-permute-start.13 = (f32[2,4096]{1,0:T(2,128)S(1)}, f32[2,4096]{1,0:T(2,128)S(1)}, u32[]{:S(2)}, u32[]{:S(2)}) collective-permute-start(f32[2,4096]{1,0:T(2,128)S(1)} %get-tuple-element.35), channel_id=1, source_target_pairs={{0,16},{1,17},{2,18},{3,19},{4,20},{5,21},{6,22},{7,23},{8,24},{9,... | collective-permute-start | bytes 98312 | tf_op jit(solution)/shard_map/ppermute | solution.py:55

commit v8 on v7

--- a/solution.py
+++ b/solution.py
@@ -9,7 +9,7 @@
 
 TILE = 8
 
-ORDERS = ((0, 3, 6, 9, 1, 4, 7, 10, 2, 5, 8, 11), (6, 9, 0, 3, 7, 10, 1, 8, 4, 11, 2, 5))
+ORDER = (0, 6, 1, 7, 2, 8, 3, 9, 4, 10, 5, 11)
 
 SHARPNESS = 50.0
 
@@ -32,14 +32,9 @@
     )
 
 
-def member(k):
-    first, second = ORDERS[0][k], ORDERS[1][k]
-    return first + lax.axis_index("pool") % 2 * (second - first)
-
-
 def trade(blocks):
     size = lax.axis_size("pool")
-    groups = [[z * size + p for z in ORDERS[p % 2]] for p in range(size)]
+    groups = [[z * size + p for z in ORDER] for p in range(size)]
     return lax.all_to_all(
         blocks, ("pb", "pool"), split_axis=0, concat_axis=0, tiled=True, axis_index_groups=groups
     )
@@ -72,7 +67,7 @@
     slots, peers = picks_ref.shape
     stores = []
     for j in range(peers * slots):
-        tile = buffer.at[picks[j % slots, member(j // slots)]]
+        tile = buffer.at[picks[j % slots, ORDER[j // slots]]]
         stores.append(pltpu.make_async_copy(tile, out_ref.at[j], store_sems.at[j]))
         stores[-1].start()
     for store in stores:
@@ -125,7 +120,7 @@
     lane = lax.broadcasted_iota(jnp.int32, (1, chosen_ref.shape[1]), 1)
     wanted = lane % TILE
     for j in range(peers * slots):
-        pick = picks_ref[j % slots, member(j // slots)]
+        pick = picks_ref[j % slots, ORDER[j // slots]]
         wanted = wanted + jnp.where(lane // TILE == j, pick * TILE, 0)
     rows = lax.broadcasted_iota(jnp.int32, chosen_ref.shape, 0)
     chosen_ref[...] = (rows == wanted).astype(jnp.float32).astype(jnp.bfloat16)
@@ -158,7 +153,7 @@
     slot = lax.broadcasted_iota(jnp.int32, (size, hard.shape[1]), 0) // TILE
     hard = jnp.concatenate(
         [
-            jnp.where(slot < counts_ref[0, member(i)], hard[i * size : (i + 1) * size], -jnp.inf)
+            jnp.where(slot < counts_ref[0, ORDER[i]], hard[i * size : (i + 1) * size], -jnp.inf)
             for i in range(peers)
         ],
         axis=0,

time: 143 us -> 141 us (0.986)
  starting transfers between devices: 90.9 us -> 88.3 us
    ppermute x19, starting transfers between devices: 69.5 us -> 65.3 us  [shifts(): lax.ppermute(block, 'pool', [(j, moved(j)) for j in range(lax.axis_size('...]
    all_to_all x2, starting transfers between devices: 21.4 us -> 23 us  [trade(): lax.all_to_all(blocks, ('pb', 'pool'), split_axis=0, concat_axis=0, tiled...]
  transfers between devices with their start and end apart: 21 -> 21, of which waited for: 9 -> 10; matrix products, arithmetic and copies ran while one was open for 3% -> 3% of each run, Pallas kernels for 4% -> 4%
where the time goes in v8:
time: 141 us; the launch traced here: 140 us
  starting transfers between devices  88.3 us (63%)
  waiting for transfers between devices  30.2 us (21%)
  Pallas kernels  14.2 us (10%)
  local copies, waits for them, and re-layouts  5.74 us (4%)
    ppermute x19, starting transfers between devices, shifts(): lax.ppermute(block, 'pool', [(j, moved(j)) for j in range(lax.axis_size('...  65.3 us
    all_to_all x2, starting transfers between devices, trade(): lax.all_to_all(blocks, ('pb', 'pool'), split_axis=0, concat_axis=0, tiled...  23 us
    ppermute x19, waiting for transfers between devices, shifts(): lax.ppermute(block, 'pool', [(j, moved(j)) for j in range(lax.axis_size('...  22.3 us
    all_to_all x2, waiting for transfers between devices, trade(): lax.all_to_all(blocks, ('pb', 'pool'), split_axis=0, concat_axis=0, tiled...  7.87 us
    pallas_call x1, Pallas kernels, weights(): pl.pallas_call(functools.partial(weights_kernel, chunk), out_shape=(pltpu...  3.31 us
    pallas_call x1, Pallas kernels, query_gradient(): pl.pallas_call(functools.partial(queries_kernel, chunk), out_shape=pltpu....  3.01 us
    concatenate x2, local copies, waits for them, and re-layouts, body(): jnp.concatenate([pooled] + [shifts(pooled, ((step, count, m),), -1) for m...  2.95 us
  transfers between devices with their start and end apart: 21, of which 10 were waited for; matrix products, arithmetic and copies ran while one was open for 3% of the time, Pallas kernels for 4%

profile of v8, /device:TPU:6, one launch (start us, length us, event | category | flops | bytes accessed | tf_op | source)
XLA Modules:
  0.0 140.3 jit_solution(12199536992851631238)
XLA Ops:
  0.6 2.6 %gather_tiles.1 = bf16[24,8,4096]{2,1,0:T(8,128)(2,1)} custom-call(s32[2,12]{1,0:T(2,128)} %bitcast.13, bf16[16,8,4096]{2,1,0:T(8,128)(2,1)} %bitcast.12), custom_call_target="tpu_custom_call" | custom-call | bytes 3145728 | tf_op jit(solution)/shard_map/gather_tiles/pallas_call | solution.py:80
  3.3 0.0 copy-start.7
  3.3 0.0 copy-start
  3.3 0.0 copy-start.4
  3.3 15.3 %all-to-all-start = ((bf16[12,16,4096]{2,1,0:T(8,128)(2,1)}), bf16[12,16,4096]{2,1,0:T(8,128)(2,1)S(1)}, u32[]{:S(2)}, u32[]{:S(2)}) async-start(bf16[12,16,4096]{2,1,0:T(8,128)(2,1)} %bitcast.17), calls=%async_computation | async-start | bytes 3145728 | tf_op jit(solution)/shard_map/all_to_all | solution.py:38
  18.6 3.5 %collective-permute-start.2 = (bf16[2,4096]{1,0:T(2,128)(2,1)S(1)}, bf16[2,4096]{1,0:T(2,128)(2,1)S(1)}, u32[]{:S(2)}, u32[]{:S(2)}) collective-permute-start(bf16[2,4096]{1,0:T(2,128)(2,1)S(1)} %copy-done.7), channel_id=1, source_target_pairs={{0,8},{1,9},{2,10},{3,11},{4,12},{5,13},{6,14},{7,15},{8,16},{9,17... | collective-permute-start | bytes 49160 | tf_op jit(solution)/shard_map/ppermute | solution.py:50
  22.1 4.5 %collective-permute-start.1 = (bf16[2,4096]{1,0:T(2,128)(2,1)S(1)}, bf16[2,4096]{1,0:T(2,128)(2,1)S(1)}, u32[]{:S(2)}, u32[]{:S(2)}) collective-permute-start(bf16[2,4096]{1,0:T(2,128)(2,1)S(1)} %copy-done.7), channel_id=1, source_target_pairs={{0,16},{1,17},{2,18},{3,19},{4,20},{5,21},{6,22},{7,23},{8,24},{9,... | collective-permute-start | bytes 49160 | tf_op jit(solution)/shard_map/ppermute | solution.py:50
  26.6 3.3 %collective-permute-start = (bf16[2,4096]{1,0:T(2,128)(2,1)S(1)}, bf16[2,4096]{1,0:T(2,128)(2,1)S(1)}, u32[]{:S(2)}, u32[]{:S(2)}) collective-permute-start(bf16[2,4096]{1,0:T(2,128)(2,1)S(1)} %copy-done.7), channel_id=1, source_target_pairs={{0,24},{1,25},{2,26},{3,27},{4,28},{5,29},{6,30},{7,31},{8,0},{9,1... | collective-permute-start | bytes 49160 | tf_op jit(solution)/shard_map/ppermute | solution.py:50
  29.9 0.0 collective-permute-done.2
  29.9 0.0 collective-permute-done.1
  29.9 2.3 %collective-permute-done = bf16[2,4096]{1,0:T(2,128)(2,1)S(1)} collective-permute-done((bf16[2,4096]{1,0:T(2,128)(2,1)S(1)}, bf16[2,4096]{1,0:T(2,128)(2,1)S(1)}, u32[]{:S(2)}, u32[]{:S(2)}) %collective-permute-start) | collective-permute-done | bytes 16416 | tf_op jit(solution)/shard_map/ppermute | solution.py:50
  32.3 0.1 pad_maximum_fusion
  32.3 5.9 %collective-permute-start.3 = (bf16[8,4096]{1,0:T(8,128)(2,1)S(1)}, bf16[8,4096]{1,0:T(8,128)(2,1)S(1)}, u32[]{:S(2)}, u32[]{:S(2)}) collective-permute-start(bf16[8,4096]{1,0:T(8,128)(2,1)S(1)} %pad_maximum_fusion), channel_id=1, source_target_pairs={{0,32},{1,33},{2,34},{3,35},{4,36},{5,37},{6,38},{7,39},{8,40},{9,... | collective-permute-start | bytes 196616 | tf_op jit(solution)/shard_map/ppermute | solution.py:50
  38.3 4.3 %collective-permute-done.3 = bf16[8,4096]{1,0:T(8,128)(2,1)S(1)} collective-permute-done((bf16[8,4096]{1,0:T(8,128)(2,1)S(1)}, bf16[8,4096]{1,0:T(8,128)(2,1)S(1)}, u32[]{:S(2)}, u32[]{:S(2)}) %collective-permute-start.3) | collective-permute-done | bytes 65568 | tf_op jit(solution)/shard_map/ppermute | solution.py:50
  42.6 0.1 concatenate.12
  42.7 2.4 %collective-permute-start.6 = (bf16[16,4096]{1,0:T(8,128)(2,1)S(1)}, bf16[16,4096]{1,0:T(8,128)(2,1)S(1)}, u32[]{:S(2)}, u32[]{:S(2)}) collective-permute-start(bf16[16,4096]{1,0:T(8,128)(2,1)S(1)} %concatenate.12), channel_id=1, source_target_pairs={{0,2},{1,3},{2,4},{3,5},{4,6},{5,7},{6,0},{7,1},{8,10},{9,11},{10,... | collective-permute-start | bytes 393224 | tf_op jit(solution)/shard_map/ppermute | solution.py:50
  45.1 4.3 %collective-permute-start.5 = (bf16[16,4096]{1,0:T(8,128)(2,1)S(1)}, bf16[16,4096]{1,0:T(8,128)(2,1)S(1)}, u32[]{:S(2)}, u32[]{:S(2)}) collective-permute-start(bf16[16,4096]{1,0:T(8,128)(2,1)S(1)} %concatenate.12), channel_id=1, source_target_pairs={{0,4},{1,5},{2,6},{3,7},{4,0},{5,1},{6,2},{7,3},{8,12},{9,13},{10,... | collective-permute-start | bytes 393224 | tf_op jit(solution)/shard_map/ppermute | solution.py:50
  49.4 1.9 %collective-permute-start.4 = (bf16[16,4096]{1,0:T(8,128)(2,1)S(1)}, bf16[16,4096]{1,0:T(8,128)(2,1)}, u32[]{:S(2)}, u32[]{:S(2)}) collective-permute-start(bf16[16,4096]{1,0:T(8,128)(2,1)S(1)} %concatenate.12), channel_id=1, source_target_pairs={{0,6},{1,7},{2,0},{3,1},{4,2},{5,3},{6,4},{7,5},{8,14},{9,15},{10,... | collective-permute-start | bytes 393224 | tf_op jit(solution)/shard_map/ppermute | solution.py:50
  51.4 0.0 collective-permute-done.6
  51.4 0.0 copy-start.8
  51.4 2.8 %collective-permute-done.5 = bf16[16,4096]{1,0:T(8,128)(2,1)S(1)} collective-permute-done((bf16[16,4096]{1,0:T(8,128)(2,1)S(1)}, bf16[16,4096]{1,0:T(8,128)(2,1)S(1)}, u32[]{:S(2)}, u32[]{:S(2)}) %collective-permute-start.5) | collective-permute-done | bytes 131104 | tf_op jit(solution)/shard_map/ppermute | solution.py:50
  54.2 0.7 copy-done.9
  54.9 2.8 %collective-permute-done.4 = bf16[16,4096]{1,0:T(8,128)(2,1)} collective-permute-done((bf16[16,4096]{1,0:T(8,128)(2,1)S(1)}, bf16[16,4096]{1,0:T(8,128)(2,1)}, u32[]{:S(2)}, u32[]{:S(2)}) %collective-permute-start.4) | collective-permute-done | bytes 131104 | tf_op jit(solution)/shard_map/ppermute | solution.py:50
  57.6 2.8 %concatenate.13.keys_ref.pool_near_ref = bf16[64,4096]{1,0:T(8,128)(2,1)S(1)} concatenate(bf16[2,4096]{1,0:T(2,128)(2,1)S(1)} %copy-done.7, bf16[2,4096]{1,0:T(2,128)(2,1)S(1)} %collective-permute-done, bf16[2,4096]{1,0:T(2,128)(2,1)S(1)} %collective-permute-done.1, bf16[2,4096]{1,0:T(2,128)(2,1)S(1)} %collective-permute-done.2, bf16[8,4096]{1,0:T(8,128)(2,1)S(1)} %collective-permute-done.3, ...), dimensions={0} | concatenate | bytes 1048576 | tf_op jit(solution)/shard_map/concatenate | solution.py:362
  60.5 0.0 copy-start.2
  60.5 1.9 %collective-permute-start.7 = (bf16[64,4096]{1,0:T(8,128)(2,1)S(1)}, bf16[64,4096]{1,0:T(8,128)(2,1)S(1)}, u32[]{:S(2)}, u32[]{:S(2)}) collective-permute-start(bf16[64,4096]{1,0:T(8,128)(2,1)S(1)} %concatenate.13.keys_ref.pool_near_ref), channel_id=1, source_target_pairs={{0,1},{1,0},{2,3},{3,2},{4,5},{5,4},{6,7},{7,6},{8,9},{9,8},{10,11... | collective-permute-start | bytes 1572872 | tf_op jit(solution)/shard_map/ppermute | solution.py:50
  62.4 0.0 copy-start.1
  62.4 1.2 copy-done.1
  63.7 1.0 local_scores.1
  64.6 0.0 copy-start.5
  64.7 0.0 copy-start.6
  64.7 0.5 scores.2.near_ref
  65.2 0.0 collective-permute-done.7.keys_ref.pool_far_ref
  65.2 0.5 scores.3.far_ref
  65.7 0.8 copy-done.3
  66.5 6.1 %all-to-all-done = bf16[12,16,4096]{2,1,0:T(8,128)(2,1)S(1)} async-done(((bf16[12,16,4096]{2,1,0:T(8,128)(2,1)}), bf16[12,16,4096]{2,1,0:T(8,128)(2,1)S(1)}, u32[]{:S(2)}, u32[]{:S(2)}) %all-to-all-start) | async-done | bytes 1572896 | tf_op jit(solution)/shard_map/all_to_all | solution.py:38
  72.6 3.3 %weights.1 = (bf16[192,4096]{1,0:T(8,128)(2,1)}, bf16[128,128]{1,0:T(8,128)(2,1)S(1)}, bf16[64,128]{1,0:T(8,128)(2,1)S(1)}, bf16[64,128]{1,0:T(8,128)(2,1)S(1)}, bf16[192,128]{1,0:T(8,128)(2,1)S(1)}) custom-call(bf16[128,4096]{1,0:T(8,128)(2,1)S(1)} %copy-done, bf16[192,4096]{1,0:T(8,128)(2,1)S(1)} %bitcast.10, f32[128,128]{1,0:T(8,128)S(1)} %get-tuple-element.16.local_ref, ...), custom_call_target="tpu_custom_call" | custom-call | flops 1048576 | bytes 1048576 | tf_op jit(solution)/shard_map/weights/pallas_call | solution.py:189
  75.9 7.7 %all-to-all-start.1 = ((bf16[12,16,4096]{2,1,0:T(8,128)(2,1)}), bf16[12,16,4096]{2,1,0:T(8,128)(2,1)}, u32[]{:S(2)}, u32[]{:S(2)}) async-start(bf16[12,16,4096]{2,1,0:T(8,128)(2,1)} %bitcast.18), calls=%async_computation.1 | async-start | bytes 3145728 | tf_op jit(solution)/shard_map/all_to_all | solution.py:38
  83.6 0.4 pool_terms.1
  84.1 1.9 %collective-permute-start.8 = (f32[64,4096]{1,0:T(8,128)S(1)}, f32[64,4096]{1,0:T(8,128)S(1)}, u32[]{:S(2)}, u32[]{:S(2)}) collective-permute-start(f32[64,4096]{1,0:T(8,128)S(1)} %get-tuple-element.24), channel_id=1, source_target_pairs={{0,1},{1,0},{2,3},{3,2},{4,5},{5,4},{6,7},{7,6},{8,9},{9,8},{10,11... | collective-permute-start | bytes 3145736 | tf_op jit(solution)/shard_map/ppermute | solution.py:50
  86.0 2.6 %collective-permute-done.8.sent_ref = f32[64,4096]{1,0:T(8,128)S(1)} collective-permute-done((f32[64,4096]{1,0:T(8,128)S(1)}, f32[64,4096]{1,0:T(8,128)S(1)}, u32[]{:S(2)}, u32[]{:S(2)}) %collective-permute-start.8) | collective-permute-done | bytes 1048608 | tf_op jit(solution)/shard_map/ppermute | solution.py:50
  88.6 0.1 join.1
  88.7 2.4 %collective-permute-start.9 = (bf16[16,4096]{1,0:T(8,128)(2,1)S(1)}, bf16[16,4096]{1,0:T(8,128)(2,1)S(1)}, u32[]{:S(2)}, u32[]{:S(2)}) collective-permute-start(bf16[16,4096]{1,0:T(8,128)(2,1)S(1)} %get-tuple-element.26), channel_id=1, source_target_pairs={{0,2},{1,3},{2,4},{3,5},{4,6},{5,7},{6,0},{7,1},{8,10},{9,11},{10,... | collective-permute-start | bytes 393224 | tf_op jit(solution)/shard_map/ppermute | solution.py:50
  91.1 4.3 %collective-permute-start.10 = (bf16[16,4096]{1,0:T(8,128)(2,1)S(1)}, bf16[16,4096]{1,0:T(8,128)(2,1)S(1)}, u32[]{:S(2)}, u32[]{:S(2)}) collective-permute-start(bf16[16,4096]{1,0:T(8,128)(2,1)S(1)} %get-tuple-element.27), channel_id=1, source_target_pairs={{0,4},{1,5},{2,6},{3,7},{4,0},{5,1},{6,2},{7,3},{8,12},{9,13},{10,... | collective-permute-start | bytes 393224 | tf_op jit(solution)/shard_map/ppermute | solution.py:50
  95.5 1.9 %collective-permute-start.11 = (bf16[16,4096]{1,0:T(8,128)(2,1)S(1)}, bf16[16,4096]{1,0:T(8,128)(2,1)S(1)}, u32[]{:S(2)}, u32[]{:S(2)}) collective-permute-start(bf16[16,4096]{1,0:T(8,128)(2,1)S(1)} %get-tuple-element.28), channel_id=1, source_target_pairs={{0,6},{1,7},{2,0},{3,1},{4,2},{5,3},{6,4},{7,5},{8,14},{9,15},{10,... | collective-permute-start | bytes 393224 | tf_op jit(solution)/shard_map/ppermute | solution.py:50
  97.4 0.0 collective-permute-done.9
  97.4 2.4 %collective-permute-done.10 = bf16[16,4096]{1,0:T(8,128)(2,1)S(1)} collective-permute-done((bf16[16,4096]{1,0:T(8,128)(2,1)S(1)}, bf16[16,4096]{1,0:T(8,128)(2,1)S(1)}, u32[]{:S(2)}, u32[]{:S(2)}) %collective-permute-start.10) | collective-permute-done | bytes 131104 | tf_op jit(solution)/shard_map/ppermute | solution.py:50
  99.8 3.8 %collective-permute-done.11 = bf16[16,4096]{1,0:T(8,128)(2,1)S(1)} collective-permute-done((bf16[16,4096]{1,0:T(8,128)(2,1)S(1)}, bf16[16,4096]{1,0:T(8,128)(2,1)S(1)}, u32[]{:S(2)}, u32[]{:S(2)}) %collective-permute-start.11) | collective-permute-done | bytes 131104 | tf_op jit(solution)/shard_map/ppermute | solution.py:50
  103.6 0.1 convert_add_fusion
  103.6 0.1 fusion.5
  103.7 3.5 %collective-permute-start.12 = (f32[2,4096]{1,0:T(2,128)S(1)}, f32[2,4096]{1,0:T(2,128)S(1)}, u32[]{:S(2)}, u32[]{:S(2)}) collective-permute-start(f32[2,4096]{1,0:T(2,128)S(1)} %get-tuple-element.29), channel_id=1, source_target_pairs={{0,8},{1,9},{2,10},{3,11},{4,12},{5,13},{6,14},{7,15},{8,16},{9,17... | collective-permute-start | bytes 98312 | tf_op jit(solution)/shard_map/ppermute | solution.py:50
  107.2 6.7 %collective-permute-start.18 = (f32[2,4096]{1,0:T(2,128)S(1)}, f32[2,4096]{1,0:T(2,128)S(1)}, u32[]{:S(2)}, u32[]{:S(2)}) collective-permute-start(f32[2,4096]{1,0:T(2,128)S(1)} %get-tuple-element.30), channel_id=1, source_target_pairs={{0,56},{1,57},{2,58},{3,59},{4,60},{5,61},{6,62},{7,63},{8,32},{9,... | collective-permute-start | bytes 98312 | tf_op jit(solution)/shard_map/ppermute | solution.py:50
  113.9 2.2 %collective-permute-start.17 = (f32[2,4096]{1,0:T(2,128)S(1)}, f32[2,4096]{1,0:T(2,128)S(1)}, u32[]{:S(2)}, u32[]{:S(2)}) collective-permute-start(f32[2,4096]{1,0:T(2,128)S(1)} %get-tuple-element.31), channel_id=1, source_target_pairs={{0,48},{1,49},{2,50},{3,51},{4,52},{5,53},{6,54},{7,55},{8,56},{9,... | collective-permute-start | bytes 98312 | tf_op jit(solution)/shard_map/ppermute | solution.py:50
  116.2 5.2 %collective-permute-start.16 = (f32[2,4096]{1,0:T(2,128)S(1)}, f32[2,4096]{1,0:T(2,128)S(1)}, u32[]{:S(2)}, u32[]{:S(2)}) collective-permute-start(f32[2,4096]{1,0:T(2,128)S(1)} %get-tuple-element.32), channel_id=1, source_target_pairs={{0,40},{1,41},{2,42},{3,43},{4,44},{5,45},{6,46},{7,47},{8,48},{9,... | collective-permute-start | bytes 98312 | tf_op jit(solution)/shard_map/ppermute | solution.py:50
  121.3 4.7 %collective-permute-start.15 = (f32[2,4096]{1,0:T(2,128)S(1)}, f32[2,4096]{1,0:T(2,128)S(1)}, u32[]{:S(2)}, u32[]{:S(2)}) collective-permute-start(f32[2,4096]{1,0:T(2,128)S(1)} %get-tuple-element.33), channel_id=1, source_target_pairs={{0,32},{1,33},{2,34},{3,35},{4,36},{5,37},{6,38},{7,39},{8,40},{9,... | collective-permute-start | bytes 98312 | tf_op jit(solution)/shard_map/ppermute | solution.py:50
  126.1 2.4 %collective-permute-start.14 = (f32[2,4096]{1,0:T(2,128)S(1)}, f32[2,4096]{1,0:T(2,128)S(1)}, u32[]{:S(2)}, u32[]{:S(2)}) collective-permute-start(f32[2,4096]{1,0:T(2,128)S(1)} %get-tuple-element.34), channel_id=1, source_target_pairs={{0,24},{1,25},{2,26},{3,27},{4,28},{5,29},{6,30},{7,31},{8,0},{9,1... | collective-permute-start | bytes 98312 | tf_op jit(solution)/shard_map/ppermute | solution.py:50
  128.4 0.0 collective-permute-done.18
  128.4 2.4 %collective-permute-start.13 = (f32[2,4096]{1,0:T(2,128)S(1)}, f32[2,4096]{1,0:T(2,128)S(1)}, u32[]{:S(2)}, u32[]{:S(2)}) collective-permute-start(f32[2,4096]{1,0:T(2,128)S(1)} %get-tuple-element.35), channel_id=1, source_target_pairs={{0,16},{1,17},{2,18},{3,19},{4,20},{5,21},{6,22},{7,23},{8,24},{9,... | collective-permute-start | bytes 98312 | tf_op jit(solution)/shard_map/ppermute | solution.py:50
  130.8 3.0 %query_gradient.1 = bf16[128,4096]{1,0:T(8,128)(2,1)} custom-call(bf16[192,128]{1,0:T(8,128)(2,1)S(1)} %get-tuple-element.17.hard_weight_ref, bf16[128,128]{1,0:T(8,128)(2,1)S(1)} %get-tuple-element.18.local_ref.weight_ref, bf16[64,128]{1,0:T(8,128)(2,1)S(1)} %get-tuple-element.19.near_ref, bf16[64,128]{1,0:T(8,128)(2,1)S(1)} %get-tuple-element.20.far_ref, ...), custom_call_target="tpu_custom_call" | custom-call | flops 1048576 | bytes 1048576 | tf_op jit(solution)/shard_map/query_gradient/pallas_call | solution.py:286
  133.9 0.0 collective-permute-done.16
  133.9 1.3 collective-permute-done.13
  135.2 0.7 add_convert_fusion
  135.8 1.7 %all-to-all-done.1 = bf16[12,16,4096]{2,1,0:T(8,128)(2,1)} async-done(((bf16[12,16,4096]{2,1,0:T(8,128)(2,1)}), bf16[12,16,4096]{2,1,0:T(8,128)(2,1)}, u32[]{:S(2)}, u32[]{:S(2)}) %all-to-all-start.1) | async-done | bytes 1572896 | tf_op jit(solution)/shard_map/all_to_all | solution.py:38
  137.5 2.7 %passage_gradient.1 = bf16[128,4096]{1,0:T(8,128)(2,1)} custom-call(bf16[128,128]{1,0:T(8,128)(2,1)S(1)} %get-tuple-element.18.local_ref.weight_ref, bf16[128,4096]{1,0:T(8,128)(2,1)S(1)} %copy-done, bf16[128,192]{1,0:T(8,128)(2,1)S(1)} %get-tuple-element.21.chosen_ref, bf16[192,4096]{1,0:T(8,128)(2,1)} %bitcast.9.returned_ref), custom_call_target="tpu_custom_call" | custom-call | flops 1048576 | bytes 1048576 | tf_op jit(solution)/shard_map/passage_gradient/pallas_call | solution.py:336
  (13 shorter events, 0.0 us)
Async XLA Ops:
  3.3 15.3 %copy-start.7 = (bf16[2,4096]{1,0:T(2,128)(2,1)S(1)}, bf16[2,4096]{1,0:T(2,128)(2,1)}, u32[]{:S(2)}) copy-start(bf16[2,4096]{1,0:T(2,128)(2,1)} %param.8) | copy-start | bytes 49156
  3.3 59.1 %copy-start = (bf16[128,4096]{1,0:T(8,128)(2,1)S(1)}, bf16[128,4096]{1,0:T(8,128)(2,1)}, u32[]{:S(2)}) copy-start(bf16[128,4096]{1,0:T(8,128)(2,1)} %queries_ref.11) | copy-start | bytes 3145732
  3.3 59.1 %copy-start.4 = (s32[1,1,12,2]{2,3,1,0:T(2,128)S(1)}, s32[1,1,12,2]{2,3,1,0:T(2,128)}, u32[]{:S(2)}) copy-start(s32[1,1,12,2]{2,3,1,0:T(2,128)} %param.10) | copy-start | bytes 292
  3.3 69.3 %all-to-all-start = ((bf16[12,16,4096]{2,1,0:T(8,128)(2,1)}), bf16[12,16,4096]{2,1,0:T(8,128)(2,1)S(1)}, u32[]{:S(2)}, u32[]{:S(2)}) async-start(bf16[12,16,4096]{2,1,0:T(8,128)(2,1)} %bitcast.17), calls=%async_computation | async-start | bytes 3145728 | tf_op jit(solution)/shard_map/all_to_all | solution.py:38
  18.6 11.3 %collective-permute-start.2 = (bf16[2,4096]{1,0:T(2,128)(2,1)S(1)}, bf16[2,4096]{1,0:T(2,128)(2,1)S(1)}, u32[]{:S(2)}, u32[]{:S(2)}) collective-permute-start(bf16[2,4096]{1,0:T(2,128)(2,1)S(1)} %copy-done.7), channel_id=1, source_target_pairs={{0,8},{1,9},{2,10},{3,11},{4,12},{5,13},{6,14},{7,15},{8,16},{9,17... | collective-permute-start | bytes 49160 | tf_op jit(solution)/shard_map/ppermute | solution.py:50
  22.1 7.8 %collective-permute-start.1 = (bf16[2,4096]{1,0:T(2,128)(2,1)S(1)}, bf16[2,4096]{1,0:T(2,128)(2,1)S(1)}, u32[]{:S(2)}, u32[]{:S(2)}) collective-permute-start(bf16[2,4096]{1,0:T(2,128)(2,1)S(1)} %copy-done.7), channel_id=1, source_target_pairs={{0,16},{1,17},{2,18},{3,19},{4,20},{5,21},{6,22},{7,23},{8,24},{9,... | collective-permute-start | bytes 49160 | tf_op jit(solution)/shard_map/ppermute | solution.py:50
  26.6 5.6 %collective-permute-start = (bf16[2,4096]{1,0:T(2,128)(2,1)S(1)}, bf16[2,4096]{1,0:T(2,128)(2,1)S(1)}, u32[]{:S(2)}, u32[]{:S(2)}) collective-permute-start(bf16[2,4096]{1,0:T(2,128)(2,1)S(1)} %copy-done.7), channel_id=1, source_target_pairs={{0,24},{1,25},{2,26},{3,27},{4,28},{5,29},{6,30},{7,31},{8,0},{9,1... | collective-permute-start | bytes 49160 | tf_op jit(solution)/shard_map/ppermute | solution.py:50
  32.3 10.3 %collective-permute-start.3 = (bf16[8,4096]{1,0:T(8,128)(2,1)S(1)}, bf16[8,4096]{1,0:T(8,128)(2,1)S(1)}, u32[]{:S(2)}, u32[]{:S(2)}) collective-permute-start(bf16[8,4096]{1,0:T(8,128)(2,1)S(1)} %pad_maximum_fusion), channel_id=1, source_target_pairs={{0,32},{1,33},{2,34},{3,35},{4,36},{5,37},{6,38},{7,39},{8,40},{9,... | collective-permute-start | bytes 196616 | tf_op jit(solution)/shard_map/ppermute | solution.py:50
  42.7 8.7 %collective-permute-start.6 = (bf16[16,4096]{1,0:T(8,128)(2,1)S(1)}, bf16[16,4096]{1,0:T(8,128)(2,1)S(1)}, u32[]{:S(2)}, u32[]{:S(2)}) collective-permute-start(bf16[16,4096]{1,0:T(8,128)(2,1)S(1)} %concatenate.12), channel_id=1, source_target_pairs={{0,2},{1,3},{2,4},{3,5},{4,6},{5,7},{6,0},{7,1},{8,10},{9,11},{10,... | collective-permute-start | bytes 393224 | tf_op jit(solution)/shard_map/ppermute | solution.py:50
  45.1 9.1 %collective-permute-start.5 = (bf16[16,4096]{1,0:T(8,128)(2,1)S(1)}, bf16[16,4096]{1,0:T(8,128)(2,1)S(1)}, u32[]{:S(2)}, u32[]{:S(2)}) collective-permute-start(bf16[16,4096]{1,0:T(8,128)(2,1)S(1)} %concatenate.12), channel_id=1, source_target_pairs={{0,4},{1,5},{2,6},{3,7},{4,0},{5,1},{6,2},{7,3},{8,12},{9,13},{10,... | collective-permute-start | bytes 393224 | tf_op jit(solution)/shard_map/ppermute | solution.py:50
  49.4 8.2 %collective-permute-start.4 = (bf16[16,4096]{1,0:T(8,128)(2,1)S(1)}, bf16[16,4096]{1,0:T(8,128)(2,1)}, u32[]{:S(2)}, u32[]{:S(2)}) collective-permute-start(bf16[16,4096]{1,0:T(8,128)(2,1)S(1)} %concatenate.12), channel_id=1, source_target_pairs={{0,6},{1,7},{2,0},{3,1},{4,2},{5,3},{6,4},{7,5},{8,14},{9,15},{10,... | collective-permute-start | bytes 393224 | tf_op jit(solution)/shard_map/ppermute | solution.py:50
  51.4 2.8 %copy-start.8 = (bf16[16,4096]{1,0:T(8,128)(2,1)}, bf16[16,4096]{1,0:T(8,128)(2,1)S(1)}, u32[]{:S(2)}) copy-start(bf16[16,4096]{1,0:T(8,128)(2,1)S(1)} %collective-permute-done.6) | copy-start | bytes 393220
  54.2 0.7 copy-start.9
  60.5 4.7 %copy-start.2 = (bf16[64,4096]{1,0:T(8,128)(2,1)}, bf16[64,4096]{1,0:T(8,128)(2,1)S(1)}, u32[]{:S(2)}) copy-start(bf16[64,4096]{1,0:T(8,128)(2,1)S(1)} %concatenate.13.keys_ref.pool_near_ref) | copy-start | bytes 1572868
  60.5 4.7 %collective-permute-start.7 = (bf16[64,4096]{1,0:T(8,128)(2,1)S(1)}, bf16[64,4096]{1,0:T(8,128)(2,1)S(1)}, u32[]{:S(2)}, u32[]{:S(2)}) collective-permute-start(bf16[64,4096]{1,0:T(8,128)(2,1)S(1)} %concatenate.13.keys_ref.pool_near_ref), channel_id=1, source_target_pairs={{0,1},{1,0},{2,3},{3,2},{4,5},{5,4},{6,7},{7,6},{8,9},{9,8},{10,11... | collective-permute-start | bytes 1572872 | tf_op jit(solution)/shard_map/ppermute | solution.py:50
  62.4 1.2 copy-start.1
  64.6 8.0 %copy-start.5 = (s32[1,1,12]{2,1,0:T(1,128)S(1)}, s32[1,1,12]{2,1,0:T(1,128)}, u32[]{:S(2)}) copy-start(s32[1,1,12]{2,1,0:T(1,128)} %param.11) | copy-start | bytes 148
  64.7 8.0 %copy-start.6 = (s32[128]{0:T(128)S(1)}, s32[128]{0:T(128)}, u32[]{:S(2)}) copy-start(s32[128]{0:T(128)} %param.9) | copy-start | bytes 1540
  65.7 0.8 copy-start.3
  75.9 61.6 %all-to-all-start.1 = ((bf16[12,16,4096]{2,1,0:T(8,128)(2,1)}), bf16[12,16,4096]{2,1,0:T(8,128)(2,1)}, u32[]{:S(2)}, u32[]{:S(2)}) async-start(bf16[12,16,4096]{2,1,0:T(8,128)(2,1)} %bitcast.18), calls=%async_computation.1 | async-start | bytes 3145728 | tf_op jit(solution)/shard_map/all_to_all | solution.py:38
  84.1 4.6 %collective-permute-start.8 = (f32[64,4096]{1,0:T(8,128)S(1)}, f32[64,4096]{1,0:T(8,128)S(1)}, u32[]{:S(2)}, u32[]{:S(2)}) collective-permute-start(f32[64,4096]{1,0:T(8,128)S(1)} %get-tuple-element.24), channel_id=1, source_target_pairs={{0,1},{1,0},{2,3},{3,2},{4,5},{5,4},{6,7},{7,6},{8,9},{9,8},{10,11... | collective-permute-start | bytes 3145736 | tf_op jit(solution)/shard_map/ppermute | solution.py:50
  88.7 8.7 %collective-permute-start.9 = (bf16[16,4096]{1,0:T(8,128)(2,1)S(1)}, bf16[16,4096]{1,0:T(8,128)(2,1)S(1)}, u32[]{:S(2)}, u32[]{:S(2)}) collective-permute-start(bf16[16,4096]{1,0:T(8,128)(2,1)S(1)} %get-tuple-element.26), channel_id=1, source_target_pairs={{0,2},{1,3},{2,4},{3,5},{4,6},{5,7},{6,0},{7,1},{8,10},{9,11},{10,... | collective-permute-start | bytes 393224 | tf_op jit(solution)/shard_map/ppermute | solution.py:50
  91.1 8.7 %collective-permute-start.10 = (bf16[16,4096]{1,0:T(8,128)(2,1)S(1)}, bf16[16,4096]{1,0:T(8,128)(2,1)S(1)}, u32[]{:S(2)}, u32[]{:S(2)}) collective-permute-start(bf16[16,4096]{1,0:T(8,128)(2,1)S(1)} %get-tuple-element.27), channel_id=1, source_target_pairs={{0,4},{1,5},{2,6},{3,7},{4,0},{5,1},{6,2},{7,3},{8,12},{9,13},{10,... | collective-permute-start | bytes 393224 | tf_op jit(solution)/shard_map/ppermute | solution.py:50
  95.5 8.1 %collective-permute-start.11 = (bf16[16,4096]{1,0:T(8,128)(2,1)S(1)}, bf16[16,4096]{1,0:T(8,128)(2,1)S(1)}, u32[]{:S(2)}, u32[]{:S(2)}) collective-permute-start(bf16[16,4096]{1,0:T(8,128)(2,1)S(1)} %get-tuple-element.28), channel_id=1, source_target_pairs={{0,6},{1,7},{2,0},{3,1},{4,2},{5,3},{6,4},{7,5},{8,14},{9,15},{10,... | collective-permute-start | bytes 393224 | tf_op jit(solution)/shard_map/ppermute | solution.py:50
  103.7 22.4 %collective-permute-start.12 = (f32[2,4096]{1,0:T(2,128)S(1)}, f32[2,4096]{1,0:T(2,128)S(1)}, u32[]{:S(2)}, u32[]{:S(2)}) collective-permute-start(f32[2,4096]{1,0:T(2,128)S(1)} %get-tuple-element.29), channel_id=1, source_target_pairs={{0,8},{1,9},{2,10},{3,11},{4,12},{5,13},{6,14},{7,15},{8,16},{9,17... | collective-permute-start | bytes 98312 | tf_op jit(solution)/shard_map/ppermute | solution.py:50
  107.2 21.2 %collective-permute-start.18 = (f32[2,4096]{1,0:T(2,128)S(1)}, f32[2,4096]{1,0:T(2,128)S(1)}, u32[]{:S(2)}, u32[]{:S(2)}) collective-permute-start(f32[2,4096]{1,0:T(2,128)S(1)} %get-tuple-element.30), channel_id=1, source_target_pairs={{0,56},{1,57},{2,58},{3,59},{4,60},{5,61},{6,62},{7,63},{8,32},{9,... | collective-permute-start | bytes 98312 | tf_op jit(solution)/shard_map/ppermute | solution.py:50
  113.9 19.9 %collective-permute-start.17 = (f32[2,4096]{1,0:T(2,128)S(1)}, f32[2,4096]{1,0:T(2,128)S(1)}, u32[]{:S(2)}, u32[]{:S(2)}) collective-permute-start(f32[2,4096]{1,0:T(2,128)S(1)} %get-tuple-element.31), channel_id=1, source_target_pairs={{0,48},{1,49},{2,50},{3,51},{4,52},{5,53},{6,54},{7,55},{8,56},{9,... | collective-permute-start | bytes 98312 | tf_op jit(solution)/shard_map/ppermute | solution.py:50
  116.2 17.7 %collective-permute-start.16 = (f32[2,4096]{1,0:T(2,128)S(1)}, f32[2,4096]{1,0:T(2,128)S(1)}, u32[]{:S(2)}, u32[]{:S(2)}) collective-permute-start(f32[2,4096]{1,0:T(2,128)S(1)} %get-tuple-element.32), channel_id=1, source_target_pairs={{0,40},{1,41},{2,42},{3,43},{4,44},{5,45},{6,46},{7,47},{8,48},{9,... | collective-permute-start | bytes 98312 | tf_op jit(solution)/shard_map/ppermute | solution.py:50
  121.3 12.5 %collective-permute-start.15 = (f32[2,4096]{1,0:T(2,128)S(1)}, f32[2,4096]{1,0:T(2,128)S(1)}, u32[]{:S(2)}, u32[]{:S(2)}) collective-permute-start(f32[2,4096]{1,0:T(2,128)S(1)} %get-tuple-element.33), channel_id=1, source_target_pairs={{0,32},{1,33},{2,34},{3,35},{4,36},{5,37},{6,38},{7,39},{8,40},{9,... | collective-permute-start | bytes 98312 | tf_op jit(solution)/shard_map/ppermute | solution.py:50
  126.1 7.8 %collective-permute-start.14 = (f32[2,4096]{1,0:T(2,128)S(1)}, f32[2,4096]{1,0:T(2,128)S(1)}, u32[]{:S(2)}, u32[]{:S(2)}) collective-permute-start(f32[2,4096]{1,0:T(2,128)S(1)} %get-tuple-element.34), channel_id=1, source_target_pairs={{0,24},{1,25},{2,26},{3,27},{4,28},{5,29},{6,30},{7,31},{8,0},{9,1... | collective-permute-start | bytes 98312 | tf_op jit(solution)/shard_map/ppermute | solution.py:50
  128.4 6.7 %collective-permute-start.13 = (f32[2,4096]{1,0:T(2,128)S(1)}, f32[2,4096]{1,0:T(2,128)S(1)}, u32[]{:S(2)}, u32[]{:S(2)}) collective-permute-start(f32[2,4096]{1,0:T(2,128)S(1)} %get-tuple-element.35), channel_id=1, source_target_pairs={{0,16},{1,17},{2,18},{3,19},{4,20},{5,21},{6,22},{7,23},{8,24},{9,... | collective-permute-start | bytes 98312 | tf_op jit(solution)/shard_map/ppermute | solution.py:50

commit v9 on v7

--- a/solution.py
+++ b/solution.py
@@ -9,7 +9,7 @@
 
 TILE = 8
 
-ORDERS = ((0, 3, 6, 9, 1, 4, 7, 10, 2, 5, 8, 11), (6, 9, 0, 3, 7, 10, 1, 8, 4, 11, 2, 5))
+ORDERS = ((0, 6, 1, 7, 2, 8, 3, 9, 4, 10, 5, 11), (0, 6, 3, 9, 1, 7, 4, 10, 2, 8, 5, 11))
 
 SHARPNESS = 50.0
 

time: 143 us -> 141 us (0.986)
  starting transfers between devices: 90.9 us -> 88.8 us
    ppermute x19, starting transfers between devices: 69.5 us -> 65.3 us  [shifts(): lax.ppermute(block, 'pool', [(j, moved(j)) for j in range(lax.axis_size('...]
    all_to_all x2, starting transfers between devices: 21.4 us -> 23.5 us  [trade(): lax.all_to_all(blocks, ('pb', 'pool'), split_axis=0, concat_axis=0, tiled...]
  transfers between devices with their start and end apart: 21 -> 21, of which waited for: 9 -> 10; matrix products, arithmetic and copies ran while one was open for 3% -> 3% of each run, Pallas kernels for 4% -> 4%
where the time goes in v9:
time: 141 us; the launch traced here: 140 us
  starting transfers between devices  88.8 us (63%)
  waiting for transfers between devices  29 us (21%)
  Pallas kernels  14.1 us (10%)
  local copies, waits for them, and re-layouts  5.74 us (4%)
    ppermute x19, starting transfers between devices, shifts(): lax.ppermute(block, 'pool', [(j, moved(j)) for j in range(lax.axis_size('...  65.3 us
    all_to_all x2, starting transfers between devices, trade(): lax.all_to_all(blocks, ('pb', 'pool'), split_axis=0, concat_axis=0, tiled...  23.5 us
    ppermute x19, waiting for transfers between devices, shifts(): lax.ppermute(block, 'pool', [(j, moved(j)) for j in range(lax.axis_size('...  22.3 us
    all_to_all x2, waiting for transfers between devices, trade(): lax.all_to_all(blocks, ('pb', 'pool'), split_axis=0, concat_axis=0, tiled...  6.69 us
    pallas_call x1, Pallas kernels, weights(): pl.pallas_call(functools.partial(weights_kernel, chunk), out_shape=(pltpu...  3.31 us
    pallas_call x1, Pallas kernels, query_gradient(): pl.pallas_call(functools.partial(queries_kernel, chunk), out_shape=pltpu....  3.01 us
    concatenate x2, local copies, waits for them, and re-layouts, body(): jnp.concatenate([pooled] + [shifts(pooled, ((step, count, m),), -1) for m...  2.95 us
  transfers between devices with their start and end apart: 21, of which 10 were waited for; matrix products, arithmetic and copies ran while one was open for 3% of the time, Pallas kernels for 4%

profile of v9, /device:TPU:6, one launch (start us, length us, event | category | flops | bytes accessed | tf_op | source)
XLA Modules:
  0.0 139.6 jit_solution(11329329424612305036)
XLA Ops:
  0.6 2.6 %gather_tiles.1 = bf16[24,8,4096]{2,1,0:T(8,128)(2,1)} custom-call(s32[2,12]{1,0:T(2,128)} %bitcast.13, bf16[16,8,4096]{2,1,0:T(8,128)(2,1)} %bitcast.12), custom_call_target="tpu_custom_call" | custom-call | bytes 3145728 | tf_op jit(solution)/shard_map/gather_tiles/pallas_call | solution.py:85
  3.3 0.0 copy-start.7
  3.3 0.0 copy-start
  3.3 0.0 copy-start.4
  3.3 15.3 %all-to-all-start = ((bf16[12,16,4096]{2,1,0:T(8,128)(2,1)}), bf16[12,16,4096]{2,1,0:T(8,128)(2,1)S(1)}, u32[]{:S(2)}, u32[]{:S(2)}) async-start(bf16[12,16,4096]{2,1,0:T(8,128)(2,1)} %bitcast.17), calls=%async_computation | async-start | bytes 3145728 | tf_op jit(solution)/shard_map/all_to_all | solution.py:43
  18.6 3.5 %collective-permute-start.2 = (bf16[2,4096]{1,0:T(2,128)(2,1)S(1)}, bf16[2,4096]{1,0:T(2,128)(2,1)S(1)}, u32[]{:S(2)}, u32[]{:S(2)}) collective-permute-start(bf16[2,4096]{1,0:T(2,128)(2,1)S(1)} %copy-done.7), channel_id=1, source_target_pairs={{0,8},{1,9},{2,10},{3,11},{4,12},{5,13},{6,14},{7,15},{8,16},{9,17... | collective-permute-start | bytes 49160 | tf_op jit(solution)/shard_map/ppermute | solution.py:55
  22.1 4.5 %collective-permute-start.1 = (bf16[2,4096]{1,0:T(2,128)(2,1)S(1)}, bf16[2,4096]{1,0:T(2,128)(2,1)S(1)}, u32[]{:S(2)}, u32[]{:S(2)}) collective-permute-start(bf16[2,4096]{1,0:T(2,128)(2,1)S(1)} %copy-done.7), channel_id=1, source_target_pairs={{0,16},{1,17},{2,18},{3,19},{4,20},{5,21},{6,22},{7,23},{8,24},{9,... | collective-permute-start | bytes 49160 | tf_op jit(solution)/shard_map/ppermute | solution.py:55
  26.6 3.3 %collective-permute-start = (bf16[2,4096]{1,0:T(2,128)(2,1)S(1)}, bf16[2,4096]{1,0:T(2,128)(2,1)S(1)}, u32[]{:S(2)}, u32[]{:S(2)}) collective-permute-start(bf16[2,4096]{1,0:T(2,128)(2,1)S(1)} %copy-done.7), channel_id=1, source_target_pairs={{0,24},{1,25},{2,26},{3,27},{4,28},{5,29},{6,30},{7,31},{8,0},{9,1... | collective-permute-start | bytes 49160 | tf_op jit(solution)/shard_map/ppermute | solution.py:55
  29.9 0.0 collective-permute-done.2
  29.9 0.0 collective-permute-done.1
  29.9 2.3 %collective-permute-done = bf16[2,4096]{1,0:T(2,128)(2,1)S(1)} collective-permute-done((bf16[2,4096]{1,0:T(2,128)(2,1)S(1)}, bf16[2,4096]{1,0:T(2,128)(2,1)S(1)}, u32[]{:S(2)}, u32[]{:S(2)}) %collective-permute-start) | collective-permute-done | bytes 16416 | tf_op jit(solution)/shard_map/ppermute | solution.py:55
  32.3 0.1 pad_maximum_fusion
  32.3 5.9 %collective-permute-start.3 = (bf16[8,4096]{1,0:T(8,128)(2,1)S(1)}, bf16[8,4096]{1,0:T(8,128)(2,1)S(1)}, u32[]{:S(2)}, u32[]{:S(2)}) collective-permute-start(bf16[8,4096]{1,0:T(8,128)(2,1)S(1)} %pad_maximum_fusion), channel_id=1, source_target_pairs={{0,32},{1,33},{2,34},{3,35},{4,36},{5,37},{6,38},{7,39},{8,40},{9,... | collective-permute-start | bytes 196616 | tf_op jit(solution)/shard_map/ppermute | solution.py:55
  38.3 4.3 %collective-permute-done.3 = bf16[8,4096]{1,0:T(8,128)(2,1)S(1)} collective-permute-done((bf16[8,4096]{1,0:T(8,128)(2,1)S(1)}, bf16[8,4096]{1,0:T(8,128)(2,1)S(1)}, u32[]{:S(2)}, u32[]{:S(2)}) %collective-permute-start.3) | collective-permute-done | bytes 65568 | tf_op jit(solution)/shard_map/ppermute | solution.py:55
  42.6 0.1 concatenate.12
  42.7 2.4 %collective-permute-start.6 = (bf16[16,4096]{1,0:T(8,128)(2,1)S(1)}, bf16[16,4096]{1,0:T(8,128)(2,1)S(1)}, u32[]{:S(2)}, u32[]{:S(2)}) collective-permute-start(bf16[16,4096]{1,0:T(8,128)(2,1)S(1)} %concatenate.12), channel_id=1, source_target_pairs={{0,2},{1,3},{2,4},{3,5},{4,6},{5,7},{6,0},{7,1},{8,10},{9,11},{10,... | collective-permute-start | bytes 393224 | tf_op jit(solution)/shard_map/ppermute | solution.py:55
  45.1 4.3 %collective-permute-start.5 = (bf16[16,4096]{1,0:T(8,128)(2,1)S(1)}, bf16[16,4096]{1,0:T(8,128)(2,1)S(1)}, u32[]{:S(2)}, u32[]{:S(2)}) collective-permute-start(bf16[16,4096]{1,0:T(8,128)(2,1)S(1)} %concatenate.12), channel_id=1, source_target_pairs={{0,4},{1,5},{2,6},{3,7},{4,0},{5,1},{6,2},{7,3},{8,12},{9,13},{10,... | collective-permute-start | bytes 393224 | tf_op jit(solution)/shard_map/ppermute | solution.py:55
  49.4 1.9 %collective-permute-start.4 = (bf16[16,4096]{1,0:T(8,128)(2,1)S(1)}, bf16[16,4096]{1,0:T(8,128)(2,1)}, u32[]{:S(2)}, u32[]{:S(2)}) collective-permute-start(bf16[16,4096]{1,0:T(8,128)(2,1)S(1)} %concatenate.12), channel_id=1, source_target_pairs={{0,6},{1,7},{2,0},{3,1},{4,2},{5,3},{6,4},{7,5},{8,14},{9,15},{10,... | collective-permute-start | bytes 393224 | tf_op jit(solution)/shard_map/ppermute | solution.py:55
  51.4 0.0 copy-start.8
  51.4 3.1 %collective-permute-done.5 = bf16[16,4096]{1,0:T(8,128)(2,1)S(1)} collective-permute-done((bf16[16,4096]{1,0:T(8,128)(2,1)S(1)}, bf16[16,4096]{1,0:T(8,128)(2,1)S(1)}, u32[]{:S(2)}, u32[]{:S(2)}) %collective-permute-start.5) | collective-permute-done | bytes 131104 | tf_op jit(solution)/shard_map/ppermute | solution.py:55
  54.5 0.7 copy-done.9
  55.2 2.5 %collective-permute-done.4 = bf16[16,4096]{1,0:T(8,128)(2,1)} collective-permute-done((bf16[16,4096]{1,0:T(8,128)(2,1)S(1)}, bf16[16,4096]{1,0:T(8,128)(2,1)}, u32[]{:S(2)}, u32[]{:S(2)}) %collective-permute-start.4) | collective-permute-done | bytes 131104 | tf_op jit(solution)/shard_map/ppermute | solution.py:55
  57.6 2.8 %concatenate.13.keys_ref.pool_near_ref = bf16[64,4096]{1,0:T(8,128)(2,1)S(1)} concatenate(bf16[2,4096]{1,0:T(2,128)(2,1)S(1)} %copy-done.7, bf16[2,4096]{1,0:T(2,128)(2,1)S(1)} %collective-permute-done, bf16[2,4096]{1,0:T(2,128)(2,1)S(1)} %collective-permute-done.1, bf16[2,4096]{1,0:T(2,128)(2,1)S(1)} %collective-permute-done.2, bf16[8,4096]{1,0:T(8,128)(2,1)S(1)} %collective-permute-done.3, ...), dimensions={0} | concatenate | bytes 1048576 | tf_op jit(solution)/shard_map/concatenate | solution.py:367
  60.5 0.0 copy-start.2
  60.5 1.9 %collective-permute-start.7 = (bf16[64,4096]{1,0:T(8,128)(2,1)S(1)}, bf16[64,4096]{1,0:T(8,128)(2,1)S(1)}, u32[]{:S(2)}, u32[]{:S(2)}) collective-permute-start(bf16[64,4096]{1,0:T(8,128)(2,1)S(1)} %concatenate.13.keys_ref.pool_near_ref), channel_id=1, source_target_pairs={{0,1},{1,0},{2,3},{3,2},{4,5},{5,4},{6,7},{7,6},{8,9},{9,8},{10,11... | collective-permute-start | bytes 1572872 | tf_op jit(solution)/shard_map/ppermute | solution.py:55
  62.4 0.0 copy-start.1
  62.4 1.2 copy-done.1
  63.7 1.0 local_scores.1
  64.6 0.0 copy-start.5
  64.7 0.0 copy-start.6
  64.7 0.5 scores.2.near_ref
  65.2 0.0 collective-permute-done.7.keys_ref.pool_far_ref
  65.2 0.5 scores.3.far_ref
  65.7 0.8 copy-done.3
  66.5 5.6 %all-to-all-done = bf16[12,16,4096]{2,1,0:T(8,128)(2,1)S(1)} async-done(((bf16[12,16,4096]{2,1,0:T(8,128)(2,1)}), bf16[12,16,4096]{2,1,0:T(8,128)(2,1)S(1)}, u32[]{:S(2)}, u32[]{:S(2)}) %all-to-all-start) | async-done | bytes 1572896 | tf_op jit(solution)/shard_map/all_to_all | solution.py:43
  72.1 3.3 %weights.1 = (bf16[192,4096]{1,0:T(8,128)(2,1)}, bf16[128,128]{1,0:T(8,128)(2,1)S(1)}, bf16[64,128]{1,0:T(8,128)(2,1)S(1)}, bf16[64,128]{1,0:T(8,128)(2,1)S(1)}, bf16[192,128]{1,0:T(8,128)(2,1)S(1)}) custom-call(bf16[128,4096]{1,0:T(8,128)(2,1)S(1)} %copy-done, bf16[192,4096]{1,0:T(8,128)(2,1)S(1)} %bitcast.10, f32[128,128]{1,0:T(8,128)S(1)} %get-tuple-element.16.local_ref, ...), custom_call_target="tpu_custom_call" | custom-call | flops 1048576 | bytes 1048576 | tf_op jit(solution)/shard_map/weights/pallas_call | solution.py:194
  75.4 8.2 %all-to-all-start.1 = ((bf16[12,16,4096]{2,1,0:T(8,128)(2,1)}), bf16[12,16,4096]{2,1,0:T(8,128)(2,1)}, u32[]{:S(2)}, u32[]{:S(2)}) async-start(bf16[12,16,4096]{2,1,0:T(8,128)(2,1)} %bitcast.18), calls=%async_computation.1 | async-start | bytes 3145728 | tf_op jit(solution)/shard_map/all_to_all | solution.py:43
  83.6 0.4 pool_terms.1
  84.1 1.9 %collective-permute-start.8 = (f32[64,4096]{1,0:T(8,128)S(1)}, f32[64,4096]{1,0:T(8,128)S(1)}, u32[]{:S(2)}, u32[]{:S(2)}) collective-permute-start(f32[64,4096]{1,0:T(8,128)S(1)} %get-tuple-element.24), channel_id=1, source_target_pairs={{0,1},{1,0},{2,3},{3,2},{4,5},{5,4},{6,7},{7,6},{8,9},{9,8},{10,11... | collective-permute-start | bytes 3145736 | tf_op jit(solution)/shard_map/ppermute | solution.py:55
  86.0 2.6 %collective-permute-done.8.sent_ref = f32[64,4096]{1,0:T(8,128)S(1)} collective-permute-done((f32[64,4096]{1,0:T(8,128)S(1)}, f32[64,4096]{1,0:T(8,128)S(1)}, u32[]{:S(2)}, u32[]{:S(2)}) %collective-permute-start.8) | collective-permute-done | bytes 1048608 | tf_op jit(solution)/shard_map/ppermute | solution.py:55
  88.6 0.1 join.1
  88.7 2.4 %collective-permute-start.9 = (bf16[16,4096]{1,0:T(8,128)(2,1)S(1)}, bf16[16,4096]{1,0:T(8,128)(2,1)S(1)}, u32[]{:S(2)}, u32[]{:S(2)}) collective-permute-start(bf16[16,4096]{1,0:T(8,128)(2,1)S(1)} %get-tuple-element.26), channel_id=1, source_target_pairs={{0,2},{1,3},{2,4},{3,5},{4,6},{5,7},{6,0},{7,1},{8,10},{9,11},{10,... | collective-permute-start | bytes 393224 | tf_op jit(solution)/shard_map/ppermute | solution.py:55
  91.1 4.3 %collective-permute-start.10 = (bf16[16,4096]{1,0:T(8,128)(2,1)S(1)}, bf16[16,4096]{1,0:T(8,128)(2,1)S(1)}, u32[]{:S(2)}, u32[]{:S(2)}) collective-permute-start(bf16[16,4096]{1,0:T(8,128)(2,1)S(1)} %get-tuple-element.27), channel_id=1, source_target_pairs={{0,4},{1,5},{2,6},{3,7},{4,0},{5,1},{6,2},{7,3},{8,12},{9,13},{10,... | collective-permute-start | bytes 393224 | tf_op jit(solution)/shard_map/ppermute | solution.py:55
  95.5 1.9 %collective-permute-start.11 = (bf16[16,4096]{1,0:T(8,128)(2,1)S(1)}, bf16[16,4096]{1,0:T(8,128)(2,1)S(1)}, u32[]{:S(2)}, u32[]{:S(2)}) collective-permute-start(bf16[16,4096]{1,0:T(8,128)(2,1)S(1)} %get-tuple-element.28), channel_id=1, source_target_pairs={{0,6},{1,7},{2,0},{3,1},{4,2},{5,3},{6,4},{7,5},{8,14},{9,15},{10,... | collective-permute-start | bytes 393224 | tf_op jit(solution)/shard_map/ppermute | solution.py:55
  97.4 0.0 collective-permute-done.9
  97.4 2.4 %collective-permute-done.10 = bf16[16,4096]{1,0:T(8,128)(2,1)S(1)} collective-permute-done((bf16[16,4096]{1,0:T(8,128)(2,1)S(1)}, bf16[16,4096]{1,0:T(8,128)(2,1)S(1)}, u32[]{:S(2)}, u32[]{:S(2)}) %collective-permute-start.10) | collective-permute-done | bytes 131104 | tf_op jit(solution)/shard_map/ppermute | solution.py:55
  99.8 3.8 %collective-permute-done.11 = bf16[16,4096]{1,0:T(8,128)(2,1)S(1)} collective-permute-done((bf16[16,4096]{1,0:T(8,128)(2,1)S(1)}, bf16[16,4096]{1,0:T(8,128)(2,1)S(1)}, u32[]{:S(2)}, u32[]{:S(2)}) %collective-permute-start.11) | collective-permute-done | bytes 131104 | tf_op jit(solution)/shard_map/ppermute | solution.py:55
  103.5 0.1 convert_add_fusion
  103.6 0.1 fusion.5
  103.7 3.5 %collective-permute-start.12 = (f32[2,4096]{1,0:T(2,128)S(1)}, f32[2,4096]{1,0:T(2,128)S(1)}, u32[]{:S(2)}, u32[]{:S(2)}) collective-permute-start(f32[2,4096]{1,0:T(2,128)S(1)} %get-tuple-element.29), channel_id=1, source_target_pairs={{0,8},{1,9},{2,10},{3,11},{4,12},{5,13},{6,14},{7,15},{8,16},{9,17... | collective-permute-start | bytes 98312 | tf_op jit(solution)/shard_map/ppermute | solution.py:55
  107.2 6.7 %collective-permute-start.18 = (f32[2,4096]{1,0:T(2,128)S(1)}, f32[2,4096]{1,0:T(2,128)S(1)}, u32[]{:S(2)}, u32[]{:S(2)}) collective-permute-start(f32[2,4096]{1,0:T(2,128)S(1)} %get-tuple-element.30), channel_id=1, source_target_pairs={{0,56},{1,57},{2,58},{3,59},{4,60},{5,61},{6,62},{7,63},{8,32},{9,... | collective-permute-start | bytes 98312 | tf_op jit(solution)/shard_map/ppermute | solution.py:55
  113.9 2.2 %collective-permute-start.17 = (f32[2,4096]{1,0:T(2,128)S(1)}, f32[2,4096]{1,0:T(2,128)S(1)}, u32[]{:S(2)}, u32[]{:S(2)}) collective-permute-start(f32[2,4096]{1,0:T(2,128)S(1)} %get-tuple-element.31), channel_id=1, source_target_pairs={{0,48},{1,49},{2,50},{3,51},{4,52},{5,53},{6,54},{7,55},{8,56},{9,... | collective-permute-start | bytes 98312 | tf_op jit(solution)/shard_map/ppermute | solution.py:55
  116.2 5.2 %collective-permute-start.16 = (f32[2,4096]{1,0:T(2,128)S(1)}, f32[2,4096]{1,0:T(2,128)S(1)}, u32[]{:S(2)}, u32[]{:S(2)}) collective-permute-start(f32[2,4096]{1,0:T(2,128)S(1)} %get-tuple-element.32), channel_id=1, source_target_pairs={{0,40},{1,41},{2,42},{3,43},{4,44},{5,45},{6,46},{7,47},{8,48},{9,... | collective-permute-start | bytes 98312 | tf_op jit(solution)/shard_map/ppermute | solution.py:55
  121.3 4.7 %collective-permute-start.15 = (f32[2,4096]{1,0:T(2,128)S(1)}, f32[2,4096]{1,0:T(2,128)S(1)}, u32[]{:S(2)}, u32[]{:S(2)}) collective-permute-start(f32[2,4096]{1,0:T(2,128)S(1)} %get-tuple-element.33), channel_id=1, source_target_pairs={{0,32},{1,33},{2,34},{3,35},{4,36},{5,37},{6,38},{7,39},{8,40},{9,... | collective-permute-start | bytes 98312 | tf_op jit(solution)/shard_map/ppermute | solution.py:55
  126.1 0.0 collective-permute-done.12
  126.1 2.4 %collective-permute-start.14 = (f32[2,4096]{1,0:T(2,128)S(1)}, f32[2,4096]{1,0:T(2,128)S(1)}, u32[]{:S(2)}, u32[]{:S(2)}) collective-permute-start(f32[2,4096]{1,0:T(2,128)S(1)} %get-tuple-element.34), channel_id=1, source_target_pairs={{0,24},{1,25},{2,26},{3,27},{4,28},{5,29},{6,30},{7,31},{8,0},{9,1... | collective-permute-start | bytes 98312 | tf_op jit(solution)/shard_map/ppermute | solution.py:55
  128.4 0.0 collective-permute-done.18
  128.4 2.4 %collective-permute-start.13 = (f32[2,4096]{1,0:T(2,128)S(1)}, f32[2,4096]{1,0:T(2,128)S(1)}, u32[]{:S(2)}, u32[]{:S(2)}) collective-permute-start(f32[2,4096]{1,0:T(2,128)S(1)} %get-tuple-element.35), channel_id=1, source_target_pairs={{0,16},{1,17},{2,18},{3,19},{4,20},{5,21},{6,22},{7,23},{8,24},{9,... | collective-permute-start | bytes 98312 | tf_op jit(solution)/shard_map/ppermute | solution.py:55
  130.8 3.0 %query_gradient.1 = bf16[128,4096]{1,0:T(8,128)(2,1)} custom-call(bf16[192,128]{1,0:T(8,128)(2,1)S(1)} %get-tuple-element.17.hard_weight_ref, bf16[128,128]{1,0:T(8,128)(2,1)S(1)} %get-tuple-element.18.local_ref.weight_ref, bf16[64,128]{1,0:T(8,128)(2,1)S(1)} %get-tuple-element.19.near_ref, bf16[64,128]{1,0:T(8,128)(2,1)S(1)} %get-tuple-element.20.far_ref, ...), custom_call_target="tpu_custom_call" | custom-call | flops 1048576 | bytes 1048576 | tf_op jit(solution)/shard_map/query_gradient/pallas_call | solution.py:291
  133.8 0.0 collective-permute-done.17
  133.9 1.3 collective-permute-done.13
  135.1 0.7 add_convert_fusion
  135.8 1.1 all-to-all-done.1
  136.9 2.7 %passage_gradient.1 = bf16[128,4096]{1,0:T(8,128)(2,1)} custom-call(bf16[128,128]{1,0:T(8,128)(2,1)S(1)} %get-tuple-element.18.local_ref.weight_ref, bf16[128,4096]{1,0:T(8,128)(2,1)S(1)} %copy-done, bf16[128,192]{1,0:T(8,128)(2,1)S(1)} %get-tuple-element.21.chosen_ref, bf16[192,4096]{1,0:T(8,128)(2,1)} %bitcast.9.returned_ref), custom_call_target="tpu_custom_call" | custom-call | flops 1048576 | bytes 1048576 | tf_op jit(solution)/shard_map/passage_gradient/pallas_call | solution.py:341
  (13 shorter events, 0.0 us)
Async XLA Ops:
  3.3 15.3 %copy-start.7 = (bf16[2,4096]{1,0:T(2,128)(2,1)S(1)}, bf16[2,4096]{1,0:T(2,128)(2,1)}, u32[]{:S(2)}) copy-start(bf16[2,4096]{1,0:T(2,128)(2,1)} %param.8) | copy-start | bytes 49156
  3.3 59.1 %copy-start = (bf16[128,4096]{1,0:T(8,128)(2,1)S(1)}, bf16[128,4096]{1,0:T(8,128)(2,1)}, u32[]{:S(2)}) copy-start(bf16[128,4096]{1,0:T(8,128)(2,1)} %queries_ref.11) | copy-start | bytes 3145732
  3.3 59.1 %copy-start.4 = (s32[1,1,12,2]{2,3,1,0:T(2,128)S(1)}, s32[1,1,12,2]{2,3,1,0:T(2,128)}, u32[]{:S(2)}) copy-start(s32[1,1,12,2]{2,3,1,0:T(2,128)} %param.10) | copy-start | bytes 292
  3.3 68.8 %all-to-all-start = ((bf16[12,16,4096]{2,1,0:T(8,128)(2,1)}), bf16[12,16,4096]{2,1,0:T(8,128)(2,1)S(1)}, u32[]{:S(2)}, u32[]{:S(2)}) async-start(bf16[12,16,4096]{2,1,0:T(8,128)(2,1)} %bitcast.17), calls=%async_computation | async-start | bytes 3145728 | tf_op jit(solution)/shard_map/all_to_all | solution.py:43
  18.6 11.3 %collective-permute-start.2 = (bf16[2,4096]{1,0:T(2,128)(2,1)S(1)}, bf16[2,4096]{1,0:T(2,128)(2,1)S(1)}, u32[]{:S(2)}, u32[]{:S(2)}) collective-permute-start(bf16[2,4096]{1,0:T(2,128)(2,1)S(1)} %copy-done.7), channel_id=1, source_target_pairs={{0,8},{1,9},{2,10},{3,11},{4,12},{5,13},{6,14},{7,15},{8,16},{9,17... | collective-permute-start | bytes 49160 | tf_op jit(solution)/shard_map/ppermute | solution.py:55
  22.1 7.8 %collective-permute-start.1 = (bf16[2,4096]{1,0:T(2,128)(2,1)S(1)}, bf16[2,4096]{1,0:T(2,128)(2,1)S(1)}, u32[]{:S(2)}, u32[]{:S(2)}) collective-permute-start(bf16[2,4096]{1,0:T(2,128)(2,1)S(1)} %copy-done.7), channel_id=1, source_target_pairs={{0,16},{1,17},{2,18},{3,19},{4,20},{5,21},{6,22},{7,23},{8,24},{9,... | collective-permute-start | bytes 49160 | tf_op jit(solution)/shard_map/ppermute | solution.py:55
  26.6 5.6 %collective-permute-start = (bf16[2,4096]{1,0:T(2,128)(2,1)S(1)}, bf16[2,4096]{1,0:T(2,128)(2,1)S(1)}, u32[]{:S(2)}, u32[]{:S(2)}) collective-permute-start(bf16[2,4096]{1,0:T(2,128)(2,1)S(1)} %copy-done.7), channel_id=1, source_target_pairs={{0,24},{1,25},{2,26},{3,27},{4,28},{5,29},{6,30},{7,31},{8,0},{9,1... | collective-permute-start | bytes 49160 | tf_op jit(solution)/shard_map/ppermute | solution.py:55
  32.3 10.3 %collective-permute-start.3 = (bf16[8,4096]{1,0:T(8,128)(2,1)S(1)}, bf16[8,4096]{1,0:T(8,128)(2,1)S(1)}, u32[]{:S(2)}, u32[]{:S(2)}) collective-permute-start(bf16[8,4096]{1,0:T(8,128)(2,1)S(1)} %pad_maximum_fusion), channel_id=1, source_target_pairs={{0,32},{1,33},{2,34},{3,35},{4,36},{5,37},{6,38},{7,39},{8,40},{9,... | collective-permute-start | bytes 196616 | tf_op jit(solution)/shard_map/ppermute | solution.py:55
  42.7 8.7 %collective-permute-start.6 = (bf16[16,4096]{1,0:T(8,128)(2,1)S(1)}, bf16[16,4096]{1,0:T(8,128)(2,1)S(1)}, u32[]{:S(2)}, u32[]{:S(2)}) collective-permute-start(bf16[16,4096]{1,0:T(8,128)(2,1)S(1)} %concatenate.12), channel_id=1, source_target_pairs={{0,2},{1,3},{2,4},{3,5},{4,6},{5,7},{6,0},{7,1},{8,10},{9,11},{10,... | collective-permute-start | bytes 393224 | tf_op jit(solution)/shard_map/ppermute | solution.py:55
  45.1 9.4 %collective-permute-start.5 = (bf16[16,4096]{1,0:T(8,128)(2,1)S(1)}, bf16[16,4096]{1,0:T(8,128)(2,1)S(1)}, u32[]{:S(2)}, u32[]{:S(2)}) collective-permute-start(bf16[16,4096]{1,0:T(8,128)(2,1)S(1)} %concatenate.12), channel_id=1, source_target_pairs={{0,4},{1,5},{2,6},{3,7},{4,0},{5,1},{6,2},{7,3},{8,12},{9,13},{10,... | collective-permute-start | bytes 393224 | tf_op jit(solution)/shard_map/ppermute | solution.py:55
  49.4 8.2 %collective-permute-start.4 = (bf16[16,4096]{1,0:T(8,128)(2,1)S(1)}, bf16[16,4096]{1,0:T(8,128)(2,1)}, u32[]{:S(2)}, u32[]{:S(2)}) collective-permute-start(bf16[16,4096]{1,0:T(8,128)(2,1)S(1)} %concatenate.12), channel_id=1, source_target_pairs={{0,6},{1,7},{2,0},{3,1},{4,2},{5,3},{6,4},{7,5},{8,14},{9,15},{10,... | collective-permute-start | bytes 393224 | tf_op jit(solution)/shard_map/ppermute | solution.py:55
  51.4 3.1 %copy-start.8 = (bf16[16,4096]{1,0:T(8,128)(2,1)}, bf16[16,4096]{1,0:T(8,128)(2,1)S(1)}, u32[]{:S(2)}) copy-start(bf16[16,4096]{1,0:T(8,128)(2,1)S(1)} %collective-permute-done.6) | copy-start | bytes 393220
  54.5 0.7 copy-start.9
  60.5 4.7 %copy-start.2 = (bf16[64,4096]{1,0:T(8,128)(2,1)}, bf16[64,4096]{1,0:T(8,128)(2,1)S(1)}, u32[]{:S(2)}) copy-start(bf16[64,4096]{1,0:T(8,128)(2,1)S(1)} %concatenate.13.keys_ref.pool_near_ref) | copy-start | bytes 1572868
  60.5 4.7 %collective-permute-start.7 = (bf16[64,4096]{1,0:T(8,128)(2,1)S(1)}, bf16[64,4096]{1,0:T(8,128)(2,1)S(1)}, u32[]{:S(2)}, u32[]{:S(2)}) collective-permute-start(bf16[64,4096]{1,0:T(8,128)(2,1)S(1)} %concatenate.13.keys_ref.pool_near_ref), channel_id=1, source_target_pairs={{0,1},{1,0},{2,3},{3,2},{4,5},{5,4},{6,7},{7,6},{8,9},{9,8},{10,11... | collective-permute-start | bytes 1572872 | tf_op jit(solution)/shard_map/ppermute | solution.py:55
  62.4 1.2 copy-start.1
  64.6 7.5 %copy-start.5 = (s32[1,1,12]{2,1,0:T(1,128)S(1)}, s32[1,1,12]{2,1,0:T(1,128)}, u32[]{:S(2)}) copy-start(s32[1,1,12]{2,1,0:T(1,128)} %param.11) | copy-start | bytes 148
  64.7 7.5 %copy-start.6 = (s32[128]{0:T(128)S(1)}, s32[128]{0:T(128)}, u32[]{:S(2)}) copy-start(s32[128]{0:T(128)} %param.9) | copy-start | bytes 1540
  65.7 0.8 copy-start.3
  75.4 61.4 %all-to-all-start.1 = ((bf16[12,16,4096]{2,1,0:T(8,128)(2,1)}), bf16[12,16,4096]{2,1,0:T(8,128)(2,1)}, u32[]{:S(2)}, u32[]{:S(2)}) async-start(bf16[12,16,4096]{2,1,0:T(8,128)(2,1)} %bitcast.18), calls=%async_computation.1 | async-start | bytes 3145728 | tf_op jit(solution)/shard_map/all_to_all | solution.py:43
  84.1 4.6 %collective-permute-start.8 = (f32[64,4096]{1,0:T(8,128)S(1)}, f32[64,4096]{1,0:T(8,128)S(1)}, u32[]{:S(2)}, u32[]{:S(2)}) collective-permute-start(f32[64,4096]{1,0:T(8,128)S(1)} %get-tuple-element.24), channel_id=1, source_target_pairs={{0,1},{1,0},{2,3},{3,2},{4,5},{5,4},{6,7},{7,6},{8,9},{9,8},{10,11... | collective-permute-start | bytes 3145736 | tf_op jit(solution)/shard_map/ppermute | solution.py:55
  88.7 8.7 %collective-permute-start.9 = (bf16[16,4096]{1,0:T(8,128)(2,1)S(1)}, bf16[16,4096]{1,0:T(8,128)(2,1)S(1)}, u32[]{:S(2)}, u32[]{:S(2)}) collective-permute-start(bf16[16,4096]{1,0:T(8,128)(2,1)S(1)} %get-tuple-element.26), channel_id=1, source_target_pairs={{0,2},{1,3},{2,4},{3,5},{4,6},{5,7},{6,0},{7,1},{8,10},{9,11},{10,... | collective-permute-start | bytes 393224 | tf_op jit(solution)/shard_map/ppermute | solution.py:55
  91.1 8.7 %collective-permute-start.10 = (bf16[16,4096]{1,0:T(8,128)(2,1)S(1)}, bf16[16,4096]{1,0:T(8,128)(2,1)S(1)}, u32[]{:S(2)}, u32[]{:S(2)}) collective-permute-start(bf16[16,4096]{1,0:T(8,128)(2,1)S(1)} %get-tuple-element.27), channel_id=1, source_target_pairs={{0,4},{1,5},{2,6},{3,7},{4,0},{5,1},{6,2},{7,3},{8,12},{9,13},{10,... | collective-permute-start | bytes 393224 | tf_op jit(solution)/shard_map/ppermute | solution.py:55
  95.5 8.1 %collective-permute-start.11 = (bf16[16,4096]{1,0:T(8,128)(2,1)S(1)}, bf16[16,4096]{1,0:T(8,128)(2,1)S(1)}, u32[]{:S(2)}, u32[]{:S(2)}) collective-permute-start(bf16[16,4096]{1,0:T(8,128)(2,1)S(1)} %get-tuple-element.28), channel_id=1, source_target_pairs={{0,6},{1,7},{2,0},{3,1},{4,2},{5,3},{6,4},{7,5},{8,14},{9,15},{10,... | collective-permute-start | bytes 393224 | tf_op jit(solution)/shard_map/ppermute | solution.py:55
  103.7 22.4 %collective-permute-start.12 = (f32[2,4096]{1,0:T(2,128)S(1)}, f32[2,4096]{1,0:T(2,128)S(1)}, u32[]{:S(2)}, u32[]{:S(2)}) collective-permute-start(f32[2,4096]{1,0:T(2,128)S(1)} %get-tuple-element.29), channel_id=1, source_target_pairs={{0,8},{1,9},{2,10},{3,11},{4,12},{5,13},{6,14},{7,15},{8,16},{9,17... | collective-permute-start | bytes 98312 | tf_op jit(solution)/shard_map/ppermute | solution.py:55
  107.2 21.2 %collective-permute-start.18 = (f32[2,4096]{1,0:T(2,128)S(1)}, f32[2,4096]{1,0:T(2,128)S(1)}, u32[]{:S(2)}, u32[]{:S(2)}) collective-permute-start(f32[2,4096]{1,0:T(2,128)S(1)} %get-tuple-element.30), channel_id=1, source_target_pairs={{0,56},{1,57},{2,58},{3,59},{4,60},{5,61},{6,62},{7,63},{8,32},{9,... | collective-permute-start | bytes 98312 | tf_op jit(solution)/shard_map/ppermute | solution.py:55
  113.9 19.9 %collective-permute-start.17 = (f32[2,4096]{1,0:T(2,128)S(1)}, f32[2,4096]{1,0:T(2,128)S(1)}, u32[]{:S(2)}, u32[]{:S(2)}) collective-permute-start(f32[2,4096]{1,0:T(2,128)S(1)} %get-tuple-element.31), channel_id=1, source_target_pairs={{0,48},{1,49},{2,50},{3,51},{4,52},{5,53},{6,54},{7,55},{8,56},{9,... | collective-permute-start | bytes 98312 | tf_op jit(solution)/shard_map/ppermute | solution.py:55
  116.2 17.7 %collective-permute-start.16 = (f32[2,4096]{1,0:T(2,128)S(1)}, f32[2,4096]{1,0:T(2,128)S(1)}, u32[]{:S(2)}, u32[]{:S(2)}) collective-permute-start(f32[2,4096]{1,0:T(2,128)S(1)} %get-tuple-element.32), channel_id=1, source_target_pairs={{0,40},{1,41},{2,42},{3,43},{4,44},{5,45},{6,46},{7,47},{8,48},{9,... | collective-permute-start | bytes 98312 | tf_op jit(solution)/shard_map/ppermute | solution.py:55
  121.3 12.5 %collective-permute-start.15 = (f32[2,4096]{1,0:T(2,128)S(1)}, f32[2,4096]{1,0:T(2,128)S(1)}, u32[]{:S(2)}, u32[]{:S(2)}) collective-permute-start(f32[2,4096]{1,0:T(2,128)S(1)} %get-tuple-element.33), channel_id=1, source_target_pairs={{0,32},{1,33},{2,34},{3,35},{4,36},{5,37},{6,38},{7,39},{8,40},{9,... | collective-permute-start | bytes 98312 | tf_op jit(solution)/shard_map/ppermute | solution.py:55
  126.1 7.8 %collective-permute-start.14 = (f32[2,4096]{1,0:T(2,128)S(1)}, f32[2,4096]{1,0:T(2,128)S(1)}, u32[]{:S(2)}, u32[]{:S(2)}) collective-permute-start(f32[2,4096]{1,0:T(2,128)S(1)} %get-tuple-element.34), channel_id=1, source_target_pairs={{0,24},{1,25},{2,26},{3,27},{4,28},{5,29},{6,30},{7,31},{8,0},{9,1... | collective-permute-start | bytes 98312 | tf_op jit(solution)/shard_map/ppermute | solution.py:55
  128.4 6.7 %collective-permute-start.13 = (f32[2,4096]{1,0:T(2,128)S(1)}, f32[2,4096]{1,0:T(2,128)S(1)}, u32[]{:S(2)}, u32[]{:S(2)}) collective-permute-start(f32[2,4096]{1,0:T(2,128)S(1)} %get-tuple-element.35), channel_id=1, source_target_pairs={{0,16},{1,17},{2,18},{3,19},{4,20},{5,21},{6,22},{7,23},{8,24},{9,... | collective-permute-start | bytes 98312 | tf_op jit(solution)/shard_map/ppermute | solution.py:55
